TPU v7x, 32 devices: a whole 2x2x4 slice. The times are simulated.
32 devices in a mesh: fsdp: 2 (over x), ctx: 4 (over y, core), tensor: 4 (over z).
Axes of the slice: x: 2, y: 2, z: 4, core: 2. Of those that a mesh axis runs over, the one named last changes fastest.
Arguments:
- prompt_in: bfloat16 [8, 2048, 1088], P(('fsdp', 'tensor'), 'ctx'), may hold values from -6 to 6
- cont_in: bfloat16 [8, 1536, 1088], P(('fsdp', 'tensor'), 'ctx'), may hold values from -6 to 6
- cont_seg: int32 [8, 1536], P(('fsdp', 'tensor')), may hold values from 0 to 4, never falling along the last dimension, each value on 1 to 384 neighbouring positions
- ln1_gain: float32 [1088], replicated, may hold values from 0.1 to 1.9
- ln1_bias: float32 [1088], replicated, may hold values from -3 to 3
- w_qkv: float32 [1088, 3264], P('fsdp'), may hold values from -0.1875 to 0.1875
- qv_bias: float32 [2, 1088], replicated, may hold values from -3 to 3
- w_out: float32 [1088, 1088], P('fsdp'), may hold values from -1.5 to 1.5
- out_bias: float32 [1088], replicated, may hold values from -3 to 3
- ln2_gain: float32 [1088], replicated, may hold values from 0.1 to 1.9
- ln2_bias: float32 [1088], replicated, may hold values from -3 to 3
- w_fc: float32 [1088, 4352], P('fsdp', 'tensor'), may hold values from -0.1875 to 0.1875
- fc_bias: float32 [4352], P('tensor'), may hold values from -3 to 3
- w_proj: float32 [4352, 1088], P('tensor', 'fsdp'), may hold values from -0.09375 to 0.09375
- proj_bias: float32 [1088], replicated, may hold values from -3 to 3
- prompt_cot: bfloat16 [8, 2048, 1088], P(('fsdp', 'tensor'), 'ctx'), may hold values from -6 to 6
- cont_cot: bfloat16 [8, 1536, 1088], P(('fsdp', 'tensor'), 'ctx'), may hold values from -6 to 6
Outputs:
- prompt_out: bfloat16 [8, 2048, 1088], P(('fsdp', 'tensor'), 'ctx')
- cont_out: bfloat16 [8, 1536, 1088], P(('fsdp', 'tensor'), 'ctx')
- prompt_grad: bfloat16 [8, 2048, 1088], P(('fsdp', 'tensor'), 'ctx')
- cont_grad: bfloat16 [8, 1536, 1088], P(('fsdp', 'tensor'), 'ctx')
- grad_ln1_gain: float32 [1088], replicated
- grad_ln1_bias: float32 [1088], replicated
- grad_w_qkv: float32 [1088, 3264], P('fsdp')
- grad_qv_bias: float32 [2, 1088], replicated
- grad_w_out: float32 [1088, 1088], P('fsdp')
- grad_out_bias: float32 [1088], replicated
- grad_ln2_gain: float32 [1088], replicated
- grad_ln2_bias: float32 [1088], replicated
- grad_w_fc: float32 [1088, 4352], P('fsdp', 'tensor')
- grad_fc_bias: float32 [4352], P('tensor')
- grad_w_proj: float32 [4352, 1088], P('tensor', 'fsdp')
- grad_proj_bias: float32 [1088], replicated
Inputs may be any that keep to these rules, and one draw needn't show every extreme that they name: `cont_seg`: in each group the numbers never fall along the tokens; each continuation is 1 to 384 consecutive tokens, one exactly 384.
All inputs are finite; a program needn't handle non-finite values.
Results may differ from a plain program's by a relative error of at most 0.012.
The roundings to bfloat16 on the way count: a program that leaves them out, or rounds other values in their place, can miss the bound.
Values may be sent and summed in bfloat16 or wider, within the bound.
A program may use at most 320 MiB of HBM per device.

v0:
```python
import jax
import jax.numpy as jnp
from jax import lax
from jax.sharding import PartitionSpec as P

HEADS = 17
HEAD = 64


def passed_along(value, axis, steps):
    count = lax.axis_size(axis)
    leading, last = (max(0, -steps), min(count, count - steps))
    return lax.ppermute(value, axis, [(source, source + steps) for source in range(leading, last)])


def layer_norm(values, norm_gain, norm_bias):
    average = jnp.mean(values, axis=-1, keepdims=True)
    centred = values - average
    variance = jnp.mean(centred * centred, axis=-1, keepdims=True)
    return centred * lax.rsqrt(variance + 1e-05) * norm_gain + norm_bias


def gelu_tanh(values):
    return jax.nn.gelu(values, approximate=True)


def inner_first(left_op, right_op):
    return lax.dot_general(
        left_op, right_op, (((0,), (0,)), ((), ())), preferred_element_type=jnp.float32
    )


def inner_last(left_op, right_op):
    return lax.dot_general(
        left_op, right_op, (((1,), (1,)), ((), ())), preferred_element_type=jnp.float32
    )


def to_heads(values):
    return jnp.swapaxes(values.reshape(values.shape[0], HEADS, HEAD), 0, 1)


def from_heads(values):
    return jnp.swapaxes(values, 0, 1).reshape(values.shape[1], values.shape[0] * values.shape[2])


def fetch_prompt(rows_kv):
    return lax.all_gather(rows_kv, "ctx", axis=0, tiled=True)


def local(
    prompt_in,
    cont_in,
    cont_seg,
    ln1_gain,
    ln1_bias,
    w_qkv,
    qv_bias,
    w_out,
    out_bias,
    ln2_gain,
    ln2_bias,
    w_fc,
    fc_bias,
    w_proj,
    proj_bias,
    prompt_cot,
    cont_cot,
):
    model_width = prompt_in.shape[2]
    prompt_rows = prompt_in.shape[1]
    cont_rows = cont_in.shape[1]
    row_count = prompt_rows + cont_rows
    ctx_count = lax.axis_size("ctx")
    ctx_place = lax.axis_index("ctx")
    prompt_total = prompt_rows * ctx_count
    qkv_full, out_full = (
        lax.all_gather(w_qkv.astype(jnp.bfloat16), "fsdp", axis=0, tiled=True),
        lax.all_gather(w_out.astype(jnp.bfloat16), "fsdp", axis=0, tiled=True),
    )
    fc_full, proj_full = (
        lax.all_gather(w_fc.astype(jnp.bfloat16), "fsdp", axis=0, tiled=True),
        lax.all_gather(w_proj.astype(jnp.bfloat16), "fsdp", axis=1, tiled=True),
    )
    row_ids = jnp.arange(row_count, dtype=jnp.int32)
    labels_all = cont_seg[0]
    own_labels = lax.dynamic_slice_in_dim(labels_all, ctx_place * cont_rows, cont_rows)
    earlier_labels = lax.dynamic_slice_in_dim(
        labels_all, jnp.maximum(ctx_place - 1, 0) * cont_rows, cont_rows
    )
    query_labels = jnp.concatenate([jnp.full((prompt_rows,), -1, jnp.int32), own_labels])
    query_prompt = ctx_place * prompt_rows + row_ids
    query_cont = ctx_place * cont_rows + row_ids - prompt_rows
    is_cont = row_ids >= prompt_rows
    prompt_ids = jnp.arange(prompt_total, dtype=jnp.int32)
    near_ids = (ctx_place - 1) * cont_rows + jnp.arange(2 * cont_rows, dtype=jnp.int32)
    near_labels = jnp.concatenate([earlier_labels, own_labels])
    allowed_far = is_cont[:, None] | (prompt_ids[None, :] <= query_prompt[:, None])
    allowed_near = (
        (query_labels[:, None] == near_labels[None, :])
        & (near_ids[None, :] <= query_cont[:, None])
        & (near_ids[None, :] >= 0)
    )
    allowed = jnp.concatenate([allowed_far, allowed_near], 1)
    inputs = jnp.concatenate([prompt_in[0], cont_in[0]], 0).astype(jnp.float32)
    normed, norm1_back = jax.vjp(layer_norm, inputs, ln1_gain, ln1_bias)
    normed_low = normed.astype(jnp.bfloat16)
    projected = jnp.dot(normed_low, qkv_full, preferred_element_type=jnp.float32)
    queries = (projected[:, :model_width] + qv_bias[0]).astype(jnp.bfloat16)
    key_value = jnp.concatenate(
        [projected[:, model_width : 2 * model_width], projected[:, 2 * model_width :] + qv_bias[1]],
        1,
    ).astype(jnp.bfloat16)
    own_cont_kv = key_value[prompt_rows:]
    earlier_kv = passed_along(own_cont_kv, "ctx", 1)
    prompt_kv = fetch_prompt(key_value[:prompt_rows])
    keys_all = jnp.concatenate([prompt_kv, earlier_kv, own_cont_kv], 0)
    query_heads = to_heads(queries)
    key_heads = to_heads(keys_all[:, :model_width])
    value_heads = to_heads(keys_all[:, model_width:])

    def head_forward(operands):
        query_head, key_head, value_head = operands
        scores = inner_last(query_head, key_head) * 0.125
        scores = jnp.where(allowed, scores, -1e30)
        row_max = jnp.max(scores, axis=1, keepdims=True)
        exponent = jnp.exp(scores - row_max)
        row_total = jnp.sum(exponent, axis=1, keepdims=True)
        probability = (exponent / row_total).astype(jnp.bfloat16)
        head_out = jnp.dot(probability, value_head, preferred_element_type=jnp.float32)
        return (head_out.astype(jnp.bfloat16), (row_max + jnp.log(row_total))[:, 0])

    heads_out, logsum = lax.map(head_forward, (query_heads, key_heads, value_heads))
    attended = from_heads(heads_out)
    hidden = inputs + jnp.dot(attended, out_full, preferred_element_type=jnp.float32) + out_bias
    mlp_in, norm2_back = jax.vjp(layer_norm, hidden, ln2_gain, ln2_bias)
    mlp_low = mlp_in.astype(jnp.bfloat16)
    mlp_rows = lax.all_gather(mlp_low, "tensor", axis=0, tiled=True)
    pre_act = jnp.dot(mlp_rows, fc_full, preferred_element_type=jnp.float32) + fc_bias
    activated, gelu_back = jax.vjp(gelu_tanh, pre_act)
    act_low = activated.astype(jnp.bfloat16)
    partial_out = jnp.dot(act_low, proj_full, preferred_element_type=jnp.float32)
    mlp_out = lax.psum_scatter(
        partial_out.astype(jnp.bfloat16), "tensor", scatter_dimension=0, tiled=True
    ).astype(jnp.float32)
    layer_out = (hidden + mlp_out + proj_bias).astype(jnp.bfloat16)
    grad_layer = jnp.concatenate([prompt_cot[0], cont_cot[0]], 0)
    grad_float = grad_layer.astype(jnp.float32)
    grad_proj_bias = jnp.sum(grad_float, axis=0)
    grad_rows = lax.all_gather(grad_layer, "tensor", axis=0, tiled=True)
    grad_w_proj = inner_first(act_low, grad_rows)
    grad_act = inner_last(grad_rows, proj_full)
    grad_pre = gelu_back(grad_act)[0].astype(jnp.bfloat16)
    grad_fc_bias = jnp.sum(grad_pre.astype(jnp.float32), axis=0)
    grad_w_fc = inner_first(mlp_rows, grad_pre)
    grad_mlp_part = inner_last(grad_pre, fc_full)
    grad_mlp_in = lax.psum_scatter(grad_mlp_part, "tensor", scatter_dimension=0, tiled=True)
    grad_hidden_norm, grad_ln2_gain, grad_ln2_bias = norm2_back(grad_mlp_in)
    grad_hidden = grad_float + grad_hidden_norm
    grad_out_bias = jnp.sum(grad_hidden, axis=0)
    grad_branch = grad_hidden.astype(jnp.bfloat16)
    grad_w_out = inner_first(attended, grad_branch)
    grad_attended = inner_last(grad_branch, out_full).astype(jnp.bfloat16)
    prompt_again = fetch_prompt(key_value[:prompt_rows])
    keys_back = jnp.concatenate([prompt_again, earlier_kv, own_cont_kv], 0)
    key_back_heads = to_heads(keys_back[:, :model_width])
    value_back_heads = to_heads(keys_back[:, model_width:])

    def head_backward(operands):
        query_head, key_head, value_head, grad_head, logsum_head = operands
        scores = inner_last(query_head, key_head) * 0.125
        scores = jnp.where(allowed, scores, -1e30)
        probability = jnp.exp(scores - logsum_head[:, None])
        prob_low = probability.astype(jnp.bfloat16)
        grad_prob = inner_last(grad_head, value_head)
        centre = jnp.sum(probability * grad_prob, axis=1, keepdims=True)
        grad_scores = (probability * (grad_prob - centre)).astype(jnp.bfloat16)
        grad_query = jnp.dot(grad_scores, key_head, preferred_element_type=jnp.float32) * 0.125
        grad_key = inner_first(grad_scores, query_head) * 0.125
        grad_value = inner_first(prob_low, grad_head)
        return (grad_query, grad_key, grad_value)

    head_operands = (query_heads, key_back_heads, value_back_heads, to_heads(grad_attended), logsum)
    grad_q_heads, grad_k_heads, grad_v_heads = lax.map(head_backward, head_operands)
    grad_queries = from_heads(grad_q_heads).astype(jnp.bfloat16)
    grad_kv = jnp.concatenate([from_heads(grad_k_heads), from_heads(grad_v_heads)], 1)
    prompt_grad_kv = lax.psum_scatter(
        grad_kv[:prompt_total], "ctx", scatter_dimension=0, tiled=True
    )
    from_later = passed_along(
        grad_kv[prompt_total : prompt_total + cont_rows].astype(jnp.bfloat16), "ctx", -1
    ).astype(jnp.float32)
    cont_grad_kv = grad_kv[prompt_total + cont_rows :] + from_later
    grad_kv_rows = jnp.concatenate([prompt_grad_kv, cont_grad_kv], 0).astype(jnp.bfloat16)
    grad_projected = jnp.concatenate([grad_queries, grad_kv_rows], 1)
    grad_qv_bias = jnp.stack(
        [
            jnp.sum(grad_queries.astype(jnp.float32), axis=0),
            jnp.sum(grad_kv_rows[:, model_width:].astype(jnp.float32), axis=0),
        ]
    )
    grad_w_qkv = inner_first(normed_low, grad_projected)
    grad_normed = inner_last(grad_projected, qkv_full)
    grad_inputs_norm, grad_ln1_gain, grad_ln1_bias = norm1_back(grad_normed)
    grad_inputs = (grad_hidden + grad_inputs_norm).astype(jnp.bfloat16)
    shard_qkv, shard_out = (
        lax.psum_scatter(
            grad_w_qkv.astype(jnp.bfloat16), "fsdp", scatter_dimension=0, tiled=True
        ).astype(jnp.float32),
        lax.psum_scatter(
            grad_w_out.astype(jnp.bfloat16), "fsdp", scatter_dimension=0, tiled=True
        ).astype(jnp.float32),
    )
    sum_qkv, sum_out = lax.psum((shard_qkv, shard_out), ("ctx", "tensor"))
    sum_fc, sum_proj, sum_fc_bias = lax.psum(
        (grad_w_fc, grad_w_proj, grad_fc_bias), ("fsdp", "ctx")
    )
    fsdp_place = lax.axis_index("fsdp")
    fsdp_rows = w_fc.shape[0]
    own_fc = lax.dynamic_slice_in_dim(sum_fc, fsdp_place * fsdp_rows, fsdp_rows, 0)
    own_proj = lax.dynamic_slice_in_dim(sum_proj, fsdp_place * fsdp_rows, fsdp_rows, 1)
    small_sums = lax.psum(
        (
            grad_ln1_gain,
            grad_ln1_bias,
            grad_qv_bias,
            grad_out_bias,
            grad_ln2_gain,
            grad_ln2_bias,
            grad_proj_bias,
        ),
        ("fsdp", "ctx", "tensor"),
    )
    return (
        layer_out[:prompt_rows][None],
        layer_out[prompt_rows:][None],
        grad_inputs[:prompt_rows][None],
        grad_inputs[prompt_rows:][None],
        small_sums[0],
        small_sums[1],
        sum_qkv,
        small_sums[2],
        sum_out,
        small_sums[3],
        small_sums[4],
        small_sums[5],
        own_fc,
        sum_fc_bias,
        own_proj,
        small_sums[6],
    )


def solution(mesh):
    placed = (
        P(("fsdp", "tensor"), "ctx", None),
        P(("fsdp", "tensor"), "ctx", None),
        P(("fsdp", "tensor"), None),
        P(),
        P(),
        P("fsdp", None),
        P(),
        P("fsdp", None),
        P(),
        P(),
        P(),
        P("fsdp", "tensor"),
        P("tensor"),
        P("tensor", "fsdp"),
        P(),
        P(("fsdp", "tensor"), "ctx", None),
        P(("fsdp", "tensor"), "ctx", None),
    )
    return jax.shard_map(
        local,
        mesh=mesh,
        in_specs=placed,
        out_specs=(
            P(("fsdp", "tensor"), "ctx", None),
            P(("fsdp", "tensor"), "ctx", None),
            P(("fsdp", "tensor"), "ctx", None),
            P(("fsdp", "tensor"), "ctx", None),
            P(),
            P(),
            P("fsdp", None),
            P(),
            P("fsdp", None),
            P(),
            P(),
            P(),
            P("fsdp", "tensor"),
            P("tensor"),
            P("tensor", "fsdp"),
            P(),
        ),
        check_vma=False,
    )
```

profile of v0, /device:TPU:0, one launch (start us, length us, event | category | flops | bytes accessed | tf_op | source)
XLA Modules:
  0.0 2594.6 jit_solution(17844384158072400370)
XLA Ops:
  14.9 91.5 %all-gather.8.cloned.1.call-done = bf16[1088,3264]{1,0:T(8,128)(2,1)} async-done(((bf16[544,3264]{1,0:T(8,128)(2,1)}), bf16[1088,3264]{1,0:T(8,128)(2,1)}) %all-gather.8.cloned.1.call-update) | async-done | bytes 7102480 | tf_op jit(solution)/shard_map/all_gather | solution.py:78
  106.5 12.2 fusion.82
  150.7 48.3 %all-gather.10.cloned.1.call-done = bf16[2048,2176]{0,1:T(8,128)(2,1)} async-done(((bf16[512,2176]{0,1:T(8,128)(2,1)}), bf16[2048,2176]{0,1:T(8,128)(2,1)}) %all-gather.10.cloned.1.call-update) | async-done | bytes 8912912 | tf_op jit(solution)/shard_map/all_gather | solution.py:48
  209.9 13.8 copy.38
  223.7 13.7 copy.39
  237.4 238.8 %while.26 = (s32[]{:T(128)}, bf16[17,896,64]{1,2,0:T(8,128)(2,1)}, f32[17,896]{1,0:T(8,128)S(1)}, bf16[17,896,64]{2,1,0:T(8,128)(2,1)}, bf16[17,2816,64]{2,1,0:T...) while((s32[]{:T(128)}, bf16[17,896,64]{1,2,0:T(8,128)(2,1)}, ...), condition=%wide.region_5.6_spmd, body=%wide.region_2.5_spmd.sunk | while | flops 666164352 | bytes 75001984 | solution.py:133
  486.0 16.9 fusion.91
  502.9 128.5 %all-gather.14.cloned.1.call-done = bf16[3584,1088]{0,1:T(8,128)(2,1)} async-done(((bf16[896,1088]{0,1:T(8,128)(2,1)}), bf16[3584,1088]{0,1:T(8,128)(2,1)}) %all-gather.14.cloned.1.call-update) | async-done | bytes 7798800 | tf_op jit(solution)/shard_map/all_gather | solution.py:138
  631.4 31.0 %convert_reduce_fusion = (f32[1088]{0:T(1024)}, bf16[3584,1088]{0,1:T(8,128)(2,1)}, f32[3584,1088]{0,1:T(8,128)}) fusion(f32[3584,1088]{0,1:T(8,128)} %fusion.91, f32[1088]{0:T(1024)S(1)} %copy-done.44, bf16[3584,1088]{0,1:T(8,128)(2,1)} %all-gather.14.cloned.1.call-done, bf16[1088,1088]{1,0:T(8,128)(2,1)} %all-gather.16.cloned.1.call-done), kind=kOutput, calls=%fused_computation.66 | convolution fusion | flops 8574761984 | bytes 49168896 | tf_op jit(solution)/shard_map/dot_general | solution.py:139
  662.4 16.8 convolution_convert_fusion
  679.2 11.4 copy.41
  690.6 16.5 fusion.93
  707.2 124.1 %reduce-scatter.16.cloned.1.call-done = bf16[896,1088]{1,0:T(8,128)(2,1)} async-done(((bf16[3584,1088]{1,0:T(8,128)(2,1)}), bf16[896,1088]{1,0:T(8,128)(2,1)}) %reduce-scatter.16.cloned.1.call-update) | async-done | bytes 1949712
  835.4 259.7 %reduce-scatter.8.cloned.1.call-done = f32[896,1088]{0,1:T(8,128)} async-done(((f32[3584,1088]{0,1:T(8,128)}), f32[896,1088]{0,1:T(8,128)}) %reduce-scatter.8.cloned.1.call-update) | async-done | bytes 3899408 | tf_op jit(solution)/shard_map/reduce_scatter | solution.py:157
  1117.4 618.3 %while.27 = (s32[]{:T(128)}, bf16[17,896,64]{1,2,0:T(8,128)(2,1)}, f32[17,2816,64]{1,2,0:T(8,128)}, f32[17,2816,64]{1,2,0:T(8,128)}, bf16[17,896,64]{2,1,0:T(8,1...) while((s32[]{:T(128)}, bf16[17,896,64]{1,2,0:T(8,128)(2,1)}, ...), condition=%wide.region_14.15_spmd, body=%wide.region_12.14_spmd.sunk | while | flops 1637751936 | bytes 138500816 | solution.py:184
  1129.8 10.7 multiply_convert_fusion.5
  1166.2 10.7 multiply_convert_fusion.5
  1202.5 10.7 multiply_convert_fusion.5
  1238.8 10.7 multiply_convert_fusion.5
  1266.0 9.2 multiply_reduce_fusion.5
  1275.2 10.7 multiply_convert_fusion.5
  1311.5 10.7 multiply_convert_fusion.5
  1347.9 10.7 multiply_convert_fusion.5
  1384.2 10.7 multiply_convert_fusion.5
  1420.5 10.7 multiply_convert_fusion.5
  1456.9 10.7 multiply_convert_fusion.5
  1493.2 10.7 multiply_convert_fusion.5
  1520.4 9.2 multiply_reduce_fusion.5
  1529.5 10.7 multiply_convert_fusion.5
  1566.0 10.7 multiply_convert_fusion.5
  1602.3 10.7 multiply_convert_fusion.5
  1629.4 9.2 multiply_reduce_fusion.5
  1638.6 10.7 multiply_convert_fusion.5
  1665.8 9.2 multiply_reduce_fusion.5
  1675.0 10.7 multiply_convert_fusion.5
  1711.3 10.7 multiply_convert_fusion.5
  1735.8 12.4 fusion.45
  1748.3 16.6 fusion.92
  1764.9 22.1 fusion.84
  1805.9 94.1 %reduce-scatter.10.cloned.1.call-done = f32[512,2176]{0,1:T(8,128)} async-done(((f32[2048,2176]{0,1:T(8,128)}), f32[512,2176]{0,1:T(8,128)}) %reduce-scatter.10.cloned.1.call-update) | async-done | bytes 4456464 | tf_op jit(solution)/shard_map/reduce_scatter | solution.py:187
  1904.0 13.0 convolution_convert_fusion.1
  1917.8 14.2 psum.93
  1932.0 118.1 %all-reduce.7.cloned.1.call-done = (f32[1088,1088]{1,0:T(8,128)}, f32[1088,1088]{0,1:T(8,128)}) async-done(((f32[1088,1088]{1,0:T(8,128)}, f32[1088,1088]{0,1:T(8,128)}), (f32[1088,1088]{1,0:T(8,128)}, f32[1088,1088]{0,1:T(8,128)})) %all-reduce.7.cloned.1.call-update) | async-done | bytes 9469968 | tf_op jit(solution)/shard_map/psum | solution.py:215
  2061.8 27.3 %reduce-scatter.14.cloned.1.call-done = bf16[544,1088]{1,0:T(8,128)(2,1)} async-done(((bf16[1088,1088]{1,0:T(8,128)(2,1)}), bf16[544,1088]{1,0:T(8,128)(2,1)}) %reduce-scatter.14.cloned.1.call-update) | async-done | bytes 1183760 | tf_op jit(solution)/shard_map/reduce_scatter | solution.py:210
  2091.9 11.6 fusion.85
  2107.0 41.6 %all-reduce.1 = (f32[1088]{0:T(1024)}, f32[1088]{0:T(1024)}, f32[2,1088]{1,0:T(2,128)}, f32[1088]{0:T(1024)}, f32[1088]{0:T(1024)}, /*index=5*/f32[1088]{0:T(1024)}, f32[1088]{0:T(1024)}) all-reduce(f32[1088]{0:T(1024)S(1)} %get-tuple-element.115, ...), channel_id=1, replica_groups=mesh['fsdp'=2,'ctx'=4,'tensor'=4] {'fsdp','ctx','tensor'}, use_global_device_ids=true, to_apply=%region_19.20 | all-reduce | flops 8704 | bytes 69632 | tf_op jit(solution)/shard_map/psum | solution.py:222
  2155.2 25.8 reduce-scatter.12.cloned.1.call-done
  2181.0 406.6 %all-reduce.8 = (f32[544,3264]{1,0:T(8,128)}, f32[544,1088]{1,0:T(8,128)}) all-reduce(bf16[544,3264]{1,0:T(8,128)(2,1)} %reduce-scatter.12.cloned.1.call-done, bf16[544,1088]{1,0:T(8,128)(2,1)S(1)} %copy-done.20), channel_id=1, replica_groups=mesh['fsdp'=2,'ctx'=4,'tensor'=4] {'ctx','tensor'}, use_global_device_ids=true, to_apply=%region_23.24 | all-reduce | flops 2367488 | bytes 14204928 | tf_op jit(solution)/shard_map/psum | solution.py:214
  (541 shorter events, 771.4 us)
Async XLA Ops:
  7.2 99.3 %all-gather.8.cloned.1.call-start = ((), (), s32[]{:S(2)}) async-start(), calls=%async_computation.5 | async-start | bytes 10862592 | tf_op jit(solution)/shard_map/all_gather | solution.py:78
  12.5 94.0 %copy-start.35 = (f32[1088]{0:T(1024)S(1)}, f32[1088]{0:T(1024)}, u32[]{:S(2)}) copy-start(f32[1088]{0:T(1024)} %param.24) | copy-start | bytes 13060
  12.5 94.0 %copy-start.45 = (f32[1088]{0:T(1024)S(1)}, f32[1088]{0:T(1024)}, u32[]{:S(2)}) copy-start(f32[1088]{0:T(1024)} %param.25) | copy-start | bytes 13060
  12.5 186.5 %all-gather.10.cloned.1.call-start = ((), (), s32[]{:S(2)}) async-start(), calls=%async_computation.6 | async-start | bytes 11141120 | tf_op jit(solution)/shard_map/all_gather | solution.py:48
  14.3 92.1 %copy-start.23 = (f32[896]{0:T(1024)}, f32[896]{0:T(1024)S(1)}, u32[]{:S(2)}) copy-start(f32[896]{0:T(1024)S(1)} %broadcast_multiply_fusion.1) | copy-start | bytes 10756
  14.9 91.5 %copy-start.27 = (f32[896]{0:T(1024)}, f32[896]{0:T(1024)S(1)}, u32[]{:S(2)}) copy-start(f32[896]{0:T(1024)S(1)} %fusion.64) | copy-start | bytes 10756
  14.9 91.5 %copy-start.29 = (f32[896]{0:T(1024)}, f32[896]{0:T(1024)S(1)}, u32[]{:S(2)}) copy-start(f32[896]{0:T(1024)S(1)} %fusion.77) | copy-start | bytes 10756
  123.5 352.8 %all-gather.12.cloned.1.call-start = ((), (), s32[]{:S(2)}) async-start(), calls=%async_computation.7 | async-start | bytes 3760128 | tf_op jit(solution)/shard_map/all_gather | solution.py:79
  126.4 359.5 %all-gather.18.cloned.1.call-start = ((), (), s32[]{:S(2)}) async-start(), calls=%async_computation.10 | async-start | bytes 3760128 | tf_op jit(solution)/shard_map/all_gather | solution.py:83
  129.4 356.6 %all-gather.20.cloned.1.call-start = ((), (), s32[]{:S(2)}) async-start(), calls=%async_computation.11 | async-start | bytes 9748480 | tf_op jit(solution)/shard_map/all_gather | solution.py:150
  132.6 370.2 %all-gather.16.cloned.1.call-start = ((), (), s32[]{:S(2)}) async-start(), calls=%async_computation.9 | async-start | bytes 3760128 | tf_op jit(solution)/shard_map/all_gather | solution.py:82
  135.9 495.5 %all-gather.14.cloned.1.call-start = ((), (), s32[]{:S(2)}) async-start(), calls=%async_computation.8 | async-start | bytes 9748480 | tf_op jit(solution)/shard_map/all_gather | solution.py:138
  138.6 12.1 collective-permute-start
  237.4 238.8 %copy-start.43 = (f32[1088]{0:T(1024)S(1)}, f32[1088]{0:T(1024)}, u32[]{:S(2)}) copy-start(f32[1088]{0:T(1024)} %param.29) | copy-start | bytes 13060
  485.9 145.5 %copy-start.44 = (f32[1088]{0:T(1024)S(1)}, f32[1088]{0:T(1024)}, u32[]{:S(2)}) copy-start(f32[1088]{0:T(1024)} %param.33) | copy-start | bytes 13060
  485.9 345.4 %reduce-scatter.16.cloned.1.call-start = ((), (), s32[]{:S(2)}) async-start(), calls=%async_computation.16 | async-start | bytes 10321920
  690.6 404.5 %reduce-scatter.8.cloned.1.call-start = ((), (), s32[]{:S(2)}) async-start(), calls=%async_computation.12 | async-start | bytes 19496960 | tf_op jit(solution)/shard_map/reduce_scatter | solution.py:157
  707.1 1192.9 %reduce-scatter.10.cloned.1.call-start = ((), (), s32[]{:S(2)}) async-start(), calls=%async_computation.13 | async-start | bytes 22282240 | tf_op jit(solution)/shard_map/reduce_scatter | solution.py:187
  835.4 265.0 %copy-start.39 = (f32[1088]{0:T(1024)S(1)}, f32[1088]{0:T(1024)}, u32[]{:S(2)}) copy-start(f32[1088]{0:T(1024)} %param.35) | copy-start | bytes 13060
  1140.5 10.4 slice-start
  1176.9 10.3 slice-start
  1213.2 10.3 slice-start
  1249.5 10.3 slice-start
  1285.9 10.3 slice-start
  1322.2 10.4 slice-start
  1358.6 10.3 slice-start
  1431.2 10.3 slice-start
  1503.9 10.4 slice-start
  1540.3 10.4 slice-start
  1576.7 10.3 slice-start
  1613.0 10.3 slice-start
  1649.3 10.3 slice-start
  1685.7 10.3 slice-start
  1722.0 10.4 slice-start
  1748.2 301.9 %all-reduce.7.cloned.1.call-start = ((), (), s32[]{:S(2)}) async-start(), calls=%async_computation.17 | async-start | bytes 20054016 | tf_op jit(solution)/shard_map/psum | solution.py:215
  1787.0 302.1 %reduce-scatter.14.cloned.1.call-start = ((), (), s32[]{:S(2)}) async-start(), calls=%async_computation.15 | async-start | bytes 3760128 | tf_op jit(solution)/shard_map/reduce_scatter | solution.py:210
  1794.6 386.4 %reduce-scatter.12.cloned.1.call-start = ((), (), s32[]{:S(2)}) async-start(), calls=%async_computation.14 | async-start | bytes 10862592 | tf_op jit(solution)/shard_map/reduce_scatter | solution.py:207
  1796.8 5.4 collective-permute-start.1
  1805.9 98.1 %copy-start.6 = (bf16[1,512,1088]{1,2,0:T(8,128)(2,1)S(1)}, bf16[1,512,1088]{1,2,0:T(8,128)(2,1)}, u32[]{:S(2)}) copy-start(bf16[1,512,1088]{1,2,0:T(8,128)(2,1)} %param.21) | copy-start | bytes 3342340
  1805.9 98.1 %copy-start.11 = (bf16[1,384,1088]{1,2,0:T(8,128)(2,1)S(1)}, bf16[1,384,1088]{1,2,0:T(8,128)(2,1)}, u32[]{:S(2)}) copy-start(bf16[1,384,1088]{1,2,0:T(8,128)(2,1)} %param.22) | copy-start | bytes 2506756
  1805.9 98.1 %copy-start.24 = (f32[896]{0:T(1024)S(1)}, f32[896]{0:T(1024)}, u32[]{:S(2)}) copy-start(f32[896]{0:T(1024)} %copy-done.23) | copy-start | bytes 10756
  1805.9 98.1 %copy-start.30 = (f32[896]{0:T(1024)S(1)}, f32[896]{0:T(1024)}, u32[]{:S(2)}) copy-start(f32[896]{0:T(1024)} %copy-done.29) | copy-start | bytes 10756
  1805.9 98.1 %copy-start.36 = (f32[1088]{0:T(1024)S(1)}, f32[1088]{0:T(1024)}, u32[]{:S(2)}) copy-start(f32[1088]{0:T(1024)} %param.24) | copy-start | bytes 13060
  1805.9 98.1 %copy-start.46 = (f32[1088]{0:T(1024)S(1)}, f32[1088]{0:T(1024)}, u32[]{:S(2)}) copy-start(f32[1088]{0:T(1024)} %param.25) | copy-start | bytes 13060
  2091.9 11.7 copy-start.28
  2103.5 45.1 %copy-start.13 = (bf16[1,512,1088]{1,2,0:T(8,128)(2,1)S(1)}, bf16[1,512,1088]{1,2,0:T(8,128)(2,1)}, u32[]{:S(2)}) copy-start(bf16[1,512,1088]{1,2,0:T(8,128)(2,1)} %param.36) | copy-start | bytes 3342340
  2103.5 45.1 %copy-start.26 = (f32[896]{0:T(1024)S(1)}, f32[896]{0:T(1024)}, u32[]{:S(2)}) copy-start(f32[896]{0:T(1024)} %copy-done.25) | copy-start | bytes 10756
  2153.1 27.8 %copy-start.20 = (bf16[544,1088]{1,0:T(8,128)(2,1)S(1)}, bf16[544,1088]{1,0:T(8,128)(2,1)}, u32[]{:S(2)}) copy-start(bf16[544,1088]{1,0:T(8,128)(2,1)} %reduce-scatter.14.cloned.1.call-done) | copy-start | bytes 3551236
  (80 other events, 421.0 us)
Sparse Core Ops, SparseCore 0:
  12.6 93.7 all-gather.7
  123.6 75.3 all-gather.9
  200.5 41.5 all-gather.11
  243.5 37.7 all-gather.17
  283.3 139.9 all-gather.19
  424.7 35.9 all-gather.15
  486.0 145.3 all-gather.13
  690.7 140.5 reduce-scatter.15
  833.8 261.1 reduce-scatter.7
  1748.3 151.6 reduce-scatter.9
  1904.4 145.7 all-reduce.6
  2052.8 36.3 reduce-scatter.13
  2092.1 88.7 reduce-scatter.11
where the time goes:
time: 2610 us; the launch traced here: 2590 us
  waiting for transfers between devices  922 us (35%)
  matrix products  778 us (30%)
  blocking collectives  462 us (18%)
  other arithmetic  287 us (11%)
  local copies, waits for them, and re-layouts  124 us (5%)
    psum x1, blocking collectives, local(): sum_qkv, sum_out = lax.psum((shard_qkv, shard_out), ('ctx', 'tensor'))  407 us
    dot_general x55, matrix products, inner_last(): lax.dot_general(left_op, right_op, (((1,), (1,)), ((), ())), preferred_el...  307 us
    reduce_scatter x1, waiting for transfers between devices, local(): lax.psum_scatter(grad_mlp_part, 'tensor', scatter_dimension=0, tiled=True)  260 us
    dot_general x38, matrix products, inner_first(): lax.dot_general(left_op, right_op, (((0,), (0,)), ((), ())), preferred_el...  233 us
    convert_element_type x17, other arithmetic, head_backward(): grad_scores = (probability * (grad_prob - centre)).astype(jnp.bfloat16)  182 us
    all_gather x1, waiting for transfers between devices, local(): mlp_rows = lax.all_gather(mlp_low, 'tensor', axis=0, tiled=True)  129 us
    unnamed x14, waiting for transfers between devices  124 us
    psum x1, waiting for transfers between devices, local(): lax.psum((grad_w_fc, grad_w_proj, grad_fc_bias), ('fsdp', 'ctx'))  118 us
  transfers between devices with their start and end apart: 15, of which 10 were waited for; matrix products, arithmetic and copies ran while one was open for 16% of the time, Pallas kernels for 0%

commit v1 on v0

--- a/solution.py
+++ b/solution.py
@@ -1,6 +1,10 @@
+import functools
+
 import jax
 import jax.numpy as jnp
 from jax import lax
+from jax.experimental import pallas as pl
+from jax.experimental.pallas import tpu as pltpu
 from jax.sharding import PartitionSpec as P
 
 HEADS = 17
@@ -48,7 +52,7 @@
     return lax.all_gather(rows_kv, "ctx", axis=0, tiled=True)
 
 
-def local(
+def local_rows(
     prompt_in,
     cont_in,
     cont_seg,
@@ -251,6 +255,819 @@
     )
 
 
+PAIRS = 2
+TILE = 2 * HEAD
+BF16 = jnp.bfloat16
+F32 = jnp.float32
+LOG2E = 1.4426950408889634
+SCALE2 = 0.125 * LOG2E
+NN = (((1,), (0,)), ((), ()))
+NT = (((1,), (1,)), ((), ()))
+TN = (((0,), (0,)), ((), ()))
+
+
+def dot(left_op, right_op, dims=NN):
+    return lax.dot_general(left_op, right_op, dims, preferred_element_type=F32)
+
+
+def swap(value, axis, bit):
+    count = lax.axis_size(axis)
+    return lax.ppermute(value, axis, [(place, place ^ bit) for place in range(count)])
+
+
+def turn(value, axis, steps):
+    count = lax.axis_size(axis)
+    return lax.ppermute(value, axis, [(place, (place + steps) % count) for place in range(count)])
+
+
+def canonical(by_distance, place):
+    low, high = place % 2 == 1, place >= 2
+    a, b, c, d = by_distance
+    a, b, c, d = (
+        jnp.where(low, b, a),
+        jnp.where(low, a, b),
+        jnp.where(low, d, c),
+        jnp.where(low, c, d),
+    )
+    return [
+        jnp.where(high, c, a),
+        jnp.where(high, d, b),
+        jnp.where(high, a, c),
+        jnp.where(high, b, d),
+    ]
+
+
+def in_order(own, other, place):
+    first = place == 0
+    return jnp.where(first, own, other), jnp.where(first, other, own)
+
+
+def project_kernel(
+    place_ref, x_ref, w_ref, gain_ref, bias_ref, col_bias_ref, *refs
+):
+    norm_ref, q_ref, k_ref, v_ref, kt_ref, vt_ref = refs[-6:]
+    values = x_ref[...].astype(F32)
+    average = jnp.mean(values, axis=1, keepdims=True)
+    centred = values - average
+    variance = jnp.mean(centred * centred, axis=1, keepdims=True)
+    normed = (centred * lax.rsqrt(variance + 1e-05) * gain_ref[...] + bias_ref[...]).astype(BF16)
+    norm_ref[0] = normed
+    tiles = q_ref.shape[0]
+    width = tiles * TILE
+    for part, out_ref, flip_ref in ((0, q_ref, None), (1, k_ref, kt_ref), (2, v_ref, vt_ref)):
+        cols = slice(part * width, (part + 1) * width)
+        out = (dot(normed, w_ref[:, cols]) + col_bias_ref[:, cols]).astype(BF16)
+        for tile in range(tiles):
+            piece = out[:, tile * TILE : (tile + 1) * TILE]
+            out_ref[tile, 0] = piece
+            if flip_ref is not None:
+                flip_ref[tile, 0] = piece.T
+
+
+def project(place, rows, w_own, gain, bias, col_bias, before, count):
+    row_count, width = rows.shape
+    tiles = w_own.shape[1] // (3 * TILE)
+    full = lambda *shape: pl.BlockSpec(shape, lambda i, p: (0,) * len(shape))
+    tall = pl.BlockSpec((tiles, 1, row_count, TILE), lambda i, p: (0, p[0], 0, 0))
+    flat = pl.BlockSpec((tiles, 1, TILE, row_count), lambda i, p: (0, p[0], 0, 0))
+    tall_shape = jax.ShapeDtypeStruct((tiles, count, row_count, TILE), BF16)
+    flat_shape = jax.ShapeDtypeStruct((tiles, count, TILE, row_count), BF16)
+    operands = (rows, w_own, gain[None], bias[None], col_bias[None])
+    aliases = {}
+    if before is not None:
+        aliases = {1 + len(operands) + i: i for i in range(len(before))}
+        operands = operands + tuple(before)
+    return pl.pallas_call(
+        project_kernel,
+        grid_spec=pltpu.PrefetchScalarGridSpec(
+            num_scalar_prefetch=1,
+            grid=(1,),
+            in_specs=[
+                full(row_count, width),
+                full(*w_own.shape),
+                full(1, width),
+                full(1, width),
+                full(1, w_own.shape[1]),
+            ]
+            + [pl.BlockSpec(memory_space=pl.ANY)] * len(aliases),
+            out_specs=[
+                pl.BlockSpec((1, row_count, width), lambda i, p: (p[0], 0, 0)),
+                tall,
+                tall,
+                tall,
+                flat,
+                flat,
+            ],
+        ),
+        out_shape=[
+            jax.ShapeDtypeStruct((count, row_count, width), BF16),
+            tall_shape,
+            tall_shape,
+            tall_shape,
+            flat_shape,
+            flat_shape,
+        ],
+        input_output_aliases=aliases,
+        compiler_params=pltpu.CompilerParams(vmem_limit_bytes=48 << 20),
+        cost_estimate=pl.CostEstimate(
+            flops=2 * row_count * width * w_own.shape[1], bytes_accessed=12 << 20, transcendentals=0
+        ),
+        name="project",
+    )(place.reshape(1), *operands)
+
+
+def halves(values):
+    lane = lax.broadcasted_iota(jnp.int32, values.shape, 1)
+    zero = jnp.zeros_like(values)
+    return [jnp.where(lane < HEAD, values, zero), jnp.where(lane >= HEAD, values, zero)]
+
+
+def own_mask(rows):
+    key_at = lax.broadcasted_iota(jnp.int32, (rows, rows), 0)
+    query_at = lax.broadcasted_iota(jnp.int32, (rows, rows), 1)
+    return key_at <= query_at
+
+
+def attend_kernel(
+    prompt_rows, items_ref, q_ref, k_ref, vt_ref, seg_col_ref, seg_row_ref, o_ref, lse_ref, acc
+):
+    item = items_ref[pl.program_id(0)]
+    count, row_count = k_ref.shape[1], k_ref.shape[2]
+    cont_rows = row_count - prompt_rows
+
+    def part(queries, block, start, size, mask, before):
+        keys = k_ref[0, block, pl.ds(start, size), :]
+        scores = [dot(keys, query, NT) for query in queries]
+        if mask is not None:
+            scores = [jnp.where(mask, score, -1e30) for score in scores]
+        tops = [jnp.max(score, axis=0, keepdims=True) for score in scores]
+        if before is not None:
+            tops = [jnp.maximum(top, state[0]) for top, state in zip(tops, before)]
+        exps = [jnp.exp2(score * SCALE2 - top * SCALE2) for score, top in zip(scores, tops)]
+        totals = [jnp.sum(exp, axis=0, keepdims=True) for exp in exps]
+        after = []
+        for head in range(2):
+            rows = slice(head * HEAD, (head + 1) * HEAD)
+            cols = slice(0, queries[head].shape[0])
+            out = dot(vt_ref[0, block, rows, pl.ds(start, size)], exps[head].astype(BF16))
+            total = totals[head]
+            if before is None:
+                acc[rows, cols] = out
+            else:
+                shrink = jnp.exp2((before[head][0] - tops[head]) * SCALE2)
+                total = total + before[head][1] * shrink
+                acc[rows, cols] = acc[rows, cols] * shrink + out
+            after.append((tops[head], total))
+        return after
+
+    def finish(block, start, size, states):
+        for head in range(2):
+            rows = slice(head * HEAD, (head + 1) * HEAD)
+            top, total = states[head]
+            acc[rows, :size] = acc[rows, :size] / total
+            lse_ref[0, block, head : head + 1, pl.ds(start, size)] = top * SCALE2 + jnp.log2(total)
+        o_ref[0, block, pl.ds(start, size), :] = acc[:, :size].T.astype(BF16)
+
+    def over_prompt(queries, blocks, states):
+        return lax.fori_loop(
+            0, blocks, lambda c, states: part(queries, c, 0, prompt_rows, None, states), states
+        )
+
+    @pl.when(item < count)
+    def _():
+        queries = halves(q_ref[0, item, :prompt_rows, :])
+        states = part(queries, item, 0, prompt_rows, own_mask(prompt_rows), None)
+        finish(item, 0, prompt_rows, over_prompt(queries, item, states))
+
+    @pl.when(item >= count)
+    def _():
+        block = item - count
+        before = jnp.maximum(block - 1, 0)
+        labels = seg_row_ref[block]
+        queries = halves(q_ref[0, block, prompt_rows:, :])
+        own = own_mask(cont_rows) & (seg_col_ref[block] == labels)
+        near = (seg_col_ref[before] == labels) & (block > 0)
+        states = part(queries, block, prompt_rows, cont_rows, own, None)
+        states = part(queries, before, prompt_rows, cont_rows, near, states)
+        finish(block, prompt_rows, cont_rows, over_prompt(queries, count, states))
+
+
+def attend(pair, items, q, k, vt, seg_col, seg_row, prompt_rows):
+    _, count, row_count, _ = q.shape
+    cont_rows = row_count - prompt_rows
+    pick = lambda i, s: (pair, 0, 0, 0)
+    first = lambda i, s: (0, 0, 0, 0)
+    labels = lambda i, s: (0, 0, 0)
+    pairs = items.shape[0] * row_count // 2 * count * row_count // 2
+    return pl.pallas_call(
+        functools.partial(attend_kernel, prompt_rows),
+        grid_spec=pltpu.PrefetchScalarGridSpec(
+            num_scalar_prefetch=1,
+            grid=(items.shape[0],),
+            in_specs=[
+                pl.BlockSpec((1, count, row_count, TILE), pick),
+                pl.BlockSpec((1, count, row_count, TILE), pick),
+                pl.BlockSpec((1, count, TILE, row_count), pick),
+                pl.BlockSpec((count, cont_rows, 1), labels),
+                pl.BlockSpec((count, 1, cont_rows), labels),
+            ],
+            out_specs=[
+                pl.BlockSpec((1, count, row_count, TILE), first),
+                pl.BlockSpec((1, count, 2, row_count), first),
+            ],
+            scratch_shapes=[pltpu.VMEM((TILE, max(prompt_rows, cont_rows)), F32)],
+        ),
+        out_shape=[
+            jax.ShapeDtypeStruct((1, count, row_count, TILE), BF16),
+            jax.ShapeDtypeStruct((1, count, 2, row_count), F32),
+        ],
+        compiler_params=pltpu.CompilerParams(vmem_limit_bytes=48 << 20),
+        cost_estimate=pl.CostEstimate(
+            flops=4 * 4 * TILE * pairs, bytes_accessed=6 << 20, transcendentals=2 * pairs
+        ),
+        name="attend",
+    )(items, q, k, vt, seg_col, seg_row)
+
+
+def attend_back_kernel(
+    prompt_rows,
+    items_ref,
+    q_ref,
+    k_ref,
+    v_ref,
+    kt_ref,
+    do_ref,
+    o_ref,
+    lse_ref,
+    seg_col_ref,
+    seg_row_ref,
+    dq_ref,
+    dk_ref,
+    dv_ref,
+    dk_acc,
+    dv_acc,
+    dq_acc,
+):
+    step = pl.program_id(0)
+    item = items_ref[step]
+    count, row_count = k_ref.shape[1], k_ref.shape[2]
+    cont_rows = row_count - prompt_rows
+
+    @pl.when(step == 0)
+    def _():
+        dk_acc[...] = jnp.zeros_like(dk_acc)
+        dv_acc[...] = jnp.zeros_like(dv_acc)
+        dq_ref[...] = jnp.zeros_like(dq_ref)
+
+    def part(given, block, start, size, mask, first):
+        rows = pl.ds(start, size)
+        for head in range(2):
+            query, grad, lse, centre = (entry[head] for entry in given)
+            cols = slice(0, query.shape[0])
+            own = slice(head * HEAD, (head + 1) * HEAD)
+            scores = dot(k_ref[0, block, rows, :], query, NT)
+            if mask is not None:
+                scores = jnp.where(mask, scores, -1e30)
+            probability = jnp.exp2(scores * SCALE2 - lse)
+            grad_probability = dot(v_ref[0, block, rows, :], grad, NT)
+            grad_scores = (probability * (grad_probability - centre)).astype(BF16)
+            dv_acc[block, rows, :] += dot(probability.astype(BF16), grad)
+            dk_acc[block, rows, :] += dot(grad_scores, query)
+            out = dot(kt_ref[0, block, own, rows], grad_scores)
+            if first:
+                dq_acc[own, cols] = out
+            else:
+                dq_acc[own, cols] += out
+
+    def setup(block, start, size):
+        rows = pl.ds(start, size)
+        grad = do_ref[0, block, rows, :]
+        product = (grad.astype(F32) * o_ref[0, block, rows, :].astype(F32)).T
+        centres = [
+            jnp.sum(product[head * HEAD : (head + 1) * HEAD], axis=0, keepdims=True)
+            for head in range(2)
+        ]
+        lses = [lse_ref[0, block, head : head + 1, rows] for head in range(2)]
+        return halves(q_ref[0, block, rows, :]), halves(grad), lses, centres
+
+    def finish(block, start, size):
+        dq_ref[0, block, pl.ds(start, size), :] = (dq_acc[:, :size].T * 0.125).astype(BF16)
+
+    @pl.when(item < count)
+    def _():
+        given = setup(item, 0, prompt_rows)
+        part(given, item, 0, prompt_rows, own_mask(prompt_rows), True)
+
+        @pl.loop(0, item)
+        def _(c):
+            part(given, c, 0, prompt_rows, None, False)
+
+        finish(item, 0, prompt_rows)
+
+    @pl.when(item >= count)
+    def _():
+        block = item - count
+        before = jnp.maximum(block - 1, 0)
+        labels = seg_row_ref[block]
+        own = own_mask(cont_rows) & (seg_col_ref[block] == labels)
+        near = (seg_col_ref[before] == labels) & (block > 0)
+        given = setup(block, prompt_rows, cont_rows)
+        part(given, block, prompt_rows, cont_rows, own, True)
+        part(given, before, prompt_rows, cont_rows, near, False)
+
+        @pl.loop(0, count)
+        def _(c):
+            part(given, c, 0, prompt_rows, None, False)
+
+        finish(block, prompt_rows, cont_rows)
+
+    @pl.when(step == pl.num_programs(0) - 1)
+    def _():
+        dk_ref[0] = (dk_acc[...] * 0.125).astype(BF16)
+        dv_ref[0] = dv_acc[...].astype(BF16)
+
+
+def attend_back(pair, items, q, k, v, kt, do, o, lse, seg_col, seg_row, prompt_rows):
+    _, count, row_count, _ = q.shape
+    cont_rows = row_count - prompt_rows
+    pick = lambda i, s: (pair, 0, 0, 0)
+    first = lambda i, s: (0, 0, 0, 0)
+    labels = lambda i, s: (0, 0, 0)
+    tall = pl.BlockSpec((1, count, row_count, TILE), pick)
+    own = pl.BlockSpec((1, count, row_count, TILE), first)
+    pairs = items.shape[0] * row_count // 2 * count * row_count // 2
+    return pl.pallas_call(
+        functools.partial(attend_back_kernel, prompt_rows),
+        grid_spec=pltpu.PrefetchScalarGridSpec(
+            num_scalar_prefetch=1,
+            grid=(items.shape[0],),
+            in_specs=[
+                tall,
+                tall,
+                tall,
+                pl.BlockSpec((1, count, TILE, row_count), pick),
+                own,
+                own,
+                pl.BlockSpec((1, count, 2, row_count), first),
+                pl.BlockSpec((count, cont_rows, 1), labels),
+                pl.BlockSpec((count, 1, cont_rows), labels),
+            ],
+            out_specs=[own] * 3,
+            scratch_shapes=[
+                pltpu.VMEM((count, row_count, TILE), F32),
+                pltpu.VMEM((count, row_count, TILE), F32),
+                pltpu.VMEM((TILE, max(prompt_rows, cont_rows)), F32),
+            ],
+        ),
+        out_shape=[jax.ShapeDtypeStruct((1, count, row_count, TILE), BF16)] * 3,
+        compiler_params=pltpu.CompilerParams(vmem_limit_bytes=56 << 20),
+        cost_estimate=pl.CostEstimate(
+            flops=10 * 4 * TILE * pairs, bytes_accessed=9 << 20, transcendentals=2 * pairs
+        ),
+        name="attend_back",
+    )(items, q, k, v, kt, do, o, lse, seg_col, seg_row)
+
+
+GELU_RATE = 0.7978845608028654
+
+
+def gelu_both(values):
+    square = values * values
+    bent = jnp.tanh(GELU_RATE * (values + 0.044715 * square * values))
+    half = 0.5 * (1.0 + bent)
+    slope = half + 0.5 * values * (1.0 - bent * bent) * (GELU_RATE * (1.0 + 0.134145 * square))
+    return values * half, slope
+
+
+def mlp_kernel(
+    x_ref,
+    g_ref,
+    xt_ref,
+    gt_ref,
+    b_ref,
+    wf_ref,
+    wp_ref,
+    out_ref,
+    gm_ref,
+    gwf_ref,
+    gwp_ref,
+    gb_ref,
+    act_s,
+    gp_s,
+):
+    hidden, width = wf_ref.shape[2], x_ref.shape[1]
+
+    def over(total, body):
+        whole = total // 256
+
+        @pl.loop(0, whole)
+        def _(i):
+            body(pl.ds(pl.multiple_of(i * 256, 256), 256))
+
+        if total % 256:
+            body(pl.ds(whole * 256, total % 256))
+
+    def up(cols):
+        pre_act = dot(x_ref[...], wf_ref[0, :, cols]) + b_ref[0, :, cols]
+        grad_act = dot(g_ref[...], wp_ref[0, :, cols])
+        activated, slope = gelu_both(pre_act)
+        grad_pre = (grad_act * slope).astype(BF16)
+        act_s[:, cols] = activated.astype(BF16)
+        gp_s[:, cols] = grad_pre
+        gb_ref[0, :, cols] = jnp.sum(grad_pre.astype(F32), axis=0, keepdims=True)
+
+    def weights(cols):
+        gwf_ref[0, :, cols] = dot(xt_ref[...], gp_s[:, cols]).astype(BF16)
+        gwp_ref[0, :, cols] = dot(gt_ref[...], act_s[:, cols]).astype(BF16)
+
+    over(hidden, up)
+    over(hidden, weights)
+
+    @pl.when(pl.program_id(0) == 0)
+    def _():
+        def down(rows):
+            out_ref[:, rows] = dot(act_s[...], wp_ref[0, rows, :], NT)
+            gm_ref[:, rows] = dot(gp_s[...], wf_ref[0, rows, :], NT)
+
+        over(width, down)
+
+    @pl.when(pl.program_id(0) > 0)
+    def _():
+        def down(rows):
+            out_ref[:, rows] += dot(act_s[...], wp_ref[0, rows, :], NT)
+            gm_ref[:, rows] += dot(gp_s[...], wf_ref[0, rows, :], NT)
+
+        over(width, down)
+
+
+def mlp(x, g, xt, gt, bias, wf, wp):
+    rows, width = x.shape
+    parts, _, hidden = wf.shape
+    full = lambda *shape: pl.BlockSpec(shape, lambda k: (0, 0))
+    each = lambda *shape: pl.BlockSpec((1,) + shape, lambda k: (k, 0, 0))
+    return pl.pallas_call(
+        mlp_kernel,
+        grid=(parts,),
+        in_specs=[
+            full(rows, width),
+            full(rows, width),
+            full(width, rows),
+            full(width, rows),
+            each(1, hidden),
+            each(width, hidden),
+            each(width, hidden),
+        ],
+        out_specs=[
+            full(rows, width),
+            full(rows, width),
+            each(width, hidden),
+            each(width, hidden),
+            each(1, hidden),
+        ],
+        out_shape=[
+            jax.ShapeDtypeStruct((rows, width), F32),
+            jax.ShapeDtypeStruct((rows, width), F32),
+            jax.ShapeDtypeStruct(wf.shape, BF16),
+            jax.ShapeDtypeStruct(wf.shape, BF16),
+            jax.ShapeDtypeStruct((parts, 1, hidden), F32),
+        ],
+        scratch_shapes=[pltpu.VMEM((rows, hidden), BF16)] * 2,
+        compiler_params=pltpu.CompilerParams(vmem_limit_bytes=60 << 20),
+        cost_estimate=pl.CostEstimate(
+            flops=12 * rows * width * hidden * parts,
+            bytes_accessed=60 << 20,
+            transcendentals=rows * hidden * parts,
+        ),
+        name="mlp",
+    )(x, g, xt, gt, bias, wf, wp)
+
+
+def project_back_kernel(place_ref, *refs):
+    grads, (w_ref, norm_ref, gn_ref, gw_ref, sum_ref, acc) = refs[:-6], refs[-6:]
+    step = pl.program_id(0)
+    joined = jnp.concatenate([ref[0, 0] for ref in grads], axis=1)
+    gn_ref[0] = dot(joined, w_ref[...], NT).astype(BF16)
+    sums = jnp.sum(joined.astype(F32), axis=0, keepdims=True)
+    normed = norm_ref[0].T
+
+    @pl.when(step == 0)
+    def _():
+        acc[...] = dot(normed, joined)
+        sum_ref[...] = sums
+
+    @pl.when(step > 0)
+    def _():
+        acc[...] += dot(normed, joined)
+        sum_ref[...] += sums
+
+    @pl.when(step == pl.num_programs(0) - 1)
+    def _():
+        gw_ref[...] = acc[...].astype(BF16)
+
+
+def project_back(place, grads, w_own, normed):
+    count, row_count, width = normed.shape
+    cols = w_own.shape[1]
+    full = lambda *shape: pl.BlockSpec(shape, lambda i, p: (0, 0))
+    return pl.pallas_call(
+        project_back_kernel,
+        grid_spec=pltpu.PrefetchScalarGridSpec(
+            num_scalar_prefetch=1,
+            grid=(count,),
+            in_specs=[
+                pl.BlockSpec((1, 1, row_count, TILE), lambda i, p: (0, (count - 1 - i) ^ p[0], 0, 0))
+            ]
+            * len(grads)
+            + [
+                full(width, cols),
+                pl.BlockSpec((1, row_count, width), lambda i, p: ((count - 1 - i) ^ p[0], 0, 0)),
+            ],
+            out_specs=[
+                pl.BlockSpec((1, row_count, width), lambda i, p: (count - 1 - i, 0, 0)),
+                full(width, cols),
+                full(1, cols),
+            ],
+            scratch_shapes=[pltpu.VMEM((width, cols), F32)],
+        ),
+        out_shape=[
+            jax.ShapeDtypeStruct((count, row_count, width), BF16),
+            jax.ShapeDtypeStruct((width, cols), BF16),
+            jax.ShapeDtypeStruct((1, cols), F32),
+        ],
+        compiler_params=pltpu.CompilerParams(vmem_limit_bytes=56 << 20),
+        cost_estimate=pl.CostEstimate(
+            flops=4 * count * row_count * width * cols,
+            bytes_accessed=30 << 20,
+            transcendentals=0,
+        ),
+        name="project_back",
+    )(place.reshape(1), *grads, w_own, normed)
+
+
+def own_columns(matrix, place):
+    width = matrix.shape[1] // 3
+    own = 2 * PAIRS * HEAD
+    blank = jnp.zeros((matrix.shape[0], TILE - HEAD), matrix.dtype)
+    pieces = []
+    for part in range(3):
+        whole = matrix[:, part * width : (part + 1) * width]
+        pieces += [
+            lax.dynamic_slice_in_dim(whole, place * own, own, 1),
+            whole[:, width - HEAD :],
+            blank,
+        ]
+    return jnp.concatenate(pieces, axis=1)
+
+
+def local_heads(
+    prompt_in,
+    cont_in,
+    cont_seg,
+    ln1_gain,
+    ln1_bias,
+    w_qkv,
+    qv_bias,
+    w_out,
+    out_bias,
+    ln2_gain,
+    ln2_bias,
+    w_fc,
+    fc_bias,
+    w_proj,
+    proj_bias,
+    prompt_cot,
+    cont_cot,
+):
+    width = prompt_in.shape[2]
+    prompt_rows, cont_rows = prompt_in.shape[1], cont_in.shape[1]
+    row_count = prompt_rows + cont_rows
+    count = lax.axis_size("ctx")
+    place = lax.axis_index("ctx")
+    core = place % 2
+    fsdp = lax.axis_index("fsdp")
+    tensor = lax.axis_index("tensor")
+    tensors = lax.axis_size("tensor")
+    own_width = 2 * PAIRS * HEAD
+    half = w_fc.shape[0]
+    quarter = half // 2
+
+    w_mine = own_columns(w_qkv, place).astype(BF16)
+    w_own = jnp.concatenate(in_order(w_mine, swap(w_mine, "fsdp", 1), fsdp), axis=0)
+    zero_bias = jnp.zeros_like(qv_bias[0])
+    col_bias = own_columns(jnp.concatenate([qv_bias[0], zero_bias, qv_bias[1]])[None], place)[0]
+
+    rows_own = jnp.concatenate([prompt_in[0], cont_in[0]], axis=0)
+    rows_across = swap(rows_own, "ctx", 2)
+    rows_beside = swap(rows_own, "ctx", 1)
+    rows_corner = swap(rows_across, "ctx", 1)
+    made = None
+    for distance, rows in enumerate((rows_own, rows_beside, rows_across, rows_corner)):
+        made = project(place ^ distance, rows, w_own, ln1_gain, ln1_bias, col_bias, made, count)
+    normed, q, k, v, kt, vt = made
+
+    fc_mine = lax.dynamic_slice_in_dim(w_fc, core * quarter, quarter, 0).astype(BF16)
+    proj_mine = lax.dynamic_slice_in_dim(w_proj, core * quarter, quarter, 1).astype(BF16).T
+    fc_parts = [jnp.stack(in_order(fc_mine, swap(fc_mine, "fsdp", 1), fsdp))]
+    proj_parts = [proj_mine]
+    for _ in range(tensors - 1):
+        fc_parts.append(turn(fc_parts[-1], "tensor", 1))
+        proj_parts.append(turn(proj_parts[-1], "tensor", 1))
+    fc_half = jnp.stack(fc_parts)
+    proj_stack = jnp.stack(proj_parts)
+    proj_half = jnp.stack(in_order(proj_stack, swap(proj_stack, "fsdp", 1), fsdp), axis=1)
+    fc_all = jnp.stack(in_order(fc_half, swap(fc_half, "ctx", 1), core), axis=2)
+    proj_all = jnp.stack(in_order(proj_half, swap(proj_half, "ctx", 1), core), axis=2)
+    fc_all = fc_all.reshape(tensors, width, w_fc.shape[1])
+    proj_all = proj_all.reshape(tensors, width, w_fc.shape[1])
+    fc_bias_parts = [fc_bias[None]]
+    for _ in range(tensors - 1):
+        fc_bias_parts.append(turn(fc_bias_parts[-1], "tensor", 1))
+    fc_bias_all = jnp.stack(fc_bias_parts)
+    out_mine = w_out.astype(BF16)
+    out_full = jnp.concatenate(in_order(out_mine, swap(out_mine, "fsdp", 1), fsdp), axis=0)
+
+    labels = cont_seg[0].reshape(count, cont_rows)
+    seg_col, seg_row = labels[:, :, None], labels[:, None, :]
+    every = jnp.arange(2 * count, dtype=jnp.int32)
+    mine = jnp.stack([place, place + count]).astype(jnp.int32)
+    heads_out, lses, returned = [], [], [[] for _ in range(count)]
+    for pair in range(PAIRS + 1):
+        out, lse = attend(
+            pair, every if pair < PAIRS else mine, q, k, vt, seg_col, seg_row, prompt_rows
+        )
+        heads_out.append(out)
+        lses.append(lse)
+        if pair < PAIRS:
+            for distance in range(count):
+                piece = lax.dynamic_index_in_dim(out[0], place ^ distance, 0, False)
+                returned[distance].append(swap(piece, "ctx", distance) if distance else piece)
+        else:
+            last_out = lax.dynamic_index_in_dim(out[0], place, 0, False)[:, :HEAD]
+    attended = jnp.concatenate(
+        canonical([jnp.concatenate(entry, axis=1) for entry in returned], place) + [last_out],
+        axis=1,
+    )
+
+    inputs = rows_own.astype(F32)
+    hidden = inputs + dot(attended, out_full) + out_bias
+    mlp_in, norm2_back = jax.vjp(layer_norm, hidden, ln2_gain, ln2_bias)
+    mlp_low = mlp_in.astype(BF16)
+    grad_layer = jnp.concatenate([prompt_cot[0], cont_cot[0]], axis=0)
+    grad_float = grad_layer.astype(F32)
+    mlp_out, grad_mlp_in, grad_fc, grad_proj, grad_fc_bias = mlp(
+        mlp_low, grad_layer, mlp_low.T, grad_layer.T, fc_bias_all, fc_all, proj_all
+    )
+    layer_out = (hidden + mlp_out + proj_bias).astype(BF16)
+    grad_proj_bias = jnp.sum(grad_float, axis=0)
+    grad_hidden_norm, grad_ln2_gain, grad_ln2_bias = norm2_back(grad_mlp_in)
+    grad_hidden = grad_float + grad_hidden_norm
+    grad_out_bias = jnp.sum(grad_hidden, axis=0)
+    grad_branch = grad_hidden.astype(BF16)
+    grad_attended = dot(grad_branch, out_full, NT).astype(BF16)
+    grad_w_out = dot(attended, grad_branch, TN).astype(BF16)
+
+    split = (tensors, 2, 2, quarter, w_fc.shape[1])
+
+    def over_cores(grad):
+        grad = grad.reshape(split)
+        other = lax.dynamic_index_in_dim(grad, 1 - core, 2, False)
+        return lax.dynamic_index_in_dim(grad, core, 2, False).astype(F32) + swap(
+            other, "ctx", 1
+        ).astype(F32)
+
+    def over_tensor(parts):
+        total = parts[tensors - 1]
+        for distance in range(tensors - 2, -1, -1):
+            total = parts[distance] + turn(total.astype(BF16), "tensor", -1).astype(F32)
+        return total
+
+    def over_fsdp(grad, axis):
+        other = lax.dynamic_index_in_dim(grad, 1 - fsdp, axis, False).astype(BF16)
+        return lax.dynamic_index_in_dim(grad, fsdp, axis, False) + swap(other, "fsdp", 1).astype(F32)
+
+    fc_sum = over_fsdp(over_tensor(over_cores(grad_fc)), 0)
+    proj_sum = over_tensor(over_fsdp(over_cores(grad_proj), 1))
+    both = jnp.stack([fc_sum, proj_sum]).astype(BF16)
+    both = both.astype(F32) + swap(both, "ctx", 2).astype(F32)
+    both = jnp.concatenate(in_order(both, swap(both, "ctx", 1), core), axis=1)
+    own_fc, own_proj = both[0], both[1].T
+
+    grads = []
+    for pair in range(PAIRS + 1):
+        if pair < PAIRS:
+            pieces = []
+            for distance in range(count):
+                start = (place ^ distance) * own_width + pair * TILE
+                piece = lax.dynamic_slice_in_dim(grad_attended, start, TILE, 1)
+                pieces.append(swap(piece, "ctx", distance) if distance else piece)
+            grad_heads = jnp.stack(canonical(pieces, place))[None]
+            items = every
+        else:
+            last = jnp.pad(grad_attended[:, width - HEAD :], ((0, 0), (0, TILE - HEAD)))
+            grad_heads = jnp.broadcast_to(last[None, None], (1, count) + last.shape)
+            items = mine
+        grads.append(
+            attend_back(
+                pair,
+                items,
+                q,
+                k,
+                v,
+                kt,
+                grad_heads,
+                heads_out[pair],
+                lses[pair],
+                seg_col,
+                seg_row,
+                prompt_rows,
+            )
+        )
+    ordered = [grads[pair][part] for part in range(3) for pair in range(PAIRS + 1)]
+    grad_normed, grad_own, col_sums = project_back(place, ordered, w_own, normed)
+    from_core = swap(grad_normed[1::2], "ctx", 1)
+    summed = grad_normed[0::2].astype(F32) + from_core.astype(F32)
+    grad_norm_rows = summed[0] + swap(summed[1].astype(BF16), "ctx", 2).astype(F32)
+    _, norm1_back = jax.vjp(layer_norm, inputs, ln1_gain, ln1_bias)
+    grad_inputs_norm, grad_ln1_gain, grad_ln1_bias = norm1_back(grad_norm_rows)
+    grad_inputs = (grad_hidden + grad_inputs_norm).astype(BF16)
+
+    def shard(grad):
+        other = lax.dynamic_slice_in_dim(grad, (1 - fsdp) * half, half, 0)
+        mine = lax.dynamic_slice_in_dim(grad, fsdp * half, half, 0)
+        return (mine.astype(F32) + swap(other, "fsdp", 1).astype(F32)).astype(BF16)
+
+    sum_out = lax.psum(shard(grad_w_out), ("ctx", "tensor")).astype(F32)
+    grad_own = lax.psum(shard(grad_own), "tensor")
+    step_width = grad_own.shape[1] // 3
+    own_part = jnp.concatenate(
+        [grad_own[:, i * step_width : i * step_width + own_width] for i in range(3)], axis=1
+    )
+    last_part = jnp.concatenate(
+        [grad_own[:, i * step_width + own_width :][:, :HEAD] for i in range(3)], axis=1
+    )
+    across = swap(own_part, "ctx", 2)
+    beside = swap(jnp.stack([own_part, across]), "ctx", 1)
+    by_place = canonical([own_part, beside[0], across, beside[1]], place)
+    last_part = lax.psum(last_part.astype(F32), "ctx")
+    columns = []
+    for i in range(3):
+        columns += [entry[:, i * own_width : (i + 1) * own_width].astype(F32) for entry in by_place]
+        columns.append(last_part[:, i * HEAD : (i + 1) * HEAD])
+    sum_qkv = jnp.concatenate(columns, axis=1)
+
+    def spread(sums):
+        full = lax.dynamic_update_slice_in_dim(
+            jnp.zeros((width,), F32), sums[:own_width], place * own_width, 0
+        )
+        return full.at[width - HEAD :].set(sums[own_width : own_width + HEAD])
+
+    grad_q_bias = spread(col_sums[0, :step_width])
+    grad_v_bias = spread(col_sums[0, 2 * step_width :])
+    fc_bias_sums = jnp.zeros((tensors, w_fc.shape[1]), F32)
+    for distance in range(tensors):
+        fc_bias_sums = lax.dynamic_update_slice_in_dim(
+            fc_bias_sums, grad_fc_bias[distance], (tensor - distance) % tensors, 0
+        )
+    vectors = lax.psum(
+        jnp.concatenate(
+            [
+                grad_ln1_gain,
+                grad_ln1_bias,
+                grad_q_bias,
+                grad_v_bias,
+                grad_out_bias,
+                grad_ln2_gain,
+                grad_ln2_bias,
+                grad_proj_bias,
+                fc_bias_sums.reshape(-1),
+            ]
+        ),
+        ("fsdp", "ctx", "tensor"),
+    )
+    vector = [vectors[i * width : (i + 1) * width] for i in range(8)]
+    fc_bias_sum = lax.dynamic_slice_in_dim(
+        vectors, 8 * width + tensor * w_fc.shape[1], w_fc.shape[1], 0
+    )
+    return (
+        layer_out[:prompt_rows][None],
+        layer_out[prompt_rows:][None],
+        grad_inputs[:prompt_rows][None],
+        grad_inputs[prompt_rows:][None],
+        vector[0],
+        vector[1],
+        sum_qkv,
+        jnp.stack([vector[2], vector[3]]),
+        sum_out,
+        vector[4],
+        vector[5],
+        vector[6],
+        own_fc,
+        fc_bias_sum,
+        own_proj,
+        vector[7],
+    )
+
+
 def solution(mesh):
     placed = (
         P(("fsdp", "tensor"), "ctx", None),
@@ -271,8 +1088,9 @@
         P(("fsdp", "tensor"), "ctx", None),
         P(("fsdp", "tensor"), "ctx", None),
     )
+    by_heads = HEADS // mesh.shape["ctx"] == PAIRS * 2 and HEADS % mesh.shape["ctx"] == 1
     return jax.shard_map(
-        local,
+        local_heads if by_heads else local_rows,
         mesh=mesh,
         in_specs=placed,
         out_specs=(

time: 2610 us -> 1130 us (0.43)
  matrix products: 778 us -> 12.5 us
  waiting for transfers between devices: 922 us -> 347 us
  blocking collectives: 462 us -> 40.1 us
  Pallas kernels: 0 us -> 329 us
  other arithmetic: 287 us -> 159 us
  starting transfers between devices: 5.2 us -> 61.7 us
  local copies, waits for them, and re-layouts: 124 us -> 153 us
    dot_general x131 -> x3, matrix products: 778 us -> 12.5 us  [dot(): return lax.dot_general(left_op, right_op, dims, preferred_element_type=F32)]
    psum x3 -> x1, blocking collectives: 462 us -> 40.1 us  [local_heads(): lax.psum(jnp.concatenate([grad_ln1_gain, grad_ln1_bias, grad_q_bias, grad...]
    reduce_scatter x4 -> x0, waiting for transfers between devices: 407 us -> none  [the longest x1 260 us: local(): lax.psum_scatter(grad_mlp_part, 'tensor', scatter_dimension=0, tiled=True)]
    pallas_call x0 -> x12, Pallas kernels: none -> 329 us  [the longest x3 106 us: attend_back(): pl.pallas_call(functools.partial(attend_back_kernel, prompt_rows), grid_s...]
    all_gather x7 -> x0, waiting for transfers between devices: 268 us -> none  [the longest x1 129 us: local(): mlp_rows = lax.all_gather(mlp_low, 'tensor', axis=0, tiled=True)]
    ppermute x2 -> x48, waiting for transfers between devices: 3.94 us -> 188 us  [the longest x15 124 us: turn(): lax.ppermute(value, axis, [(place, (place + steps) % count) for place in...]
    convert_element_type x23 -> x14, other arithmetic: 203 us -> 26 us  [the longest x2 6.02 us: shard(): return (mine.astype(F32) + swap(other, 'fsdp', 1).astype(F32)).astype(BF16)]
    unnamed x14 -> x3, waiting for transfers between devices: 124 us -> 0.05 us
  transfers between devices with their start and end apart: 15 -> 51, of which waited for: 10 -> 20; matrix products, arithmetic and copies ran while one was open for 16% -> 23% of each run, Pallas kernels for 0% -> 21%
where the time goes in v1:
time: 1130 us; the launch traced here: 1120 us
  waiting for transfers between devices  347 us (31%)
  Pallas kernels  329 us (29%)
  other arithmetic  159 us (14%)
  local copies, waits for them, and re-layouts  153 us (14%)
  starting transfers between devices  61.7 us (5%)
  blocking collectives  40.1 us (4%)
  between operations  15.7 us (1%)
  matrix products  12.5 us (1%)
    ppermute x15, waiting for transfers between devices, turn(): lax.ppermute(value, axis, [(place, (place + steps) % count) for place in...  124 us
    pallas_call x3, Pallas kernels, attend_back(): pl.pallas_call(functools.partial(attend_back_kernel, prompt_rows), grid_s...  106 us
    pallas_call x1, Pallas kernels, mlp(): pl.pallas_call(mlp_kernel, grid=(parts,), in_specs=[full(rows, width), fu...  98.7 us
    psum x1, waiting for transfers between devices, local_heads(): sum_out = lax.psum(shard(grad_w_out), ('ctx', 'tensor')).astype(F32)  93.2 us
    pallas_call x3, Pallas kernels, attend(): pl.pallas_call(functools.partial(attend_kernel, prompt_rows), grid_spec=p...  66.9 us
    ppermute x33, waiting for transfers between devices, swap(): lax.ppermute(value, axis, [(place, place ^ bit) for place in range(count)])  63.4 us
    psum x1, blocking collectives, local_heads(): lax.psum(jnp.concatenate([grad_ln1_gain, grad_ln1_bias, grad_q_bias, grad...  40.1 us
    psum x1, waiting for transfers between devices, local_heads(): grad_own = lax.psum(shard(grad_own), 'tensor')  34 us
  transfers between devices with their start and end apart: 51, of which 20 were waited for; matrix products, arithmetic and copies ran while one was open for 23% of the time, Pallas kernels for 21%

profile of v1, /device:TPU:0, one launch (start us, length us, event | category | flops | bytes accessed | tf_op | source)
XLA Modules:
  0.0 1118.9 jit_solution(9759583898318568422)
XLA Ops:
  30.4 5.7 fusion.47
  36.1 5.3 convert.43
  75.3 15.6 %collective-permute-done.20 = bf16[272,1088]{1,0:T(8,128)(2,1)S(1)} collective-permute-done((bf16[272,1088]{1,0:T(8,128)(2,1)}, bf16[272,1088]{1,0:T(8,128)(2,1)S(1)}, u32[]{:S(2)}, u32[]{:S(2)}) %collective-permute-start.20) | collective-permute-done | bytes 591904 | tf_op jit(solution)/shard_map/ppermute | solution.py:280
  94.7 6.2 collective-permute-done.2
  101.2 22.1 %collective-permute-done.15 = bf16[2,272,1088]{2,1,0:T(8,128)(2,1)} collective-permute-done((bf16[2,272,1088]{2,1,0:T(8,128)(2,1)S(1)}, bf16[2,272,1088]{2,1,0:T(8,128)(2,1)}, u32[]{:S(2)}, u32[]{:S(2)}) %collective-permute-start.15) | collective-permute-done | bytes 1183776 | tf_op jit(solution)/shard_map/ppermute | solution.py:280
  125.1 6.7 project.4
  131.8 4.8 collective-permute-done.21
  149.9 6.7 project.5
  156.6 6.7 project.6
  169.3 6.7 project.7
  177.7 29.7 %attend.3 = (bf16[1,4,896,128]{3,2,1,0:T(8,128)(2,1)S(1)}, f32[1,4,2,896]{3,2,1,0:T(2,128)S(1)}) custom-call(s32[8]{0:T(128)S(1)} %iota.9.items_ref, bf16[3,4,896,128]{3,2,1,0:T(8,128)(2,1)S(1)} %copy-done.1, bf16[3,4,896,128]{3,2,1,0:T(8,128)(2,1)} %get-tuple-element.106.k_ref, bf16[3,4,128,896]{3,2,1,0:T(8,128)(2,1)} %get-tuple-element.107.vt_ref, ...), custom_call_target="tpu_custom_call" | custom-call | flops 13153337344 | bytes 6291456 | tf_op jit(solution)/shard_map/attend/pallas_call | solution.py:462
  208.5 7.4 attend.5
  215.9 29.8 %attend.4 = (bf16[1,4,896,128]{3,2,1,0:T(8,128)(2,1)S(1)}, f32[1,4,2,896]{3,2,1,0:T(2,128)S(1)}) custom-call(s32[8]{0:T(128)S(1)} %iota.10.items_ref, bf16[3,4,896,128]{3,2,1,0:T(8,128)(2,1)S(1)} %copy-done.1, bf16[3,4,896,128]{3,2,1,0:T(8,128)(2,1)} %get-tuple-element.106.k_ref, bf16[3,4,128,896]{3,2,1,0:T(8,128)(2,1)} %get-tuple-element.107.vt_ref, ...), custom_call_target="tpu_custom_call" | custom-call | flops 13153337344 | bytes 6291456 | tf_op jit(solution)/shard_map/attend/pallas_call | solution.py:462
  250.2 6.2 collective-permute-done.6
  277.8 6.3 pad_maximum_fusion.2
  300.1 7.8 select_bitcast_fusion.1
  307.9 8.9 pad_maximum_fusion.1
  316.8 8.5 copy.114
  325.3 9.1 select_bitcast_fusion.3
  334.4 8.9 pad_maximum_fusion
  343.3 8.4 copy.113
  351.7 98.7 %mlp.1 = (f32[896,1088]{1,0:T(8,128)}, f32[896,1088]{1,0:T(8,128)}, bf16[4,1088,1088]{2,1,0:T(8,128)(2,1)}, bf16[4,1088,1088]{2,1,0:T(8,128)(2,1)}, f32[4,1,1088]{2,1,0:T(1,128)}) custom-call(bf16[896,1088]{1,0:T(8,128)(2,1)} %add_convert_fusion.2.x_ref, bf16[896,1088]{1,0:T(8,128)(2,1)} %get-tuple-element.240.g_ref, bf16[1088,896]{1,0:T(8,128)(2,1)} %copy.115.xt_ref, ...), custom_call_target="tpu_custom_call" | custom-call | flops 50910461952 | bytes 62914560 | tf_op jit(solution)/shard_map/mlp/pallas_call | solution.py:708
  454.8 5.2 fusion.46
  460.1 4.7 convolution_convert_fusion
  472.4 7.0 constant_dynamic-slice_fusion.1
  485.6 14.0 %attend_back.5 = (bf16[1,4,896,128]{3,2,1,0:T(8,128)(2,1)}, bf16[1,4,896,128]{3,2,1,0:T(8,128)(2,1)}, bf16[1,4,896,128]{3,2,1,0:T(8,128)(2,1)}) custom-call(s32[2]{0:T(128)} %copy-done.12, bf16[3,4,896,128]{3,2,1,0:T(8,128)(2,1)} %get-tuple-element.105.q_ref, bf16[3,4,896,128]{3,2,1,0:T(8,128)(2,1)} %get-tuple-element.106.k_ref, ...), custom_call_target="tpu_custom_call" | custom-call | flops 8220835840 | bytes 9437184 | tf_op jit(solution)/shard_map/attend_back/pallas_call | solution.py:599
  500.3 6.1 collective-permute-start.24
  508.1 45.9 %attend_back.4 = (bf16[1,4,896,128]{3,2,1,0:T(8,128)(2,1)}, bf16[1,4,896,128]{3,2,1,0:T(8,128)(2,1)}, bf16[1,4,896,128]{3,2,1,0:T(8,128)(2,1)}) custom-call(s32[8]{0:T(128)} %iota.12.items_ref, bf16[3,4,896,128]{3,2,1,0:T(8,128)(2,1)} %get-tuple-element.105.q_ref, bf16[3,4,896,128]{3,2,1,0:T(8,128)(2,1)} %get-tuple-element.106.k_ref, ...), custom_call_target="tpu_custom_call" | custom-call | flops 32883343360 | bytes 9437184 | tf_op jit(solution)/shard_map/attend_back/pallas_call | solution.py:599
  555.9 45.9 %attend_back.3 = (bf16[1,4,896,128]{3,2,1,0:T(8,128)(2,1)}, bf16[1,4,896,128]{3,2,1,0:T(8,128)(2,1)}, bf16[1,4,896,128]{3,2,1,0:T(8,128)(2,1)}) custom-call(s32[8]{0:T(128)} %iota.11.items_ref, bf16[3,4,896,128]{3,2,1,0:T(8,128)(2,1)} %get-tuple-element.105.q_ref, bf16[3,4,896,128]{3,2,1,0:T(8,128)(2,1)} %get-tuple-element.106.k_ref, ...), custom_call_target="tpu_custom_call" | custom-call | flops 32883343360 | bytes 9437184 | tf_op jit(solution)/shard_map/attend_back/pallas_call | solution.py:599
  601.8 31.0 %project_back.1 = (bf16[4,896,1088]{2,1,0:T(8,128)(2,1)}, bf16[1088,1152]{1,0:T(8,128)(2,1)}, f32[1,1152]{1,0:T(1,128)}) custom-call(s32[1]{0:T(128)} %bitcast.5.place_ref, bf16[1,4,896,128]{3,2,1,0:T(8,128)(2,1)} %get-tuple-element.116.refs_0_, bf16[1,4,896,128]{3,2,1,0:T(8,128)(2,1)} %get-tuple-element.118.refs_1_, ...), custom_call_target="tpu_custom_call" | custom-call | flops 17968398336 | bytes 31457280 | tf_op jit(solution)/shard_map/project_back/pallas_call | solution.py:772
  643.1 6.5 copy.121
  651.4 14.7 %collective-permute-done.32 = bf16[544,1152]{1,0:T(8,128)(2,1)} collective-permute-done((bf16[544,1152]{1,0:T(8,128)(2,1)}, bf16[544,1152]{1,0:T(8,128)(2,1)}, u32[]{:S(2)}, u32[]{:S(2)}) %collective-permute-start.32) | collective-permute-done | bytes 1253408 | tf_op jit(solution)/shard_map/ppermute | solution.py:275
  671.1 21.3 %collective-permute-done.35 = bf16[544,1088]{1,0:T(8,128)(2,1)} collective-permute-done((bf16[544,1088]{1,0:T(8,128)(2,1)}, bf16[544,1088]{1,0:T(8,128)(2,1)}, u32[]{:S(2)}, u32[]{:S(2)}) %collective-permute-start.35) | collective-permute-done | bytes 1183776 | tf_op jit(solution)/shard_map/ppermute | solution.py:275
  695.7 34.0 %all-reduce.5.cloned.1.call-done = bf16[544,1152]{1,0:T(8,128)(2,1)} async-done(((bf16[544,1152]{1,0:T(8,128)(2,1)}), bf16[544,1152]{1,0:T(8,128)(2,1)}) %all-reduce.5.cloned.1.call-update) | async-done | bytes 1253392 | tf_op jit(solution)/shard_map/psum | solution.py:1000
  735.2 93.2 %all-reduce.9.cloned.1.call-done = bf16[544,1088]{1,0:T(8,128)(2,1)} async-done(((bf16[544,1088]{1,0:T(8,128)(2,1)}), bf16[544,1088]{1,0:T(8,128)(2,1)}) %all-reduce.9.cloned.1.call-update) | async-done | bytes 1183760 | tf_op jit(solution)/shard_map/psum | solution.py:999
  831.3 32.6 %all-reduce.7.cloned.1.call-done = f32[544,192]{1,0:T(8,128)} async-done(((f32[544,192]{1,0:T(8,128)}), f32[544,192]{1,0:T(8,128)}) %all-reduce.7.cloned.1.call-update) | async-done | bytes 417808 | tf_op jit(solution)/shard_map/psum | solution.py:1011
  867.3 6.5 copy.122
  873.8 5.0 convert_add_fusion.1
  883.5 7.3 convert_add_fusion
  896.5 14.9 %collective-permute-done.37 = bf16[2,272,1088]{2,1,0:T(8,128)(2,1)} collective-permute-done((bf16[2,272,1088]{2,1,0:T(8,128)(2,1)}, bf16[2,272,1088]{2,1,0:T(8,128)(2,1)}, u32[]{:S(2)}, u32[]{:S(2)}) %collective-permute-start.37) | collective-permute-done | bytes 1183776 | tf_op jit(solution)/shard_map/ppermute | solution.py:280
  927.8 17.4 %collective-permute-done.38 = bf16[2,272,1088]{2,1,0:T(8,128)(2,1)} collective-permute-done((bf16[2,272,1088]{2,1,0:T(8,128)(2,1)}, bf16[2,272,1088]{2,1,0:T(8,128)(2,1)}, u32[]{:S(2)}, u32[]{:S(2)}) %collective-permute-start.38) | collective-permute-done | bytes 1183776 | tf_op jit(solution)/shard_map/ppermute | solution.py:280
  962.5 28.5 %collective-permute-done.43 = bf16[272,1088]{1,0:T(8,128)(2,1)S(1)} collective-permute-done((bf16[272,1088]{1,0:T(8,128)(2,1)S(1)}, bf16[272,1088]{1,0:T(8,128)(2,1)S(1)}, u32[]{:S(2)}, u32[]{:S(2)}) %collective-permute-start.43) | collective-permute-done | bytes 591904 | tf_op jit(solution)/shard_map/ppermute | solution.py:280
  999.2 7.8 collective-permute-done.44
  1007.1 4.6 collective-permute-start.45
  1013.0 9.2 collective-permute-done.45
  1026.5 8.6 concatenate.71
  1043.9 5.5 collective-permute-done.46
  1058.7 40.1 %psum.28 = f32[13056]{0:T(1024)S(1)} all-reduce(f32[13056]{0:T(1024)S(1)} %concatenate.68), channel_id=1, replica_groups=mesh['fsdp'=2,'ctx'=4,'tensor'=4] {'fsdp','ctx','tensor'}, use_global_device_ids=true, to_apply=%region_14.15 | all-reduce | flops 13056 | bytes 104448 | tf_op jit(solution)/shard_map/psum | solution.py:1031
  (447 shorter events, 269.4 us)
Async XLA Ops:
  7.2 722.5 %all-reduce.5.cloned.1.call-start = ((), (), s32[]{:S(2)}) async-start(), calls=%async_computation | async-start | bytes 2506752 | tf_op jit(solution)/shard_map/psum | solution.py:1000
  9.8 61.1 %collective-permute-start.19 = (bf16[272,1088]{1,0:T(8,128)(2,1)}, bf16[272,1088]{1,0:T(8,128)(2,1)}, u32[]{:S(2)}, u32[]{:S(2)}) collective-permute-start(bf16[272,1088]{1,0:T(8,128)(2,1)} %get-tuple-element.228), channel_id=1, source_target_pairs={{0,1},{1,2},{2,3},{3,0},{4,5},{5,6},{6,7},{7,4},{8,9},{9,10},{10,1... | collective-permute-start | bytes 1775624 | tf_op jit(solution)/shard_map/ppermute | solution.py:280
  15.0 57.4 %collective-permute-start.14 = (bf16[272,1088]{1,0:T(8,128)(2,1)}, bf16[272,1088]{1,0:T(8,128)(2,1)}, u32[]{:S(2)}, u32[]{:S(2)}) collective-permute-start(bf16[272,1088]{1,0:T(8,128)(2,1)} %dynamic-slice_convert_fusion.3), channel_id=1, source_target_pairs={{0,16},{16,0},{1,17},{17,1},{2,18},{18,2},{3,19},{19,3},{4,20},{20... | collective-permute-start | bytes 1775624 | tf_op jit(solution)/shard_map/ppermute | solution.py:275
  23.3 71.4 %collective-permute-start = (bf16[896,1088]{0,1:T(8,128)(2,1)}, bf16[896,1088]{0,1:T(8,128)(2,1)}, u32[]{:S(2)}, u32[]{:S(2)}) collective-permute-start(bf16[896,1088]{0,1:T(8,128)(2,1)} %copy.99), channel_id=1, source_target_pairs={{0,8},{4,12},{8,0},{12,4},{1,9},{5,13},{9,1},{13,5},{2,10},{6,14},... | collective-permute-start | bytes 5849096 | tf_op jit(solution)/shard_map/ppermute | solution.py:275
  27.7 63.3 %collective-permute-start.10 = (bf16[544,1088]{1,0:T(8,128)(2,1)}, bf16[544,1088]{1,0:T(8,128)(2,1)}, u32[]{:S(2)}, u32[]{:S(2)}) collective-permute-start(bf16[544,1088]{1,0:T(8,128)(2,1)} %convert_element_type.191), channel_id=1, source_target_pairs={{0,16},{16,0},{1,17},{17,1},{2,18},{18,2},{3,19},{19,3},{4,20},{20... | collective-permute-start | bytes 3551240 | tf_op jit(solution)/shard_map/ppermute | solution.py:275
  28.8 28.9 %collective-permute-start.11 = (f32[1,1088]{1,0:T(1,128)}, f32[1,1088]{1,0:T(1,128)}, u32[]{:S(2)}, u32[]{:S(2)}) collective-permute-start(f32[1,1088]{1,0:T(1,128)} %broadcast_in_dim.77), channel_id=1, source_target_pairs={{0,1},{1,2},{2,3},{3,0},{4,5},{5,6},{6,7},{7,4},{8,9},{9,10},{10,1... | collective-permute-start | bytes 13064 | tf_op jit(solution)/shard_map/ppermute | solution.py:280
  69.5 74.8 %collective-permute-start.3 = (bf16[896,1088]{0,1:T(8,128)(2,1)}, bf16[896,1088]{0,1:T(8,128)(2,1)}, u32[]{:S(2)}, u32[]{:S(2)}) collective-permute-start(bf16[896,1088]{0,1:T(8,128)(2,1)} %copy.99), channel_id=1, source_target_pairs={{0,4},{4,0},{8,12},{12,8},{1,5},{5,1},{9,13},{13,9},{2,6},{6,2},{1... | collective-permute-start | bytes 5849096 | tf_op jit(solution)/shard_map/ppermute | solution.py:275
  70.9 29.9 %collective-permute-start.2 = (bf16[544,1152]{1,0:T(8,128)(2,1)S(1)}, bf16[544,1152]{1,0:T(8,128)(2,1)S(1)}, u32[]{:S(2)}, u32[]{:S(2)}) collective-permute-start(bf16[544,1152]{1,0:T(8,128)(2,1)S(1)} %concatenate.57), channel_id=1, source_target_pairs={{0,16},{16,0},{1,17},{17,1},{2,18},{18,2},{3,19},{19,3},{4,20},{20... | collective-permute-start | bytes 3760136 | tf_op jit(solution)/shard_map/ppermute | solution.py:275
  72.4 18.5 %collective-permute-start.20 = (bf16[272,1088]{1,0:T(8,128)(2,1)}, bf16[272,1088]{1,0:T(8,128)(2,1)S(1)}, u32[]{:S(2)}, u32[]{:S(2)}) collective-permute-start(bf16[272,1088]{1,0:T(8,128)(2,1)} %collective-permute-done.19), channel_id=1, source_target_pairs={{0,1},{1,2},{2,3},{3,0},{4,5},{5,6},{6,7},{7,4},{8,9},{9,10},{10,1... | collective-permute-start | bytes 1775624 | tf_op jit(solution)/shard_map/ppermute | solution.py:280
  90.9 32.4 %collective-permute-start.15 = (bf16[2,272,1088]{2,1,0:T(8,128)(2,1)S(1)}, bf16[2,272,1088]{2,1,0:T(8,128)(2,1)}, u32[]{:S(2)}, u32[]{:S(2)}) collective-permute-start(bf16[2,272,1088]{2,1,0:T(8,128)(2,1)S(1)} %get-tuple-element.248), channel_id=1, source_target_pairs={{0,1},{1,2},{2,3},{3,0},{4,5},{5,6},{6,7},{7,4},{8,9},{9,10},{10,1... | collective-permute-start | bytes 3551240 | tf_op jit(solution)/shard_map/ppermute | solution.py:280
  90.9 45.7 %collective-permute-start.21 = (bf16[272,1088]{1,0:T(8,128)(2,1)S(1)}, bf16[272,1088]{1,0:T(8,128)(2,1)S(1)}, u32[]{:S(2)}, u32[]{:S(2)}) collective-permute-start(bf16[272,1088]{1,0:T(8,128)(2,1)S(1)} %collective-permute-done.20), channel_id=1, source_target_pairs={{0,1},{1,2},{2,3},{3,0},{4,5},{5,6},{6,7},{7,4},{8,9},{9,10},{10,1... | collective-permute-start | bytes 1775624 | tf_op jit(solution)/shard_map/ppermute | solution.py:280
  94.7 68.6 %collective-permute-start.1 = (bf16[896,1088]{0,1:T(8,128)(2,1)}, bf16[896,1088]{0,1:T(8,128)(2,1)}, u32[]{:S(2)}, u32[]{:S(2)}) collective-permute-start(bf16[896,1088]{0,1:T(8,128)(2,1)} %collective-permute-done), channel_id=1, source_target_pairs={{0,4},{4,0},{8,12},{12,8},{1,5},{5,1},{9,13},{13,9},{2,6},{6,2},{1... | collective-permute-start | bytes 5849096 | tf_op jit(solution)/shard_map/ppermute | solution.py:275
  123.3 40.0 %collective-permute-start.16 = (bf16[2,272,1088]{2,1,0:T(8,128)(2,1)}, bf16[2,272,1088]{2,1,0:T(8,128)(2,1)}, u32[]{:S(2)}, u32[]{:S(2)}) collective-permute-start(bf16[2,272,1088]{2,1,0:T(8,128)(2,1)} %collective-permute-done.15), channel_id=1, source_target_pairs={{0,1},{1,2},{2,3},{3,0},{4,5},{5,6},{6,7},{7,4},{8,9},{9,10},{10,1... | collective-permute-start | bytes 3551240 | tf_op jit(solution)/shard_map/ppermute | solution.py:280
  139.8 130.4 %collective-permute-start.22 = (bf16[4,272,1088]{2,1,0:T(8,128)(2,1)}, bf16[4,272,1088]{2,1,0:T(8,128)(2,1)}, u32[]{:S(2)}, u32[]{:S(2)}) collective-permute-start(bf16[4,272,1088]{2,1,0:T(8,128)(2,1)} %pad_maximum_fusion.7), channel_id=1, source_target_pairs={{0,16},{16,0},{1,17},{17,1},{2,18},{18,2},{3,19},{19,3},{4,20},{20... | collective-permute-start | bytes 7102472 | tf_op jit(solution)/shard_map/ppermute | solution.py:275
  163.3 113.8 %collective-permute-start.17 = (bf16[2,272,1088]{2,1,0:T(8,128)(2,1)}, bf16[2,272,1088]{2,1,0:T(8,128)(2,1)}, u32[]{:S(2)}, u32[]{:S(2)}) collective-permute-start(bf16[2,272,1088]{2,1,0:T(8,128)(2,1)} %collective-permute-done.16), channel_id=1, source_target_pairs={{0,1},{1,2},{2,3},{3,0},{4,5},{5,6},{6,7},{7,4},{8,9},{9,10},{10,1... | collective-permute-start | bytes 3551240 | tf_op jit(solution)/shard_map/ppermute | solution.py:280
  208.4 41.7 %collective-permute-start.8 = (bf16[896,128]{1,0:T(8,128)(2,1)S(1)}, bf16[896,128]{1,0:T(8,128)(2,1)S(1)}, u32[]{:S(2)}, u32[]{:S(2)}) collective-permute-start(bf16[896,128]{1,0:T(8,128)(2,1)S(1)} %get-tuple-element.252), channel_id=1, source_target_pairs={{0,4},{4,0},{8,12},{12,8},{1,5},{5,1},{9,13},{13,9},{2,6},{6,2},{1... | collective-permute-start | bytes 688136 | tf_op jit(solution)/shard_map/ppermute | solution.py:275
  245.9 17.0 %collective-permute-start.9 = (bf16[896,128]{1,0:T(8,128)(2,1)S(1)}, bf16[896,128]{1,0:T(8,128)(2,1)S(1)}, u32[]{:S(2)}, u32[]{:S(2)}) collective-permute-start(bf16[896,128]{1,0:T(8,128)(2,1)S(1)} %get-tuple-element.256), channel_id=1, source_target_pairs={{0,4},{4,0},{8,12},{12,8},{1,5},{5,1},{9,13},{13,9},{2,6},{6,2},{1... | collective-permute-start | bytes 688136 | tf_op jit(solution)/shard_map/ppermute | solution.py:275
  250.1 10.9 collective-permute-start.4
  256.5 9.8 collective-permute-start.7
  261.0 9.1 collective-permute-start.5
  275.6 24.5 %collective-permute-start.23 = (bf16[4,2,272,1088]{3,2,0,1:T(8,128)(2,1)}, bf16[4,2,272,1088]{3,2,0,1:T(8,128)(2,1)}, u32[]{:S(2)}, u32[]{:S(2)}) collective-permute-start(bf16[4,2,272,1088]{3,2,0,1:T(8,128)(2,1)} %pad_maximum_fusion.3), channel_id=1, source_target_pairs={{0,4},{4,0},{8,12},{12,8},{1,5},{5,1},{9,13},{13,9},{2,6},{6,2},{1... | collective-permute-start | bytes 14204936 | tf_op jit(solution)/shard_map/ppermute | solution.py:275
  284.2 41.1 %collective-permute-start.18 = (bf16[4,2,272,1088]{3,2,0,1:T(8,128)(2,1)}, bf16[4,2,272,1088]{3,2,0,1:T(8,128)(2,1)}, u32[]{:S(2)}, u32[]{:S(2)}) collective-permute-start(bf16[4,2,272,1088]{3,2,0,1:T(8,128)(2,1)} %pad_maximum_fusion.2), channel_id=1, source_target_pairs={{0,4},{4,0},{8,12},{12,8},{1,5},{5,1},{9,13},{13,9},{2,6},{6,2},{1... | collective-permute-start | bytes 14204936 | tf_op jit(solution)/shard_map/ppermute | solution.py:275
  472.0 401.8 %collective-permute-start.36 = (bf16[4,2,272,1088]{3,2,1,0:T(8,128)(2,1)}, bf16[4,2,272,1088]{3,2,1,0:T(8,128)(2,1)}, u32[]{:S(2)}, u32[]{:S(2)}) collective-permute-start(bf16[4,2,272,1088]{3,2,1,0:T(8,128)(2,1)} %dynamic-slice_bitcast_fusion), channel_id=1, source_target_pairs={{0,4},{4,0},{8,12},{12,8},{1,5},{5,1},{9,13},{13,9},{2,6},{6,2},{1... | collective-permute-start | bytes 14204936 | tf_op jit(solution)/shard_map/ppermute | solution.py:275
  482.0 401.5 %collective-permute-start.41 = (bf16[4,2,272,1088]{3,2,0,1:T(8,128)(2,1)}, bf16[4,2,272,1088]{3,2,0,1:T(8,128)(2,1)}, u32[]{:S(2)}, u32[]{:S(2)}) collective-permute-start(bf16[4,2,272,1088]{3,2,0,1:T(8,128)(2,1)} %bitcast.240), channel_id=1, source_target_pairs={{0,4},{4,0},{8,12},{12,8},{1,5},{5,1},{9,13},{13,9},{2,6},{6,2},{1... | collective-permute-start | bytes 14204936 | tf_op jit(solution)/shard_map/ppermute | solution.py:275
  482.5 17.1 %collective-permute-start.27 = (bf16[896,128]{1,0:T(8,128)(2,1)S(1)}, bf16[896,128]{1,0:T(8,128)(2,1)S(1)}, u32[]{:S(2)}, u32[]{:S(2)}) collective-permute-start(bf16[896,128]{1,0:T(8,128)(2,1)S(1)} %get-tuple-element.238), channel_id=1, source_target_pairs={{0,12},{4,8},{8,4},{12,0},{1,13},{5,9},{9,5},{13,1},{2,14},{6,10},... | collective-permute-start | bytes 688136 | tf_op jit(solution)/shard_map/ppermute | solution.py:275
  484.3 15.4 %collective-permute-start.28 = (bf16[896,128]{1,0:T(8,128)(2,1)S(1)}, bf16[896,128]{1,0:T(8,128)(2,1)S(1)}, u32[]{:S(2)}, u32[]{:S(2)}) collective-permute-start(bf16[896,128]{1,0:T(8,128)(2,1)S(1)} %get-tuple-element.237), channel_id=1, source_target_pairs={{0,8},{4,12},{8,0},{12,4},{1,9},{5,13},{9,1},{13,5},{2,10},{6,14},... | collective-permute-start | bytes 688136 | tf_op jit(solution)/shard_map/ppermute | solution.py:275
  484.6 15.1 %collective-permute-start.29 = (bf16[896,128]{1,0:T(8,128)(2,1)S(1)}, bf16[896,128]{1,0:T(8,128)(2,1)S(1)}, u32[]{:S(2)}, u32[]{:S(2)}) collective-permute-start(bf16[896,128]{1,0:T(8,128)(2,1)S(1)} %get-tuple-element.236), channel_id=1, source_target_pairs={{0,4},{4,0},{8,12},{12,8},{1,5},{5,1},{9,13},{13,9},{2,6},{6,2},{1... | collective-permute-start | bytes 688136 | tf_op jit(solution)/shard_map/ppermute | solution.py:275
  500.3 53.8 %collective-permute-start.24 = (bf16[896,128]{1,0:T(8,128)(2,1)S(1)}, bf16[896,128]{1,0:T(8,128)(2,1)S(1)}, u32[]{:S(2)}, u32[]{:S(2)}) collective-permute-start(bf16[896,128]{1,0:T(8,128)(2,1)S(1)} %get-tuple-element.235), channel_id=1, source_target_pairs={{0,12},{4,8},{8,4},{12,0},{1,13},{5,9},{9,5},{13,1},{2,14},{6,10},... | collective-permute-start | bytes 688136 | tf_op jit(solution)/shard_map/ppermute | solution.py:275
  506.4 47.6 %collective-permute-start.25 = (bf16[896,128]{1,0:T(8,128)(2,1)S(1)}, bf16[896,128]{1,0:T(8,128)(2,1)S(1)}, u32[]{:S(2)}, u32[]{:S(2)}) collective-permute-start(bf16[896,128]{1,0:T(8,128)(2,1)S(1)} %get-tuple-element.234), channel_id=1, source_target_pairs={{0,8},{4,12},{8,0},{12,4},{1,9},{5,13},{9,1},{13,5},{2,10},{6,14},... | collective-permute-start | bytes 688136 | tf_op jit(solution)/shard_map/ppermute | solution.py:275
  506.4 47.6 %collective-permute-start.26 = (bf16[896,128]{1,0:T(8,128)(2,1)S(1)}, bf16[896,128]{1,0:T(8,128)(2,1)S(1)}, u32[]{:S(2)}, u32[]{:S(2)}) collective-permute-start(bf16[896,128]{1,0:T(8,128)(2,1)S(1)} %get-tuple-element.233), channel_id=1, source_target_pairs={{0,4},{4,0},{8,12},{12,8},{1,5},{5,1},{9,13},{13,9},{2,6},{6,2},{1... | collective-permute-start | bytes 688136 | tf_op jit(solution)/shard_map/ppermute | solution.py:275
  635.4 30.7 %collective-permute-start.32 = (bf16[544,1152]{1,0:T(8,128)(2,1)}, bf16[544,1152]{1,0:T(8,128)(2,1)}, u32[]{:S(2)}, u32[]{:S(2)}) collective-permute-start(bf16[544,1152]{1,0:T(8,128)(2,1)} %constant_dynamic-slice_fusion.3), channel_id=1, source_target_pairs={{0,16},{16,0},{1,17},{17,1},{2,18},{18,2},{3,19},{19,3},{4,20},{20... | collective-permute-start | bytes 3760136 | tf_op jit(solution)/shard_map/ppermute | solution.py:275
  638.1 54.3 %collective-permute-start.35 = (bf16[544,1088]{1,0:T(8,128)(2,1)}, bf16[544,1088]{1,0:T(8,128)(2,1)}, u32[]{:S(2)}, u32[]{:S(2)}) collective-permute-start(bf16[544,1088]{1,0:T(8,128)(2,1)} %constant_dynamic-slice_fusion.2), channel_id=1, source_target_pairs={{0,16},{16,0},{1,17},{17,1},{2,18},{18,2},{3,19},{19,3},{4,20},{20... | collective-permute-start | bytes 3551240 | tf_op jit(solution)/shard_map/ppermute | solution.py:275
  649.5 217.8 %collective-permute-start.30 = (bf16[2,896,1088]{1,2,0:T(8,128)(2,1)}, bf16[2,896,1088]{1,2,0:T(8,128)(2,1)}, u32[]{:S(2)}, u32[]{:S(2)}) collective-permute-start(bf16[2,896,1088]{1,2,0:T(8,128)(2,1)} %copy.121), channel_id=1, source_target_pairs={{0,4},{4,0},{8,12},{12,8},{1,5},{5,1},{9,13},{13,9},{2,6},{6,2},{1... | collective-permute-start | bytes 11698184 | tf_op jit(solution)/shard_map/ppermute | solution.py:275
  669.1 159.3 %all-reduce.9.cloned.1.call-start = ((), (), s32[]{:S(2)}) async-start(), calls=%async_computation.2 | async-start | bytes 2506752 | tf_op jit(solution)/shard_map/psum | solution.py:999
  695.4 168.5 %all-reduce.7.cloned.1.call-start = ((), (), s32[]{:S(2)}) async-start(), calls=%async_computation.1 | async-start | bytes 1114112 | tf_op jit(solution)/shard_map/psum | solution.py:1011
  731.7 134.3 %collective-permute-start.33 = (bf16[544,768]{1,0:T(8,128)(2,1)S(1)}, bf16[544,768]{1,0:T(8,128)(2,1)S(1)}, u32[]{:S(2)}, u32[]{:S(2)}) collective-permute-start(bf16[544,768]{1,0:T(8,128)(2,1)S(1)} %get-tuple-element.272), channel_id=1, source_target_pairs={{0,8},{4,12},{8,0},{12,4},{1,9},{5,13},{9,1},{13,5},{2,10},{6,14},... | collective-permute-start | bytes 2506760 | tf_op jit(solution)/shard_map/ppermute | solution.py:275
  867.3 91.1 %collective-permute-start.34 = (bf16[2,544,768]{2,1,0:T(8,128)(2,1)}, bf16[2,544,768]{2,1,0:T(8,128)(2,1)}, u32[]{:S(2)}, u32[]{:S(2)}) collective-permute-start(bf16[2,544,768]{2,1,0:T(8,128)(2,1)} %pad_maximum_fusion.10), channel_id=1, source_target_pairs={{0,4},{4,0},{8,12},{12,8},{1,5},{5,1},{9,13},{13,9},{2,6},{6,2},{1... | collective-permute-start | bytes 5013512 | tf_op jit(solution)/shard_map/ppermute | solution.py:275
  880.2 31.1 %collective-permute-start.37 = (bf16[2,272,1088]{2,1,0:T(8,128)(2,1)}, bf16[2,272,1088]{2,1,0:T(8,128)(2,1)}, u32[]{:S(2)}, u32[]{:S(2)}) collective-permute-start(bf16[2,272,1088]{2,1,0:T(8,128)(2,1)} %fusion.20), channel_id=1, source_target_pairs={{0,3},{1,0},{2,1},{3,2},{4,7},{5,4},{6,5},{7,6},{8,11},{9,8},{10,9... | collective-permute-start | bytes 3551240 | tf_op jit(solution)/shard_map/ppermute | solution.py:280
  895.0 56.8 %collective-permute-start.42 = (bf16[4,272,1088]{2,1,0:T(8,128)(2,1)}, bf16[4,272,1088]{2,1,0:T(8,128)(2,1)}, u32[]{:S(2)}, u32[]{:S(2)}) collective-permute-start(bf16[4,272,1088]{2,1,0:T(8,128)(2,1)} %fusion.10), channel_id=1, source_target_pairs={{0,16},{16,0},{1,17},{17,1},{2,18},{18,2},{3,19},{19,3},{4,20},{20... | collective-permute-start | bytes 7102472 | tf_op jit(solution)/shard_map/ppermute | solution.py:275
  913.9 31.3 %collective-permute-start.38 = (bf16[2,272,1088]{2,1,0:T(8,128)(2,1)}, bf16[2,272,1088]{2,1,0:T(8,128)(2,1)}, u32[]{:S(2)}, u32[]{:S(2)}) collective-permute-start(bf16[2,272,1088]{2,1,0:T(8,128)(2,1)} %fusion.15), channel_id=1, source_target_pairs={{0,3},{1,0},{2,1},{3,2},{4,7},{5,4},{6,5},{7,6},{8,11},{9,8},{10,9... | collective-permute-start | bytes 3551240 | tf_op jit(solution)/shard_map/ppermute | solution.py:280
  927.3 107.8 %collective-permute-start.31 = (bf16[896,1088]{0,1:T(8,128)(2,1)}, bf16[896,1088]{0,1:T(8,128)(2,1)}, u32[]{:S(2)}, u32[]{:S(2)}) collective-permute-start(bf16[896,1088]{0,1:T(8,128)(2,1)} %copy.123), channel_id=1, source_target_pairs={{0,8},{4,12},{8,0},{12,4},{1,9},{5,13},{9,1},{13,5},{2,10},{6,14},... | collective-permute-start | bytes 5849096 | tf_op jit(solution)/shard_map/ppermute | solution.py:275
  947.5 48.0 %collective-permute-start.39 = (bf16[2,272,1088]{2,1,0:T(8,128)(2,1)S(1)}, bf16[2,272,1088]{2,1,0:T(8,128)(2,1)S(1)}, u32[]{:S(2)}, u32[]{:S(2)}) collective-permute-start(bf16[2,272,1088]{2,1,0:T(8,128)(2,1)S(1)} %fusion.17), channel_id=1, source_target_pairs={{0,3},{1,0},{2,1},{3,2},{4,7},{5,4},{6,5},{7,6},{8,11},{9,8},{10,9... | collective-permute-start | bytes 3551240 | tf_op jit(solution)/shard_map/ppermute | solution.py:280
  955.5 35.5 %collective-permute-start.43 = (bf16[272,1088]{1,0:T(8,128)(2,1)S(1)}, bf16[272,1088]{1,0:T(8,128)(2,1)S(1)}, u32[]{:S(2)}, u32[]{:S(2)}) collective-permute-start(bf16[272,1088]{1,0:T(8,128)(2,1)S(1)} %fusion.33), channel_id=1, source_target_pairs={{0,3},{1,0},{2,1},{3,2},{4,7},{5,4},{6,5},{7,6},{8,11},{9,8},{10,9... | collective-permute-start | bytes 1775624 | tf_op jit(solution)/shard_map/ppermute | solution.py:280
  991.2 15.8 %collective-permute-start.44 = (bf16[272,1088]{1,0:T(8,128)(2,1)S(1)}, bf16[272,1088]{1,0:T(8,128)(2,1)S(1)}, u32[]{:S(2)}, u32[]{:S(2)}) collective-permute-start(bf16[272,1088]{1,0:T(8,128)(2,1)S(1)} %fusion.22), channel_id=1, source_target_pairs={{0,3},{1,0},{2,1},{3,2},{4,7},{5,4},{6,5},{7,6},{8,11},{9,8},{10,9... | collective-permute-start | bytes 1775624 | tf_op jit(solution)/shard_map/ppermute | solution.py:280
  997.6 15.3 %collective-permute-start.40 = (bf16[272,1088]{1,0:T(8,128)(2,1)S(1)}, bf16[272,1088]{1,0:T(8,128)(2,1)S(1)}, u32[]{:S(2)}, u32[]{:S(2)}) collective-permute-start(bf16[272,1088]{1,0:T(8,128)(2,1)S(1)} %fusion.30), channel_id=1, source_target_pairs={{0,16},{16,0},{1,17},{17,1},{2,18},{18,2},{3,19},{19,3},{4,20},{20... | collective-permute-start | bytes 1775624 | tf_op jit(solution)/shard_map/ppermute | solution.py:275
  1007.1 15.1 %collective-permute-start.45 = (bf16[272,1088]{1,0:T(8,128)(2,1)S(1)}, bf16[272,1088]{1,0:T(8,128)(2,1)S(1)}, u32[]{:S(2)}, u32[]{:S(2)}) collective-permute-start(bf16[272,1088]{1,0:T(8,128)(2,1)S(1)} %fusion.24), channel_id=1, source_target_pairs={{0,3},{1,0},{2,1},{3,2},{4,7},{5,4},{6,5},{7,6},{8,11},{9,8},{10,9... | collective-permute-start | bytes 1775624 | tf_op jit(solution)/shard_map/ppermute | solution.py:280
  1023.6 25.8 %collective-permute-start.46 = (bf16[2,272,1088]{2,1,0:T(8,128)(2,1)}, bf16[2,272,1088]{2,1,0:T(8,128)(2,1)}, u32[]{:S(2)}, u32[]{:S(2)}) collective-permute-start(bf16[2,272,1088]{2,1,0:T(8,128)(2,1)} %pad_maximum_fusion.14), channel_id=1, source_target_pairs={{0,8},{4,12},{8,0},{12,4},{1,9},{5,13},{9,1},{13,5},{2,10},{6,14},... | collective-permute-start | bytes 3551240 | tf_op jit(solution)/shard_map/ppermute | solution.py:275
  1052.4 54.4 %collective-permute-start.47 = (f32[2,272,1088]{2,1,0:T(8,128)}, f32[2,272,1088]{2,1,0:T(8,128)}, u32[]{:S(2)}, u32[]{:S(2)}) collective-permute-start(f32[2,272,1088]{2,1,0:T(8,128)} %convert_add_fusion.5), channel_id=1, source_target_pairs={{0,4},{4,0},{8,12},{12,8},{1,5},{5,1},{9,13},{13,9},{2,6},{6,2},{1... | collective-permute-start | bytes 7102472 | tf_op jit(solution)/shard_map/ppermute | solution.py:275
  (104 other events, 1251.3 us)
Sparse Core Ops, SparseCore 0:
  669.2 60.4 all-reduce.4
  734.2 94.1 all-reduce.8
  831.4 32.4 all-reduce.6

commit v2 on v0

--- a/solution.py
+++ b/solution.py
@@ -1,6 +1,10 @@
+import functools
+
 import jax
 import jax.numpy as jnp
 from jax import lax
+from jax.experimental import pallas as pl
+from jax.experimental.pallas import tpu as pltpu
 from jax.sharding import PartitionSpec as P
 
 HEADS = 17
@@ -48,7 +52,7 @@
     return lax.all_gather(rows_kv, "ctx", axis=0, tiled=True)
 
 
-def local(
+def local_rows(
     prompt_in,
     cont_in,
     cont_seg,
@@ -251,6 +255,1562 @@
     )
 
 
+PAIRS = 2
+TILE = 2 * HEAD
+BF16 = jnp.bfloat16
+F32 = jnp.float32
+LOG2E = 1.4426950408889634
+SCALE2 = 0.125 * LOG2E
+HINT = 0.2
+NN = (((1,), (0,)), ((), ()))
+NT = (((1,), (1,)), ((), ()))
+TN = (((0,), (0,)), ((), ()))
+
+
+def dot(left_op, right_op, dims=NN):
+    return lax.dot_general(left_op, right_op, dims, preferred_element_type=F32)
+
+
+def swap(value, axis, bit):
+    count = lax.axis_size(axis)
+    return lax.ppermute(value, axis, [(place, place ^ bit) for place in range(count)])
+
+
+def turn(value, axis, steps):
+    count = lax.axis_size(axis)
+    return lax.ppermute(value, axis, [(place, (place + steps) % count) for place in range(count)])
+
+
+def halves(values, heads=2):
+    lane = lax.broadcasted_iota(jnp.int32, values.shape, 1)
+    zero = jnp.zeros_like(values)
+    return [jnp.where((lane < HEAD) == (head == 0), values, zero) for head in range(heads)]
+
+
+ANYWHERE = pl.BlockSpec(memory_space=pl.ANY)
+
+
+def blocks(*shape):
+    return pl.BlockSpec(shape, lambda i, *_: (0,) * len(shape))
+
+
+def shape_of(*shape, kind=BF16):
+    return jax.ShapeDtypeStruct(shape, kind)
+
+
+def launch(
+    kernel, name, scalars, grid, operands, in_specs, outs, scratch=(), limit=48, flops=0, traffic=16, exps=0, after=(), carry=(), aliases=None
+):
+    out_specs, out_shapes = [out[0] for out in outs], [out[1] for out in outs]
+    given = len(scalars) + len(operands)
+    tied = given + len(after) + len(carry)
+
+    def body(*refs):
+        made = refs[tied : tied + len(outs)]
+        kernel(*refs[:given], *made, *refs[tied + len(outs) + len(carry) :])
+
+    links = {len(scalars) + here: there for here, there in (aliases or {}).items()}
+    links.update({given + len(after) + i: len(outs) + i for i in range(len(carry))})
+    out = pl.pallas_call(
+        body,
+        grid_spec=pltpu.PrefetchScalarGridSpec(
+            num_scalar_prefetch=len(scalars),
+            grid=grid,
+            in_specs=list(in_specs) + [ANYWHERE] * (len(after) + len(carry)),
+            out_specs=out_specs + [ANYWHERE] * len(carry),
+            scratch_shapes=list(scratch),
+        ),
+        out_shape=out_shapes + [shape_of(*entry.shape, kind=entry.dtype) for entry in carry],
+        input_output_aliases=links,
+        compiler_params=pltpu.CompilerParams(vmem_limit_bytes=limit << 20),
+        cost_estimate=pl.CostEstimate(
+            flops=int(flops * HINT),
+            bytes_accessed=int(traffic * HINT * (1 << 20)),
+            transcendentals=int(exps * HINT),
+        ),
+        name=name,
+    )(*scalars, *operands, *after, *carry)
+    return (out[: len(outs)], *out[len(outs) :]) if carry else out
+
+
+def behind(arrays, token):
+    out = launch(
+        lambda *refs: None, "behind", (), (1,), (), (), (), after=(token,), carry=tuple(arrays)
+    )
+    return out[1:]
+
+
+def whole_out(*shape, kind=BF16):
+    return blocks(*shape), shape_of(*shape, kind=kind)
+
+
+def pack_kernel(place_ref, prompt_ref, cont_ref, w_ref, rows_ref, out_ref):
+    prompt_rows, width = prompt_ref.shape[1], prompt_ref.shape[2]
+    rows_ref[:prompt_rows, :width] = prompt_ref[0]
+    rows_ref[prompt_rows:, :width] = cont_ref[0]
+    rows_ref[:, width:] = jnp.zeros((rows_ref.shape[0], rows_ref.shape[1] - width), BF16)
+    place = place_ref[0]
+    own = 2 * PAIRS * HEAD
+    step = out_ref.shape[1] // 3
+    for part in range(3):
+        for at in range((width - HEAD) // own):
+
+            @pl.when(place == at)
+            def _():
+                cols = slice(part * width + at * own, part * width + (at + 1) * own)
+                out_ref[:, part * step : part * step + own] = w_ref[:, cols].astype(BF16)
+
+        last = w_ref[:, (part + 1) * width - HEAD : (part + 1) * width].astype(BF16)
+        out_ref[:, part * step + own : (part + 1) * step] = jnp.concatenate(
+            [last, jnp.zeros((last.shape[0], step - own - HEAD), BF16)], axis=1
+        )
+
+
+def pack(place, prompt_in, cont_in, w_qkv, padded):
+    rows = prompt_in.shape[1] + cont_in.shape[1]
+    operands = (prompt_in, cont_in, w_qkv)
+    return launch(
+        pack_kernel,
+        "pack",
+        (place,),
+        (1,),
+        operands,
+        [blocks(*entry.shape) for entry in operands],
+        [whole_out(rows, padded), whole_out(w_qkv.shape[0], 3 * (PAIRS + 1) * TILE)],
+    )
+
+
+def pack_more_kernel(
+    core_ref, fc_ref, proj_ref, bias_ref, prompt_ref, cont_ref, mine_ref, *refs
+):
+    copy_refs, (g_ref, gt_ref) = refs[:-2], refs[-2:]
+    quarter = fc_ref.shape[0] // 2
+    prompt_rows = prompt_ref.shape[1]
+    start = pl.multiple_of(core_ref[0] * quarter, quarter)
+    mine_ref[:quarter] = fc_ref[pl.ds(start, quarter), :].astype(BF16)
+    for core in range(2):
+
+        @pl.when(core_ref[0] == core)
+        def _():
+            mine_ref[quarter : 2 * quarter] = (
+                proj_ref[:, core * quarter : (core + 1) * quarter].T.astype(BF16)
+            )
+
+    bias = bias_ref[...]
+    pieces = []
+    for _ in range(3):
+        piece = bias.astype(BF16)
+        pieces.append(piece)
+        bias = bias - piece.astype(F32)
+    spare = mine_ref.shape[0] - 2 * quarter
+    pieces.append(jnp.zeros((spare - 3, bias.shape[1]), BF16))
+    mine_ref[2 * quarter :] = jnp.concatenate(pieces, axis=0)
+    for ref in copy_refs:
+        ref[...] = mine_ref[...]
+    g_ref[:prompt_rows] = prompt_ref[0]
+    g_ref[prompt_rows:] = cont_ref[0]
+    gt_ref[:, :prompt_rows] = prompt_ref[0].T
+    gt_ref[:, prompt_rows:] = cont_ref[0].T
+
+
+def pack_more(core, w_fc, w_proj, fc_bias, prompt_cot, cont_cot, after):
+    rows, width = prompt_cot.shape[1] + cont_cot.shape[1], prompt_cot.shape[2]
+    operands = (w_fc, w_proj, fc_bias[None], prompt_cot, cont_cot)
+    return launch(
+        pack_more_kernel,
+        "pack_more",
+        (core,),
+        (1,),
+        operands,
+        [blocks(*entry.shape) for entry in operands],
+        [
+            *[whole_out(w_fc.shape[0] + 16, w_fc.shape[1])] * 4,
+            whole_out(rows, width),
+            whole_out(width, rows),
+        ],
+        after=after,
+    )
+
+
+def in_order(own, other, place):
+    first = place == 0
+    return jnp.where(first, own, other), jnp.where(first, other, own)
+
+
+def project_kernel(
+    place_ref, x_ref, w_ref, gain_ref, bias_ref, col_bias_ref, *refs
+):
+    norm_ref, q_ref, k_ref, v_ref, kt_ref, vt_ref = refs[-6:]
+    values = x_ref[:, : w_ref.shape[0]].astype(F32)
+    average = jnp.mean(values, axis=1, keepdims=True)
+    centred = values - average
+    variance = jnp.mean(centred * centred, axis=1, keepdims=True)
+    normed = (centred * lax.rsqrt(variance + 1e-05) * gain_ref[...] + bias_ref[...]).astype(BF16)
+    norm_ref[0, : w_ref.shape[0]] = normed.T
+    extra = norm_ref.shape[1] - w_ref.shape[0]
+    at_row = lax.broadcasted_iota(jnp.int32, (extra, normed.shape[0]), 0)
+    norm_ref[0, w_ref.shape[0] :] = jnp.where(at_row == 0, 1.0, 0.0).astype(BF16)
+    tiles = q_ref.shape[0]
+    width = tiles * TILE
+    for part, out_ref, flip_ref in ((0, q_ref, None), (1, k_ref, kt_ref), (2, v_ref, vt_ref)):
+        cols = slice(part * width, (part + 1) * width)
+        out = (dot(normed, w_ref[:, cols]) + col_bias_ref[:, cols]).astype(BF16)
+        for tile in range(tiles):
+            piece = out[:, tile * TILE : (tile + 1) * TILE]
+            out_ref[tile, 0] = piece
+            if flip_ref is not None:
+                flip_ref[tile, 0] = piece.T
+
+
+def project(place, rows, w_own, gain, bias, col_bias, before, count, after=(), carry=()):
+    row_count, width = rows.shape[0], w_own.shape[0]
+    tiles = w_own.shape[1] // (3 * TILE)
+    tall = (
+        pl.BlockSpec((tiles, 1, row_count, TILE), lambda i, p: (0, p[0], 0, 0)),
+        shape_of(tiles, count, row_count, TILE),
+    )
+    flat = (
+        pl.BlockSpec((tiles, 1, TILE, row_count), lambda i, p: (0, p[0], 0, 0)),
+        shape_of(tiles, count, TILE, row_count),
+    )
+    operands = (rows, w_own, gain[None], bias[None], col_bias[None])
+    before = tuple(before or ())
+    return launch(
+        lambda *refs: project_kernel(*refs[:6], *refs[-6:]),
+        "project",
+        (place,),
+        (1,),
+        operands + before,
+        [blocks(*entry.shape) for entry in operands] + [ANYWHERE] * len(before),
+        [
+            (
+                pl.BlockSpec((1, width + 16, row_count), lambda i, p: (p[0], 0, 0)),
+                shape_of(count, width + 16, row_count),
+            ),
+            tall,
+            tall,
+            tall,
+            flat,
+            flat,
+        ],
+        aliases={len(operands) + i: i for i in range(len(before))},
+        flops=2 * row_count * width * w_own.shape[1],
+        after=after,
+        carry=carry,
+    )
+
+
+def own_mask(rows):
+    key_at = lax.broadcasted_iota(jnp.int32, (rows, rows), 0)
+    query_at = lax.broadcasted_iota(jnp.int32, (rows, rows), 1)
+    return key_at <= query_at
+
+
+def attend_kernel(
+    heads, spans, prompt_rows, place_ref, q_ref, k_ref, vt_ref, seg_col_ref, seg_row_ref, *refs
+):
+    o_refs, lse_ref, acc = refs[:spans], refs[-2], refs[-1]
+    step = pl.program_id(0)
+    distance = step % spans
+    block = place_ref[0] ^ distance
+    count, row_count = k_ref.shape[1], k_ref.shape[2]
+    cont_rows = row_count - prompt_rows
+
+    def part(queries, at, start, size, mask, before):
+        keys = k_ref[0, at, pl.ds(start, size), :]
+        scores = [dot(keys, query, NT) for query in queries]
+        if mask is not None:
+            scores = [jnp.where(mask, score, -1e30) for score in scores]
+        tops = [jnp.max(score, axis=0, keepdims=True) for score in scores]
+        if before is not None:
+            tops = [jnp.maximum(top, state[0]) for top, state in zip(tops, before)]
+        exps = [jnp.exp2(score * SCALE2 - top * SCALE2) for score, top in zip(scores, tops)]
+        totals = [jnp.sum(exp, axis=0, keepdims=True) for exp in exps]
+        after = []
+        for head in range(heads):
+            rows = slice(head * HEAD, (head + 1) * HEAD)
+            cols = slice(0, queries[head].shape[0])
+            out = dot(vt_ref[0, at, rows, pl.ds(start, size)], exps[head].astype(BF16))
+            total = totals[head]
+            if before is None:
+                acc[rows, cols] = out
+            else:
+                shrink = jnp.exp2((before[head][0] - tops[head]) * SCALE2)
+                total = total + before[head][1] * shrink
+                acc[rows, cols] = acc[rows, cols] * shrink + out
+            after.append((tops[head], total))
+        return after
+
+    def finish(start, size, states):
+        for head in range(heads):
+            rows = slice(head * HEAD, (head + 1) * HEAD)
+            top, total = states[head]
+            acc[rows, :size] = acc[rows, :size] / total
+            lse_ref[0, block, head : head + 1, pl.ds(start, size)] = top * SCALE2 + jnp.log2(total)
+        if heads == 1:
+            acc[HEAD:, :size] = jnp.zeros((TILE - HEAD, size), F32)
+        out = acc[:, :size].T.astype(BF16)
+        for at in range(spans):
+
+            @pl.when(distance == at)
+            def _():
+                o_refs[at][pl.ds(start, size), :] = out
+
+    def over_prompt(queries, total, states):
+        return lax.fori_loop(
+            0, total, lambda c, states: part(queries, c, 0, prompt_rows, None, states), states
+        )
+
+    @pl.when(step >= spans)
+    def _():
+        queries = halves(q_ref[0, block, :prompt_rows, :], heads)
+        states = part(queries, block, 0, prompt_rows, own_mask(prompt_rows), None)
+        finish(0, prompt_rows, over_prompt(queries, block, states))
+
+    @pl.when(step < spans)
+    def _():
+        before = jnp.maximum(block - 1, 0)
+        labels = seg_row_ref[block]
+        queries = halves(q_ref[0, block, prompt_rows:, :], heads)
+        own = own_mask(cont_rows) & (seg_col_ref[block] == labels)
+        near = (seg_col_ref[before] == labels) & (block > 0)
+        states = part(queries, block, prompt_rows, cont_rows, own, None)
+        states = part(queries, before, prompt_rows, cont_rows, near, states)
+        finish(prompt_rows, cont_rows, over_prompt(queries, count, states))
+
+
+def attend(pair, heads, spans, place, q, k, vt, seg_col, seg_row, prompt_rows, after=(), carry=()):
+    _, count, row_count, _ = q.shape
+    cont_rows = row_count - prompt_rows
+    pick = lambda i, s: (pair, 0, 0, 0)
+    pairs = spans * (prompt_rows + 2 * cont_rows) * prompt_rows * count // 2
+    return launch(
+        functools.partial(attend_kernel, heads, spans, prompt_rows),
+        "attend",
+        (place,),
+        (2 * spans,),
+        (q, k, vt, seg_col, seg_row),
+        [
+            pl.BlockSpec((1, count, row_count, TILE), pick),
+            pl.BlockSpec((1, count, row_count, TILE), pick),
+            pl.BlockSpec((1, count, TILE, row_count), pick),
+            blocks(count, cont_rows, 1),
+            blocks(count, 1, cont_rows),
+        ],
+        [whole_out(row_count, TILE)] * spans + [whole_out(1, count, 2, row_count, kind=F32)],
+        scratch=[pltpu.VMEM((TILE, max(prompt_rows, cont_rows)), F32)],
+        flops=4 * heads * TILE * pairs,
+        exps=heads * pairs,
+        after=after,
+        carry=carry,
+    )
+
+
+def attend_back_kernel(
+    heads,
+    spans,
+    prompt_rows,
+    place_ref,
+    q_ref,
+    k_ref,
+    v_ref,
+    kt_ref,
+    lse_ref,
+    seg_col_ref,
+    seg_row_ref,
+    *refs,
+):
+    do_refs, o_refs, refs = refs[:spans], refs[spans : 2 * spans], refs[2 * spans :]
+    dq_ref, dk_ref, dv_ref, dk_acc, dv_acc, dq_acc, do_s, o_s = refs
+    step = pl.program_id(0)
+    distance = step % spans
+    block = place_ref[0] ^ distance
+    count, row_count = k_ref.shape[1], k_ref.shape[2]
+    cont_rows = row_count - prompt_rows
+
+    @pl.when(step == 0)
+    def _():
+        dk_acc[...] = jnp.zeros_like(dk_acc)
+        dv_acc[...] = jnp.zeros_like(dv_acc)
+        if spans < count:
+            dq_ref[...] = jnp.zeros_like(dq_ref)
+
+    def part(given, at, start, size, mask, first):
+        rows = pl.ds(start, size)
+        for head in range(heads):
+            query, grad, lse, centre = (entry[head] for entry in given)
+            cols = slice(0, query.shape[0])
+            own = slice(head * HEAD, (head + 1) * HEAD)
+            scores = dot(k_ref[0, at, rows, :], query, NT)
+            if mask is not None:
+                scores = jnp.where(mask, scores, -1e30)
+            probability = jnp.exp2(scores * SCALE2 - lse)
+            grad_probability = dot(v_ref[0, at, rows, :], grad, NT)
+            grad_scores = (probability * (grad_probability - centre)).astype(BF16)
+            dv_acc[at, rows, :] += dot(probability.astype(BF16), grad)
+            dk_acc[at, rows, :] += dot(grad_scores, query)
+            out = dot(kt_ref[0, at, own, rows], grad_scores)
+            if first:
+                dq_acc[own, cols] = out
+            else:
+                dq_acc[own, cols] += out
+
+    def setup(start, size):
+        rows = pl.ds(start, size)
+        for at in range(spans):
+
+            @pl.when(distance == at)
+            def _():
+                do_s[:size] = do_refs[at][rows, :]
+                o_s[:size] = o_refs[at][rows, :]
+
+        grad = do_s[:size]
+        product = (grad.astype(F32) * o_s[:size].astype(F32)).T
+        centres = [
+            jnp.sum(product[head * HEAD : (head + 1) * HEAD], axis=0, keepdims=True)
+            for head in range(heads)
+        ]
+        lses = [lse_ref[0, block, head : head + 1, rows] for head in range(heads)]
+        return halves(q_ref[0, block, rows, :], heads), halves(grad, heads), lses, centres
+
+    def finish(start, size):
+        if heads == 1:
+            dq_acc[HEAD:, :size] = jnp.zeros((TILE - HEAD, size), F32)
+        dq_ref[0, block, pl.ds(start, size), :] = (dq_acc[:, :size].T * 0.125).astype(BF16)
+
+    @pl.when(step >= spans)
+    def _():
+        given = setup(0, prompt_rows)
+        part(given, block, 0, prompt_rows, own_mask(prompt_rows), True)
+
+        @pl.loop(0, block)
+        def _(c):
+            part(given, c, 0, prompt_rows, None, False)
+
+        finish(0, prompt_rows)
+
+    @pl.when(step < spans)
+    def _():
+        before = jnp.maximum(block - 1, 0)
+        labels = seg_row_ref[block]
+        own = own_mask(cont_rows) & (seg_col_ref[block] == labels)
+        near = (seg_col_ref[before] == labels) & (block > 0)
+        given = setup(prompt_rows, cont_rows)
+        part(given, block, prompt_rows, cont_rows, own, True)
+        part(given, before, prompt_rows, cont_rows, near, False)
+
+        @pl.loop(0, count)
+        def _(c):
+            part(given, c, 0, prompt_rows, None, False)
+
+        finish(prompt_rows, cont_rows)
+
+    @pl.when(step == pl.num_programs(0) - 1)
+    def _():
+        dk_ref[0] = (dk_acc[...] * 0.125).astype(BF16)
+        dv_ref[0] = dv_acc[...].astype(BF16)
+
+
+def attend_back(
+    pair, tile, heads, place, q, k, v, kt, lse, seg_col, seg_row, grads, outs, prompt_rows, after=(), carry=()
+):
+    _, count, row_count, _ = q.shape
+    spans = len(grads)
+    cont_rows = row_count - prompt_rows
+    pick = lambda i, s: (pair, 0, 0, 0)
+    tall = pl.BlockSpec((1, count, row_count, TILE), pick)
+    most = max(prompt_rows, cont_rows)
+    pairs = spans * (prompt_rows + 2 * cont_rows) * prompt_rows * count // 2
+    return launch(
+        functools.partial(attend_back_kernel, heads, spans, prompt_rows),
+        "attend_back",
+        (place,),
+        (2 * spans,),
+        (q, k, v, kt, lse, seg_col, seg_row, *grads, *outs),
+        [
+            tall,
+            tall,
+            tall,
+            pl.BlockSpec((1, count, TILE, row_count), pick),
+            blocks(1, count, 2, row_count),
+            blocks(count, cont_rows, 1),
+            blocks(count, 1, cont_rows),
+        ]
+        + [pl.BlockSpec((row_count, TILE), lambda i, s: (0, tile))] * spans
+        + [blocks(row_count, TILE)] * spans,
+        [whole_out(1, count, row_count, TILE)] * 3,
+        scratch=[
+            pltpu.VMEM((count, row_count, TILE), F32),
+            pltpu.VMEM((count, row_count, TILE), F32),
+            pltpu.VMEM((TILE, most), F32),
+            pltpu.VMEM((most, TILE), BF16),
+            pltpu.VMEM((most, TILE), BF16),
+        ],
+        limit=56,
+        flops=10 * heads * TILE * pairs,
+        exps=heads * pairs,
+        after=after,
+        carry=carry,
+    )
+
+
+def normalize(values):
+    average = jnp.mean(values, axis=1, keepdims=True)
+    centred = values - average
+    variance = jnp.mean(centred * centred, axis=1, keepdims=True)
+    rate = lax.rsqrt(variance + 1e-05)
+    return centred * rate, rate
+
+
+def normalize_back(unit, rate, grad):
+    shift = jnp.mean(grad, axis=1, keepdims=True)
+    along = jnp.mean(grad * unit, axis=1, keepdims=True)
+    return rate * (grad - shift - unit * along)
+
+
+def merge_kernel(places, place_ref, x_ref, w_ref, out_bias_ref, gain_ref, bias_ref, *refs):
+    pieces, last_ref, (hidden_ref, low_ref, flip_ref) = refs[:-4], refs[-4], refs[-3:]
+    own = 2 * PAIRS * HEAD
+    width = hidden_ref.shape[1]
+    total = x_ref[:, :width].astype(F32) + out_bias_ref[...]
+    for distance in range(places):
+        start = pl.multiple_of((place_ref[0] ^ distance) * own, own)
+        joined = jnp.concatenate(
+            [ref[...] for ref in pieces[distance * PAIRS : (distance + 1) * PAIRS]], axis=1
+        )
+        total = total + dot(joined, w_ref[pl.ds(start, own), :])
+    total = total + dot(last_ref[:, :HEAD], w_ref[width - HEAD :, :])
+    hidden_ref[...] = total
+    unit, _ = normalize(total)
+    low = (unit * gain_ref[...] + bias_ref[...]).astype(BF16)
+    low_ref[...] = low
+    flip_ref[...] = low.T
+
+
+def merge(place, rows, w_out, out_bias, gain, bias, pieces, last, after=(), carry=()):
+    row_count, width = rows.shape[0], w_out.shape[1]
+    size = 128
+    by_row = lambda cols: pl.BlockSpec((size, cols), lambda i, p: (i, 0))
+    return launch(
+        functools.partial(merge_kernel, len(pieces) // PAIRS),
+        "merge",
+        (place,),
+        (row_count // size,),
+        (rows, w_out, out_bias[None], gain[None], bias[None], *pieces, last),
+        [by_row(rows.shape[1]), blocks(*w_out.shape)]
+        + [blocks(1, width)] * 3
+        + [by_row(TILE)] * (len(pieces) + 1),
+        [
+            (by_row(width), shape_of(row_count, width, kind=F32)),
+            (by_row(width), shape_of(row_count, width)),
+            (
+                pl.BlockSpec((width, size), lambda i, p: (0, i)),
+                shape_of(width, row_count),
+            ),
+        ],
+        flops=2 * row_count * width * width,
+        after=after,
+        carry=carry,
+    )
+
+
+def bend_kernel(
+    places,
+    prompt_steps,
+    place_ref,
+    mlp_ref,
+    gm_ref,
+    hidden_ref,
+    g_ref,
+    w_ref,
+    gain_ref,
+    proj_bias_ref,
+    *refs,
+):
+    pieces, last_ref, refs = refs[: places * PAIRS], refs[places * PAIRS], refs[places * PAIRS + 1 :]
+    prompt_ref, cont_ref, gh_ref = refs[:3]
+    ga_refs, (ga_last_ref, *gw_refs, sums_ref, acc) = refs[3 : 3 + places], refs[3 + places :]
+    step = pl.program_id(0)
+    own = 2 * PAIRS * HEAD
+    width = hidden_ref.shape[1]
+    hidden = hidden_ref[...]
+    layer_out = (hidden + mlp_ref[...] + proj_bias_ref[...]).astype(BF16)
+
+    @pl.when(step < prompt_steps)
+    def _():
+        prompt_ref[0] = layer_out
+
+    @pl.when(step >= prompt_steps)
+    def _():
+        cont_ref[0] = layer_out
+
+    unit, rate = normalize(hidden)
+    grad_in = gm_ref[...]
+    grad_layer = g_ref[...].astype(F32)
+    grad_hidden = grad_layer + normalize_back(unit, rate, grad_in * gain_ref[...])
+    gh_ref[...] = grad_hidden
+    branch = grad_hidden.astype(BF16)
+    sums = [grad_hidden, grad_in * unit, grad_in, grad_layer]
+    sums = jnp.concatenate([jnp.sum(entry, axis=0, keepdims=True) for entry in sums], axis=0)
+
+    @pl.when(step == 0)
+    def _():
+        acc[...] = jnp.zeros_like(acc)
+        sums_ref[...] = sums
+
+    @pl.when(step > 0)
+    def _():
+        sums_ref[...] += sums
+
+    for distance in range(places):
+        start = pl.multiple_of((place_ref[0] ^ distance) * own, own)
+        rows = pl.ds(start, own)
+        ga_refs[distance][...] = dot(branch, w_ref[rows, :], NT).astype(BF16)
+        joined = jnp.concatenate(
+            [ref[...] for ref in pieces[distance * PAIRS : (distance + 1) * PAIRS]], axis=1
+        )
+        acc[rows, :] += dot(joined.T, branch)
+    last = dot(branch, w_ref[width - HEAD :, :], NT).astype(BF16)
+    ga_last_ref[...] = jnp.concatenate([last, jnp.zeros_like(last)], axis=1)
+    acc[width - HEAD :, :] += dot(last_ref[:, :HEAD].T, branch)
+
+    @pl.when(step == pl.num_programs(0) - 1)
+    def _():
+        quarter = width // 4
+        core, fsdp = place_ref[0] % 2, place_ref[1]
+        for beside, ref in enumerate(gw_refs):
+            for away in range(2):
+                start = ((fsdp ^ away) * 2 + (core ^ beside)) * quarter
+                ref[away] = acc[pl.ds(pl.multiple_of(start, 16), quarter), :].astype(BF16)
+
+
+def bend(place, mlp_out, gm, hidden, g, w_out, gain, proj_bias, pieces, last, prompt_rows, after=(), carry=()):
+    row_count, width = hidden.shape
+    size = 128
+    places = len(pieces) // PAIRS
+    prompt_steps = prompt_rows // size
+    own = 2 * PAIRS * HEAD
+    by_row = lambda cols: pl.BlockSpec((size, cols), lambda i, p: (i, 0))
+    return launch(
+        functools.partial(bend_kernel, places, prompt_steps),
+        "bend",
+        (place,),
+        (row_count // size,),
+        (mlp_out, gm, hidden, g, w_out, gain[None], proj_bias[None], *pieces, last),
+        [by_row(width)] * 4
+        + [blocks(*w_out.shape)]
+        + [blocks(1, width)] * 2
+        + [by_row(TILE)] * (len(pieces) + 1),
+        [
+            (
+                pl.BlockSpec((1, size, width), lambda i, p: (0, jnp.minimum(i, prompt_steps - 1), 0)),
+                shape_of(1, prompt_rows, width),
+            ),
+            (
+                pl.BlockSpec((1, size, width), lambda i, p: (0, jnp.maximum(i - prompt_steps, 0), 0)),
+                shape_of(1, row_count - prompt_rows, width),
+            ),
+            (by_row(width), shape_of(row_count, width, kind=F32)),
+        ]
+        + [(by_row(own), shape_of(row_count, own))] * places
+        + [
+            (by_row(TILE), shape_of(row_count, TILE)),
+            whole_out(2, width // 4, width),
+            whole_out(2, width // 4, width),
+            whole_out(4, width, kind=F32),
+        ],
+        scratch=[pltpu.VMEM((width, width), F32)],
+        flops=4 * row_count * width * width,
+        traffic=30,
+        after=after,
+        carry=carry,
+    )
+
+
+GELU_RATE = 0.7978845608028654
+
+
+def gelu_both(values):
+    square = values * values
+    bent = jnp.tanh(GELU_RATE * (values + 0.044715 * square * values))
+    half = 0.5 * (1.0 + bent)
+    slope = half + 0.5 * values * (1.0 - bent * bent) * (GELU_RATE * (1.0 + 0.134145 * square))
+    return values * half, slope
+
+
+def mlp_kernel(
+    parts,
+    first,
+    spot_ref,
+    x_ref,
+    g_ref,
+    xt_ref,
+    gt_ref,
+    *refs,
+):
+    own, far, beside = refs[:parts], refs[parts : 2 * parts], refs[2 * parts : 3 * parts]
+    before_refs = refs[3 * parts : 3 * parts + 2]
+    refs = refs[3 * parts + (0 if first else 2) :]
+    out_ref, gm_ref, keep_f, send_f, keep_p, send_p, gb_ref = refs[:7]
+    wf_s, wp_s, bias_s, biases, act_s, gp_s, wide, sems = refs[7:]
+    step = pl.program_id(0)
+    core, fsdp = spot_ref[0], spot_ref[1]
+    slot = step % 2
+    _, width, hidden = wf_s.shape
+    quarter = width // 4
+
+    def spot(away, across):
+        start = ((fsdp ^ away) * 2 + (core ^ across)) * quarter
+        return pl.ds(pl.multiple_of(start, 16), quarter)
+
+    def loads(at, to):
+        moves = [(own[at].at[pl.ds(2 * quarter, 16)], bias_s.at[to])]
+        for away, local in enumerate((own[at], far[at])):
+            for across, source in enumerate((local, beside[at].at[away])):
+                for weight, target in enumerate((wf_s, wp_s)):
+                    moves.append(
+                        (
+                            source.at[pl.ds(weight * quarter, quarter)],
+                            target.at[to, spot(away, across)],
+                        )
+                    )
+        return [
+            pltpu.make_async_copy(source, target, sems.at[to, i])
+            for i, (source, target) in enumerate(moves)
+        ]
+
+    @pl.when(step == 0)
+    def _():
+        for part in range(parts):
+            for copy in loads(part, part):
+                copy.start()
+
+    for part in range(parts):
+
+        @pl.when(step == part)
+        def _():
+            for copy in loads(part, part):
+                copy.wait()
+
+    bias = jnp.sum(bias_s[slot, :3, :].astype(F32), axis=0, keepdims=True)
+    biases[...] = bias
+
+    def over(total, body):
+        whole = total // 256
+
+        @pl.loop(0, whole)
+        def _(i):
+            body(pl.multiple_of(i * 256, 256), 256)
+
+        if total % 256:
+            body(whole * 256, total % 256)
+
+    def up(start, size):
+        cols = pl.ds(start, size)
+        pre_act = dot(x_ref[...], wf_s[slot, :, cols]) + biases[:, cols]
+        grad_act = dot(g_ref[...], wp_s[slot, :, cols])
+        activated, slope = gelu_both(pre_act)
+        grad_pre = (grad_act * slope).astype(BF16)
+        act_s[:, cols] = activated.astype(BF16)
+        gp_s[:, cols] = grad_pre
+        gb_ref[0, :, cols] = jnp.sum(grad_pre.astype(F32), axis=0, keepdims=True)
+
+    def weights(start, size):
+        cols = pl.ds(start, size)
+        for left, right, keep, send, by_part in (
+            (xt_ref, gp_s, keep_f, send_f, True),
+            (gt_ref, act_s, keep_p, send_p, False),
+        ):
+            wide[:, :size] = dot(left[...], right[:, cols]).astype(BF16)
+            for far in range(2):
+                for beside, to in enumerate((keep, send)):
+                    piece = wide[spot(far, beside), :size]
+                    if by_part:
+                        to[0, far, :, cols] = piece
+                    else:
+                        to[far, 0, :, cols] = piece
+
+    over(hidden, up)
+    over(hidden, weights)
+
+    if first:
+
+        @pl.when(step == 0)
+        def _():
+            out_ref[...] = jnp.zeros_like(out_ref)
+            gm_ref[...] = jnp.zeros_like(gm_ref)
+
+    else:
+
+        @pl.when(step == 0)
+        def _():
+            out_ref[...] = before_refs[0][...]
+            gm_ref[...] = before_refs[1][...]
+
+    def down(start, size):
+        rows = pl.ds(start, size)
+        out_ref[:, rows] += dot(act_s[...], wp_s[slot, rows, :], NT)
+        gm_ref[:, rows] += dot(gp_s[...], wf_s[slot, rows, :], NT)
+
+    over(width, down)
+
+
+def mlp(spot, x, g, xt, gt, own, far, beside, before=(), after=(), carry=()):
+    rows, width = x.shape
+    hidden = own[0].shape[1]
+    parts, quarter = len(own), width // 4
+    once = pl.Buffered(buffer_count=1)
+    whole = lambda *shape: pl.BlockSpec(shape, lambda k, s: (0,) * len(shape), pipeline_mode=once)
+    by_part = pl.BlockSpec((1, 2, quarter, hidden), lambda k, s: (k, 0, 0, 0))
+    by_far = pl.BlockSpec((2, 1, quarter, hidden), lambda k, s: (0, k, 0, 0))
+    total = (whole(rows, width), shape_of(rows, width, kind=F32))
+    by_part = (by_part, shape_of(parts, 2, quarter, hidden))
+    by_far = (by_far, shape_of(2, parts, quarter, hidden))
+    return launch(
+        functools.partial(mlp_kernel, parts, not before),
+        "mlp",
+        (spot,),
+        (parts,),
+        (x, g, xt, gt, *own, *far, *beside, *before),
+        [
+            whole(rows, width),
+            whole(rows, width),
+            whole(width, rows),
+            whole(width, rows),
+        ]
+        + [ANYWHERE] * (3 * parts)
+        + [whole(rows, width)] * len(before),
+        [
+            total,
+            total,
+            by_part,
+            by_part,
+            by_far,
+            by_far,
+            (
+                pl.BlockSpec((1, 1, hidden), lambda k, s: (k, 0, 0)),
+                shape_of(parts, 1, hidden, kind=F32),
+            ),
+        ],
+        scratch=[
+            pltpu.VMEM((2, width, hidden), BF16),
+            pltpu.VMEM((2, width, hidden), BF16),
+            pltpu.VMEM((2, 16, hidden), BF16),
+            pltpu.VMEM((1, hidden), F32),
+            pltpu.VMEM((rows, hidden), BF16),
+            pltpu.VMEM((rows, hidden), BF16),
+            pltpu.VMEM((width, 256), BF16),
+            pltpu.SemaphoreType.DMA((2, 9)),
+        ],
+        limit=62,
+        flops=12 * rows * width * hidden * parts,
+        traffic=40,
+        exps=rows * hidden * parts,
+        after=after,
+        carry=carry,
+    )
+
+
+def tail_kernel(prompt_rows, *refs):
+    grads, refs = refs[:9], refs[9:]
+    w_ref, norm_ref, rows_ref, gh_ref, keep_ref, come_ref, gain_ref, given_ref = refs[:8]
+    prompt_ref, cont_ref, qkv_ref, wo_ref, vec_ref = refs[8:13]
+    (
+        norms,
+        rows_s,
+        gh_s,
+        joined,
+        hold,
+        core_out,
+        core_in,
+        chip_out,
+        chip_in,
+        acc,
+        keep,
+        far_out,
+        far_in,
+        sums,
+        sums_in,
+        ring_in,
+        ring_all,
+        whole,
+        near_in,
+        left_out,
+        left_in,
+        vec_out,
+        vec_in,
+        wo_near,
+        wo_sum,
+        wo_ring,
+        wo_chip,
+        wo_all,
+        wo_core,
+        local_sem,
+        send_sem,
+        recv_sem,
+    ) = refs[13:]
+    place = lax.axis_index("ctx")
+    fsdp = lax.axis_index("fsdp")
+    tensor = lax.axis_index("tensor")
+    tensors = lax.axis_size("tensor")
+    count, row_count = grads[0].shape[1], grads[0].shape[2]
+    width = w_ref.shape[0]
+    half = width // 2
+    own = acc.shape[1]
+    shard = ring_in.shape[2]
+    chunk = 128
+    beside, across, far = {"ctx": place ^ 1}, {"ctx": place ^ 2}, {"fsdp": 1 - fsdp}
+    others = [{"tensor": lax.rem(tensor + k, tensors)} for k in range(1, tensors)]
+
+    barrier = pltpu.get_barrier_semaphore()
+    for partner in (beside, across, far, *others):
+        pl.semaphore_signal(barrier, inc=1, device_id=partner, device_id_type=pl.DeviceIdType.MESH)
+
+    loads = [pltpu.make_async_copy(norm_ref, norms, local_sem.at[0])]
+    loads.append(pltpu.make_async_copy(keep_ref, wo_core.at[0], local_sem.at[1]))
+    loads.append(pltpu.make_async_copy(come_ref, wo_near, local_sem.at[2]))
+    for load in loads:
+        load.start()
+    sent, used = [], []
+
+    def push(source, target, partner):
+        at = len(used)
+        used.append(at)
+        copy = pltpu.make_async_remote_copy(
+            src_ref=source,
+            dst_ref=target,
+            send_sem=send_sem.at[at],
+            recv_sem=recv_sem.at[at],
+            device_id=partner,
+            device_id_type=pl.DeviceIdType.MESH,
+        )
+        copy.start()
+        sent.append(copy)
+        return copy
+
+    quarter, part_rows = wo_sum.shape[0], wo_ring.shape[1]
+
+    def part_start(owner):
+        return pl.multiple_of(jnp.minimum(owner * part_rows, quarter - part_rows), 16)
+
+    def rows_grad(distance, out):
+        block = place ^ distance
+        for i, ref in enumerate(grads):
+            joined[:, i * TILE : (i + 1) * TILE] = ref[0, block]
+
+        @pl.loop(0, width // 256)
+        def _(i):
+            cols = pl.ds(pl.multiple_of(i * 256, 256), 256)
+            out[:, cols] = dot(joined[...], w_ref[cols, :], NT).astype(out.dtype)
+
+        if width % 256:
+            cols = pl.ds(width // 256 * 256, width % 256)
+            out[:, cols] = dot(joined[...], w_ref[cols, :], NT).astype(out.dtype)
+
+    rows_grad(3, core_out)
+    pl.semaphore_wait(barrier, 3 + len(others))
+    to_core = push(core_out, core_in.at[0], beside)
+    loads[1].wait()
+    loads[2].wait()
+    wo_sum[...] = (wo_core[0].astype(F32) + wo_near[...].astype(F32)).astype(BF16)
+    wo_to_ring = [
+        push(wo_sum.at[pl.ds(part_start(other["tensor"]), part_rows)], wo_ring.at[k], other)
+        for k, other in enumerate(others)
+    ]
+    rows_grad(2, hold)
+    to_core.wait_recv()
+
+    @pl.loop(0, row_count // chunk)
+    def _(i):
+        rows = pl.ds(pl.multiple_of(i * chunk, chunk), chunk)
+        chip_out[rows, :] = (hold[rows, :] + core_in[0, rows, :].astype(F32)).astype(BF16)
+
+    to_chip = push(chip_out, chip_in, across)
+
+    loads[0].wait()
+    to_far = [None] * 4
+
+    def weights(part):
+        @pl.loop(0, count)
+        def _(block):
+            if part < 3:
+                pieces = [grads[3 * part + pair][0, block] for pair in range(PAIRS)]
+            else:
+                pieces = [grads[3 * i + PAIRS][0, block][:, :HEAD] for i in range(3)]
+                pieces.append(jnp.zeros((row_count, own - 3 * HEAD), BF16))
+            piece = dot(norms[block], jnp.concatenate(pieces, axis=1))
+
+            @pl.when(block == 0)
+            def _():
+                acc[...] = piece
+
+            @pl.when(block > 0)
+            def _():
+                acc[...] += piece
+
+        sums[part] = acc[width : width + 8, :]
+        keep[part] = acc[pl.ds(pl.multiple_of(fsdp * half, 16), half), :]
+        far_out[part] = acc[pl.ds(pl.multiple_of((1 - fsdp) * half, 16), half), :].astype(BF16)
+        to_far[part] = push(far_out.at[part], far_in.at[part], far)
+
+    def joined_far(part):
+        to_far[part].wait_recv()
+        return keep[part] + far_in[part].astype(F32)
+
+    def start_of(owner):
+        return pl.multiple_of(jnp.minimum(owner * shard, half - shard), 16)
+
+    to_ring, to_all, to_near = [None] * 4, [None] * 4, [None] * 4
+
+    def ring(part, total):
+        sums_in[part] = total.astype(BF16)
+        to_ring[part] = [
+            push(
+                sums_in.at[part, pl.ds(start_of(other["tensor"]), shard)],
+                ring_in.at[part, k],
+                other,
+            )
+            for k, other in enumerate(others)
+        ]
+
+    def spread(part):
+        total = sums_in[part, pl.ds(start_of(tensor), shard), :].astype(F32)
+        for k, copy in enumerate(to_ring[part]):
+            copy.wait_recv()
+            total = total + ring_in[part, k].astype(F32)
+        ring_all[part, tensor] = total.astype(BF16)
+        to_all[part] = [
+            push(ring_all.at[part, tensor], ring_all.at[part, tensor], other) for other in others
+        ]
+
+    def gather(part):
+        for copy in to_all[part]:
+            copy.wait_recv()
+        for owner in range(tensors - 1):
+            whole[part, owner * shard : (owner + 1) * shard] = ring_all[part, owner]
+        rest = (tensors - 1) * shard
+        whole[part, rest:] = ring_all[part, tensors - 1, tensors * shard - half :]
+        if part < 3:
+            to_near[part] = [
+                push(whole.at[part], near_in.at[part, 0], beside),
+                push(whole.at[part], near_in.at[part, 1], across),
+            ]
+
+    weights(3)
+    to_core.wait_send()
+    sent.remove(to_core)
+    rows_grad(1, core_out)
+    to_core_2 = push(core_out, core_in.at[1], beside)
+    left_out[0] = joined_far(3).astype(BF16)
+    to_left = push(left_out.at[0], left_in.at[0], beside)
+    weights(0)
+    to_left.wait_recv()
+    left_out[1] = (left_out[0].astype(F32) + left_in[0].astype(F32)).astype(BF16)
+    to_left = push(left_out.at[1], left_in.at[1], across)
+    ring(0, joined_far(0))
+    weights(1)
+    wo_total = wo_sum[pl.ds(part_start(tensor), part_rows), :].astype(F32)
+    for k, copy in enumerate(wo_to_ring):
+        copy.wait_recv()
+        wo_total = wo_total + wo_ring[k].astype(F32)
+    wo_chip[0] = wo_total.astype(BF16)
+    wo_to_chip = push(wo_chip.at[0], wo_chip.at[1], across)
+    ring(1, joined_far(1))
+    weights(2)
+    spread(0)
+    rows_grad(0, hold)
+    ring(2, joined_far(2))
+    to_left.wait_recv()
+    ring(3, left_out[1].astype(F32) + left_in[1].astype(F32))
+    to_core_2.wait_recv()
+    wo_to_chip.wait_recv()
+    wo_all[tensor] = (wo_chip[0].astype(F32) + wo_chip[1].astype(F32)).astype(BF16)
+    wo_to_all = [push(wo_all.at[tensor], wo_all.at[tensor], other) for other in others]
+    spread(1)
+    gather(0)
+    to_chip.wait_recv()
+
+    vec_out[0, :8] = jnp.zeros((8, vec_out.shape[2]), F32)
+    vec_out[0, 8:] = given_ref[...]
+    chunks = row_count // chunk
+
+    def chunk_rows(i):
+        return pl.ds(pl.multiple_of(i * chunk, chunk), chunk)
+
+    def row_loads(i):
+        slot = i % 2
+        return [
+            pltpu.make_async_copy(gh_ref.at[chunk_rows(i)], gh_s.at[slot], local_sem.at[3 + slot]),
+            pltpu.make_async_copy(rows_ref.at[chunk_rows(i)], rows_s.at[slot], local_sem.at[5 + slot]),
+        ]
+
+    for load in row_loads(0):
+        load.start()
+
+    @pl.loop(0, chunks)
+    def _(i):
+        @pl.when(i + 1 < chunks)
+        def _():
+            for load in row_loads(i + 1):
+                load.start()
+
+        for load in row_loads(i):
+            load.wait()
+
+        rows = chunk_rows(i)
+        unit, rate = normalize(rows_s[i % 2, :, :width].astype(F32))
+        grad = hold[rows, :] + core_in[1, rows, :].astype(F32) + chip_in[rows, :].astype(F32)
+        back = normalize_back(unit, rate, grad * gain_ref[...])
+        out = (gh_s[i % 2] + back).astype(BF16)
+
+        @pl.when(i < prompt_rows // chunk)
+        def _():
+            prompt_ref[0, rows, :] = out
+
+        @pl.when(i >= prompt_rows // chunk)
+        def _():
+            cont_ref[0, chunk_rows(i - prompt_rows // chunk), :] = out
+
+        vec_out[0, 0:1, :width] += jnp.sum(grad * unit, axis=0, keepdims=True)
+        vec_out[0, 1:2, :width] += jnp.sum(grad, axis=0, keepdims=True)
+
+    spread(2)
+    for row, part in ((2, 0), (3, 2)):
+        cols = pl.ds(pl.multiple_of(place * own, own), own)
+        vec_out[0, row : row + 1, cols] = sums[part, 0:1, :]
+        left = slice(part * HEAD, (part + 1) * HEAD)
+        vec_out[0, row : row + 1, width - HEAD : width] = sums[3, 0:1, left]
+    spread(3)
+    gather(1)
+
+    def forward(part):
+        to_near[part][1].wait_recv()
+        return push(near_in.at[part, 1], near_in.at[part, 2], beside)
+
+    def store(part, passed):
+        to_near[part][0].wait_recv()
+        passed.wait_recv()
+        sources = [whole.at[part]] + [near_in.at[part, i] for i in range(3)]
+        for distance, source in enumerate(sources):
+            for block in range(count):
+
+                @pl.when(place ^ distance == block)
+                def _():
+                    start = part * width + block * own
+                    qkv_ref[:, start : start + own] = source[...]
+
+    partners = (beside, across, far, {"tensor": tensor ^ 1}, {"tensor": tensor ^ 2})
+
+    def exchange(level):
+        return push(vec_out.at[level], vec_in.at[level], partners[level])
+
+    def add(level, copy):
+        copy.wait_recv()
+        vec_out[level + 1] = vec_out[level] + vec_in[level]
+
+    add(0, exchange(0))
+    passed_0 = forward(0)
+    step = exchange(1)
+    gather(2)
+    add(1, step)
+    step = exchange(2)
+    gather(3)
+    store(0, passed_0)
+    add(2, step)
+    for copy in wo_to_all:
+        copy.wait_recv()
+    for owner in range(tensors - 1):
+        wo_core[0, owner * part_rows : (owner + 1) * part_rows] = wo_all[owner]
+    rest = (tensors - 1) * part_rows
+    wo_core[0, rest:] = wo_all[tensors - 1, tensors * part_rows - quarter :]
+    wo_to_core = push(wo_core.at[0], wo_core.at[1], beside)
+    step = exchange(3)
+    passed_1 = forward(1)
+    for part in range(3):
+        cols = slice((part + 1) * width - HEAD, (part + 1) * width)
+        qkv_ref[:, cols] = whole[3, :, part * HEAD : (part + 1) * HEAD]
+    add(3, step)
+    step = exchange(4)
+    store(1, passed_1)
+    passed_2 = forward(2)
+    add(4, step)
+    vec_ref[...] = vec_out[5]
+    wo_to_core.wait_recv()
+    core = place % 2
+    for away in range(2):
+        wo_ref[pl.ds(pl.multiple_of((core ^ away) * quarter, 16), quarter), :] = wo_core[away]
+    store(2, passed_2)
+    for copy in sent:
+        copy.wait_send()
+
+
+def tail(
+    grads, w_own, normed, rows, grad_hidden, gain, vectors, out_keep, out_come, prompt_rows, after=()
+):
+    count, depth, row_count = normed.shape
+    width, cols = w_own.shape
+    half, own = width // 2, 2 * PAIRS * HEAD
+    tensors = lax.axis_size("tensor")
+    shard = -(-half // tensors // 16) * 16
+    padded = rows.shape[1]
+    in_vmem = pl.BlockSpec(memory_space=pltpu.VMEM)
+    vmem = lambda *shape, kind=BF16: pltpu.VMEM(shape, kind)
+    copies = 4 + 4 * 2 * (tensors - 1) + 3 + 3 * 3 + 2 + 5 + 2 * (tensors - 1) + 2
+    given = len(grads) + 8
+    quarter = width // 4
+    part_rows = -(-quarter // tensors // 16) * 16
+
+    def body(*refs):
+        tail_kernel(prompt_rows, *refs[:given], *refs[given + len(after) :])
+
+    return pl.pallas_call(
+        body,
+        in_specs=[in_vmem] * (len(grads) + 1) + [ANYWHERE] * 5 + [in_vmem] * 2 + [ANYWHERE] * len(after),
+        out_specs=[in_vmem] * 5,
+        out_shape=[
+            shape_of(1, prompt_rows, width),
+            shape_of(1, row_count - prompt_rows, width),
+            shape_of(half, 3 * width),
+            shape_of(half, width),
+            shape_of(16, padded, kind=F32),
+        ],
+        scratch_shapes=[
+            vmem(*normed.shape),
+            vmem(2, TILE, padded),
+            vmem(2, TILE, width, kind=F32),
+            vmem(row_count, cols),
+            vmem(row_count, width, kind=F32),
+            vmem(row_count, width),
+            vmem(2, row_count, width),
+            vmem(row_count, width),
+            vmem(row_count, width),
+            vmem(depth, own, kind=F32),
+            vmem(4, half, own, kind=F32),
+            vmem(4, half, own),
+            vmem(4, half, own),
+            vmem(4, 8, own, kind=F32),
+            vmem(4, half, own),
+            vmem(4, tensors - 1, shard, own),
+            vmem(4, tensors, shard, own),
+            vmem(4, half, own),
+            vmem(3, 3, half, own),
+            vmem(2, half, own),
+            vmem(2, half, own),
+            vmem(6, 16, padded, kind=F32),
+            vmem(5, 16, padded, kind=F32),
+            vmem(quarter, width),
+            vmem(quarter, width),
+            vmem(tensors - 1, part_rows, width),
+            vmem(2, part_rows, width),
+            vmem(tensors, part_rows, width),
+            vmem(2, quarter, width),
+            pltpu.SemaphoreType.DMA((7,)),
+            pltpu.SemaphoreType.DMA((copies,)),
+            pltpu.SemaphoreType.DMA((copies,)),
+        ],
+        compiler_params=pltpu.CompilerParams(
+            vmem_limit_bytes=62 << 20, collective_id=1, has_side_effects=True
+        ),
+        cost_estimate=pl.CostEstimate(
+            flops=4 * count * row_count * width * cols, bytes_accessed=30 << 20, transcendentals=0
+        ),
+        name="tail",
+    )(*grads, w_own, normed, rows, grad_hidden, out_keep, out_come, gain[None], vectors, *after)
+
+
+def join_kernel(spot_ref, *refs):
+    firsts, lasts, (keep_o, come_o) = refs[:4], refs[4:8], refs[8:10]
+    out_f, sum_f, out_p, sum_p, out_o, sum_o, total = refs[10:]
+    step = pl.program_id(0)
+    eighth = out_f.shape[2]
+    chip = spot_ref[4] // 2
+    sums_o = (keep_o[...].astype(F32) + come_o[...].astype(F32)).astype(BF16)
+    sum_o[...] = sums_o[0]
+    out_o[...] = sums_o[1]
+    for entries, here in ((firsts, step < 2), (lasts, step >= 2)):
+        keep_f, come_f, keep_p, come_p = entries
+
+        @pl.when(here)
+        def _():
+            for at in range(2):
+                total[...] = keep_f[0, at].astype(F32) + come_f[0, at].astype(F32)
+                for target, away in ((sum_f, 0), (out_f, 1)):
+                    rows = pl.ds(pl.multiple_of((chip ^ away) * eighth, 8), eighth)
+                    target[0, at] = total[rows, :].astype(BF16)
+            for target, at in ((sum_p, 0), (out_p, 1)):
+                target[0] = (keep_p[at, 0].astype(F32) + come_p[at, 0].astype(F32)).astype(BF16)
+
+
+def join(spot, firsts, lasts, outs, after=()):
+    _, _, quarter, hidden = firsts[0].shape
+    specs = []
+    for part in (lambda k: jnp.minimum(k, 1), lambda k: jnp.maximum(k - 2, 0)):
+        by_part = pl.BlockSpec((1, 2, quarter, hidden), lambda k, s, part=part: (part(k), 0, 0, 0))
+        by_far = pl.BlockSpec((2, 1, quarter, hidden), lambda k, s, part=part: (0, part(k), 0, 0))
+        specs += [by_part, by_part, by_far, by_far]
+    eighth = quarter // 2
+    fc = pl.BlockSpec((1, 2, eighth, hidden), lambda k, s: (k, 0, 0, 0))
+    proj = pl.BlockSpec((1, quarter, hidden), lambda k, s: (k, 0, 0))
+    return launch(
+        join_kernel,
+        "join",
+        (spot,),
+        (4,),
+        (*firsts, *lasts, *outs),
+        specs + [blocks(*entry.shape) for entry in outs],
+        [
+            (fc, shape_of(4, 2, eighth, hidden)),
+            (fc, shape_of(4, 2, eighth, hidden)),
+            (proj, shape_of(4, quarter, hidden)),
+            (proj, shape_of(4, quarter, hidden)),
+            whole_out(*outs[0].shape[1:]),
+            whole_out(*outs[0].shape[1:]),
+        ],
+        scratch=[pltpu.VMEM((quarter, hidden), F32)],
+        traffic=30,
+        after=after,
+    )
+
+
+def own_columns(matrix, place):
+    width = matrix.shape[1] // 3
+    own = 2 * PAIRS * HEAD
+    blank = jnp.zeros((matrix.shape[0], TILE - HEAD), matrix.dtype)
+    pieces = []
+    for part in range(3):
+        whole = matrix[:, part * width : (part + 1) * width]
+        pieces += [
+            lax.dynamic_slice_in_dim(whole, place * own, own, 1),
+            whole[:, width - HEAD :],
+            blank,
+        ]
+    return jnp.concatenate(pieces, axis=1)
+
+
+def local_heads(
+    prompt_in,
+    cont_in,
+    cont_seg,
+    ln1_gain,
+    ln1_bias,
+    w_qkv,
+    qv_bias,
+    w_out,
+    out_bias,
+    ln2_gain,
+    ln2_bias,
+    w_fc,
+    fc_bias,
+    w_proj,
+    proj_bias,
+    prompt_cot,
+    cont_cot,
+):
+    width = prompt_in.shape[2]
+    prompt_rows, cont_rows = prompt_in.shape[1], cont_in.shape[1]
+    row_count = prompt_rows + cont_rows
+    count = lax.axis_size("ctx")
+    place = lax.axis_index("ctx")
+    core, chip = place % 2, place // 2
+    fsdp = lax.axis_index("fsdp")
+    tensor = lax.axis_index("tensor")
+    tensors = lax.axis_size("tensor")
+    own_width = 2 * PAIRS * HEAD
+    half, hidden_units = w_fc.shape
+    quarter = half // 2
+    eighth = quarter // 2
+    padded = (width + TILE - 1) // TILE * TILE
+    at = place.reshape(1)
+    spot = jnp.stack([core, fsdp, tensor, jnp.int32(tensors), place])
+
+    rows_own, w_mine = pack(at, prompt_in, cont_in, w_qkv, padded)
+    rows_across = swap(rows_own, "ctx", 2)
+    rows_beside = swap(rows_own, "ctx", 1)
+    w_far = swap(w_mine, "fsdp", 1)
+    zero_bias = jnp.zeros_like(qv_bias[0])
+    col_bias = own_columns(jnp.concatenate([qv_bias[0], zero_bias, qv_bias[1]])[None], place)[0]
+
+    mine, for_far, for_two, for_three, grad_layer, grad_flip = pack_more(
+        core.reshape(1), w_fc, w_proj, fc_bias, prompt_cot, cont_cot, (rows_own,)
+    )
+    out_mine = w_out.astype(BF16)
+    one_away = turn(mine, "tensor", 1)
+
+    w_own = jnp.concatenate(in_order(w_mine, w_far, fsdp), axis=0)
+    step_in = functools.partial(
+        project, w_own=w_own, gain=ln1_gain, bias=ln1_bias, col_bias=col_bias, count=count
+    )
+    made = step_in(at, rows_own, before=None, after=(mine,))
+    made, for_far, out_mine = step_in(
+        at ^ 1, rows_beside, before=made, carry=(for_far, out_mine)
+    )
+    near_far, out_far = swap(for_far, "fsdp", 1), swap(out_mine, "fsdp", 1)
+    (rows_across,) = behind((rows_across,), made[1])
+    rows_corner = swap(rows_across, "ctx", 1)
+    made = step_in(at ^ 2, rows_across, before=made, after=(one_away,))
+    made, for_two = step_in(at ^ 3, rows_corner, before=made, carry=(for_two,))
+    two_away, one_far = turn(for_two, "tensor", 2), swap(one_away, "fsdp", 1)
+    normed, q, k, v, kt, vt = made
+
+    labels = cont_seg[0].reshape(count, cont_rows)
+    seg_col, seg_row = labels[:, :, None], labels[:, None, :]
+    near = (q, k, vt, seg_col, seg_row, prompt_rows)
+    heads_out, lses = [], []
+    returned = [[] for _ in range(count)]
+
+    def send_back(outs, lse):
+        heads_out.append(outs)
+        lses.append(lse)
+        for distance, out in enumerate(outs):
+            returned[distance].append(swap(out, "ctx", distance) if distance else out)
+
+    (*outs, lse), for_three = attend(0, 2, count, at, *near, carry=(for_three,))
+    three_away = turn(for_three, "tensor", 3)
+    send_back(outs, lse)
+    *outs, lse = attend(1, 2, count, at, *near, after=(outs[0],))
+    send_back(outs, lse)
+    (two_away,) = behind((two_away,), outs[0])
+    two_far = swap(two_away, "fsdp", 1)
+    last_out, lse = attend(PAIRS, 1, 1, at, *near, after=(outs[0], two_away))
+    lses.append(lse)
+    near_far, one_far = behind((near_far, one_far), last_out)
+    beside_first = (
+        swap(jnp.stack([mine, near_far]), "ctx", 1),
+        swap(jnp.stack([one_away, one_far]), "ctx", 1),
+    )
+    out_full = jnp.concatenate(in_order(out_mine, out_far, fsdp), axis=0)
+    pieces = [piece for entry in returned for piece in entry]
+    (hidden, mlp_low, mlp_flip), three_away, two_far = merge(
+        at,
+        rows_own,
+        out_full,
+        out_bias,
+        ln2_gain,
+        ln2_bias,
+        pieces,
+        last_out,
+        carry=(three_away, two_far),
+    )
+    three_far = swap(three_away, "fsdp", 1)
+    beside_two = swap(jnp.stack([two_away, two_far]), "ctx", 1)
+
+    given = (spot, mlp_low, grad_layer, mlp_flip, grad_flip)
+    mlp_out, grad_mlp_in, *grads_first, bias_first = mlp(
+        *given, (mine, one_away), (near_far, one_far), beside_first
+    )
+    (three_far,) = behind((three_far,), bias_first)
+    beside_last = (beside_two, swap(jnp.stack([three_away, three_far]), "ctx", 1))
+    come_first = [swap(grads_first[1], "ctx", 1), swap(grads_first[3], "ctx", 1)]
+    mlp_out, grad_mlp_in, *grads_last, bias_last = mlp(
+        *given,
+        (two_away, three_away),
+        (two_far, three_far),
+        beside_last,
+        before=(mlp_out, grad_mlp_in),
+    )
+    come_last = [swap(grads_last[1], "ctx", 1), swap(grads_last[3], "ctx", 1)]
+    grad_fc_bias = jnp.concatenate([bias_first, bias_last], axis=0)
+    prompt_out, cont_out, grad_hidden, *rest = bend(
+        jnp.stack([place, fsdp]),
+        mlp_out,
+        grad_mlp_in,
+        hidden,
+        grad_layer,
+        out_full,
+        ln2_gain,
+        proj_bias,
+        pieces,
+        last_out,
+        prompt_rows,
+    )
+    grads_own, (grad_last, out_keep, out_send, sums2) = rest[:count], rest[count:]
+    grads_all = [grads_own[0]] + [swap(grads_own[k], "ctx", k) for k in range(1, count)]
+
+    def added(left, right):
+        return left.astype(F32) + right.astype(F32)
+
+    def over_tensor(parts, token):
+        come = [turn(parts[k], "tensor", -k) for k in range(1, tensors)]
+        total = parts[0].astype(F32)
+        for part in behind(come, token):
+            total = total + part.astype(F32)
+        return total
+
+    def back(pair, tile, heads, grads, outs, after=()):
+        return attend_back(
+            pair, tile, heads, at, q, k, v, kt, lses[pair], seg_col, seg_row, grads, outs, prompt_rows, after
+        )
+
+    grads_left = back(PAIRS, 0, 1, [grad_last], [last_out])
+    out_f, sum_f, out_p, sum_p, out_o, sum_o = join(
+        spot,
+        (grads_first[0], come_first[0], grads_first[2], come_first[1]),
+        (grads_last[0], come_last[0], grads_last[2], come_last[1]),
+        (out_keep, swap(out_send, "ctx", 1)),
+        (grads_left[0], *grads_all[1:]),
+    )
+    grads_pair = [back(0, 0, 2, grads_all, heads_out[0], (out_f, out_p))]
+    come_o = swap(out_o, "fsdp", 1)
+    come_f, come_p = swap(out_f, "ctx", 2), swap(out_p, "fsdp", 1)
+    come_f, come_p = behind((come_f, come_p), grads_pair[0][0])
+    sum_f = added(sum_f, come_f).astype(BF16)
+    sum_p = added(sum_p, come_p).astype(BF16)
+    out_f, sum_f = sum_f[:, 1], sum_f[:, 0]
+    grads_pair.append(back(1, 1, 2, grads_all, heads_out[1], (out_f, sum_p, grads_pair[0][0])))
+    (come_f,) = behind((swap(out_f, "fsdp", 1),), grads_pair[1][0])
+    sum_f = added(sum_f, come_f).astype(BF16)
+    sum_p = over_tensor(sum_p, grads_pair[1][0]).astype(BF16)
+    ordered = [entry[part] for part in range(3) for entry in (*grads_pair, grads_left)]
+    vectors = jnp.concatenate([sums2, jnp.zeros((tensors, hidden_units), F32)], axis=0)
+    for distance in range(tensors):
+        vectors = lax.dynamic_update_slice(
+            vectors, grad_fc_bias[distance], (4 + (tensor - distance) % tensors, 0)
+        )
+    vectors = jnp.pad(vectors, ((0, 0), (0, padded - width)))
+    prompt_grad, cont_grad, sum_qkv, sum_out, late = tail(
+        ordered,
+        w_own,
+        normed,
+        rows_own,
+        grad_hidden,
+        ln1_gain,
+        vectors,
+        sum_o,
+        come_o,
+        prompt_rows,
+        (sum_f, sum_p),
+    )
+    sum_f = over_tensor(sum_f, late).astype(BF16)
+    (come_p,) = behind((swap(sum_p, "ctx", 2),), late)
+    sum_p = added(sum_p, come_p).astype(BF16)
+    far_f = swap(sum_f, "ctx", 2)
+    sum_f = jnp.concatenate(in_order(sum_f, far_f, chip), axis=0)
+    both = jnp.stack([sum_f, sum_p])
+    both = jnp.concatenate(in_order(both, swap(both, "ctx", 1), core), axis=1).astype(F32)
+    own_fc, own_proj = both[0], both[1].T
+
+
+    fc_bias_sum = lax.dynamic_index_in_dim(late, 12 + tensor, 0, False)[:hidden_units]
+    return (
+        prompt_out,
+        cont_out,
+        prompt_grad,
+        cont_grad,
+        late[0, :width],
+        late[1, :width],
+        sum_qkv.astype(F32),
+        late[2:4, :width],
+        sum_out.astype(F32),
+        late[8, :width],
+        late[9, :width],
+        late[10, :width],
+        own_fc,
+        fc_bias_sum,
+        own_proj,
+        late[11, :width],
+    )
+
+
 def solution(mesh):
     placed = (
         P(("fsdp", "tensor"), "ctx", None),
@@ -271,8 +1831,9 @@
         P(("fsdp", "tensor"), "ctx", None),
         P(("fsdp", "tensor"), "ctx", None),
     )
+    by_heads = HEADS // mesh.shape["ctx"] == PAIRS * 2 and HEADS % mesh.shape["ctx"] == 1
     return jax.shard_map(
-        local,
+        local_heads if by_heads else local_rows,
         mesh=mesh,
         in_specs=placed,
         out_specs=(

time: 2610 us -> 750 us (0.29)
  waiting for transfers between devices: 922 us -> 108 us
  matrix products: 778 us -> 0 us
  Pallas kernels: 0 us -> 500 us
  blocking collectives: 462 us -> 0 us
  other arithmetic: 287 us -> 37.9 us
  local copies, waits for them, and re-layouts: 124 us -> 59.2 us
  starting transfers between devices: 5.2 us -> 37.9 us
    dot_general x131 -> x0, matrix products: 778 us -> none  [the longest x55 307 us: inner_last(): lax.dot_general(left_op, right_op, (((1,), (1,)), ((), ())), preferred_el...]
    pallas_call x0 -> x27, Pallas kernels: none -> 500 us  [the longest x26 374 us: launch(): pl.pallas_call(body, grid_spec=pltpu.PrefetchScalarGridSpec(num_scalar_pr...]
    psum x3 -> x0, blocking collectives: 462 us -> none  [the longest x1 407 us: local(): sum_qkv, sum_out = lax.psum((shard_qkv, shard_out), ('ctx', 'tensor'))]
    reduce_scatter x4 -> x0, waiting for transfers between devices: 407 us -> none  [the longest x1 260 us: local(): lax.psum_scatter(grad_mlp_part, 'tensor', scatter_dimension=0, tiled=True)]
    all_gather x7 -> x0, waiting for transfers between devices: 268 us -> none  [the longest x1 129 us: local(): mlp_rows = lax.all_gather(mlp_low, 'tensor', axis=0, tiled=True)]
    convert_element_type x23 -> x9, other arithmetic: 203 us -> 16.3 us  [the longest x1 5.67 us: local_heads(): sum_qkv.astype(F32)]
    unnamed x14 -> x0, waiting for transfers between devices: 124 us -> none
    psum x1 -> x0, waiting for transfers between devices: 118 us -> none  [local(): lax.psum((grad_w_fc, grad_w_proj, grad_fc_bias), ('fsdp', 'ctx'))]
  transfers between devices with their start and end apart: 15 -> 43, of which waited for: 10 -> 15; matrix products, arithmetic and copies ran while one was open for 16% -> 7% of each run, Pallas kernels for 0% -> 64%
where the time goes in v2:
time: 750 us; the launch traced here: 745 us
  Pallas kernels  500 us (67%)
  waiting for transfers between devices  108 us (14%)
  local copies, waits for them, and re-layouts  59.2 us (8%)
  starting transfers between devices  37.9 us (5%)
  other arithmetic  37.9 us (5%)
    pallas_call x26, Pallas kernels, launch(): pl.pallas_call(body, grid_spec=pltpu.PrefetchScalarGridSpec(num_scalar_pr...  374 us
    pallas_call x1, Pallas kernels, tail(): pl.pallas_call(body, in_specs=[in_vmem] * (len(grads) + 1) + [ANYWHERE] *...  127 us
    ppermute x34, waiting for transfers between devices, swap(): lax.ppermute(value, axis, [(place, place ^ bit) for place in range(count)])  59.7 us
    unnamed x183, local copies, waits for them, and re-layouts  48.9 us
    ppermute x9, waiting for transfers between devices, turn(): lax.ppermute(value, axis, [(place, (place + steps) % count) for place in...  48 us
    ppermute x34, starting transfers between devices, swap(): lax.ppermute(value, axis, [(place, place ^ bit) for place in range(count)])  26.3 us
  transfers between devices with their start and end apart: 43, of which 15 were waited for; matrix products, arithmetic and copies ran while one was open for 7% of the time, Pallas kernels for 64%

profile of v2, /device:TPU:0, one launch (start us, length us, event | category | flops | bytes accessed | tf_op | source)
XLA Modules:
  0.0 745.0 jit_solution(1665750009785859466)
XLA Ops:
  5.6 4.7 pack.1
  10.3 2.9 collective-permute-start.1
  15.0 3.5 copy.85.refs_2_
  20.0 2.2 copy.87.refs_5_
  26.6 6.9 pack_more.1
  34.8 6.3 collective-permute-done.1
  43.3 2.3 copy-done.8
  45.9 7.0 project.4
  52.9 9.3 %project.5 = (bf16[4,1104,896]{2,1,0:T(8,128)(2,1)}, bf16[3,4,896,128]{3,2,1,0:T(8,128)(2,1)}, bf16[3,4,896,128]{3,2,1,0:T(8,128)(2,1)}, bf16[3,4,896,128]{3,2,1...) custom-call(s32[1]{0:T(128)S(6)} %xor.9.refs_0_, ...), custom_call_target="tpu_custom_call", output_to_operand_aliasing={{0}: (6, {}), {1}: (7, {}), {2}: (8, {}), {3}: (9, {}), {4}... | custom-call | flops 449209952 | bytes 3355443 | tf_op jit(solution)/shard_map/project/pallas_call | solution.py:314
  66.0 31.1 %collective-permute-done.5.refs_12_.refs_6_ = bf16[560,1088]{1,0:T(8,128)(2,1)} collective-permute-done((bf16[560,1088]{1,0:T(8,128)(2,1)S(1)}, bf16[560,1088]{1,0:T(8,128)(2,1)}, u32[]{:S(2)}, u32[]{:S(2)}) %collective-permute-start.5) | collective-permute-done | bytes 1218592 | tf_op jit(solution)/shard_map/ppermute | solution.py:281
  97.2 8.6 %project.6 = (bf16[4,1104,896]{2,1,0:T(8,128)(2,1)}, bf16[3,4,896,128]{3,2,1,0:T(8,128)(2,1)}, bf16[3,4,896,128]{3,2,1,0:T(8,128)(2,1)}, bf16[3,4,896,128]{3,2,1...) custom-call(s32[1]{0:T(128)S(6)} %xor.11.refs_0_, ...), custom_call_target="tpu_custom_call", output_to_operand_aliasing={{0}: (6, {}), {1}: (7, {}), {2}: (8, {}), {3}: (9, {}), {4}... | custom-call | flops 449209952 | bytes 3355443 | tf_op jit(solution)/shard_map/project/pallas_call | solution.py:314
  105.8 7.0 project.7
  117.7 2.1 copy-done.1
  121.1 29.9 %attend.3 = (bf16[896,128]{1,0:T(8,128)(2,1)S(1)}, bf16[896,128]{1,0:T(8,128)(2,1)S(1)}, bf16[896,128]{1,0:T(8,128)(2,1)S(1)}, bf16[896,128]{1,0:T(8,128)(2,1)S(...) custom-call(s32[1]{0:T(128)} %bitcast.refs_0_, ...), custom_call_target="tpu_custom_call", output_to_operand_aliasing={{5}: (6, {})} | custom-call | flops 1073741824 | bytes 3355443 | tf_op jit(solution)/shard_map/attend/pallas_call | solution.py:314
  152.0 29.6 %attend.4 = (bf16[896,128]{1,0:T(8,128)(2,1)S(1)}, bf16[896,128]{1,0:T(8,128)(2,1)S(1)}, bf16[896,128]{1,0:T(8,128)(2,1)S(1)}, bf16[896,128]{1,0:T(8,128)(2,1)S(1)}, f32[1,4,2,896]{3,2,1,0:T(2,128)S(1)}) custom-call(s32[1]{0:T(128)} %bitcast.refs_0_, bf16[3,4,896,128]{3,2,1,0:T(8,128)(2,1)S(1)} %copy-done.2, ...), custom_call_target="tpu_custom_call" | custom-call | flops 1073741824 | bytes 3355443 | tf_op jit(solution)/shard_map/attend/pallas_call | solution.py:314
  182.4 6.4 attend.5
  188.8 3.6 pad_maximum_fusion.1
  192.4 2.1 collective-permute-start.18
  194.6 3.2 pad_maximum_fusion
  200.4 2.7 collective-permute-done.7.refs_9_.refs_11_
  204.4 2.3 collective-permute-done.9.refs_11_.refs_13_
  206.7 3.7 collective-permute-done.10.refs_12_.refs_14_
  215.5 5.2 collective-permute-done.8.refs_10_.refs_12_
  220.7 13.0 %collective-permute-done.13.refs_15_ = bf16[560,1088]{1,0:T(8,128)(2,1)} collective-permute-done((bf16[560,1088]{1,0:T(8,128)(2,1)S(1)}, bf16[560,1088]{1,0:T(8,128)(2,1)}, u32[]{:S(2)}, u32[]{:S(2)}) %collective-permute-start.13) | collective-permute-done | bytes 1218592 | tf_op jit(solution)/shard_map/ppermute | solution.py:281
  233.8 7.7 %collective-permute-done.14.refs_16_ = bf16[560,1088]{1,0:T(8,128)(2,1)S(1)} collective-permute-done((bf16[560,1088]{1,0:T(8,128)(2,1)S(1)}, bf16[560,1088]{1,0:T(8,128)(2,1)S(1)}, u32[]{:S(2)}, u32[]{:S(2)}) %collective-permute-start.14) | collective-permute-done | bytes 1218592 | tf_op jit(solution)/shard_map/ppermute | solution.py:276
  241.5 10.4 %merge.1 = (f32[896,1088]{1,0:T(8,128)}, bf16[896,1088]{1,0:T(8,128)(2,1)}, bf16[1088,896]{1,0:T(8,128)(2,1)}, bf16[560,1088]{1,0:T(8,128)(2,1)}, bf16[560,1088]{1,0:T(8,128)(2,1)S(1)}) custom-call(s32[1]{0:T(128)} %bitcast.refs_0_, bf16[896,1152]{1,0:T(8,128)(2,1)} %copy-done.7, ...), custom_call_target="tpu_custom_call", output_to_operand_aliasing={{3}: (15, {}), {4}: (16, {})} | custom-call | flops 424253856 | bytes 3355443 | tf_op jit(solution)/shard_map/merge/pallas_call | solution.py:314
  254.2 3.1 pad_maximum_fusion.2
  257.3 56.5 %mlp.2 = (f32[896,1088]{1,0:T(8,128)}, f32[896,1088]{1,0:T(8,128)}, bf16[2,2,272,1088]{3,2,1,0:T(8,128)(2,1)}, bf16[2,2,272,1088]{3,2,1,0:T(8,128)(2,1)}, bf16[2...) custom-call(s32[5]{0:T(128)} %stack.70.refs_0_, ...), custom_call_target="tpu_custom_call" | custom-call | flops 5091046400 | bytes 8388608 | tf_op jit(solution)/shard_map/mlp/pallas_call | solution.py:314
  314.6 2.1 pad_maximum_fusion.3
  317.7 6.9 collective-permute-done.21.refs_10_
  326.2 59.3 %mlp.3 = (f32[896,1088]{1,0:T(8,128)}, f32[896,1088]{1,0:T(8,128)}, bf16[2,2,272,1088]{3,2,1,0:T(8,128)(2,1)}, bf16[2,2,272,1088]{3,2,1,0:T(8,128)(2,1)}, bf16[2...) custom-call(s32[5]{0:T(128)} %stack.70.refs_0_, ...), custom_call_target="tpu_custom_call" | custom-call | flops 5091046400 | bytes 8388608 | tf_op jit(solution)/shard_map/mlp/pallas_call | solution.py:314
  387.1 21.9 %bend.1 = (bf16[1,512,1088]{2,1,0:T(8,128)(2,1)}, bf16[1,384,1088]{2,1,0:T(8,128)(2,1)S(1)}, f32[896,1088]{1,0:T(8,128)}, bf16[896,256]{1,0:T(8,128)(2,1)S(1)}, ...) custom-call(s32[2]{0:T(128)S(1)} %pad_add_fusion.refs_0_, ...), custom_call_target="tpu_custom_call" | custom-call | flops 848507712 | bytes 6291456 | tf_op jit(solution)/shard_map/bend/pallas_call | solution.py:314
  412.9 2.1 collective-permute-done.22.refs_12_.refs_9_
  416.0 9.5 %attend_back.3 = (bf16[1,4,896,128]{3,2,1,0:T(8,128)(2,1)}, bf16[1,4,896,128]{3,2,1,0:T(8,128)(2,1)}, bf16[1,4,896,128]{3,2,1,0:T(8,128)(2,1)}) custom-call(s32[1]{0:T(128)} %bitcast.refs_0_, bf16[3,4,896,128]{3,2,1,0:T(8,128)(2,1)} %get-tuple-element.148.refs_1_, bf16[3,4,896,128]{3,2,1,0:T(8,128)(2,1)} %get-tuple-element.149.refs_2_, ...), custom_call_target="tpu_custom_call" | custom-call | flops 335544320 | bytes 3355443 | tf_op jit(solution)/shard_map/attend_back/pallas_call | solution.py:314
  425.4 8.5 %collective-permute-done.24.refs_14_.refs_11_ = bf16[896,256]{1,0:T(8,128)(2,1)S(1)} collective-permute-done((bf16[896,256]{1,0:T(8,128)(2,1)S(1)}, bf16[896,256]{1,0:T(8,128)(2,1)S(1)}, u32[]{:S(2)}, u32[]{:S(2)}) %collective-permute-start.24) | collective-permute-done | bytes 458784 | tf_op jit(solution)/shard_map/ppermute | solution.py:276
  435.3 14.4 %join.1 = (bf16[4,2,136,1088]{3,2,1,0:T(8,128)(2,1)}, bf16[4,2,136,1088]{3,2,1,0:T(8,128)(2,1)}, bf16[4,272,1088]{2,1,0:T(8,128)(2,1)}, bf16[4,272,1088]{2,1,0:T...) custom-call(s32[5]{0:T(128)S(1)} %copy-done.64, ...), custom_call_target="tpu_custom_call" | custom-call | bytes 6291456 | tf_op jit(solution)/shard_map/join/pallas_call | solution.py:314
  454.7 46.3 %attend_back.4 = (bf16[1,4,896,128]{3,2,1,0:T(8,128)(2,1)}, bf16[1,4,896,128]{3,2,1,0:T(8,128)(2,1)}, bf16[1,4,896,128]{3,2,1,0:T(8,128)(2,1)}) custom-call(s32[1]{0:T(128)} %bitcast.refs_0_, bf16[3,4,896,128]{3,2,1,0:T(8,128)(2,1)} %get-tuple-element.148.refs_1_, bf16[3,4,896,128]{3,2,1,0:T(8,128)(2,1)} %get-tuple-element.149.refs_2_, ...), custom_call_target="tpu_custom_call" | custom-call | flops 2684354560 | bytes 3355443 | tf_op jit(solution)/shard_map/attend_back/pallas_call | solution.py:314
  501.0 7.3 collective-permute-done.30.refs_1_
  516.0 2.4 add_convert_fusion.refs_17_
  526.8 46.1 %attend_back.5 = (bf16[1,4,896,128]{3,2,1,0:T(8,128)(2,1)}, bf16[1,4,896,128]{3,2,1,0:T(8,128)(2,1)}, bf16[1,4,896,128]{3,2,1,0:T(8,128)(2,1)}) custom-call(s32[1]{0:T(128)} %bitcast.refs_0_, bf16[3,4,896,128]{3,2,1,0:T(8,128)(2,1)} %get-tuple-element.148.refs_1_, bf16[3,4,896,128]{3,2,1,0:T(8,128)(2,1)} %get-tuple-element.149.refs_2_, ...), custom_call_target="tpu_custom_call" | custom-call | flops 2684354560 | bytes 3355443 | tf_op jit(solution)/shard_map/attend_back/pallas_call | solution.py:314
  572.9 3.8 collective-permute-done.35.refs_2_
  578.0 2.4 fusion.3.refs_18_
  585.5 126.7 %tail.1 = (bf16[1,512,1088]{2,1,0:T(8,128)(2,1)}, bf16[1,384,1088]{2,1,0:T(8,128)(2,1)}, bf16[544,3264]{1,0:T(8,128)(2,1)}, bf16[544,1088]{1,0:T(8,128)(2,1)}, f32[16,1152]{1,0:T(8,128)}) custom-call(bf16[1,4,896,128]{3,2,1,0:T(8,128)(2,1)} %get-tuple-element.202.refs_0_.refs_18_, bf16[1,4,896,128]{3,2,1,0:T(8,128)(2,1)} %get-tuple-element.208.refs_0_.refs_1_, ...), custom_call_target="tpu_custom_call" | custom-call | flops 17968398336 | bytes 31457280 | tf_op jit(solution)/shard_map/tail/pallas_call | solution.py:1466
  717.0 6.0 collective-permute-done.40
  724.4 2.4 copy.96
  728.6 5.7 convert_element_type.106
  735.9 2.3 copy.98
  742.2 2.6 slice_bitcast_fusion
  (305 shorter events, 91.3 us)
Async XLA Ops:
  10.3 30.8 %collective-permute-start.1 = (bf16[544,1152]{1,0:T(8,128)(2,1)}, bf16[544,1152]{1,0:T(8,128)(2,1)}, u32[]{:S(2)}, u32[]{:S(2)}) collective-permute-start(bf16[544,1152]{1,0:T(8,128)(2,1)} %get-tuple-element.125), channel_id=1, source_target_pairs={{0,16},{16,0},{1,17},{17,1},{2,18},{18,2},{3,19},{19,3},{4,20},{20... | collective-permute-start | bytes 3760136 | tf_op jit(solution)/shard_map/ppermute | solution.py:276
  13.3 39.6 %collective-permute-start = (bf16[896,1152]{1,0:T(8,128)(2,1)S(1)}, bf16[896,1152]{1,0:T(8,128)(2,1)}, u32[]{:S(2)}, u32[]{:S(2)}) collective-permute-start(bf16[896,1152]{1,0:T(8,128)(2,1)S(1)} %get-tuple-element.124.refs_6_.refs_1_.refs_11_), channel_id=1, source_target_pairs={{0,4},{4,0},{8,12},{12,8},{1,5},{5,1},{9,13},{13,9},{2,6},{6,2},{1... | collective-permute-start | bytes 6193160 | tf_op jit(solution)/shard_map/ppermute | solution.py:276
  13.3 48.9 %collective-permute-start.3 = (bf16[896,1152]{1,0:T(8,128)(2,1)S(1)}, bf16[896,1152]{1,0:T(8,128)(2,1)}, u32[]{:S(2)}, u32[]{:S(2)}) collective-permute-start(bf16[896,1152]{1,0:T(8,128)(2,1)S(1)} %get-tuple-element.124.refs_6_.refs_1_.refs_11_), channel_id=1, source_target_pairs={{0,8},{4,12},{8,0},{12,4},{1,9},{5,13},{9,1},{13,5},{2,10},{6,14},... | collective-permute-start | bytes 6193160 | tf_op jit(solution)/shard_map/ppermute | solution.py:276
  22.2 83.5 %copy-start.58 = (f32[1,1088]{1,0:T(1,128)}, f32[1,1088]{1,0:T(1,128)S(1)}, u32[]{:S(2)}) copy-start(f32[1,1088]{1,0:T(1,128)S(1)} %broadcast_in_dim.39.refs_3_.refs_15_) | copy-start | bytes 13060
  64.0 41.7 %collective-permute-start.4 = (bf16[896,1152]{1,0:T(8,128)(2,1)}, bf16[896,1152]{1,0:T(8,128)(2,1)S(1)}, u32[]{:S(2)}, u32[]{:S(2)}) collective-permute-start(bf16[896,1152]{1,0:T(8,128)(2,1)} %behind.9.refs_1_), channel_id=1, source_target_pairs={{0,4},{4,0},{8,12},{12,8},{1,5},{5,1},{9,13},{13,9},{2,6},{6,2},{1... | collective-permute-start | bytes 6193160 | tf_op jit(solution)/shard_map/ppermute | solution.py:276
  64.0 33.2 %collective-permute-start.5 = (bf16[560,1088]{1,0:T(8,128)(2,1)S(1)}, bf16[560,1088]{1,0:T(8,128)(2,1)}, u32[]{:S(2)}, u32[]{:S(2)}) collective-permute-start(bf16[560,1088]{1,0:T(8,128)(2,1)S(1)} %copy-done.14), channel_id=1, source_target_pairs={{0,1},{1,2},{2,3},{3,0},{4,5},{5,6},{6,7},{7,4},{8,9},{9,10},{10,1... | collective-permute-start | bytes 3655688 | tf_op jit(solution)/shard_map/ppermute | solution.py:281
  112.8 69.5 %collective-permute-start.12 = (bf16[560,1088]{1,0:T(8,128)(2,1)}, bf16[560,1088]{1,0:T(8,128)(2,1)S(1)}, u32[]{:S(2)}, u32[]{:S(2)}) collective-permute-start(bf16[560,1088]{1,0:T(8,128)(2,1)} %get-tuple-element.160), channel_id=1, source_target_pairs={{0,2},{1,3},{2,0},{3,1},{4,6},{5,7},{6,4},{7,5},{8,10},{9,11},{10,... | collective-permute-start | bytes 3655688 | tf_op jit(solution)/shard_map/ppermute | solution.py:281
  113.5 75.3 %collective-permute-start.16 = (bf16[560,1088]{1,0:T(8,128)(2,1)}, bf16[560,1088]{1,0:T(8,128)(2,1)}, u32[]{:S(2)}, u32[]{:S(2)}) collective-permute-start(bf16[560,1088]{1,0:T(8,128)(2,1)} %collective-permute-done.5.refs_12_.refs_6_), channel_id=1, source_target_pairs={{0,16},{16,0},{1,17},{17,1},{2,18},{18,2},{3,19},{19,3},{4,20},{20... | collective-permute-start | bytes 3655688 | tf_op jit(solution)/shard_map/ppermute | solution.py:276
  115.0 73.8 %collective-permute-start.15 = (bf16[560,1088]{1,0:T(8,128)(2,1)}, bf16[560,1088]{1,0:T(8,128)(2,1)}, u32[]{:S(2)}, u32[]{:S(2)}) collective-permute-start(bf16[560,1088]{1,0:T(8,128)(2,1)} %get-tuple-element.169), channel_id=1, source_target_pairs={{0,16},{16,0},{1,17},{17,1},{2,18},{18,2},{3,19},{19,3},{4,20},{20... | collective-permute-start | bytes 3655688 | tf_op jit(solution)/shard_map/ppermute | solution.py:276
  115.6 82.7 %collective-permute-start.2 = (bf16[544,1088]{1,0:T(8,128)(2,1)S(1)}, bf16[544,1088]{1,0:T(8,128)(2,1)}, u32[]{:S(2)}, u32[]{:S(2)}) collective-permute-start(bf16[544,1088]{1,0:T(8,128)(2,1)S(1)} %get-tuple-element.134), channel_id=1, source_target_pairs={{0,16},{16,0},{1,17},{17,1},{2,18},{18,2},{3,19},{19,3},{4,20},{20... | collective-permute-start | bytes 3551240 | tf_op jit(solution)/shard_map/ppermute | solution.py:276
  117.7 64.7 %copy-start.5 = (s32[4,384,1]{2,1,0:T(8,128)}, s32[4,384,1]{2,1,0:T(8,128)S(1)}, u32[]{:S(2)}) copy-start(s32[4,384,1]{2,1,0:T(8,128)S(1)} %broadcast_in_dim_reshape_squeeze.8.refs_4_.refs_6_) | copy-start | bytes 18436
  152.0 60.5 %copy-start.55 = (bf16[896,128]{1,0:T(8,128)(2,1)}, bf16[896,128]{1,0:T(8,128)(2,1)S(1)}, u32[]{:S(2)}) copy-start(bf16[896,128]{1,0:T(8,128)(2,1)S(1)} %get-tuple-element.156.refs_14_) | copy-start | bytes 688132
  152.0 89.5 %copy-start.20 = (bf16[896,128]{1,0:T(8,128)(2,1)}, bf16[896,128]{1,0:T(8,128)(2,1)S(1)}, u32[]{:S(2)}) copy-start(bf16[896,128]{1,0:T(8,128)(2,1)S(1)} %get-tuple-element.152.refs_6_.refs_8_.refs_12_) | copy-start | bytes 688132
  182.3 18.0 %collective-permute-start.11 = (bf16[896,128]{1,0:T(8,128)(2,1)S(1)}, bf16[896,128]{1,0:T(8,128)(2,1)S(1)}, u32[]{:S(2)}, u32[]{:S(2)}) collective-permute-start(bf16[896,128]{1,0:T(8,128)(2,1)S(1)} %get-tuple-element.159.refs_15_), channel_id=1, source_target_pairs={{0,12},{4,8},{8,4},{12,0},{1,13},{5,9},{9,5},{13,1},{2,14},{6,10},... | collective-permute-start | bytes 688136 | tf_op jit(solution)/shard_map/ppermute | solution.py:276
  182.4 71.8 %copy-start.6 = (bf16[560,1088]{1,0:T(8,128)(2,1)}, bf16[560,1088]{1,0:T(8,128)(2,1)S(1)}, u32[]{:S(2)}) copy-start(bf16[560,1088]{1,0:T(8,128)(2,1)S(1)} %behind.10.refs_7_.refs_5_) | copy-start | bytes 3655684
  192.4 64.9 %collective-permute-start.18 = (bf16[2,560,1088]{2,1,0:T(8,128)(2,1)}, bf16[2,560,1088]{2,1,0:T(8,128)(2,1)}, u32[]{:S(2)}, u32[]{:S(2)}) collective-permute-start(bf16[2,560,1088]{2,1,0:T(8,128)(2,1)} %pad_maximum_fusion.1), channel_id=1, source_target_pairs={{0,4},{4,0},{8,12},{12,8},{1,5},{5,1},{9,13},{13,9},{2,6},{6,2},{1... | collective-permute-start | bytes 7311368 | tf_op jit(solution)/shard_map/ppermute | solution.py:276
  197.8 59.6 %collective-permute-start.17 = (bf16[2,560,1088]{2,1,0:T(8,128)(2,1)}, bf16[2,560,1088]{2,1,0:T(8,128)(2,1)}, u32[]{:S(2)}, u32[]{:S(2)}) collective-permute-start(bf16[2,560,1088]{2,1,0:T(8,128)(2,1)} %pad_maximum_fusion), channel_id=1, source_target_pairs={{0,4},{4,0},{8,12},{12,8},{1,5},{5,1},{9,13},{13,9},{2,6},{6,2},{1... | collective-permute-start | bytes 7311368 | tf_op jit(solution)/shard_map/ppermute | solution.py:276
  197.8 5.3 collective-permute-start.7
  198.3 8.4 %collective-permute-start.9 = (bf16[896,128]{1,0:T(8,128)(2,1)S(1)}, bf16[896,128]{1,0:T(8,128)(2,1)S(1)}, u32[]{:S(2)}, u32[]{:S(2)}) collective-permute-start(bf16[896,128]{1,0:T(8,128)(2,1)S(1)} %get-tuple-element.157.refs_14_), channel_id=1, source_target_pairs={{0,8},{4,12},{8,0},{12,4},{1,9},{5,13},{9,1},{13,5},{2,10},{6,14},... | collective-permute-start | bytes 688136 | tf_op jit(solution)/shard_map/ppermute | solution.py:276
  200.2 10.1 %collective-permute-start.10 = (bf16[896,128]{1,0:T(8,128)(2,1)S(1)}, bf16[896,128]{1,0:T(8,128)(2,1)S(1)}, u32[]{:S(2)}, u32[]{:S(2)}) collective-permute-start(bf16[896,128]{1,0:T(8,128)(2,1)S(1)} %get-tuple-element.158.refs_15_), channel_id=1, source_target_pairs={{0,12},{4,8},{8,4},{12,0},{1,13},{5,9},{9,5},{13,1},{2,14},{6,10},... | collective-permute-start | bytes 688136 | tf_op jit(solution)/shard_map/ppermute | solution.py:276
  203.1 30.7 %collective-permute-start.13 = (bf16[560,1088]{1,0:T(8,128)(2,1)S(1)}, bf16[560,1088]{1,0:T(8,128)(2,1)}, u32[]{:S(2)}, u32[]{:S(2)}) collective-permute-start(bf16[560,1088]{1,0:T(8,128)(2,1)S(1)} %copy-done.31), channel_id=1, source_target_pairs={{0,3},{1,0},{2,1},{3,2},{4,7},{5,4},{6,5},{7,6},{8,11},{9,8},{10,9... | collective-permute-start | bytes 3655688 | tf_op jit(solution)/shard_map/ppermute | solution.py:281
  206.7 5.7 collective-permute-start.6
  210.4 31.1 %collective-permute-start.14 = (bf16[560,1088]{1,0:T(8,128)(2,1)S(1)}, bf16[560,1088]{1,0:T(8,128)(2,1)S(1)}, u32[]{:S(2)}, u32[]{:S(2)}) collective-permute-start(bf16[560,1088]{1,0:T(8,128)(2,1)S(1)} %behind.10.refs_7_.refs_5_), channel_id=1, source_target_pairs={{0,16},{16,0},{1,17},{17,1},{2,18},{18,2},{3,19},{19,3},{4,20},{20... | collective-permute-start | bytes 3655688 | tf_op jit(solution)/shard_map/ppermute | solution.py:276
  212.5 8.3 %collective-permute-start.8 = (bf16[896,128]{1,0:T(8,128)(2,1)S(1)}, bf16[896,128]{1,0:T(8,128)(2,1)S(1)}, u32[]{:S(2)}, u32[]{:S(2)}) collective-permute-start(bf16[896,128]{1,0:T(8,128)(2,1)S(1)} %get-tuple-element.156.refs_14_), channel_id=1, source_target_pairs={{0,8},{4,12},{8,0},{12,4},{1,9},{5,13},{9,1},{13,5},{2,10},{6,14},... | collective-permute-start | bytes 688136 | tf_op jit(solution)/shard_map/ppermute | solution.py:276
  253.0 60.8 %collective-permute-start.19 = (bf16[560,1088]{1,0:T(8,128)(2,1)}, bf16[560,1088]{1,0:T(8,128)(2,1)S(1)}, u32[]{:S(2)}, u32[]{:S(2)}) collective-permute-start(bf16[560,1088]{1,0:T(8,128)(2,1)} %get-tuple-element.167.refs_6_), channel_id=1, source_target_pairs={{0,16},{16,0},{1,17},{17,1},{2,18},{18,2},{3,19},{19,3},{4,20},{20... | collective-permute-start | bytes 3655688 | tf_op jit(solution)/shard_map/ppermute | solution.py:276
  257.3 60.4 %collective-permute-start.20 = (bf16[2,560,1088]{2,1,0:T(8,128)(2,1)}, bf16[2,560,1088]{2,1,0:T(8,128)(2,1)}, u32[]{:S(2)}, u32[]{:S(2)}) collective-permute-start(bf16[2,560,1088]{2,1,0:T(8,128)(2,1)} %pad_maximum_fusion.2), channel_id=1, source_target_pairs={{0,4},{4,0},{8,12},{12,8},{1,5},{5,1},{9,13},{13,9},{2,6},{6,2},{1... | collective-permute-start | bytes 7311368 | tf_op jit(solution)/shard_map/ppermute | solution.py:276
  316.6 7.9 %collective-permute-start.21 = (bf16[2,560,1088]{2,1,0:T(8,128)(2,1)S(1)}, bf16[2,560,1088]{2,1,0:T(8,128)(2,1)S(1)}, u32[]{:S(2)}, u32[]{:S(2)}) collective-permute-start(bf16[2,560,1088]{2,1,0:T(8,128)(2,1)S(1)} %pad_maximum_fusion.3), channel_id=1, source_target_pairs={{0,4},{4,0},{8,12},{12,8},{1,5},{5,1},{9,13},{13,9},{2,6},{6,2},{1... | collective-permute-start | bytes 7311368 | tf_op jit(solution)/shard_map/ppermute | solution.py:276
  317.2 94.6 %collective-permute-start.25 = (bf16[2,2,272,1088]{3,2,1,0:T(8,128)(2,1)}, bf16[2,2,272,1088]{3,2,1,0:T(8,128)(2,1)}, u32[]{:S(2)}, u32[]{:S(2)}) collective-permute-start(bf16[2,2,272,1088]{3,2,1,0:T(8,128)(2,1)} %get-tuple-element.188), channel_id=1, source_target_pairs={{0,4},{4,0},{8,12},{12,8},{1,5},{5,1},{9,13},{13,9},{2,6},{6,2},{1... | collective-permute-start | bytes 7102472 | tf_op jit(solution)/shard_map/ppermute | solution.py:276
  317.3 94.6 %collective-permute-start.26 = (bf16[2,2,272,1088]{3,2,1,0:T(8,128)(2,1)}, bf16[2,2,272,1088]{3,2,1,0:T(8,128)(2,1)}, u32[]{:S(2)}, u32[]{:S(2)}) collective-permute-start(bf16[2,2,272,1088]{3,2,1,0:T(8,128)(2,1)} %get-tuple-element.190), channel_id=1, source_target_pairs={{0,4},{4,0},{8,12},{12,8},{1,5},{5,1},{9,13},{13,9},{2,6},{6,2},{1... | collective-permute-start | bytes 7102472 | tf_op jit(solution)/shard_map/ppermute | solution.py:276
  385.5 48.5 %collective-permute-start.27 = (bf16[2,2,272,1088]{3,2,1,0:T(8,128)(2,1)}, bf16[2,2,272,1088]{3,2,1,0:T(8,128)(2,1)}, u32[]{:S(2)}, u32[]{:S(2)}) collective-permute-start(bf16[2,2,272,1088]{3,2,1,0:T(8,128)(2,1)} %get-tuple-element.192), channel_id=1, source_target_pairs={{0,4},{4,0},{8,12},{12,8},{1,5},{5,1},{9,13},{13,9},{2,6},{6,2},{1... | collective-permute-start | bytes 7102472 | tf_op jit(solution)/shard_map/ppermute | solution.py:276
  385.9 48.1 %collective-permute-start.28 = (bf16[2,2,272,1088]{3,2,1,0:T(8,128)(2,1)}, bf16[2,2,272,1088]{3,2,1,0:T(8,128)(2,1)}, u32[]{:S(2)}, u32[]{:S(2)}) collective-permute-start(bf16[2,2,272,1088]{3,2,1,0:T(8,128)(2,1)} %get-tuple-element.194), channel_id=1, source_target_pairs={{0,4},{4,0},{8,12},{12,8},{1,5},{5,1},{9,13},{13,9},{2,6},{6,2},{1... | collective-permute-start | bytes 7102472 | tf_op jit(solution)/shard_map/ppermute | solution.py:276
  411.4 22.6 %collective-permute-start.29 = (bf16[2,272,1088]{2,1,0:T(8,128)(2,1)}, bf16[2,272,1088]{2,1,0:T(8,128)(2,1)S(1)}, u32[]{:S(2)}, u32[]{:S(2)}) collective-permute-start(bf16[2,272,1088]{2,1,0:T(8,128)(2,1)} %get-tuple-element.196), channel_id=1, source_target_pairs={{0,4},{4,0},{8,12},{12,8},{1,5},{5,1},{9,13},{13,9},{2,6},{6,2},{1... | collective-permute-start | bytes 3551240 | tf_op jit(solution)/shard_map/ppermute | solution.py:276
  411.8 3.2 collective-permute-start.22
  411.9 13.5 %collective-permute-start.23 = (bf16[896,256]{1,0:T(8,128)(2,1)S(1)}, bf16[896,256]{1,0:T(8,128)(2,1)S(1)}, u32[]{:S(2)}, u32[]{:S(2)}) collective-permute-start(bf16[896,256]{1,0:T(8,128)(2,1)S(1)} %get-tuple-element.185), channel_id=1, source_target_pairs={{0,8},{4,12},{8,0},{12,4},{1,9},{5,13},{9,1},{13,5},{2,10},{6,14},... | collective-permute-start | bytes 1376264 | tf_op jit(solution)/shard_map/ppermute | solution.py:276
  415.0 19.0 %collective-permute-start.24 = (bf16[896,256]{1,0:T(8,128)(2,1)S(1)}, bf16[896,256]{1,0:T(8,128)(2,1)S(1)}, u32[]{:S(2)}, u32[]{:S(2)}) collective-permute-start(bf16[896,256]{1,0:T(8,128)(2,1)S(1)} %get-tuple-element.186), channel_id=1, source_target_pairs={{0,12},{4,8},{8,4},{12,0},{1,13},{5,9},{9,5},{13,1},{2,14},{6,10},... | collective-permute-start | bytes 1376264 | tf_op jit(solution)/shard_map/ppermute | solution.py:276
  451.5 56.9 %collective-permute-start.30 = (bf16[4,2,136,1088]{3,2,1,0:T(8,128)(2,1)}, bf16[4,2,136,1088]{3,2,1,0:T(8,128)(2,1)S(1)}, u32[]{:S(2)}, u32[]{:S(2)}) collective-permute-start(bf16[4,2,136,1088]{3,2,1,0:T(8,128)(2,1)} %get-tuple-element.200.refs_16_), channel_id=1, source_target_pairs={{0,8},{4,12},{8,0},{12,4},{1,9},{5,13},{9,1},{13,5},{2,10},{6,14},... | collective-permute-start | bytes 7102472 | tf_op jit(solution)/shard_map/ppermute | solution.py:276
  452.4 56.9 %collective-permute-start.31 = (bf16[4,272,1088]{2,1,0:T(8,128)(2,1)}, bf16[4,272,1088]{2,1,0:T(8,128)(2,1)}, u32[]{:S(2)}, u32[]{:S(2)}) collective-permute-start(bf16[4,272,1088]{2,1,0:T(8,128)(2,1)} %get-tuple-element.201.refs_17_), channel_id=1, source_target_pairs={{0,16},{16,0},{1,17},{17,1},{2,18},{18,2},{3,19},{19,3},{4,20},{20... | collective-permute-start | bytes 7102472 | tf_op jit(solution)/shard_map/ppermute | solution.py:276
  519.7 53.2 %collective-permute-start.34 = (bf16[272,1088]{1,0:T(8,128)(2,1)}, bf16[272,1088]{1,0:T(8,128)(2,1)S(1)}, u32[]{:S(2)}, u32[]{:S(2)}) collective-permute-start(bf16[272,1088]{1,0:T(8,128)(2,1)} %get-tuple-element.279), channel_id=1, source_target_pairs={{0,3},{1,0},{2,1},{3,2},{4,7},{5,4},{6,5},{7,6},{8,11},{9,8},{10,9... | collective-permute-start | bytes 1775624 | tf_op jit(solution)/shard_map/ppermute | solution.py:281
  521.1 55.7 %collective-permute-start.35 = (bf16[272,1088]{1,0:T(8,128)(2,1)}, bf16[272,1088]{1,0:T(8,128)(2,1)S(1)}, u32[]{:S(2)}, u32[]{:S(2)}) collective-permute-start(bf16[272,1088]{1,0:T(8,128)(2,1)} %get-tuple-element.278), channel_id=1, source_target_pairs={{0,2},{1,3},{2,0},{3,1},{4,6},{5,7},{6,4},{7,5},{8,10},{9,11},{10,... | collective-permute-start | bytes 1775624 | tf_op jit(solution)/shard_map/ppermute | solution.py:281
  522.8 54.0 %collective-permute-start.36 = (bf16[272,1088]{1,0:T(8,128)(2,1)}, bf16[272,1088]{1,0:T(8,128)(2,1)S(1)}, u32[]{:S(2)}, u32[]{:S(2)}) collective-permute-start(bf16[272,1088]{1,0:T(8,128)(2,1)} %get-tuple-element.277), channel_id=1, source_target_pairs={{0,1},{1,2},{2,3},{3,0},{4,5},{5,6},{6,7},{7,4},{8,9},{9,10},{10,1... | collective-permute-start | bytes 1775624 | tf_op jit(solution)/shard_map/ppermute | solution.py:281
  524.0 57.0 %collective-permute-start.33 = (bf16[4,136,1088]{2,1,0:T(8,128)(2,1)}, bf16[4,136,1088]{2,1,0:T(8,128)(2,1)S(1)}, u32[]{:S(2)}, u32[]{:S(2)}) collective-permute-start(bf16[4,136,1088]{2,1,0:T(8,128)(2,1)} %slice_bitcast_fusion.3.refs_16_), channel_id=1, source_target_pairs={{0,16},{16,0},{1,17},{17,1},{2,18},{18,2},{3,19},{19,3},{4,20},{20... | collective-permute-start | bytes 3551240 | tf_op jit(solution)/shard_map/ppermute | solution.py:276
  526.6 59.0 %collective-permute-start.32 = (bf16[272,1088]{1,0:T(8,128)(2,1)}, bf16[272,1088]{1,0:T(8,128)(2,1)}, u32[]{:S(2)}, u32[]{:S(2)}) collective-permute-start(bf16[272,1088]{1,0:T(8,128)(2,1)} %copy-done.66), channel_id=1, source_target_pairs={{0,16},{16,0},{1,17},{17,1},{2,18},{18,2},{3,19},{19,3},{4,20},{20... | collective-permute-start | bytes 1775624 | tf_op jit(solution)/shard_map/ppermute | solution.py:276
  580.3 131.9 %collective-permute-start.41 = (bf16[272,1088]{1,0:T(8,128)(2,1)}, bf16[272,1088]{1,0:T(8,128)(2,1)S(1)}, u32[]{:S(2)}, u32[]{:S(2)}) collective-permute-start(bf16[272,1088]{1,0:T(8,128)(2,1)} %fusion.3.refs_18_), channel_id=1, source_target_pairs={{0,8},{4,12},{8,0},{12,4},{1,9},{5,13},{9,1},{13,5},{2,10},{6,14},... | collective-permute-start | bytes 1775624 | tf_op jit(solution)/shard_map/ppermute | solution.py:276
  582.2 130.9 %collective-permute-start.37 = (bf16[136,1088]{1,0:T(8,128)(2,1)}, bf16[136,1088]{1,0:T(8,128)(2,1)S(1)}, u32[]{:S(2)}, u32[]{:S(2)}) collective-permute-start(bf16[136,1088]{1,0:T(8,128)(2,1)} %get-tuple-element.286), channel_id=1, source_target_pairs={{0,3},{1,0},{2,1},{3,2},{4,7},{5,4},{6,5},{7,6},{8,11},{9,8},{10,9... | collective-permute-start | bytes 887816 | tf_op jit(solution)/shard_map/ppermute | solution.py:281
  582.2 130.9 %collective-permute-start.38 = (bf16[136,1088]{1,0:T(8,128)(2,1)}, bf16[136,1088]{1,0:T(8,128)(2,1)S(1)}, u32[]{:S(2)}, u32[]{:S(2)}) collective-permute-start(bf16[136,1088]{1,0:T(8,128)(2,1)} %get-tuple-element.285), channel_id=1, source_target_pairs={{0,2},{1,3},{2,0},{3,1},{4,6},{5,7},{6,4},{7,5},{8,10},{9,11},{10,... | collective-permute-start | bytes 887816 | tf_op jit(solution)/shard_map/ppermute | solution.py:281
  583.5 129.6 %collective-permute-start.39 = (bf16[136,1088]{1,0:T(8,128)(2,1)S(1)}, bf16[136,1088]{1,0:T(8,128)(2,1)S(1)}, u32[]{:S(2)}, u32[]{:S(2)}) collective-permute-start(bf16[136,1088]{1,0:T(8,128)(2,1)S(1)} %get-tuple-element.284), channel_id=1, source_target_pairs={{0,1},{1,2},{2,3},{3,0},{4,5},{5,6},{6,7},{7,4},{8,9},{9,10},{10,1... | collective-permute-start | bytes 887816 | tf_op jit(solution)/shard_map/ppermute | solution.py:281
  714.3 8.7 %collective-permute-start.40 = (bf16[136,1088]{1,0:T(8,128)(2,1)S(1)}, bf16[136,1088]{1,0:T(8,128)(2,1)S(1)}, u32[]{:S(2)}, u32[]{:S(2)}) collective-permute-start(bf16[136,1088]{1,0:T(8,128)(2,1)S(1)} %fusion.7), channel_id=1, source_target_pairs={{0,8},{4,12},{8,0},{12,4},{1,9},{5,13},{9,1},{13,5},{2,10},{6,14},... | collective-permute-start | bytes 887816 | tf_op jit(solution)/shard_map/ppermute | solution.py:276
  724.4 15.9 %collective-permute-start.42 = (bf16[2,272,1088]{2,1,0:T(8,128)(2,1)}, bf16[2,272,1088]{2,1,0:T(8,128)(2,1)}, u32[]{:S(2)}, u32[]{:S(2)}) collective-permute-start(bf16[2,272,1088]{2,1,0:T(8,128)(2,1)} %pad_maximum_fusion.6), channel_id=1, source_target_pairs={{0,4},{4,0},{8,12},{12,8},{1,5},{5,1},{9,13},{13,9},{2,6},{6,2},{1... | collective-permute-start | bytes 3551240 | tf_op jit(solution)/shard_map/ppermute | solution.py:276
  (82 other events, 1369.2 us)

commit v3 on v2

--- a/solution.py
+++ b/solution.py
@@ -344,159 +344,315 @@
     return blocks(*shape), shape_of(*shape, kind=kind)
 
 
-def pack_kernel(place_ref, prompt_ref, cont_ref, w_ref, rows_ref, out_ref):
-    prompt_rows, width = prompt_ref.shape[1], prompt_ref.shape[2]
-    rows_ref[:prompt_rows, :width] = prompt_ref[0]
-    rows_ref[prompt_rows:, :width] = cont_ref[0]
-    rows_ref[:, width:] = jnp.zeros((rows_ref.shape[0], rows_ref.shape[1] - width), BF16)
-    place = place_ref[0]
+def in_order(own, other, place):
+    first = place == 0
+    return jnp.where(first, own, other), jnp.where(first, other, own)
+
+
+def open_kernel(*refs):
+    prompt_ref, cont_ref, w_ref, fc_ref, proj_ref, wo_ref, gp_ref, gc_ref = refs[:8]
+    fc_bias_ref, gain_ref, bias_ref, col_bias_ref = refs[8:12]
+    norm_ref, q_ref, k_ref, v_ref, kt_ref, vt_ref = refs[12:18]
+    w_own_ref, rows_ref, g_ref, gt_ref, mine_ref, one_ref, three_ref, far_ref, out_ref = refs[18:27]
+    (
+        rows_t,
+        w_s,
+        w_own,
+        w_out,
+        fc_s,
+        proj_s,
+        mine_s,
+        g_t,
+        normed,
+        norms,
+        tall_s,
+        flat_s,
+        turned,
+        wo_f,
+        wo_s,
+        local_sem,
+        send_sem,
+        recv_sem,
+        out_sem,
+    ) = refs[27:]
+    place = lax.axis_index("ctx")
+    fsdp = lax.axis_index("fsdp")
+    tensor = lax.axis_index("tensor")
+    tensors = lax.axis_size("tensor")
+    core = place % 2
+    width, row_count = rows_t.shape[1], rows_t.shape[2]
+    prompt_rows = prompt_ref.shape[1]
+    half, quarter = width // 2, width // 4
     own = 2 * PAIRS * HEAD
-    step = out_ref.shape[1] // 3
+    beside, across, far = {"ctx": place ^ 1}, {"ctx": place ^ 2}, {"fsdp": 1 - fsdp}
+    others = [{"tensor": lax.rem(tensor + k, tensors)} for k in range(1, tensors)]
+
+    barrier = pltpu.get_barrier_semaphore()
+    for partner in (beside, across, far, *others):
+        pl.semaphore_signal(barrier, inc=1, device_id=partner, device_id_type=pl.DeviceIdType.MESH)
+
+    def load(source, target, at):
+        copy = pltpu.make_async_copy(source, target, local_sem.at[at])
+        copy.start()
+        return copy
+
+    def spans(ref):
+        return ref.at[:, :prompt_rows], ref.at[:, prompt_rows:]
+
+    own_prompt, own_cont = spans(rows_t.at[0])
+    load_rows = [load(prompt_ref, own_prompt, 0), load(cont_ref, own_cont, 1)]
+    load_w = load(w_ref, w_s, 2)
+    mine_rows = pl.ds(pl.multiple_of(core * quarter, 16), quarter)
+    load_mine = [load(fc_ref.at[mine_rows], fc_s, 3), load(proj_ref.at[mine_rows], proj_s, 4)]
+    g_prompt, g_cont = spans(g_t)
+    load_g = [load(gp_ref, g_prompt, 5), load(gc_ref, g_cont, 6)]
+    load_wo = load(wo_ref, wo_f, 7)
+    sent, used = [], []
+
+    def push(source, target, partner):
+        at = len(used)
+        used.append(at)
+        copy = pltpu.make_async_remote_copy(
+            src_ref=source,
+            dst_ref=target,
+            send_sem=send_sem.at[at],
+            recv_sem=recv_sem.at[at],
+            device_id=partner,
+            device_id_type=pl.DeviceIdType.MESH,
+        )
+        copy.start()
+        sent.append(copy)
+        return copy
+
+    for copy in load_rows:
+        copy.wait()
+    pl.semaphore_wait(barrier, 3 + len(others))
+    to_chip = [
+        push(source, target, across) for source, target in zip(spans(rows_t.at[0]), spans(rows_t.at[2]))
+    ]
+    to_core = push(rows_t.at[0], rows_t.at[1], beside)
+
+    load_w.wait()
+    step = w_own.shape[1] // 3
     for part in range(3):
         for at in range((width - HEAD) // own):
 
             @pl.when(place == at)
             def _():
-                cols = slice(part * width + at * own, part * width + (at + 1) * own)
-                out_ref[:, part * step : part * step + own] = w_ref[:, cols].astype(BF16)
-
-        last = w_ref[:, (part + 1) * width - HEAD : (part + 1) * width].astype(BF16)
-        out_ref[:, part * step + own : (part + 1) * step] = jnp.concatenate(
-            [last, jnp.zeros((last.shape[0], step - own - HEAD), BF16)], axis=1
+                start = part * width + at * own
+                w_out[:, part * step : part * step + own] = w_s[:, start : start + own].astype(BF16)
+
+        last = w_s[:, (part + 1) * width - HEAD : (part + 1) * width].astype(BF16)
+        w_out[:, part * step + own : (part + 1) * step] = jnp.concatenate(
+            [last, jnp.zeros((half, step - own - HEAD), BF16)], axis=1
         )
-
-
-def pack(place, prompt_in, cont_in, w_qkv, padded):
-    rows = prompt_in.shape[1] + cont_in.shape[1]
-    operands = (prompt_in, cont_in, w_qkv)
-    return launch(
-        pack_kernel,
-        "pack",
-        (place,),
-        (1,),
-        operands,
-        [blocks(*entry.shape) for entry in operands],
-        [whole_out(rows, padded), whole_out(w_qkv.shape[0], 3 * (PAIRS + 1) * TILE)],
-    )
-
-
-def pack_more_kernel(
-    core_ref, fc_ref, proj_ref, bias_ref, prompt_ref, cont_ref, mine_ref, *refs
-):
-    copy_refs, (g_ref, gt_ref) = refs[:-2], refs[-2:]
-    quarter = fc_ref.shape[0] // 2
-    prompt_rows = prompt_ref.shape[1]
-    start = pl.multiple_of(core_ref[0] * quarter, quarter)
-    mine_ref[:quarter] = fc_ref[pl.ds(start, quarter), :].astype(BF16)
-    for core in range(2):
-
-        @pl.when(core_ref[0] == core)
-        def _():
-            mine_ref[quarter : 2 * quarter] = (
-                proj_ref[:, core * quarter : (core + 1) * quarter].T.astype(BF16)
-            )
-
-    bias = bias_ref[...]
+    mine_half = pl.ds(pl.multiple_of(fsdp * half, 16), half)
+    to_far = push(w_out, w_own.at[mine_half], far)
+    w_own[mine_half, :] = w_out[...]
+
+    for copy in load_mine:
+        copy.wait()
+    mine_s[:quarter] = fc_s[...].astype(BF16)
+    mine_s[quarter : 2 * quarter] = proj_s[...].astype(BF16)
+    bias = fc_bias_ref[...]
     pieces = []
     for _ in range(3):
         piece = bias.astype(BF16)
         pieces.append(piece)
         bias = bias - piece.astype(F32)
-    spare = mine_ref.shape[0] - 2 * quarter
-    pieces.append(jnp.zeros((spare - 3, bias.shape[1]), BF16))
-    mine_ref[2 * quarter :] = jnp.concatenate(pieces, axis=0)
-    for ref in copy_refs:
-        ref[...] = mine_ref[...]
-    g_ref[:prompt_rows] = prompt_ref[0]
-    g_ref[prompt_rows:] = cont_ref[0]
-    gt_ref[:, :prompt_rows] = prompt_ref[0].T
-    gt_ref[:, prompt_rows:] = cont_ref[0].T
-
-
-def pack_more(core, w_fc, w_proj, fc_bias, prompt_cot, cont_cot, after):
-    rows, width = prompt_cot.shape[1] + cont_cot.shape[1], prompt_cot.shape[2]
-    operands = (w_fc, w_proj, fc_bias[None], prompt_cot, cont_cot)
-    return launch(
-        pack_more_kernel,
-        "pack_more",
-        (core,),
-        (1,),
-        operands,
-        [blocks(*entry.shape) for entry in operands],
-        [
-            *[whole_out(w_fc.shape[0] + 16, w_fc.shape[1])] * 4,
-            whole_out(rows, width),
-            whole_out(width, rows),
+    pieces.append(jnp.zeros((mine_s.shape[0] - 2 * quarter - 3, width), BF16))
+    mine_s[2 * quarter :] = jnp.concatenate(pieces, axis=0)
+    to_one = push(mine_s, one_ref, others[0])
+    to_near = push(mine_s, far_ref, far)
+    to_three = push(mine_s, three_ref, others[2])
+    outs, put_at = [], []
+
+    def put(source, target):
+        copy = pltpu.make_async_copy(source, target, out_sem.at[len(put_at)])
+        put_at.append(len(put_at))
+        copy.start()
+        outs.append(copy)
+        return copy
+
+    def take(copies):
+        for copy in copies:
+            copy.wait()
+        outs[:] = [copy for copy in outs if all(copy is not done for done in copies)]
+
+    put(mine_s, mine_ref)
+
+    def out_rows(away):
+        return pl.ds(pl.multiple_of((fsdp ^ away) * half + core * quarter, 16), quarter)
+
+    load_wo.wait()
+    wo_s[...] = wo_f[...].astype(BF16)
+    put(wo_s, out_ref.at[mine_half])
+    to_out = push(wo_s.at[mine_rows], out_ref.at[out_rows(0)], far)
+    chunk = 128
+
+    def over_rows(body):
+        @pl.loop(0, row_count // chunk)
+        def _(i):
+            body(pl.ds(pl.multiple_of(i * chunk, chunk), chunk))
+
+    for copy in load_g:
+        copy.wait()
+    put(g_t, gt_ref)
+
+    def turn_rows(source, target):
+        def body(rows):
+            target[rows, :] = source[:, rows].T
+
+        over_rows(body)
+
+    turn_rows(g_t, turned.at[0])
+    put(turned.at[0], g_ref)
+    turn_rows(rows_t.at[0], turned.at[1])
+    put(turned.at[1], rows_ref)
+
+    extra = norms.shape[1] - width
+    at_row = lax.broadcasted_iota(jnp.int32, (extra, row_count), 0)
+    ones = jnp.where(at_row == 0, 1.0, 0.0).astype(BF16)
+    norms[0, width:] = ones
+    norms[1, width:] = ones
+
+    def normalise(distance, slot):
+        def body(rows):
+            values = rows_t[distance, :, rows].astype(F32)
+            average = jnp.mean(values, axis=0, keepdims=True)
+            centred = values - average
+            variance = jnp.mean(centred * centred, axis=0, keepdims=True)
+            low = centred * lax.rsqrt(variance + 1e-05) * gain_ref[...] + bias_ref[...]
+            low = low.astype(BF16)
+            norms[slot, :width, rows] = low
+            normed[rows, :] = low.T
+
+        over_rows(body)
+
+    def project(distance, slot):
+        block = place ^ distance
+        made = [put(norms.at[slot], norm_ref.at[block])]
+        tiles = step // TILE
+        for part, (out, flip) in enumerate(((q_ref, None), (k_ref, kt_ref), (v_ref, vt_ref))):
+            cols = slice(part * step, (part + 1) * step)
+            value = (dot(normed[...], w_own[:, cols]) + col_bias_ref[:, cols]).astype(BF16)
+            for tile in range(tiles):
+                piece = value[:, tile * TILE : (tile + 1) * TILE]
+                tall_s[slot, :, (part * tiles + tile) * TILE : (part * tiles + tile + 1) * TILE] = piece
+                if flip is not None:
+                    flat_s[slot, part - 1, tile] = piece.T
+            for tile in range(tiles):
+                lanes = slice((part * tiles + tile) * TILE, (part * tiles + tile + 1) * TILE)
+                made.append(put(tall_s.at[slot, :, lanes], out.at[tile, block]))
+                if flip is not None:
+                    made.append(put(flat_s.at[slot, part - 1, tile], flip.at[tile, block]))
+        return made
+
+    normalise(0, 0)
+    to_far.wait_recv()
+    put(w_own, w_own_ref)
+    first = project(0, 0)
+    to_core.wait_recv()
+    normalise(1, 1)
+    second = project(1, 1)
+    to_corner = []
+    for copy, source, target in zip(to_chip, spans(rows_t.at[2]), spans(rows_t.at[3])):
+        copy.wait_recv()
+        to_corner.append(push(source, target, beside))
+    take(first)
+    normalise(2, 0)
+    project(2, 0)
+    for copy in to_corner:
+        copy.wait_recv()
+    take(second)
+    normalise(3, 1)
+    project(3, 1)
+    to_out.wait_recv()
+    to_out_beside = push(out_ref.at[out_rows(1)], out_ref.at[out_rows(1)], beside)
+    for copy in outs:
+        copy.wait()
+    for copy in (to_one, to_near, to_three, to_out_beside):
+        copy.wait_recv()
+    for copy in sent:
+        copy.wait_send()
+
+
+def open_up(
+    prompt_in, cont_in, w_qkv, w_fc, w_proj, w_out, fc_bias, prompt_cot, cont_cot, gain, bias, col_bias, count
+):
+    prompt_rows, width = prompt_in.shape[1:]
+    row_count = prompt_rows + cont_in.shape[1]
+    half, quarter = width // 2, width // 4
+    tiles = PAIRS + 1
+    cols = 3 * tiles * TILE
+    in_vmem = pl.BlockSpec(memory_space=pltpu.VMEM)
+    vmem = lambda *shape, kind=BF16: pltpu.VMEM(shape, kind)
+    tall, flat = (tiles, count, row_count, TILE), (tiles, count, TILE, row_count)
+    mine = (2 * quarter + 16, w_fc.shape[1])
+    outs = [
+        (count, width + 16, row_count),
+        tall,
+        tall,
+        tall,
+        flat,
+        flat,
+        (width, cols),
+        (row_count, width),
+        (row_count, width),
+        (width, row_count),
+        mine,
+        mine,
+        mine,
+        mine,
+        (width, width),
+    ]
+    copies = 2 + 1 + 1 + 3 + 2 + 2
+    return pl.pallas_call(
+        open_kernel,
+        in_specs=[ANYWHERE] * 8 + [in_vmem] * 4,
+        out_specs=[ANYWHERE] * len(outs),
+        out_shape=[shape_of(*out) for out in outs],
+        scratch_shapes=[
+            vmem(4, width, row_count),
+            vmem(*w_qkv.shape, kind=F32),
+            vmem(width, cols),
+            vmem(half, cols),
+            vmem(quarter, w_fc.shape[1], kind=F32),
+            vmem(quarter, w_fc.shape[1], kind=F32),
+            vmem(*mine),
+            vmem(width, row_count),
+            vmem(row_count, width),
+            vmem(2, width + 16, row_count),
+            vmem(2, row_count, cols),
+            vmem(2, 2, tiles, TILE, row_count),
+            vmem(2, row_count, width),
+            vmem(half, width, kind=F32),
+            vmem(half, width),
+            pltpu.SemaphoreType.DMA((8,)),
+            pltpu.SemaphoreType.DMA((copies,)),
+            pltpu.SemaphoreType.DMA((copies,)),
+            pltpu.SemaphoreType.DMA((80,)),
         ],
-        after=after,
-    )
-
-
-def in_order(own, other, place):
-    first = place == 0
-    return jnp.where(first, own, other), jnp.where(first, other, own)
-
-
-def project_kernel(
-    place_ref, x_ref, w_ref, gain_ref, bias_ref, col_bias_ref, *refs
-):
-    norm_ref, q_ref, k_ref, v_ref, kt_ref, vt_ref = refs[-6:]
-    values = x_ref[:, : w_ref.shape[0]].astype(F32)
-    average = jnp.mean(values, axis=1, keepdims=True)
-    centred = values - average
-    variance = jnp.mean(centred * centred, axis=1, keepdims=True)
-    normed = (centred * lax.rsqrt(variance + 1e-05) * gain_ref[...] + bias_ref[...]).astype(BF16)
-    norm_ref[0, : w_ref.shape[0]] = normed.T
-    extra = norm_ref.shape[1] - w_ref.shape[0]
-    at_row = lax.broadcasted_iota(jnp.int32, (extra, normed.shape[0]), 0)
-    norm_ref[0, w_ref.shape[0] :] = jnp.where(at_row == 0, 1.0, 0.0).astype(BF16)
-    tiles = q_ref.shape[0]
-    width = tiles * TILE
-    for part, out_ref, flip_ref in ((0, q_ref, None), (1, k_ref, kt_ref), (2, v_ref, vt_ref)):
-        cols = slice(part * width, (part + 1) * width)
-        out = (dot(normed, w_ref[:, cols]) + col_bias_ref[:, cols]).astype(BF16)
-        for tile in range(tiles):
-            piece = out[:, tile * TILE : (tile + 1) * TILE]
-            out_ref[tile, 0] = piece
-            if flip_ref is not None:
-                flip_ref[tile, 0] = piece.T
-
-
-def project(place, rows, w_own, gain, bias, col_bias, before, count, after=(), carry=()):
-    row_count, width = rows.shape[0], w_own.shape[0]
-    tiles = w_own.shape[1] // (3 * TILE)
-    tall = (
-        pl.BlockSpec((tiles, 1, row_count, TILE), lambda i, p: (0, p[0], 0, 0)),
-        shape_of(tiles, count, row_count, TILE),
-    )
-    flat = (
-        pl.BlockSpec((tiles, 1, TILE, row_count), lambda i, p: (0, p[0], 0, 0)),
-        shape_of(tiles, count, TILE, row_count),
-    )
-    operands = (rows, w_own, gain[None], bias[None], col_bias[None])
-    before = tuple(before or ())
-    return launch(
-        lambda *refs: project_kernel(*refs[:6], *refs[-6:]),
-        "project",
-        (place,),
-        (1,),
-        operands + before,
-        [blocks(*entry.shape) for entry in operands] + [ANYWHERE] * len(before),
-        [
-            (
-                pl.BlockSpec((1, width + 16, row_count), lambda i, p: (p[0], 0, 0)),
-                shape_of(count, width + 16, row_count),
-            ),
-            tall,
-            tall,
-            tall,
-            flat,
-            flat,
-        ],
-        aliases={len(operands) + i: i for i in range(len(before))},
-        flops=2 * row_count * width * w_own.shape[1],
-        after=after,
-        carry=carry,
+        compiler_params=pltpu.CompilerParams(
+            vmem_limit_bytes=60 << 20, collective_id=2, has_side_effects=True
+        ),
+        cost_estimate=pl.CostEstimate(
+            flops=2 * count * row_count * width * cols, bytes_accessed=40 << 20, transcendentals=0
+        ),
+        name="open",
+    )(
+        prompt_in[0].T,
+        cont_in[0].T,
+        w_qkv,
+        w_fc,
+        w_proj.T,
+        w_out,
+        prompt_cot[0].T,
+        cont_cot[0].T,
+        fc_bias[None],
+        gain[:, None],
+        bias[:, None],
+        col_bias[None],
     )
 
 
@@ -506,104 +662,205 @@
     return key_at <= query_at
 
 
-def attend_kernel(
-    heads, spans, prompt_rows, place_ref, q_ref, k_ref, vt_ref, seg_col_ref, seg_row_ref, *refs
-):
-    o_refs, lse_ref, acc = refs[:spans], refs[-2], refs[-1]
+def attend_kernel(prompt_rows, q_ref, k_ref, vt_ref, seg_col_ref, seg_row_ref, *refs):
+    mine_ref, near_ref, one_ref, three_ref = refs[:4]
+    lse_ref, outs_ref, pieces_ref, last_ref, two_ref, one_far_ref, three_far_ref = refs[4:11]
+    beside_refs, (acc, o_s, send_sem, recv_sem, out_sem) = refs[11:17], refs[17:]
     step = pl.program_id(0)
-    distance = step % spans
-    block = place_ref[0] ^ distance
+    place = lax.axis_index("ctx")
+    fsdp = lax.axis_index("fsdp")
+    tensor = lax.axis_index("tensor")
+    tensors = lax.axis_size("tensor")
     count, row_count = k_ref.shape[1], k_ref.shape[2]
     cont_rows = row_count - prompt_rows
-
-    def part(queries, at, start, size, mask, before):
+    per_pair = 2 * count
+    steps = PAIRS * per_pair
+    beside, far = {"ctx": place ^ 1}, {"fsdp": 1 - fsdp}
+    after, before = lax.rem(tensor + 1, tensors), lax.rem(tensor + tensors - 1, tensors)
+    distance = jnp.where(step < steps, count - 1 - step % per_pair // 2, 0)
+    block = place ^ distance
+
+    def copy_to(at, source, target, partner):
+        return pltpu.make_async_remote_copy(
+            src_ref=source,
+            dst_ref=target,
+            send_sem=send_sem.at[at],
+            recv_sem=recv_sem.at[at],
+            device_id=partner,
+            device_id_type=pl.DeviceIdType.MESH,
+        )
+
+    b_mine, b_near, b_one, b_one_far, b_three, b_three_far = beside_refs
+    returns = {}
+    for pair in range(PAIRS):
+        for away in range(1, count):
+            returns[pair, away] = copy_to(
+                pair * (count - 1) + away - 1,
+                o_s.at[pair, away],
+                pieces_ref.at[pair, away - 1],
+                {"ctx": place ^ away},
+            )
+    base = PAIRS * (count - 1)
+    early = [
+        copy_to(base, one_ref, one_far_ref, far),
+        copy_to(base + 1, one_ref, two_ref, {"tensor": after}),
+        copy_to(base + 2, mine_ref, b_mine, beside),
+        copy_to(base + 3, near_ref, b_near, beside),
+        copy_to(base + 4, one_ref, b_one, beside),
+        copy_to(base + 5, three_ref, b_three, beside),
+        copy_to(base + 6, three_ref, three_far_ref, far),
+    ]
+    late = [
+        copy_to(base + 7, one_far_ref, b_one_far, beside),
+        copy_to(base + 8, three_far_ref, b_three_far, beside),
+    ]
+
+    @pl.when(step == 0)
+    def _():
+        barrier = pltpu.get_barrier_semaphore()
+        partners = [{"ctx": place ^ away} for away in range(1, count)]
+        partners += [far, {"tensor": after}, {"tensor": before}]
+        for partner in partners:
+            pl.semaphore_signal(
+                barrier, inc=1, device_id=partner, device_id_type=pl.DeviceIdType.MESH
+            )
+        pl.semaphore_wait(barrier, len(partners))
+        for copy in early:
+            copy.start()
+
+    @pl.when(step == per_pair + 2)
+    def _():
+        early[0].wait_recv()
+        late[0].start()
+
+    @pl.when(step == steps)
+    def _():
+        early[6].wait_recv()
+        late[1].start()
+
+    def part(queries, at, start, size, mask, states):
         keys = k_ref[0, at, pl.ds(start, size), :]
         scores = [dot(keys, query, NT) for query in queries]
         if mask is not None:
             scores = [jnp.where(mask, score, -1e30) for score in scores]
         tops = [jnp.max(score, axis=0, keepdims=True) for score in scores]
-        if before is not None:
-            tops = [jnp.maximum(top, state[0]) for top, state in zip(tops, before)]
+        if states is not None:
+            tops = [jnp.maximum(top, state[0]) for top, state in zip(tops, states)]
         exps = [jnp.exp2(score * SCALE2 - top * SCALE2) for score, top in zip(scores, tops)]
         totals = [jnp.sum(exp, axis=0, keepdims=True) for exp in exps]
-        after = []
-        for head in range(heads):
+        made = []
+        for head in range(len(queries)):
             rows = slice(head * HEAD, (head + 1) * HEAD)
             cols = slice(0, queries[head].shape[0])
             out = dot(vt_ref[0, at, rows, pl.ds(start, size)], exps[head].astype(BF16))
             total = totals[head]
-            if before is None:
+            if states is None:
                 acc[rows, cols] = out
             else:
-                shrink = jnp.exp2((before[head][0] - tops[head]) * SCALE2)
-                total = total + before[head][1] * shrink
+                shrink = jnp.exp2((states[head][0] - tops[head]) * SCALE2)
+                total = total + states[head][1] * shrink
                 acc[rows, cols] = acc[rows, cols] * shrink + out
-            after.append((tops[head], total))
-        return after
+            made.append((tops[head], total))
+        return made
 
     def finish(start, size, states):
-        for head in range(heads):
+        for head, (top, total) in enumerate(states):
             rows = slice(head * HEAD, (head + 1) * HEAD)
-            top, total = states[head]
             acc[rows, :size] = acc[rows, :size] / total
             lse_ref[0, block, head : head + 1, pl.ds(start, size)] = top * SCALE2 + jnp.log2(total)
-        if heads == 1:
+        if len(states) == 1:
             acc[HEAD:, :size] = jnp.zeros((TILE - HEAD, size), F32)
-        out = acc[:, :size].T.astype(BF16)
-        for at in range(spans):
-
-            @pl.when(distance == at)
-            def _():
-                o_refs[at][pl.ds(start, size), :] = out
+        pair = step // per_pair
+        o_s[pair, distance, pl.ds(start, size), :] = acc[:, :size].T.astype(BF16)
 
     def over_prompt(queries, total, states):
         return lax.fori_loop(
             0, total, lambda c, states: part(queries, c, 0, prompt_rows, None, states), states
         )
 
-    @pl.when(step >= spans)
+    for heads, here in ((2, step < steps), (1, step >= steps)):
+
+        @pl.when(here & (step % 2 == 1))
+        def _():
+            queries = halves(q_ref[0, block, :prompt_rows, :], heads)
+            states = part(queries, block, 0, prompt_rows, own_mask(prompt_rows), None)
+            finish(0, prompt_rows, over_prompt(queries, block, states))
+
+        @pl.when(here & (step % 2 == 0))
+        def _():
+            previous = jnp.maximum(block - 1, 0)
+            labels = seg_row_ref[block]
+            queries = halves(q_ref[0, block, prompt_rows:, :], heads)
+            own = own_mask(cont_rows) & (seg_col_ref[block] == labels)
+            near = (seg_col_ref[previous] == labels) & (block > 0)
+            states = part(queries, block, prompt_rows, cont_rows, own, None)
+            states = part(queries, previous, prompt_rows, cont_rows, near, states)
+            finish(prompt_rows, cont_rows, over_prompt(queries, count, states))
+
+    for pair in range(PAIRS):
+        for away in range(1, count):
+
+            @pl.when(step == pair * per_pair + 2 * (count - 1 - away) + 1)
+            def _():
+                returns[pair, away].start()
+
+    @pl.when(step == steps + 1)
     def _():
-        queries = halves(q_ref[0, block, :prompt_rows, :], heads)
-        states = part(queries, block, 0, prompt_rows, own_mask(prompt_rows), None)
-        finish(0, prompt_rows, over_prompt(queries, block, states))
-
-    @pl.when(step < spans)
-    def _():
-        before = jnp.maximum(block - 1, 0)
-        labels = seg_row_ref[block]
-        queries = halves(q_ref[0, block, prompt_rows:, :], heads)
-        own = own_mask(cont_rows) & (seg_col_ref[block] == labels)
-        near = (seg_col_ref[before] == labels) & (block > 0)
-        states = part(queries, block, prompt_rows, cont_rows, own, None)
-        states = part(queries, before, prompt_rows, cont_rows, near, states)
-        finish(prompt_rows, cont_rows, over_prompt(queries, count, states))
-
-
-def attend(pair, heads, spans, place, q, k, vt, seg_col, seg_row, prompt_rows, after=(), carry=()):
-    _, count, row_count, _ = q.shape
+        stores = [
+            pltpu.make_async_copy(o_s.at[pl.ds(0, PAIRS)], outs_ref, out_sem.at[0]),
+            pltpu.make_async_copy(o_s.at[PAIRS, 0], last_ref, out_sem.at[1]),
+        ]
+        for store in stores:
+            store.start()
+        for copy in early[1:6] + late + list(returns.values()):
+            copy.wait_recv()
+        for copy in early + late + list(returns.values()):
+            copy.wait_send()
+        for store in stores:
+            store.wait()
+
+
+def attend(q, k, vt, seg_col, seg_row, prompt_rows, weights):
+    groups, count, row_count, _ = q.shape
     cont_rows = row_count - prompt_rows
-    pick = lambda i, s: (pair, 0, 0, 0)
-    pairs = spans * (prompt_rows + 2 * cont_rows) * prompt_rows * count // 2
-    return launch(
-        functools.partial(attend_kernel, heads, spans, prompt_rows),
-        "attend",
-        (place,),
-        (2 * spans,),
-        (q, k, vt, seg_col, seg_row),
-        [
-            pl.BlockSpec((1, count, row_count, TILE), pick),
-            pl.BlockSpec((1, count, row_count, TILE), pick),
-            pl.BlockSpec((1, count, TILE, row_count), pick),
-            blocks(count, cont_rows, 1),
-            blocks(count, 1, cont_rows),
+    pair = lambda i: (jnp.minimum(i // (2 * count), PAIRS), 0, 0, 0)
+    pairs = groups * count * (prompt_rows + 2 * cont_rows) * prompt_rows * count // 2
+    mine = weights[0].shape
+    copies = PAIRS * (count - 1) + 9
+    outs = [
+        (pl.BlockSpec((1, count, 2, row_count), pair), shape_of(groups, count, 2, row_count, kind=F32)),
+        (ANYWHERE, shape_of(PAIRS, count, row_count, TILE)),
+        (ANYWHERE, shape_of(PAIRS, count - 1, row_count, TILE)),
+        (ANYWHERE, shape_of(row_count, TILE)),
+    ] + [(ANYWHERE, shape_of(*mine))] * 9
+    return pl.pallas_call(
+        functools.partial(attend_kernel, prompt_rows),
+        grid=(PAIRS * 2 * count + 2,),
+        in_specs=[
+            pl.BlockSpec((1, count, row_count, TILE), pair),
+            pl.BlockSpec((1, count, row_count, TILE), pair),
+            pl.BlockSpec((1, count, TILE, row_count), pair),
+            pl.BlockSpec((count, cont_rows, 1), lambda i: (0, 0, 0)),
+            pl.BlockSpec((count, 1, cont_rows), lambda i: (0, 0, 0)),
+        ]
+        + [ANYWHERE] * len(weights),
+        out_specs=[out[0] for out in outs],
+        out_shape=[out[1] for out in outs],
+        scratch_shapes=[
+            pltpu.VMEM((TILE, max(prompt_rows, cont_rows)), F32),
+            pltpu.VMEM((groups, count, row_count, TILE), BF16),
+            pltpu.SemaphoreType.DMA((copies,)),
+            pltpu.SemaphoreType.DMA((copies,)),
+            pltpu.SemaphoreType.DMA((2,)),
         ],
-        [whole_out(row_count, TILE)] * spans + [whole_out(1, count, 2, row_count, kind=F32)],
-        scratch=[pltpu.VMEM((TILE, max(prompt_rows, cont_rows)), F32)],
-        flops=4 * heads * TILE * pairs,
-        exps=heads * pairs,
-        after=after,
-        carry=carry,
-    )
+        compiler_params=pltpu.CompilerParams(
+            vmem_limit_bytes=56 << 20, collective_id=3, has_side_effects=True
+        ),
+        cost_estimate=pl.CostEstimate(
+            flops=8 * TILE * pairs, bytes_accessed=20 << 20, transcendentals=2 * pairs
+        ),
+        name="attend",
+    )(q, k, vt, seg_col, seg_row, *weights)
 
 
 def attend_back_kernel(
@@ -662,7 +919,7 @@
             @pl.when(distance == at)
             def _():
                 do_s[:size] = do_refs[at][rows, :]
-                o_s[:size] = o_refs[at][rows, :]
+                o_s[:size] = o_refs[at][0, 0, rows, :]
 
         grad = do_s[:size]
         product = (grad.astype(F32) * o_s[:size].astype(F32)).T
@@ -726,18 +983,21 @@
         "attend_back",
         (place,),
         (2 * spans,),
-        (q, k, v, kt, lse, seg_col, seg_row, *grads, *outs),
+        (q, k, v, kt, lse, seg_col, seg_row, *grads, *[outs] * spans),
         [
             tall,
             tall,
             tall,
             pl.BlockSpec((1, count, TILE, row_count), pick),
-            blocks(1, count, 2, row_count),
+            pl.BlockSpec((1, count, 2, row_count), pick),
             blocks(count, cont_rows, 1),
             blocks(count, 1, cont_rows),
         ]
         + [pl.BlockSpec((row_count, TILE), lambda i, s: (0, tile))] * spans
-        + [blocks(row_count, TILE)] * spans,
+        + [
+            pl.BlockSpec((1, 1, row_count, TILE), lambda i, s, away=away: (tile, away, 0, 0))
+            for away in range(spans)
+        ],
         [whole_out(1, count, row_count, TILE)] * 3,
         scratch=[
             pltpu.VMEM((count, row_count, TILE), F32),
@@ -768,16 +1028,29 @@
     return rate * (grad - shift - unit * along)
 
 
+def piece_of(own_ref, pieces_ref, distance):
+    tiles = [
+        pieces_ref[pair, distance - 1] if distance else own_ref[pair, 0] for pair in range(PAIRS)
+    ]
+    return jnp.concatenate(tiles, axis=1)
+
+
+def piece_specs(places, size):
+    return [
+        pl.BlockSpec((PAIRS, 1, size, TILE), lambda i, p: (0, 0, i, 0)),
+        pl.BlockSpec((PAIRS, places - 1, size, TILE), lambda i, p: (0, 0, i, 0)),
+        pl.BlockSpec((size, TILE), lambda i, p: (i, 0)),
+    ]
+
+
 def merge_kernel(places, place_ref, x_ref, w_ref, out_bias_ref, gain_ref, bias_ref, *refs):
-    pieces, last_ref, (hidden_ref, low_ref, flip_ref) = refs[:-4], refs[-4], refs[-3:]
+    own_ref, pieces_ref, last_ref, hidden_ref, low_ref, flip_ref = refs
     own = 2 * PAIRS * HEAD
     width = hidden_ref.shape[1]
     total = x_ref[:, :width].astype(F32) + out_bias_ref[...]
     for distance in range(places):
         start = pl.multiple_of((place_ref[0] ^ distance) * own, own)
-        joined = jnp.concatenate(
-            [ref[...] for ref in pieces[distance * PAIRS : (distance + 1) * PAIRS]], axis=1
-        )
+        joined = piece_of(own_ref, pieces_ref, distance)
         total = total + dot(joined, w_ref[pl.ds(start, own), :])
     total = total + dot(last_ref[:, :HEAD], w_ref[width - HEAD :, :])
     hidden_ref[...] = total
@@ -787,19 +1060,19 @@
     flip_ref[...] = low.T
 
 
-def merge(place, rows, w_out, out_bias, gain, bias, pieces, last, after=(), carry=()):
+def merge(place, rows, w_out, out_bias, gain, bias, pieces, after=(), carry=()):
     row_count, width = rows.shape[0], w_out.shape[1]
     size = 128
     by_row = lambda cols: pl.BlockSpec((size, cols), lambda i, p: (i, 0))
     return launch(
-        functools.partial(merge_kernel, len(pieces) // PAIRS),
+        functools.partial(merge_kernel, pieces[0].shape[1]),
         "merge",
         (place,),
         (row_count // size,),
-        (rows, w_out, out_bias[None], gain[None], bias[None], *pieces, last),
+        (rows, w_out, out_bias[None], gain[None], bias[None], *pieces),
         [by_row(rows.shape[1]), blocks(*w_out.shape)]
         + [blocks(1, width)] * 3
-        + [by_row(TILE)] * (len(pieces) + 1),
+        + piece_specs(pieces[0].shape[1], size),
         [
             (by_row(width), shape_of(row_count, width, kind=F32)),
             (by_row(width), shape_of(row_count, width)),
@@ -827,7 +1100,7 @@
     proj_bias_ref,
     *refs,
 ):
-    pieces, last_ref, refs = refs[: places * PAIRS], refs[places * PAIRS], refs[places * PAIRS + 1 :]
+    own_ref, pieces_ref, last_ref, refs = *refs[:3], refs[3:]
     prompt_ref, cont_ref, gh_ref = refs[:3]
     ga_refs, (ga_last_ref, *gw_refs, sums_ref, acc) = refs[3 : 3 + places], refs[3 + places :]
     step = pl.program_id(0)
@@ -866,9 +1139,7 @@
         start = pl.multiple_of((place_ref[0] ^ distance) * own, own)
         rows = pl.ds(start, own)
         ga_refs[distance][...] = dot(branch, w_ref[rows, :], NT).astype(BF16)
-        joined = jnp.concatenate(
-            [ref[...] for ref in pieces[distance * PAIRS : (distance + 1) * PAIRS]], axis=1
-        )
+        joined = piece_of(own_ref, pieces_ref, distance)
         acc[rows, :] += dot(joined.T, branch)
     last = dot(branch, w_ref[width - HEAD :, :], NT).astype(BF16)
     ga_last_ref[...] = jnp.concatenate([last, jnp.zeros_like(last)], axis=1)
@@ -884,10 +1155,12 @@
                 ref[away] = acc[pl.ds(pl.multiple_of(start, 16), quarter), :].astype(BF16)
 
 
-def bend(place, mlp_out, gm, hidden, g, w_out, gain, proj_bias, pieces, last, prompt_rows, after=(), carry=()):
+def bend(
+    place, mlp_out, gm, hidden, g, w_out, gain, proj_bias, pieces, prompt_rows, after=(), carry=()
+):
     row_count, width = hidden.shape
     size = 128
-    places = len(pieces) // PAIRS
+    places = pieces[0].shape[1]
     prompt_steps = prompt_rows // size
     own = 2 * PAIRS * HEAD
     by_row = lambda cols: pl.BlockSpec((size, cols), lambda i, p: (i, 0))
@@ -896,11 +1169,11 @@
         "bend",
         (place,),
         (row_count // size,),
-        (mlp_out, gm, hidden, g, w_out, gain[None], proj_bias[None], *pieces, last),
+        (mlp_out, gm, hidden, g, w_out, gain[None], proj_bias[None], *pieces),
         [by_row(width)] * 4
         + [blocks(*w_out.shape)]
         + [blocks(1, width)] * 2
-        + [by_row(TILE)] * (len(pieces) + 1),
+        + piece_specs(places, size),
         [
             (
                 pl.BlockSpec((1, size, width), lambda i, p: (0, jnp.minimum(i, prompt_steps - 1), 0)),
@@ -948,9 +1221,9 @@
     gt_ref,
     *refs,
 ):
-    own, far, beside = refs[:parts], refs[parts : 2 * parts], refs[2 * parts : 3 * parts]
-    before_refs = refs[3 * parts : 3 * parts + 2]
-    refs = refs[3 * parts + (0 if first else 2) :]
+    own, far, own_2, far_2 = (refs[i * parts : (i + 1) * parts] for i in range(4))
+    before_refs = refs[4 * parts : 4 * parts + 2]
+    refs = refs[4 * parts + (0 if first else 2) :]
     out_ref, gm_ref, keep_f, send_f, keep_p, send_p, gb_ref = refs[:7]
     wf_s, wp_s, bias_s, biases, act_s, gp_s, wide, sems = refs[7:]
     step = pl.program_id(0)
@@ -965,8 +1238,8 @@
 
     def loads(at, to):
         moves = [(own[at].at[pl.ds(2 * quarter, 16)], bias_s.at[to])]
-        for away, local in enumerate((own[at], far[at])):
-            for across, source in enumerate((local, beside[at].at[away])):
+        for away, sources in enumerate(((own[at], own_2[at]), (far[at], far_2[at]))):
+            for across, source in enumerate(sources):
                 for weight, target in enumerate((wf_s, wp_s)):
                     moves.append(
                         (
@@ -1055,7 +1328,7 @@
     over(width, down)
 
 
-def mlp(spot, x, g, xt, gt, own, far, beside, before=(), after=(), carry=()):
+def mlp(spot, x, g, xt, gt, own, far, own_2, far_2, before=(), after=(), carry=()):
     rows, width = x.shape
     hidden = own[0].shape[1]
     parts, quarter = len(own), width // 4
@@ -1071,14 +1344,14 @@
         "mlp",
         (spot,),
         (parts,),
-        (x, g, xt, gt, *own, *far, *beside, *before),
+        (x, g, xt, gt, *own, *far, *own_2, *far_2, *before),
         [
             whole(rows, width),
             whole(rows, width),
             whole(width, rows),
             whole(width, rows),
         ]
-        + [ANYWHERE] * (3 * parts)
+        + [ANYWHERE] * (4 * parts)
         + [whole(rows, width)] * len(before),
         [
             total,
@@ -1452,7 +1725,7 @@
     half, own = width // 2, 2 * PAIRS * HEAD
     tensors = lax.axis_size("tensor")
     shard = -(-half // tensors // 16) * 16
-    padded = rows.shape[1]
+    padded = vectors.shape[1]
     in_vmem = pl.BlockSpec(memory_space=pltpu.VMEM)
     vmem = lambda *shape, kind=BF16: pltpu.VMEM(shape, kind)
     copies = 4 + 4 * 2 * (tensors - 1) + 3 + 3 * 3 + 2 + 5 + 2 * (tensors - 1) + 2
@@ -1476,7 +1749,7 @@
         ],
         scratch_shapes=[
             vmem(*normed.shape),
-            vmem(2, TILE, padded),
+            vmem(2, TILE, width),
             vmem(2, TILE, width, kind=F32),
             vmem(row_count, cols),
             vmem(row_count, width, kind=F32),
@@ -1623,89 +1896,51 @@
     at = place.reshape(1)
     spot = jnp.stack([core, fsdp, tensor, jnp.int32(tensors), place])
 
-    rows_own, w_mine = pack(at, prompt_in, cont_in, w_qkv, padded)
-    rows_across = swap(rows_own, "ctx", 2)
-    rows_beside = swap(rows_own, "ctx", 1)
-    w_far = swap(w_mine, "fsdp", 1)
     zero_bias = jnp.zeros_like(qv_bias[0])
     col_bias = own_columns(jnp.concatenate([qv_bias[0], zero_bias, qv_bias[1]])[None], place)[0]
-
-    mine, for_far, for_two, for_three, grad_layer, grad_flip = pack_more(
-        core.reshape(1), w_fc, w_proj, fc_bias, prompt_cot, cont_cot, (rows_own,)
-    )
-    out_mine = w_out.astype(BF16)
-    one_away = turn(mine, "tensor", 1)
-
-    w_own = jnp.concatenate(in_order(w_mine, w_far, fsdp), axis=0)
-    step_in = functools.partial(
-        project, w_own=w_own, gain=ln1_gain, bias=ln1_bias, col_bias=col_bias, count=count
-    )
-    made = step_in(at, rows_own, before=None, after=(mine,))
-    made, for_far, out_mine = step_in(
-        at ^ 1, rows_beside, before=made, carry=(for_far, out_mine)
-    )
-    near_far, out_far = swap(for_far, "fsdp", 1), swap(out_mine, "fsdp", 1)
-    (rows_across,) = behind((rows_across,), made[1])
-    rows_corner = swap(rows_across, "ctx", 1)
-    made = step_in(at ^ 2, rows_across, before=made, after=(one_away,))
-    made, for_two = step_in(at ^ 3, rows_corner, before=made, carry=(for_two,))
-    two_away, one_far = turn(for_two, "tensor", 2), swap(one_away, "fsdp", 1)
-    normed, q, k, v, kt, vt = made
+    normed, q, k, v, kt, vt, w_own, rows_own, grad_layer, grad_flip, *mines, out_full = open_up(
+        prompt_in,
+        cont_in,
+        w_qkv,
+        w_fc,
+        w_proj,
+        w_out,
+        fc_bias,
+        prompt_cot,
+        cont_cot,
+        ln1_gain,
+        ln1_bias,
+        col_bias,
+        count,
+    )
+
+    mine, one_away, three_away, near_far = mines
 
     labels = cont_seg[0].reshape(count, cont_rows)
     seg_col, seg_row = labels[:, :, None], labels[:, None, :]
-    near = (q, k, vt, seg_col, seg_row, prompt_rows)
-    heads_out, lses = [], []
-    returned = [[] for _ in range(count)]
-
-    def send_back(outs, lse):
-        heads_out.append(outs)
-        lses.append(lse)
-        for distance, out in enumerate(outs):
-            returned[distance].append(swap(out, "ctx", distance) if distance else out)
-
-    (*outs, lse), for_three = attend(0, 2, count, at, *near, carry=(for_three,))
-    three_away = turn(for_three, "tensor", 3)
-    send_back(outs, lse)
-    *outs, lse = attend(1, 2, count, at, *near, after=(outs[0],))
-    send_back(outs, lse)
-    (two_away,) = behind((two_away,), outs[0])
+    lse, outs, came, last_out, two_away, one_far, three_far, *others = attend(
+        q, k, vt, seg_col, seg_row, prompt_rows, (mine, near_far, one_away, three_away)
+    )
+    mine_2, near_2, one_2, one_far_2, three_2, three_far_2 = others
     two_far = swap(two_away, "fsdp", 1)
-    last_out, lse = attend(PAIRS, 1, 1, at, *near, after=(outs[0], two_away))
-    lses.append(lse)
-    near_far, one_far = behind((near_far, one_far), last_out)
-    beside_first = (
-        swap(jnp.stack([mine, near_far]), "ctx", 1),
-        swap(jnp.stack([one_away, one_far]), "ctx", 1),
-    )
-    out_full = jnp.concatenate(in_order(out_mine, out_far, fsdp), axis=0)
-    pieces = [piece for entry in returned for piece in entry]
-    (hidden, mlp_low, mlp_flip), three_away, two_far = merge(
-        at,
-        rows_own,
-        out_full,
-        out_bias,
-        ln2_gain,
-        ln2_bias,
-        pieces,
-        last_out,
-        carry=(three_away, two_far),
-    )
-    three_far = swap(three_away, "fsdp", 1)
-    beside_two = swap(jnp.stack([two_away, two_far]), "ctx", 1)
+    pieces = (outs, came, last_out)
+    hidden, mlp_low, mlp_flip = merge(
+        at, rows_own, out_full, out_bias, ln2_gain, ln2_bias, pieces
+    )
 
     given = (spot, mlp_low, grad_layer, mlp_flip, grad_flip)
     mlp_out, grad_mlp_in, *grads_first, bias_first = mlp(
-        *given, (mine, one_away), (near_far, one_far), beside_first
-    )
-    (three_far,) = behind((three_far,), bias_first)
-    beside_last = (beside_two, swap(jnp.stack([three_away, three_far]), "ctx", 1))
+        *given, (mine, one_away), (near_far, one_far), (mine_2, one_2), (near_2, one_far_2)
+    )
+    (two_far,) = behind((two_far,), bias_first)
+    two_2, two_far_2 = swap(two_away, "ctx", 1), swap(two_far, "ctx", 1)
     come_first = [swap(grads_first[1], "ctx", 1), swap(grads_first[3], "ctx", 1)]
     mlp_out, grad_mlp_in, *grads_last, bias_last = mlp(
         *given,
-        (two_away, three_away),
-        (two_far, three_far),
-        beside_last,
+        (three_away, two_away),
+        (three_far, two_far),
+        (three_2, two_2),
+        (three_far_2, two_far_2),
         before=(mlp_out, grad_mlp_in),
     )
     come_last = [swap(grads_last[1], "ctx", 1), swap(grads_last[3], "ctx", 1)]
@@ -1720,7 +1955,6 @@
         ln2_gain,
         proj_bias,
         pieces,
-        last_out,
         prompt_rows,
     )
     grads_own, (grad_last, out_keep, out_send, sums2) = rest[:count], rest[count:]
@@ -1729,8 +1963,10 @@
     def added(left, right):
         return left.astype(F32) + right.astype(F32)
 
+    steps_away = (0, 1, 3, 2)
+
     def over_tensor(parts, token):
-        come = [turn(parts[k], "tensor", -k) for k in range(1, tensors)]
+        come = [turn(parts[k], "tensor", -steps_away[k]) for k in range(1, tensors)]
         total = parts[0].astype(F32)
         for part in behind(come, token):
             total = total + part.astype(F32)
@@ -1738,10 +1974,10 @@
 
     def back(pair, tile, heads, grads, outs, after=()):
         return attend_back(
-            pair, tile, heads, at, q, k, v, kt, lses[pair], seg_col, seg_row, grads, outs, prompt_rows, after
+            pair, tile, heads, at, q, k, v, kt, lse, seg_col, seg_row, grads, outs, prompt_rows, after
         )
 
-    grads_left = back(PAIRS, 0, 1, [grad_last], [last_out])
+    grads_left = back(PAIRS, 0, 1, [grad_last], last_out[None, None])
     out_f, sum_f, out_p, sum_p, out_o, sum_o = join(
         spot,
         (grads_first[0], come_first[0], grads_first[2], come_first[1]),
@@ -1749,22 +1985,22 @@
         (out_keep, swap(out_send, "ctx", 1)),
         (grads_left[0], *grads_all[1:]),
     )
-    grads_pair = [back(0, 0, 2, grads_all, heads_out[0], (out_f, out_p))]
+    grads_pair = [back(0, 0, 2, grads_all, outs, (out_f, out_p))]
     come_o = swap(out_o, "fsdp", 1)
     come_f, come_p = swap(out_f, "ctx", 2), swap(out_p, "fsdp", 1)
     come_f, come_p = behind((come_f, come_p), grads_pair[0][0])
     sum_f = added(sum_f, come_f).astype(BF16)
     sum_p = added(sum_p, come_p).astype(BF16)
     out_f, sum_f = sum_f[:, 1], sum_f[:, 0]
-    grads_pair.append(back(1, 1, 2, grads_all, heads_out[1], (out_f, sum_p, grads_pair[0][0])))
+    grads_pair.append(back(1, 1, 2, grads_all, outs, (out_f, sum_p, grads_pair[0][0])))
     (come_f,) = behind((swap(out_f, "fsdp", 1),), grads_pair[1][0])
     sum_f = added(sum_f, come_f).astype(BF16)
     sum_p = over_tensor(sum_p, grads_pair[1][0]).astype(BF16)
     ordered = [entry[part] for part in range(3) for entry in (*grads_pair, grads_left)]
     vectors = jnp.concatenate([sums2, jnp.zeros((tensors, hidden_units), F32)], axis=0)
-    for distance in range(tensors):
+    for k, distance in enumerate(steps_away):
         vectors = lax.dynamic_update_slice(
-            vectors, grad_fc_bias[distance], (4 + (tensor - distance) % tensors, 0)
+            vectors, grad_fc_bias[k], (4 + (tensor - distance) % tensors, 0)
         )
     vectors = jnp.pad(vectors, ((0, 0), (0, padded - width)))
     prompt_grad, cont_grad, sum_qkv, sum_out, late = tail(

time: 750 us -> 661 us (0.88)
  waiting for transfers between devices: 108 us -> 28.3 us
  Pallas kernels: 500 us -> 544 us
  other arithmetic: 37.9 us -> 19.5 us
  starting transfers between devices: 37.9 us -> 21.1 us
  local copies, waits for them, and re-layouts: 59.2 us -> 43.4 us
    pallas_call x0 -> x2, Pallas kernels: none -> 152 us  [the longest x1 80 us: open_up(): pl.pallas_call(open_kernel, in_specs=[ANYWHERE] * 8 + [in_vmem] * 4, out_...]
    pallas_call x26 -> x14, Pallas kernels: 374 us -> 263 us  [launch(): pl.pallas_call(body, grid_spec=pltpu.PrefetchScalarGridSpec(num_scalar_pr...]
    ppermute x9 -> x6, waiting for transfers between devices: 48 us -> 3.43 us  [turn(): lax.ppermute(value, axis, [(place, (place + steps) % count) for place in...]
    ppermute x34 -> x18, waiting for transfers between devices: 59.7 us -> 24.9 us  [swap(): lax.ppermute(value, axis, [(place, place ^ bit) for place in range(count)])]
    unnamed x183 -> x86, local copies, waits for them, and re-layouts: 48.9 us -> 25.6 us
    another operation x4 -> x0, other arithmetic: 12 us -> none  [the longest x1 3.59 us: local_heads(): jnp.stack([one_away, one_far])]
    ppermute x34 -> x18, starting transfers between devices: 26.3 us -> 14.6 us  [swap(): lax.ppermute(value, axis, [(place, place ^ bit) for place in range(count)])]
  transfers between devices with their start and end apart: 43 -> 24, of which waited for: 15 -> 7; matrix products, arithmetic and copies ran while one was open for 7% -> 3% of each run, Pallas kernels for 64% -> 57%
where the time goes in v3:
time: 661 us; the launch traced here: 658 us
  Pallas kernels  544 us (82%)
  local copies, waits for them, and re-layouts  43.4 us (7%)
  waiting for transfers between devices  28.3 us (4%)
  starting transfers between devices  21.1 us (3%)
  other arithmetic  19.5 us (3%)
    pallas_call x14, Pallas kernels, launch(): pl.pallas_call(body, grid_spec=pltpu.PrefetchScalarGridSpec(num_scalar_pr...  263 us
    pallas_call x1, Pallas kernels, tail(): pl.pallas_call(body, in_specs=[in_vmem] * (len(grads) + 1) + [ANYWHERE] *...  129 us
    pallas_call x1, Pallas kernels, open_up(): pl.pallas_call(open_kernel, in_specs=[ANYWHERE] * 8 + [in_vmem] * 4, out_...  80 us
    pallas_call x1, Pallas kernels, attend(): pl.pallas_call(functools.partial(attend_kernel, prompt_rows), grid=(PAIRS...  72.1 us
    unnamed x86, local copies, waits for them, and re-layouts  25.6 us
    ppermute x18, waiting for transfers between devices, swap(): lax.ppermute(value, axis, [(place, place ^ bit) for place in range(count)])  24.9 us
    ppermute x18, starting transfers between devices, swap(): lax.ppermute(value, axis, [(place, place ^ bit) for place in range(count)])  14.6 us
  transfers between devices with their start and end apart: 24, of which 7 were waited for; matrix products, arithmetic and copies ran while one was open for 3% of the time, Pallas kernels for 57%

profile of v3, /device:TPU:0, one launch (start us, length us, event | category | flops | bytes accessed | tf_op | source)
XLA Modules:
  0.0 657.5 jit_solution(6859244281989727839)
XLA Ops:
  1.7 1.7 broadcast_in_dim.50.refs_9_
  3.4 1.7 broadcast_in_dim.51.refs_10_
  5.1 1.3 broadcast_in_dim.38.refs_8_
  7.1 1.5 broadcast_in_dim_reshape_squeeze.8.seg_col_ref.refs_6_
  9.5 80.0 %open.1 = (bf16[4,1104,896]{2,1,0:T(8,128)(2,1)}, bf16[3,4,896,128]{3,2,1,0:T(8,128)(2,1)}, bf16[3,4,896,128]{3,2,1,0:T(8,128)(2,1)}, bf16[3,4,896,128]{3,2,1,0:...) custom-call(bf16[1088,512]{1,0:T(8,128)(2,1)} %bitcast.72, ...), custom_call_target="tpu_custom_call" | custom-call | flops 8984199168 | bytes 41943040 | tf_op jit(solution)/shard_map/open/pallas_call | solution.py:610
  89.5 72.1 %attend.1 = (f32[3,4,2,896]{3,2,1,0:T(2,128)}, bf16[2,4,896,128]{3,2,1,0:T(8,128)(2,1)}, bf16[2,3,896,128]{3,2,1,0:T(8,128)(2,1)}, bf16[896,128]{1,0:T(8,128)(2,...) custom-call(bf16[3,4,896,128]{3,2,1,0:T(8,128)(2,1)} %get-tuple-elem, ...), custom_call_target="tpu_custom_call" | custom-call | flops 16106127360 | bytes 20971520 | tf_op jit(solution)/shard_map/attend/pallas_call | solution.py:836
  162.9 1.5 copy-done
  164.4 1.3 copy-done.1
  166.7 9.6 %merge.1 = (f32[896,1088]{1,0:T(8,128)}, bf16[896,1088]{1,0:T(8,128)(2,1)}, bf16[1088,896]{1,0:T(8,128)(2,1)S(1)}) custom-call(s32[1]{0:T(128)} %bitcast.refs_0_, bf16[896,1088]{1,0:T(8,128)(2,1)} %get-tuple-element.100.refs_1_.refs_11_, bf16[1088,1088]{1,0:T(8,128)(2,1)} %get-tuple-element.101.refs_2_.refs_5_, f32[1,1088]{1,0:T(1,128)S(1)} %broadcast_in_dim.44.refs_3_, ...), custom_call_target="tpu_custom_call" | custom-call | flops 424253856 | bytes 3355443 | tf_op jit(solution)/shard_map/merge/pallas_call | solution.py:314
  176.3 1.3 copy-done.10
  177.6 56.6 %mlp.2 = (f32[896,1088]{1,0:T(8,128)}, f32[896,1088]{1,0:T(8,128)}, bf16[2,2,272,1088]{3,2,1,0:T(8,128)(2,1)}, bf16[2,2,272,1088]{3,2,1,0:T(8,128)(2,1)}, bf16[2...) custom-call(s32[5]{0:T(128)} %stack.34.refs_0_, ...), custom_call_target="tpu_custom_call" | custom-call | flops 5091046400 | bytes 8388608 | tf_op jit(solution)/shard_map/mlp/pallas_call | solution.py:314
  235.9 3.6 collective-permute-done.2.refs_12_
  240.6 59.4 %mlp.3 = (f32[896,1088]{1,0:T(8,128)}, f32[896,1088]{1,0:T(8,128)}, bf16[2,2,272,1088]{3,2,1,0:T(8,128)(2,1)}, bf16[2,2,272,1088]{3,2,1,0:T(8,128)(2,1)}, bf16[2...) custom-call(s32[5]{0:T(128)} %stack.34.refs_0_, ...), custom_call_target="tpu_custom_call" | custom-call | flops 5091046400 | bytes 8388608 | tf_op jit(solution)/shard_map/mlp/pallas_call | solution.py:314
  300.7 21.2 %bend.1 = (bf16[1,512,1088]{2,1,0:T(8,128)(2,1)S(1)}, bf16[1,384,1088]{2,1,0:T(8,128)(2,1)S(1)}, f32[896,1088]{1,0:T(8,128)}, bf16[896,256]{1,0:T(8,128)(2,1)S(1...) custom-call(s32[2]{0:T(128)S(1)} %pad_add_fusion.refs_0_, ...), custom_call_target="tpu_custom_call" | custom-call | flops 848507712 | bytes 6291456 | tf_op jit(solution)/shard_map/bend/pallas_call | solution.py:314
  325.9 2.6 collective-permute-start.4
  329.0 2.3 collective-permute-start.5
  331.3 9.3 %attend_back.3 = (bf16[1,4,896,128]{3,2,1,0:T(8,128)(2,1)}, bf16[1,4,896,128]{3,2,1,0:T(8,128)(2,1)}, bf16[1,4,896,128]{3,2,1,0:T(8,128)(2,1)}) custom-call(s32[1]{0:T(128)} %bitcast.refs_0_, bf16[3,4,896,128]{3,2,1,0:T(8,128)(2,1)} %get-tuple-element.102.q_ref.refs_1_, bf16[3,4,896,128]{3,2,1,0:T(8,128)(2,1)} %get-tuple-element.103.k_ref.refs_2_, ...), custom_call_target="tpu_custom_call" | custom-call | flops 335544320 | bytes 3355443 | tf_op jit(solution)/shard_map/attend_back/pallas_call | solution.py:314
  340.6 8.0 %collective-permute-done.5.refs_14_.refs_11_ = bf16[896,256]{1,0:T(8,128)(2,1)S(1)} collective-permute-done((bf16[896,256]{1,0:T(8,128)(2,1)S(1)}, bf16[896,256]{1,0:T(8,128)(2,1)S(1)}, u32[]{:S(2)}, u32[]{:S(2)}) %collective-permute-start.5) | collective-permute-done | bytes 458784 | tf_op jit(solution)/shard_map/ppermute | solution.py:276
  348.7 1.3 copy-done.14
  350.0 14.4 %join.1 = (bf16[4,2,136,1088]{3,2,1,0:T(8,128)(2,1)}, bf16[4,2,136,1088]{3,2,1,0:T(8,128)(2,1)}, bf16[4,272,1088]{2,1,0:T(8,128)(2,1)}, bf16[4,272,1088]{2,1,0:T...) custom-call(s32[5]{0:T(128)S(1)} %copy-done.22, ...), custom_call_target="tpu_custom_call" | custom-call | bytes 6291456 | tf_op jit(solution)/shard_map/join/pallas_call | solution.py:314
  366.1 1.4 collective-permute-start.11
  367.5 1.5 collective-permute-start.12
  369.9 46.1 %attend_back.4 = (bf16[1,4,896,128]{3,2,1,0:T(8,128)(2,1)}, bf16[1,4,896,128]{3,2,1,0:T(8,128)(2,1)}, bf16[1,4,896,128]{3,2,1,0:T(8,128)(2,1)}) custom-call(s32[1]{0:T(128)} %bitcast.refs_0_, bf16[3,4,896,128]{3,2,1,0:T(8,128)(2,1)} %get-tuple-element.102.q_ref.refs_1_, bf16[3,4,896,128]{3,2,1,0:T(8,128)(2,1)} %get-tuple-element.103.k_ref.refs_2_, ...), custom_call_target="tpu_custom_call" | custom-call | flops 2684354560 | bytes 3355443 | tf_op jit(solution)/shard_map/attend_back/pallas_call | solution.py:314
  416.0 6.9 %collective-permute-done.11.refs_1_ = bf16[4,2,136,1088]{3,2,1,0:T(8,128)(2,1)S(1)} collective-permute-done((bf16[4,2,136,1088]{3,2,1,0:T(8,128)(2,1)}, bf16[4,2,136,1088]{3,2,1,0:T(8,128)(2,1)S(1)}, u32[]{:S(2)}, u32[]{:S(2)}) %collective-permute-start.11) | collective-permute-done | bytes 2367520 | tf_op jit(solution)/shard_map/ppermute | solution.py:276
  422.9 1.6 collective-permute-done.12.refs_2_
  424.5 1.2 copy-done.6
  425.7 1.7 copy-done.30
  431.1 2.4 add_convert_fusion.refs_17_
  433.5 1.4 slice_bitcast_fusion.4
  434.9 1.5 collective-permute-start.15
  437.5 1.5 collective-permute-start.14
  440.4 46.1 %attend_back.5 = (bf16[1,4,896,128]{3,2,1,0:T(8,128)(2,1)}, bf16[1,4,896,128]{3,2,1,0:T(8,128)(2,1)}, bf16[1,4,896,128]{3,2,1,0:T(8,128)(2,1)}) custom-call(s32[1]{0:T(128)} %bitcast.refs_0_, bf16[3,4,896,128]{3,2,1,0:T(8,128)(2,1)} %get-tuple-element.102.q_ref.refs_1_, bf16[3,4,896,128]{3,2,1,0:T(8,128)(2,1)} %get-tuple-element.103.k_ref.refs_2_, ...), custom_call_target="tpu_custom_call" | custom-call | flops 2684354560 | bytes 3355443 | tf_op jit(solution)/shard_map/attend_back/pallas_call | solution.py:314
  486.5 3.4 collective-permute-done.17.refs_3_
  491.1 2.4 fusion.3.refs_18_
  495.4 3.4 collective-permute-start.18
  499.4 129.1 %tail.1 = (bf16[1,512,1088]{2,1,0:T(8,128)(2,1)}, bf16[1,384,1088]{2,1,0:T(8,128)(2,1)}, bf16[544,3264]{1,0:T(8,128)(2,1)}, bf16[544,1088]{1,0:T(8,128)(2,1)}, f32[16,1152]{1,0:T(8,128)}) custom-call(bf16[1,4,896,128]{3,2,1,0:T(8,128)(2,1)} %get-tuple-element.154.refs_0_.refs_18_, bf16[1,4,896,128]{3,2,1,0:T(8,128)(2,1)} %get-tuple-element.159.refs_0_.refs_1_, ...), custom_call_target="tpu_custom_call" | custom-call | flops 17968398336 | bytes 31457280 | tf_op jit(solution)/shard_map/tail/pallas_call | solution.py:1739
  630.5 1.6 collective-permute-start.21
  632.1 1.2 fusion.4
  633.3 4.2 collective-permute-done.21
  637.7 1.2 pad_maximum_fusion
  638.9 1.4 copy.58
  640.2 1.3 copy.59
  642.1 5.7 convert_element_type.102
  647.8 1.6 convert_element_type.103
  649.5 1.4 copy.60
  650.9 1.3 copy.61
  652.8 1.6 broadcast_select_fusion.1
  654.8 2.6 slice_bitcast_fusion
  (152 shorter events, 29.0 us)
Async XLA Ops:
  89.5 72.7 %copy-start.37 = (f32[1088]{0:T(1024)S(1)}, f32[1088]{0:T(1024)}, u32[]{:S(2)}) copy-start(f32[1088]{0:T(1024)} %param.26) | copy-start | bytes 13060
  89.5 72.7 %copy-start.38 = (f32[1088]{0:T(1024)S(1)}, f32[1088]{0:T(1024)}, u32[]{:S(2)}) copy-start(f32[1088]{0:T(1024)} %param.25) | copy-start | bytes 13060
  89.5 72.8 %copy-start.39 = (f32[1088]{0:T(1024)S(1)}, f32[1088]{0:T(1024)}, u32[]{:S(2)}) copy-start(f32[1088]{0:T(1024)} %param.27) | copy-start | bytes 13060
  161.7 72.6 %collective-permute-start = (bf16[560,1088]{1,0:T(8,128)(2,1)}, bf16[560,1088]{1,0:T(8,128)(2,1)S(1)}, u32[]{:S(2)}, u32[]{:S(2)}) collective-permute-start(bf16[560,1088]{1,0:T(8,128)(2,1)} %get-tuple-element.116.refs_6_), channel_id=1, source_target_pairs={{0,16},{16,0},{1,17},{17,1},{2,18},{18,2},{3,19},{19,3},{4,20},{20... | collective-permute-start | bytes 3655688 | tf_op jit(solution)/shard_map/ppermute | solution.py:276
  162.2 73.7 %collective-permute-start.1 = (bf16[560,1088]{1,0:T(8,128)(2,1)}, bf16[560,1088]{1,0:T(8,128)(2,1)}, u32[]{:S(2)}, u32[]{:S(2)}) collective-permute-start(bf16[560,1088]{1,0:T(8,128)(2,1)} %get-tuple-element.116.refs_6_), channel_id=1, source_target_pairs={{0,4},{4,0},{8,12},{12,8},{1,5},{5,1},{9,13},{13,9},{2,6},{6,2},{1... | collective-permute-start | bytes 3655688 | tf_op jit(solution)/shard_map/ppermute | solution.py:276
  234.9 5.7 copy-start.2
  234.9 4.6 collective-permute-start.2
  235.4 90.3 %collective-permute-start.6 = (bf16[2,2,272,1088]{3,2,1,0:T(8,128)(2,1)}, bf16[2,2,272,1088]{3,2,1,0:T(8,128)(2,1)}, u32[]{:S(2)}, u32[]{:S(2)}) collective-permute-start(bf16[2,2,272,1088]{3,2,1,0:T(8,128)(2,1)} %get-tuple-element.141), channel_id=1, source_target_pairs={{0,4},{4,0},{8,12},{12,8},{1,5},{5,1},{9,13},{13,9},{2,6},{6,2},{1... | collective-permute-start | bytes 7102472 | tf_op jit(solution)/shard_map/ppermute | solution.py:276
  235.4 90.5 %collective-permute-start.7 = (bf16[2,2,272,1088]{3,2,1,0:T(8,128)(2,1)}, bf16[2,2,272,1088]{3,2,1,0:T(8,128)(2,1)}, u32[]{:S(2)}, u32[]{:S(2)}) collective-permute-start(bf16[2,2,272,1088]{3,2,1,0:T(8,128)(2,1)} %get-tuple-element.143), channel_id=1, source_target_pairs={{0,4},{4,0},{8,12},{12,8},{1,5},{5,1},{9,13},{13,9},{2,6},{6,2},{1... | collective-permute-start | bytes 7102472 | tf_op jit(solution)/shard_map/ppermute | solution.py:276
  240.6 60.0 %copy-start.40 = (f32[1088]{0:T(1024)S(1)}, f32[1088]{0:T(1024)}, u32[]{:S(2)}) copy-start(f32[1088]{0:T(1024)} %param.31) | copy-start | bytes 13060
  240.6 60.1 %copy-start.9 = (bf16[896,128]{1,0:T(8,128)(2,1)S(1)}, bf16[896,128]{1,0:T(8,128)(2,1)}, u32[]{:S(2)}) copy-start(bf16[896,128]{1,0:T(8,128)(2,1)} %get-tuple-element.111.refs_8_.refs_10_) | copy-start | bytes 688132
  300.0 48.6 %collective-permute-start.8 = (bf16[2,2,272,1088]{3,2,1,0:T(8,128)(2,1)}, bf16[2,2,272,1088]{3,2,1,0:T(8,128)(2,1)}, u32[]{:S(2)}, u32[]{:S(2)}) collective-permute-start(bf16[2,2,272,1088]{3,2,1,0:T(8,128)(2,1)} %get-tuple-element.145), channel_id=1, source_target_pairs={{0,4},{4,0},{8,12},{12,8},{1,5},{5,1},{9,13},{13,9},{2,6},{6,2},{1... | collective-permute-start | bytes 7102472 | tf_op jit(solution)/shard_map/ppermute | solution.py:276
  300.5 48.2 %collective-permute-start.9 = (bf16[2,2,272,1088]{3,2,1,0:T(8,128)(2,1)}, bf16[2,2,272,1088]{3,2,1,0:T(8,128)(2,1)}, u32[]{:S(2)}, u32[]{:S(2)}) collective-permute-start(bf16[2,2,272,1088]{3,2,1,0:T(8,128)(2,1)} %get-tuple-element.147), channel_id=1, source_target_pairs={{0,4},{4,0},{8,12},{12,8},{1,5},{5,1},{9,13},{13,9},{2,6},{6,2},{1... | collective-permute-start | bytes 7102472 | tf_op jit(solution)/shard_map/ppermute | solution.py:276
  325.4 23.2 %collective-permute-start.10 = (bf16[2,272,1088]{2,1,0:T(8,128)(2,1)}, bf16[2,272,1088]{2,1,0:T(8,128)(2,1)S(1)}, u32[]{:S(2)}, u32[]{:S(2)}) collective-permute-start(bf16[2,272,1088]{2,1,0:T(8,128)(2,1)} %get-tuple-element.149), channel_id=1, source_target_pairs={{0,4},{4,0},{8,12},{12,8},{1,5},{5,1},{9,13},{13,9},{2,6},{6,2},{1... | collective-permute-start | bytes 3551240 | tf_op jit(solution)/shard_map/ppermute | solution.py:276
  325.8 3.2 collective-permute-start.3
  325.9 14.7 %collective-permute-start.4 = (bf16[896,256]{1,0:T(8,128)(2,1)S(1)}, bf16[896,256]{1,0:T(8,128)(2,1)S(1)}, u32[]{:S(2)}, u32[]{:S(2)}) collective-permute-start(bf16[896,256]{1,0:T(8,128)(2,1)S(1)} %get-tuple-element.138), channel_id=1, source_target_pairs={{0,8},{4,12},{8,0},{12,4},{1,9},{5,13},{9,1},{13,5},{2,10},{6,14},... | collective-permute-start | bytes 1376264 | tf_op jit(solution)/shard_map/ppermute | solution.py:276
  329.0 19.7 %copy-start.3 = (bf16[896,256]{1,0:T(8,128)(2,1)}, bf16[896,256]{1,0:T(8,128)(2,1)S(1)}, u32[]{:S(2)}) copy-start(bf16[896,256]{1,0:T(8,128)(2,1)S(1)} %collective-permute-done.3.refs_12_.refs_9_) | copy-start | bytes 1376260
  329.0 19.6 %collective-permute-start.5 = (bf16[896,256]{1,0:T(8,128)(2,1)S(1)}, bf16[896,256]{1,0:T(8,128)(2,1)S(1)}, u32[]{:S(2)}, u32[]{:S(2)}) collective-permute-start(bf16[896,256]{1,0:T(8,128)(2,1)S(1)} %get-tuple-element.139), channel_id=1, source_target_pairs={{0,12},{4,8},{8,4},{12,0},{1,13},{5,9},{9,5},{13,1},{2,14},{6,10},... | collective-permute-start | bytes 1376264 | tf_op jit(solution)/shard_map/ppermute | solution.py:276
  331.3 17.4 %copy-start.22 = (s32[5]{0:T(128)S(1)}, s32[5]{0:T(128)}, u32[]{:S(2)}) copy-start(s32[5]{0:T(128)} %stack.34.refs_0_) | copy-start | bytes 64
  340.6 23.8 %copy-start.4 = (bf16[896,256]{1,0:T(8,128)(2,1)}, bf16[896,256]{1,0:T(8,128)(2,1)S(1)}, u32[]{:S(2)}) copy-start(bf16[896,256]{1,0:T(8,128)(2,1)S(1)} %collective-permute-done.4.refs_13_.refs_10_) | copy-start | bytes 1376260
  348.6 15.8 %copy-start.5 = (bf16[896,256]{1,0:T(8,128)(2,1)}, bf16[896,256]{1,0:T(8,128)(2,1)S(1)}, u32[]{:S(2)}) copy-start(bf16[896,256]{1,0:T(8,128)(2,1)S(1)} %collective-permute-done.5.refs_14_.refs_11_) | copy-start | bytes 1376260
  350.0 19.0 %copy-start.35 = (f32[1088]{0:T(1024)S(1)}, f32[1088]{0:T(1024)}, u32[]{:S(2)}) copy-start(f32[1088]{0:T(1024)} %param.20) | copy-start | bytes 13060
  350.0 19.6 %copy-start.21 = (f32[2,1,1088]{2,1,0:T(1,128)S(1)}, f32[2,1,1088]{2,1,0:T(1,128)}, u32[]{:S(2)}) copy-start(f32[2,1,1088]{2,1,0:T(1,128)} %get-tuple-element.123.refs_0_) | copy-start | bytes 26116
  366.1 56.8 %collective-permute-start.11 = (bf16[4,2,136,1088]{3,2,1,0:T(8,128)(2,1)}, bf16[4,2,136,1088]{3,2,1,0:T(8,128)(2,1)S(1)}, u32[]{:S(2)}, u32[]{:S(2)}) collective-permute-start(bf16[4,2,136,1088]{3,2,1,0:T(8,128)(2,1)} %get-tuple-element.152.refs_16_), channel_id=1, source_target_pairs={{0,8},{4,12},{8,0},{12,4},{1,9},{5,13},{9,1},{13,5},{2,10},{6,14},... | collective-permute-start | bytes 7102472 | tf_op jit(solution)/shard_map/ppermute | solution.py:276
  367.5 57.0 %collective-permute-start.12 = (bf16[4,272,1088]{2,1,0:T(8,128)(2,1)}, bf16[4,272,1088]{2,1,0:T(8,128)(2,1)}, u32[]{:S(2)}, u32[]{:S(2)}) collective-permute-start(bf16[4,272,1088]{2,1,0:T(8,128)(2,1)} %get-tuple-element.153.refs_17_), channel_id=1, source_target_pairs={{0,16},{16,0},{1,17},{17,1},{2,18},{18,2},{3,19},{19,3},{4,20},{20... | collective-permute-start | bytes 7102472 | tf_op jit(solution)/shard_map/ppermute | solution.py:276
  425.7 1.7 copy-start.30
  428.1 1.9 copy-start.26
  428.1 3.1 copy-start.29
  433.5 3.4 copy-start.25
  433.5 5.5 copy-start.36
  434.9 51.6 %collective-permute-start.15 = (bf16[272,1088]{1,0:T(8,128)(2,1)}, bf16[272,1088]{1,0:T(8,128)(2,1)S(1)}, u32[]{:S(2)}, u32[]{:S(2)}) collective-permute-start(bf16[272,1088]{1,0:T(8,128)(2,1)} %get-tuple-element.231), channel_id=1, source_target_pairs={{0,3},{1,0},{2,1},{3,2},{4,7},{5,4},{6,5},{7,6},{8,11},{9,8},{10,9... | collective-permute-start | bytes 1775624 | tf_op jit(solution)/shard_map/ppermute | solution.py:281
  436.4 50.1 %collective-permute-start.16 = (bf16[272,1088]{1,0:T(8,128)(2,1)}, bf16[272,1088]{1,0:T(8,128)(2,1)S(1)}, u32[]{:S(2)}, u32[]{:S(2)}) collective-permute-start(bf16[272,1088]{1,0:T(8,128)(2,1)} %get-tuple-element.230), channel_id=1, source_target_pairs={{0,1},{1,2},{2,3},{3,0},{4,5},{5,6},{6,7},{7,4},{8,9},{9,10},{10,1... | collective-permute-start | bytes 1775624 | tf_op jit(solution)/shard_map/ppermute | solution.py:281
  436.9 53.0 %collective-permute-start.17 = (bf16[272,1088]{1,0:T(8,128)(2,1)}, bf16[272,1088]{1,0:T(8,128)(2,1)S(1)}, u32[]{:S(2)}, u32[]{:S(2)}) collective-permute-start(bf16[272,1088]{1,0:T(8,128)(2,1)} %get-tuple-element.229), channel_id=1, source_target_pairs={{0,2},{1,3},{2,0},{3,1},{4,6},{5,7},{6,4},{7,5},{8,10},{9,11},{10,... | collective-permute-start | bytes 1775624 | tf_op jit(solution)/shard_map/ppermute | solution.py:281
  437.5 56.5 %collective-permute-start.14 = (bf16[4,136,1088]{2,1,0:T(8,128)(2,1)}, bf16[4,136,1088]{2,1,0:T(8,128)(2,1)S(1)}, u32[]{:S(2)}, u32[]{:S(2)}) collective-permute-start(bf16[4,136,1088]{2,1,0:T(8,128)(2,1)} %slice_bitcast_fusion.3.refs_16_), channel_id=1, source_target_pairs={{0,16},{16,0},{1,17},{17,1},{2,18},{18,2},{3,19},{19,3},{4,20},{20... | collective-permute-start | bytes 3551240 | tf_op jit(solution)/shard_map/ppermute | solution.py:276
  439.9 59.5 %collective-permute-start.13 = (bf16[272,1088]{1,0:T(8,128)(2,1)}, bf16[272,1088]{1,0:T(8,128)(2,1)}, u32[]{:S(2)}, u32[]{:S(2)}) collective-permute-start(bf16[272,1088]{1,0:T(8,128)(2,1)} %copy-done.24), channel_id=1, source_target_pairs={{0,16},{16,0},{1,17},{17,1},{2,18},{18,2},{3,19},{19,3},{4,20},{20... | collective-permute-start | bytes 1775624 | tf_op jit(solution)/shard_map/ppermute | solution.py:276
  491.1 2.9 copy-start.27
  493.5 134.9 %collective-permute-start.22 = (bf16[272,1088]{1,0:T(8,128)(2,1)}, bf16[272,1088]{1,0:T(8,128)(2,1)S(1)}, u32[]{:S(2)}, u32[]{:S(2)}) collective-permute-start(bf16[272,1088]{1,0:T(8,128)(2,1)} %fusion.3.refs_18_), channel_id=1, source_target_pairs={{0,8},{4,12},{8,0},{12,4},{1,9},{5,13},{9,1},{13,5},{2,10},{6,14},... | collective-permute-start | bytes 1775624 | tf_op jit(solution)/shard_map/ppermute | solution.py:276
  494.4 4.4 copy-start.28
  495.4 133.9 %collective-permute-start.18 = (bf16[136,1088]{1,0:T(8,128)(2,1)}, bf16[136,1088]{1,0:T(8,128)(2,1)S(1)}, u32[]{:S(2)}, u32[]{:S(2)}) collective-permute-start(bf16[136,1088]{1,0:T(8,128)(2,1)} %get-tuple-element.234), channel_id=1, source_target_pairs={{0,3},{1,0},{2,1},{3,2},{4,7},{5,4},{6,5},{7,6},{8,11},{9,8},{10,9... | collective-permute-start | bytes 887816 | tf_op jit(solution)/shard_map/ppermute | solution.py:281
  498.8 130.6 %collective-permute-start.19 = (bf16[136,1088]{1,0:T(8,128)(2,1)}, bf16[136,1088]{1,0:T(8,128)(2,1)S(1)}, u32[]{:S(2)}, u32[]{:S(2)}) collective-permute-start(bf16[136,1088]{1,0:T(8,128)(2,1)} %get-tuple-element.233), channel_id=1, source_target_pairs={{0,1},{1,2},{2,3},{3,0},{4,5},{5,6},{6,7},{7,4},{8,9},{9,10},{10,1... | collective-permute-start | bytes 887816 | tf_op jit(solution)/shard_map/ppermute | solution.py:281
  498.8 130.5 %collective-permute-start.20 = (bf16[136,1088]{1,0:T(8,128)(2,1)S(1)}, bf16[136,1088]{1,0:T(8,128)(2,1)S(1)}, u32[]{:S(2)}, u32[]{:S(2)}) collective-permute-start(bf16[136,1088]{1,0:T(8,128)(2,1)S(1)} %get-tuple-element.232), channel_id=1, source_target_pairs={{0,2},{1,3},{2,0},{3,1},{4,6},{5,7},{6,4},{7,5},{8,10},{9,11},{10,... | collective-permute-start | bytes 887816 | tf_op jit(solution)/shard_map/ppermute | solution.py:281
  630.5 7.0 %collective-permute-start.21 = (bf16[136,1088]{1,0:T(8,128)(2,1)S(1)}, bf16[136,1088]{1,0:T(8,128)(2,1)S(1)}, u32[]{:S(2)}, u32[]{:S(2)}) collective-permute-start(bf16[136,1088]{1,0:T(8,128)(2,1)S(1)} %fusion.7), channel_id=1, source_target_pairs={{0,8},{4,12},{8,0},{12,4},{1,9},{5,13},{9,1},{13,5},{2,10},{6,14},... | collective-permute-start | bytes 887816 | tf_op jit(solution)/shard_map/ppermute | solution.py:276
  633.3 5.5 copy-start.13
  637.7 2.6 copy-start.16
  638.9 2.7 copy-start.18
  638.9 14.0 %collective-permute-start.23 = (bf16[2,272,1088]{2,1,0:T(8,128)(2,1)}, bf16[2,272,1088]{2,1,0:T(8,128)(2,1)}, u32[]{:S(2)}, u32[]{:S(2)}) collective-permute-start(bf16[2,272,1088]{2,1,0:T(8,128)(2,1)} %pad_maximum_fusion), channel_id=1, source_target_pairs={{0,4},{4,0},{8,12},{12,8},{1,5},{5,1},{9,13},{13,9},{2,6},{6,2},{1... | collective-permute-start | bytes 3551240 | tf_op jit(solution)/shard_map/ppermute | solution.py:276
  642.1 5.7 copy-start.32
  647.8 3.0 copy-start.34
  (17 other events, 18.2 us)

commit v4 on v3

--- a/solution.py
+++ b/solution.py
@@ -299,7 +299,7 @@
 
 
 def launch(
-    kernel, name, scalars, grid, operands, in_specs, outs, scratch=(), limit=48, flops=0, traffic=16, exps=0, after=(), carry=(), aliases=None
+    kernel, name, scalars, grid, operands, in_specs, outs, scratch=(), limit=48, flops=0, traffic=16, exps=0, after=(), carry=(), aliases=None, meet=None
 ):
     out_specs, out_shapes = [out[0] for out in outs], [out[1] for out in outs]
     given = len(scalars) + len(operands)
@@ -322,7 +322,9 @@
         ),
         out_shape=out_shapes + [shape_of(*entry.shape, kind=entry.dtype) for entry in carry],
         input_output_aliases=links,
-        compiler_params=pltpu.CompilerParams(vmem_limit_bytes=limit << 20),
+        compiler_params=pltpu.CompilerParams(
+            vmem_limit_bytes=limit << 20, collective_id=meet, has_side_effects=meet is not None
+        ),
         cost_estimate=pl.CostEstimate(
             flops=int(flops * HINT),
             bytes_accessed=int(traffic * HINT * (1 << 20)),
@@ -481,13 +483,9 @@
 
     put(mine_s, mine_ref)
 
-    def out_rows(away):
-        return pl.ds(pl.multiple_of((fsdp ^ away) * half + core * quarter, 16), quarter)
-
     load_wo.wait()
     wo_s[...] = wo_f[...].astype(BF16)
     put(wo_s, out_ref.at[mine_half])
-    to_out = push(wo_s.at[mine_rows], out_ref.at[out_rows(0)], far)
     chunk = 128
 
     def over_rows(body):
@@ -567,11 +565,9 @@
     take(second)
     normalise(3, 1)
     project(3, 1)
-    to_out.wait_recv()
-    to_out_beside = push(out_ref.at[out_rows(1)], out_ref.at[out_rows(1)], beside)
     for copy in outs:
         copy.wait()
-    for copy in (to_one, to_near, to_three, to_out_beside):
+    for copy in (to_one, to_near, to_three):
         copy.wait_recv()
     for copy in sent:
         copy.wait_send()
@@ -606,7 +602,7 @@
         mine,
         (width, width),
     ]
-    copies = 2 + 1 + 1 + 3 + 2 + 2
+    copies = 2 + 1 + 1 + 3 + 2
     return pl.pallas_call(
         open_kernel,
         in_specs=[ANYWHERE] * 8 + [in_vmem] * 4,
@@ -664,8 +660,8 @@
 
 def attend_kernel(prompt_rows, q_ref, k_ref, vt_ref, seg_col_ref, seg_row_ref, *refs):
     mine_ref, near_ref, one_ref, three_ref = refs[:4]
-    lse_ref, outs_ref, pieces_ref, last_ref, two_ref, one_far_ref, three_far_ref = refs[4:11]
-    beside_refs, (acc, o_s, send_sem, recv_sem, out_sem) = refs[11:17], refs[17:]
+    lse_ref, outs_ref, pieces_ref, last_ref, two_ref, one_far_ref, three_far_ref = refs[5:12]
+    beside_refs, out_ref, (acc, o_s, send_sem, recv_sem, out_sem) = refs[12:18], refs[18], refs[19:]
     step = pl.program_id(0)
     place = lax.axis_index("ctx")
     fsdp = lax.axis_index("fsdp")
@@ -701,6 +697,11 @@
                 {"ctx": place ^ away},
             )
     base = PAIRS * (count - 1)
+    quarter = out_ref.shape[0] // 4
+
+    def out_rows(away):
+        return out_ref.at[pl.ds(pl.multiple_of(((fsdp ^ away) * 2 + place % 2) * quarter, 16), quarter)]
+
     early = [
         copy_to(base, one_ref, one_far_ref, far),
         copy_to(base + 1, one_ref, two_ref, {"tensor": after}),
@@ -709,10 +710,12 @@
         copy_to(base + 4, one_ref, b_one, beside),
         copy_to(base + 5, three_ref, b_three, beside),
         copy_to(base + 6, three_ref, three_far_ref, far),
+        copy_to(base + 9, out_rows(0), out_rows(0), far),
     ]
     late = [
         copy_to(base + 7, one_far_ref, b_one_far, beside),
         copy_to(base + 8, three_far_ref, b_three_far, beside),
+        copy_to(base + 10, out_rows(1), out_rows(1), beside),
     ]
 
     @pl.when(step == 0)
@@ -725,7 +728,7 @@
                 barrier, inc=1, device_id=partner, device_id_type=pl.DeviceIdType.MESH
             )
         pl.semaphore_wait(barrier, len(partners))
-        for copy in early:
+        for copy in early[:1] + early[7:] + early[1:7]:
             copy.start()
 
     @pl.when(step == per_pair + 2)
@@ -733,7 +736,12 @@
         early[0].wait_recv()
         late[0].start()
 
-    @pl.when(step == steps)
+    @pl.when(step == per_pair + 5)
+    def _():
+        early[7].wait_recv()
+        late[2].start()
+
+    @pl.when(step == steps + 1)
     def _():
         early[6].wait_recv()
         late[1].start()
@@ -820,19 +828,20 @@
             store.wait()
 
 
-def attend(q, k, vt, seg_col, seg_row, prompt_rows, weights):
+def attend(q, k, vt, seg_col, seg_row, prompt_rows, weights, w_out):
     groups, count, row_count, _ = q.shape
     cont_rows = row_count - prompt_rows
     pair = lambda i: (jnp.minimum(i // (2 * count), PAIRS), 0, 0, 0)
     pairs = groups * count * (prompt_rows + 2 * cont_rows) * prompt_rows * count // 2
     mine = weights[0].shape
-    copies = PAIRS * (count - 1) + 9
+    copies = PAIRS * (count - 1) + 11
     outs = [
         (pl.BlockSpec((1, count, 2, row_count), pair), shape_of(groups, count, 2, row_count, kind=F32)),
         (ANYWHERE, shape_of(PAIRS, count, row_count, TILE)),
         (ANYWHERE, shape_of(PAIRS, count - 1, row_count, TILE)),
         (ANYWHERE, shape_of(row_count, TILE)),
     ] + [(ANYWHERE, shape_of(*mine))] * 9
+    outs.append((ANYWHERE, shape_of(*w_out.shape)))
     return pl.pallas_call(
         functools.partial(attend_kernel, prompt_rows),
         grid=(PAIRS * 2 * count + 2,),
@@ -843,7 +852,8 @@
             pl.BlockSpec((count, cont_rows, 1), lambda i: (0, 0, 0)),
             pl.BlockSpec((count, 1, cont_rows), lambda i: (0, 0, 0)),
         ]
-        + [ANYWHERE] * len(weights),
+        + [ANYWHERE] * (len(weights) + 1),
+        input_output_aliases={5 + len(weights): len(outs) - 1},
         out_specs=[out[0] for out in outs],
         out_shape=[out[1] for out in outs],
         scratch_shapes=[
@@ -860,7 +870,7 @@
             flops=8 * TILE * pairs, bytes_accessed=20 << 20, transcendentals=2 * pairs
         ),
         name="attend",
-    )(q, k, vt, seg_col, seg_row, *weights)
+    )(q, k, vt, seg_col, seg_row, *weights, w_out)
 
 
 def attend_back_kernel(
@@ -1037,9 +1047,9 @@
 
 def piece_specs(places, size):
     return [
-        pl.BlockSpec((PAIRS, 1, size, TILE), lambda i, p: (0, 0, i, 0)),
-        pl.BlockSpec((PAIRS, places - 1, size, TILE), lambda i, p: (0, 0, i, 0)),
-        pl.BlockSpec((size, TILE), lambda i, p: (i, 0)),
+        pl.BlockSpec((PAIRS, 1, size, TILE), lambda i, *_: (0, 0, i, 0)),
+        pl.BlockSpec((PAIRS, places - 1, size, TILE), lambda i, *_: (0, 0, i, 0)),
+        pl.BlockSpec((size, TILE), lambda i, *_: (i, 0)),
     ]
 
 
@@ -1088,41 +1098,65 @@
 
 
 def bend_kernel(
-    places,
-    prompt_steps,
-    place_ref,
-    mlp_ref,
-    gm_ref,
-    hidden_ref,
-    g_ref,
-    w_ref,
-    gain_ref,
-    proj_bias_ref,
-    *refs,
+    places, mlp_ref, gm_ref, hidden_ref, g_ref, w_ref, gain_ref, proj_bias_ref, own_ref, pieces_ref, last_ref, *refs
 ):
-    own_ref, pieces_ref, last_ref, refs = *refs[:3], refs[3:]
-    prompt_ref, cont_ref, gh_ref = refs[:3]
-    ga_refs, (ga_last_ref, *gw_refs, sums_ref, acc) = refs[3 : 3 + places], refs[3 + places :]
+    out_ref, gh_ref, ga_ref, ga_last_ref, *refs = refs
+    come_refs, gw_refs, refs = refs[: places - 1], refs[places - 1 : places + 1], refs[places + 1 :]
+    sums_ref, acc, ga_s, send_sem, recv_sem = refs
     step = pl.program_id(0)
+    steps = pl.num_programs(0)
+    place, fsdp = lax.axis_index("ctx"), lax.axis_index("fsdp")
     own = 2 * PAIRS * HEAD
-    width = hidden_ref.shape[1]
+    size, width = hidden_ref.shape
+    mesh_id = pl.DeviceIdType.MESH
+
+    def copies(at):
+        rows = pl.ds(pl.multiple_of(at * size, 16), size)
+        return [
+            pltpu.make_async_remote_copy(
+                src_ref=ga_s.at[away - 1, rows],
+                dst_ref=come_refs[away - 1].at[rows],
+                send_sem=send_sem.at[at, away - 1],
+                recv_sem=recv_sem.at[at, away - 1],
+                device_id={"ctx": place ^ away},
+                device_id_type=mesh_id,
+            )
+            for away in range(1, places)
+        ]
+
+    @pl.when(step == 0)
+    def _():
+        barrier = pltpu.get_barrier_semaphore()
+        for away in range(1, places):
+            pl.semaphore_signal(
+                barrier, inc=1, device_id={"ctx": place ^ away}, device_id_type=mesh_id
+            )
+
     hidden = hidden_ref[...]
-    layer_out = (hidden + mlp_ref[...] + proj_bias_ref[...]).astype(BF16)
-
-    @pl.when(step < prompt_steps)
-    def _():
-        prompt_ref[0] = layer_out
-
-    @pl.when(step >= prompt_steps)
-    def _():
-        cont_ref[0] = layer_out
-
+    out_ref[...] = (hidden + mlp_ref[...] + proj_bias_ref[...]).astype(BF16)
     unit, rate = normalize(hidden)
     grad_in = gm_ref[...]
     grad_layer = g_ref[...].astype(F32)
     grad_hidden = grad_layer + normalize_back(unit, rate, grad_in * gain_ref[...])
     gh_ref[...] = grad_hidden
     branch = grad_hidden.astype(BF16)
+    rows = pl.ds(pl.multiple_of(step * size, 16), size)
+    for distance in range(places - 1, -1, -1):
+        heads = pl.ds(pl.multiple_of((place ^ distance) * own, own), own)
+        piece = dot(branch, w_ref[heads, :], NT).astype(BF16)
+        if distance:
+            ga_s[distance - 1, rows, :] = piece
+        else:
+            ga_ref[...] = piece
+
+    @pl.when(step == 0)
+    def _():
+        pl.semaphore_wait(pltpu.get_barrier_semaphore(), places - 1)
+
+    for copy in copies(step):
+        copy.start()
+    last = dot(branch, w_ref[width - HEAD :, :], NT).astype(BF16)
+    ga_last_ref[...] = jnp.concatenate([last, jnp.zeros_like(last)], axis=1)
     sums = [grad_hidden, grad_in * unit, grad_in, grad_layer]
     sums = jnp.concatenate([jnp.sum(entry, axis=0, keepdims=True) for entry in sums], axis=0)
 
@@ -1136,38 +1170,36 @@
         sums_ref[...] += sums
 
     for distance in range(places):
-        start = pl.multiple_of((place_ref[0] ^ distance) * own, own)
-        rows = pl.ds(start, own)
-        ga_refs[distance][...] = dot(branch, w_ref[rows, :], NT).astype(BF16)
+        heads = pl.ds(pl.multiple_of((place ^ distance) * own, own), own)
         joined = piece_of(own_ref, pieces_ref, distance)
-        acc[rows, :] += dot(joined.T, branch)
-    last = dot(branch, w_ref[width - HEAD :, :], NT).astype(BF16)
-    ga_last_ref[...] = jnp.concatenate([last, jnp.zeros_like(last)], axis=1)
+        acc[heads, :] += dot(joined.T, branch)
     acc[width - HEAD :, :] += dot(last_ref[:, :HEAD].T, branch)
 
-    @pl.when(step == pl.num_programs(0) - 1)
+    @pl.when(step == steps - 1)
     def _():
         quarter = width // 4
-        core, fsdp = place_ref[0] % 2, place_ref[1]
         for beside, ref in enumerate(gw_refs):
             for away in range(2):
-                start = ((fsdp ^ away) * 2 + (core ^ beside)) * quarter
+                start = ((fsdp ^ away) * 2 + (place % 2 ^ beside)) * quarter
                 ref[away] = acc[pl.ds(pl.multiple_of(start, 16), quarter), :].astype(BF16)
 
-
-def bend(
-    place, mlp_out, gm, hidden, g, w_out, gain, proj_bias, pieces, prompt_rows, after=(), carry=()
-):
+        @pl.loop(0, steps)
+        def _(i):
+            for copy in copies(i):
+                copy.wait_recv()
+                copy.wait_send()
+
+
+def bend(mlp_out, gm, hidden, g, w_out, gain, proj_bias, pieces):
     row_count, width = hidden.shape
-    size = 128
+    size = row_count // 4
     places = pieces[0].shape[1]
-    prompt_steps = prompt_rows // size
     own = 2 * PAIRS * HEAD
-    by_row = lambda cols: pl.BlockSpec((size, cols), lambda i, p: (i, 0))
+    by_row = lambda cols: pl.BlockSpec((size, cols), lambda i: (i, 0))
     return launch(
-        functools.partial(bend_kernel, places, prompt_steps),
+        functools.partial(bend_kernel, places),
         "bend",
-        (place,),
+        (),
         (row_count // size,),
         (mlp_out, gm, hidden, g, w_out, gain[None], proj_bias[None], *pieces),
         [by_row(width)] * 4
@@ -1175,28 +1207,27 @@
         + [blocks(1, width)] * 2
         + piece_specs(places, size),
         [
-            (
-                pl.BlockSpec((1, size, width), lambda i, p: (0, jnp.minimum(i, prompt_steps - 1), 0)),
-                shape_of(1, prompt_rows, width),
-            ),
-            (
-                pl.BlockSpec((1, size, width), lambda i, p: (0, jnp.maximum(i - prompt_steps, 0), 0)),
-                shape_of(1, row_count - prompt_rows, width),
-            ),
+            (by_row(width), shape_of(row_count, width)),
             (by_row(width), shape_of(row_count, width, kind=F32)),
+            (by_row(own), shape_of(row_count, own)),
+            (by_row(TILE), shape_of(row_count, TILE)),
         ]
-        + [(by_row(own), shape_of(row_count, own))] * places
+        + [(ANYWHERE, shape_of(row_count, own))] * (places - 1)
         + [
-            (by_row(TILE), shape_of(row_count, TILE)),
             whole_out(2, width // 4, width),
             whole_out(2, width // 4, width),
             whole_out(4, width, kind=F32),
         ],
-        scratch=[pltpu.VMEM((width, width), F32)],
+        scratch=[
+            pltpu.VMEM((width, width), F32),
+            pltpu.VMEM((places - 1, row_count, own), BF16),
+            pltpu.SemaphoreType.DMA((row_count // size, places - 1)),
+            pltpu.SemaphoreType.DMA((row_count // size, places - 1)),
+        ],
+        limit=56,
         flops=4 * row_count * width * width,
         traffic=30,
-        after=after,
-        carry=carry,
+        meet=6,
     )
 
 
@@ -1214,7 +1245,6 @@
 def mlp_kernel(
     parts,
     first,
-    spot_ref,
     x_ref,
     g_ref,
     xt_ref,
@@ -1225,9 +1255,13 @@
     before_refs = refs[4 * parts : 4 * parts + 2]
     refs = refs[4 * parts + (0 if first else 2) :]
     out_ref, gm_ref, keep_f, send_f, keep_p, send_p, gb_ref = refs[:7]
-    wf_s, wp_s, bias_s, biases, act_s, gp_s, wide, sems = refs[7:]
+    wf_s, wp_s, bias_s, biases, act_s, gp_s, wide, keep_s, send_s, come_s, total = refs[7:18]
+    sems, send_sem, recv_sem = refs[18:]
     step = pl.program_id(0)
-    core, fsdp = spot_ref[0], spot_ref[1]
+    place, fsdp = lax.axis_index("ctx"), lax.axis_index("fsdp")
+    core, chip = place % 2, place // 2
+    beside = {"ctx": place ^ 1}
+    mesh_id = pl.DeviceIdType.MESH
     slot = step % 2
     _, width, hidden = wf_s.shape
     quarter = width // 4
@@ -1252,11 +1286,24 @@
             for i, (source, target) in enumerate(moves)
         ]
 
+    def exchange(at):
+        return pltpu.make_async_remote_copy(
+            src_ref=send_s,
+            dst_ref=come_s.at[at],
+            send_sem=send_sem.at[at],
+            recv_sem=recv_sem.at[at],
+            device_id=beside,
+            device_id_type=mesh_id,
+        )
+
     @pl.when(step == 0)
     def _():
         for part in range(parts):
             for copy in loads(part, part):
                 copy.start()
+        barrier = pltpu.get_barrier_semaphore()
+        pl.semaphore_signal(barrier, inc=1, device_id=beside, device_id_type=mesh_id)
+        pl.semaphore_wait(barrier, 1)
 
     for part in range(parts):
 
@@ -1290,21 +1337,25 @@
 
     def weights(start, size):
         cols = pl.ds(start, size)
-        for left, right, keep, send, by_part in (
-            (xt_ref, gp_s, keep_f, send_f, True),
-            (gt_ref, act_s, keep_p, send_p, False),
-        ):
+        for weight, (left, right) in enumerate(((xt_ref, gp_s), (gt_ref, act_s))):
             wide[:, :size] = dot(left[...], right[:, cols]).astype(BF16)
             for far in range(2):
-                for beside, to in enumerate((keep, send)):
-                    piece = wide[spot(far, beside), :size]
-                    if by_part:
-                        to[0, far, :, cols] = piece
-                    else:
-                        to[far, 0, :, cols] = piece
+                for across, to in enumerate((keep_s, send_s)):
+                    to[weight, far, :, cols] = wide[spot(far, across), :size]
 
     over(hidden, up)
+    for part in range(1, parts):
+
+        @pl.when(step == part)
+        def _():
+            exchange(part - 1).wait_send()
+
     over(hidden, weights)
+    for part in range(parts):
+
+        @pl.when(step == part)
+        def _():
+            exchange(part).start()
 
     if first:
 
@@ -1326,23 +1377,38 @@
         gm_ref[:, rows] += dot(gp_s[...], wf_s[slot, rows, :], NT)
 
     over(width, down)
-
-
-def mlp(spot, x, g, xt, gt, own, far, own_2, far_2, before=(), after=(), carry=()):
+    for part in range(parts):
+
+        @pl.when(step == part)
+        def _():
+            exchange(part).wait_recv()
+            for far in range(2):
+                total[...] = keep_s[0, far].astype(F32) + come_s[part, 0, far].astype(F32)
+                for to, away in ((keep_f, 0), (send_f, 1)):
+                    eighth = quarter // 2
+                    rows = pl.ds(pl.multiple_of((chip ^ away) * eighth, 8), eighth)
+                    to[far, 0] = total[rows, :].astype(BF16)
+            for far, to in enumerate((keep_p, send_p)):
+                to[0] = (keep_s[1, far].astype(F32) + come_s[part, 1, far].astype(F32)).astype(BF16)
+            if part == parts - 1:
+                exchange(part).wait_send()
+
+
+def mlp(meet, x, g, xt, gt, own, far, own_2, far_2, before=(), after=(), carry=()):
     rows, width = x.shape
     hidden = own[0].shape[1]
     parts, quarter = len(own), width // 4
     once = pl.Buffered(buffer_count=1)
-    whole = lambda *shape: pl.BlockSpec(shape, lambda k, s: (0,) * len(shape), pipeline_mode=once)
-    by_part = pl.BlockSpec((1, 2, quarter, hidden), lambda k, s: (k, 0, 0, 0))
-    by_far = pl.BlockSpec((2, 1, quarter, hidden), lambda k, s: (0, k, 0, 0))
+    whole = lambda *shape: pl.BlockSpec(shape, lambda k: (0,) * len(shape), pipeline_mode=once)
+    by_far = pl.BlockSpec((2, 1, quarter // 2, hidden), lambda k: (0, k, 0, 0))
+    by_part = pl.BlockSpec((1, quarter, hidden), lambda k: (k, 0, 0))
     total = (whole(rows, width), shape_of(rows, width, kind=F32))
-    by_part = (by_part, shape_of(parts, 2, quarter, hidden))
-    by_far = (by_far, shape_of(2, parts, quarter, hidden))
+    by_far = (by_far, shape_of(2, parts, quarter // 2, hidden))
+    by_part = (by_part, shape_of(parts, quarter, hidden))
     return launch(
         functools.partial(mlp_kernel, parts, not before),
         "mlp",
-        (spot,),
+        (),
         (parts,),
         (x, g, xt, gt, *own, *far, *own_2, *far_2, *before),
         [
@@ -1356,12 +1422,12 @@
         [
             total,
             total,
+            by_far,
+            by_far,
             by_part,
             by_part,
-            by_far,
-            by_far,
             (
-                pl.BlockSpec((1, 1, hidden), lambda k, s: (k, 0, 0)),
+                pl.BlockSpec((1, 1, hidden), lambda k: (k, 0, 0)),
                 shape_of(parts, 1, hidden, kind=F32),
             ),
         ],
@@ -1373,8 +1439,15 @@
             pltpu.VMEM((rows, hidden), BF16),
             pltpu.VMEM((rows, hidden), BF16),
             pltpu.VMEM((width, 256), BF16),
+            pltpu.VMEM((2, 2, quarter, hidden), BF16),
+            pltpu.VMEM((2, 2, quarter, hidden), BF16),
+            pltpu.VMEM((parts, 2, 2, quarter, hidden), BF16),
+            pltpu.VMEM((quarter, hidden), F32),
             pltpu.SemaphoreType.DMA((2, 9)),
+            pltpu.SemaphoreType.DMA((parts,)),
+            pltpu.SemaphoreType.DMA((parts,)),
         ],
+        meet=meet,
         limit=62,
         flops=12 * rows * width * hidden * parts,
         traffic=40,
@@ -1412,10 +1485,9 @@
         left_in,
         vec_out,
         vec_in,
-        wo_near,
         wo_sum,
         wo_ring,
-        wo_chip,
+        wo_half,
         wo_all,
         wo_core,
         local_sem,
@@ -1441,7 +1513,7 @@
 
     loads = [pltpu.make_async_copy(norm_ref, norms, local_sem.at[0])]
     loads.append(pltpu.make_async_copy(keep_ref, wo_core.at[0], local_sem.at[1]))
-    loads.append(pltpu.make_async_copy(come_ref, wo_near, local_sem.at[2]))
+    loads.append(pltpu.make_async_copy(come_ref, core_out.at[pl.ds(0, come_ref.shape[0])], local_sem.at[2]))
     for load in loads:
         load.start()
     sent, used = [], []
@@ -1461,10 +1533,14 @@
         sent.append(copy)
         return copy
 
-    quarter, part_rows = wo_sum.shape[0], wo_ring.shape[1]
+    quarter, part_rows, most_rows = wo_sum.shape[0], wo_ring.shape[1], wo_half.shape[1]
+    chip = place // 2
 
     def part_start(owner):
-        return pl.multiple_of(jnp.minimum(owner * part_rows, quarter - part_rows), 16)
+        return pl.multiple_of(jnp.minimum(owner * part_rows, most_rows - part_rows), 16)
+
+    def chip_start(owner):
+        return pl.ds(pl.multiple_of(owner * (quarter - most_rows), 16), most_rows)
 
     def rows_grad(distance, out):
         block = place ^ distance
@@ -1480,27 +1556,6 @@
             cols = pl.ds(width // 256 * 256, width % 256)
             out[:, cols] = dot(joined[...], w_ref[cols, :], NT).astype(out.dtype)
 
-    rows_grad(3, core_out)
-    pl.semaphore_wait(barrier, 3 + len(others))
-    to_core = push(core_out, core_in.at[0], beside)
-    loads[1].wait()
-    loads[2].wait()
-    wo_sum[...] = (wo_core[0].astype(F32) + wo_near[...].astype(F32)).astype(BF16)
-    wo_to_ring = [
-        push(wo_sum.at[pl.ds(part_start(other["tensor"]), part_rows)], wo_ring.at[k], other)
-        for k, other in enumerate(others)
-    ]
-    rows_grad(2, hold)
-    to_core.wait_recv()
-
-    @pl.loop(0, row_count // chunk)
-    def _(i):
-        rows = pl.ds(pl.multiple_of(i * chunk, chunk), chunk)
-        chip_out[rows, :] = (hold[rows, :] + core_in[0, rows, :].astype(F32)).astype(BF16)
-
-    to_chip = push(chip_out, chip_in, across)
-
-    loads[0].wait()
     to_far = [None] * 4
 
     def weights(part):
@@ -1569,38 +1624,66 @@
                 push(whole.at[part], near_in.at[part, 1], across),
             ]
 
+    loads[1].wait()
+    loads[2].wait()
+    wo_sum[...] = (wo_core[0].astype(F32) + core_out[:quarter].astype(F32)).astype(BF16)
+    pl.semaphore_wait(barrier, 3 + len(others))
+    wo_to_chip = push(wo_sum.at[chip_start(1 - chip)], wo_half.at[1], across)
+    loads[0].wait()
     weights(3)
-    to_core.wait_send()
-    sent.remove(to_core)
-    rows_grad(1, core_out)
-    to_core_2 = push(core_out, core_in.at[1], beside)
+    weights(0)
+
+    rows_grad(3, core_out)
+    to_core = push(core_out, core_in.at[0], beside)
     left_out[0] = joined_far(3).astype(BF16)
     to_left = push(left_out.at[0], left_in.at[0], beside)
-    weights(0)
+    wo_to_chip.wait_recv()
+    wo_half[0] = (wo_sum[chip_start(chip), :].astype(F32) + wo_half[1].astype(F32)).astype(BF16)
+    wo_to_ring = [
+        push(wo_half.at[0, pl.ds(part_start(other["tensor"]), part_rows)], wo_ring.at[k], other)
+        for k, other in enumerate(others)
+    ]
+    ring(0, joined_far(0))
+    rows_grad(2, hold)
+    to_core.wait_recv()
+
+    @pl.loop(0, row_count // chunk)
+    def _(i):
+        rows = pl.ds(pl.multiple_of(i * chunk, chunk), chunk)
+        chip_out[rows, :] = (hold[rows, :] + core_in[0, rows, :].astype(F32)).astype(BF16)
+
     to_left.wait_recv()
     left_out[1] = (left_out[0].astype(F32) + left_in[0].astype(F32)).astype(BF16)
     to_left = push(left_out.at[1], left_in.at[1], across)
-    ring(0, joined_far(0))
+    to_chip = push(chip_out, chip_in, across)
     weights(1)
-    wo_total = wo_sum[pl.ds(part_start(tensor), part_rows), :].astype(F32)
+    wo_total = wo_half[0, pl.ds(part_start(tensor), part_rows), :].astype(F32)
     for k, copy in enumerate(wo_to_ring):
         copy.wait_recv()
         wo_total = wo_total + wo_ring[k].astype(F32)
-    wo_chip[0] = wo_total.astype(BF16)
-    wo_to_chip = push(wo_chip.at[0], wo_chip.at[1], across)
+    wo_all[tensor] = wo_total.astype(BF16)
+    wo_to_all = [push(wo_all.at[tensor], wo_all.at[tensor], other) for other in others]
+    to_left.wait_recv()
+    ring(3, left_out[1].astype(F32) + left_in[1].astype(F32))
     ring(1, joined_far(1))
     weights(2)
     spread(0)
+    to_core.wait_send()
+    sent[:] = [copy for copy in sent if copy is not to_core]
+    rows_grad(1, core_out)
+    to_core_2 = push(core_out, core_in.at[1], beside)
+    ring(2, joined_far(2))
+    spread(3)
     rows_grad(0, hold)
-    ring(2, joined_far(2))
-    to_left.wait_recv()
-    ring(3, left_out[1].astype(F32) + left_in[1].astype(F32))
+    spread(1)
+    for copy in wo_to_all:
+        copy.wait_recv()
+    for owner in range(tensors):
+        start = min(owner * part_rows, most_rows - part_rows)
+        wo_half[2, start : start + part_rows] = wo_all[owner]
+    wo_to_other = push(wo_half.at[2], wo_half.at[3], across)
+    gather(0)
     to_core_2.wait_recv()
-    wo_to_chip.wait_recv()
-    wo_all[tensor] = (wo_chip[0].astype(F32) + wo_chip[1].astype(F32)).astype(BF16)
-    wo_to_all = [push(wo_all.at[tensor], wo_all.at[tensor], other) for other in others]
-    spread(1)
-    gather(0)
     to_chip.wait_recv()
 
     vec_out[0, :8] = jnp.zeros((8, vec_out.shape[2]), F32)
@@ -1653,7 +1736,6 @@
         vec_out[0, row : row + 1, cols] = sums[part, 0:1, :]
         left = slice(part * HEAD, (part + 1) * HEAD)
         vec_out[0, row : row + 1, width - HEAD : width] = sums[3, 0:1, left]
-    spread(3)
     gather(1)
 
     def forward(part):
@@ -1690,12 +1772,14 @@
     gather(3)
     store(0, passed_0)
     add(2, step)
-    for copy in wo_to_all:
-        copy.wait_recv()
-    for owner in range(tensors - 1):
-        wo_core[0, owner * part_rows : (owner + 1) * part_rows] = wo_all[owner]
-    rest = (tensors - 1) * part_rows
-    wo_core[0, rest:] = wo_all[tensors - 1, tensors * part_rows - quarter :]
+    wo_to_other.wait_recv()
+    for at in range(2):
+
+        @pl.when(chip == at)
+        def _():
+            wo_core[0, :most_rows] = wo_half[2 + at]
+            wo_core[0, most_rows:] = wo_half[3 - at, 2 * most_rows - quarter :]
+
     wo_to_core = push(wo_core.at[0], wo_core.at[1], beside)
     step = exchange(3)
     passed_1 = forward(1)
@@ -1728,10 +1812,11 @@
     padded = vectors.shape[1]
     in_vmem = pl.BlockSpec(memory_space=pltpu.VMEM)
     vmem = lambda *shape, kind=BF16: pltpu.VMEM(shape, kind)
-    copies = 4 + 4 * 2 * (tensors - 1) + 3 + 3 * 3 + 2 + 5 + 2 * (tensors - 1) + 2
+    copies = 4 + 4 * 2 * (tensors - 1) + 3 + 3 * 3 + 2 + 5 + 2 * (tensors - 1) + 3
     given = len(grads) + 8
     quarter = width // 4
-    part_rows = -(-quarter // tensors // 16) * 16
+    most_rows = -(-quarter // 2 // 16) * 16
+    part_rows = -(-most_rows // tensors // 16) * 16
 
     def body(*refs):
         tail_kernel(prompt_rows, *refs[:given], *refs[given + len(after) :])
@@ -1772,9 +1857,8 @@
             vmem(6, 16, padded, kind=F32),
             vmem(5, 16, padded, kind=F32),
             vmem(quarter, width),
-            vmem(quarter, width),
             vmem(tensors - 1, part_rows, width),
-            vmem(2, part_rows, width),
+            vmem(4, most_rows, width),
             vmem(tensors, part_rows, width),
             vmem(2, quarter, width),
             pltpu.SemaphoreType.DMA((7,)),
@@ -1789,60 +1873,6 @@
         ),
         name="tail",
     )(*grads, w_own, normed, rows, grad_hidden, out_keep, out_come, gain[None], vectors, *after)
-
-
-def join_kernel(spot_ref, *refs):
-    firsts, lasts, (keep_o, come_o) = refs[:4], refs[4:8], refs[8:10]
-    out_f, sum_f, out_p, sum_p, out_o, sum_o, total = refs[10:]
-    step = pl.program_id(0)
-    eighth = out_f.shape[2]
-    chip = spot_ref[4] // 2
-    sums_o = (keep_o[...].astype(F32) + come_o[...].astype(F32)).astype(BF16)
-    sum_o[...] = sums_o[0]
-    out_o[...] = sums_o[1]
-    for entries, here in ((firsts, step < 2), (lasts, step >= 2)):
-        keep_f, come_f, keep_p, come_p = entries
-
-        @pl.when(here)
-        def _():
-            for at in range(2):
-                total[...] = keep_f[0, at].astype(F32) + come_f[0, at].astype(F32)
-                for target, away in ((sum_f, 0), (out_f, 1)):
-                    rows = pl.ds(pl.multiple_of((chip ^ away) * eighth, 8), eighth)
-                    target[0, at] = total[rows, :].astype(BF16)
-            for target, at in ((sum_p, 0), (out_p, 1)):
-                target[0] = (keep_p[at, 0].astype(F32) + come_p[at, 0].astype(F32)).astype(BF16)
-
-
-def join(spot, firsts, lasts, outs, after=()):
-    _, _, quarter, hidden = firsts[0].shape
-    specs = []
-    for part in (lambda k: jnp.minimum(k, 1), lambda k: jnp.maximum(k - 2, 0)):
-        by_part = pl.BlockSpec((1, 2, quarter, hidden), lambda k, s, part=part: (part(k), 0, 0, 0))
-        by_far = pl.BlockSpec((2, 1, quarter, hidden), lambda k, s, part=part: (0, part(k), 0, 0))
-        specs += [by_part, by_part, by_far, by_far]
-    eighth = quarter // 2
-    fc = pl.BlockSpec((1, 2, eighth, hidden), lambda k, s: (k, 0, 0, 0))
-    proj = pl.BlockSpec((1, quarter, hidden), lambda k, s: (k, 0, 0))
-    return launch(
-        join_kernel,
-        "join",
-        (spot,),
-        (4,),
-        (*firsts, *lasts, *outs),
-        specs + [blocks(*entry.shape) for entry in outs],
-        [
-            (fc, shape_of(4, 2, eighth, hidden)),
-            (fc, shape_of(4, 2, eighth, hidden)),
-            (proj, shape_of(4, quarter, hidden)),
-            (proj, shape_of(4, quarter, hidden)),
-            whole_out(*outs[0].shape[1:]),
-            whole_out(*outs[0].shape[1:]),
-        ],
-        scratch=[pltpu.VMEM((quarter, hidden), F32)],
-        traffic=30,
-        after=after,
-    )
 
 
 def own_columns(matrix, place):
@@ -1898,7 +1928,7 @@
 
     zero_bias = jnp.zeros_like(qv_bias[0])
     col_bias = own_columns(jnp.concatenate([qv_bias[0], zero_bias, qv_bias[1]])[None], place)[0]
-    normed, q, k, v, kt, vt, w_own, rows_own, grad_layer, grad_flip, *mines, out_full = open_up(
+    normed, q, k, v, kt, vt, w_own, rows_own, grad_layer, grad_flip, *mines, out_own = open_up(
         prompt_in,
         cont_in,
         w_qkv,
@@ -1918,8 +1948,8 @@
 
     labels = cont_seg[0].reshape(count, cont_rows)
     seg_col, seg_row = labels[:, :, None], labels[:, None, :]
-    lse, outs, came, last_out, two_away, one_far, three_far, *others = attend(
-        q, k, vt, seg_col, seg_row, prompt_rows, (mine, near_far, one_away, three_away)
+    lse, outs, came, last_out, two_away, one_far, three_far, *others, out_full = attend(
+        q, k, vt, seg_col, seg_row, prompt_rows, (mine, near_far, one_away, three_away), out_own
     )
     mine_2, near_2, one_2, one_far_2, three_2, three_far_2 = others
     two_far = swap(two_away, "fsdp", 1)
@@ -1928,14 +1958,15 @@
         at, rows_own, out_full, out_bias, ln2_gain, ln2_bias, pieces
     )
 
-    given = (spot, mlp_low, grad_layer, mlp_flip, grad_flip)
+    given = (mlp_low, grad_layer, mlp_flip, grad_flip)
     mlp_out, grad_mlp_in, *grads_first, bias_first = mlp(
+        4,
         *given, (mine, one_away), (near_far, one_far), (mine_2, one_2), (near_2, one_far_2)
     )
     (two_far,) = behind((two_far,), bias_first)
     two_2, two_far_2 = swap(two_away, "ctx", 1), swap(two_far, "ctx", 1)
-    come_first = [swap(grads_first[1], "ctx", 1), swap(grads_first[3], "ctx", 1)]
     mlp_out, grad_mlp_in, *grads_last, bias_last = mlp(
+        5,
         *given,
         (three_away, two_away),
         (three_far, two_far),
@@ -1943,22 +1974,11 @@
         (three_far_2, two_far_2),
         before=(mlp_out, grad_mlp_in),
     )
-    come_last = [swap(grads_last[1], "ctx", 1), swap(grads_last[3], "ctx", 1)]
     grad_fc_bias = jnp.concatenate([bias_first, bias_last], axis=0)
-    prompt_out, cont_out, grad_hidden, *rest = bend(
-        jnp.stack([place, fsdp]),
-        mlp_out,
-        grad_mlp_in,
-        hidden,
-        grad_layer,
-        out_full,
-        ln2_gain,
-        proj_bias,
-        pieces,
-        prompt_rows,
-    )
-    grads_own, (grad_last, out_keep, out_send, sums2) = rest[:count], rest[count:]
-    grads_all = [grads_own[0]] + [swap(grads_own[k], "ctx", k) for k in range(1, count)]
+    layer_out, grad_hidden, grads_own, grad_last, *rest = bend(
+        mlp_out, grad_mlp_in, hidden, grad_layer, out_full, ln2_gain, proj_bias, pieces
+    )
+    grads_all, (out_keep, out_send, sums2) = [grads_own, *rest[:-3]], rest[-3:]
 
     def added(left, right):
         return left.astype(F32) + right.astype(F32)
@@ -1977,24 +1997,24 @@
             pair, tile, heads, at, q, k, v, kt, lse, seg_col, seg_row, grads, outs, prompt_rows, after
         )
 
-    grads_left = back(PAIRS, 0, 1, [grad_last], last_out[None, None])
-    out_f, sum_f, out_p, sum_p, out_o, sum_o = join(
-        spot,
-        (grads_first[0], come_first[0], grads_first[2], come_first[1]),
-        (grads_last[0], come_last[0], grads_last[2], come_last[1]),
-        (out_keep, swap(out_send, "ctx", 1)),
-        (grads_left[0], *grads_all[1:]),
-    )
-    grads_pair = [back(0, 0, 2, grads_all, outs, (out_f, out_p))]
-    come_o = swap(out_o, "fsdp", 1)
-    come_f, come_p = swap(out_f, "ctx", 2), swap(out_p, "fsdp", 1)
-    come_f, come_p = behind((come_f, come_p), grads_pair[0][0])
-    sum_f = added(sum_f, come_f).astype(BF16)
-    sum_p = added(sum_p, come_p).astype(BF16)
-    out_f, sum_f = sum_f[:, 1], sum_f[:, 0]
-    grads_pair.append(back(1, 1, 2, grads_all, outs, (out_f, sum_p, grads_pair[0][0])))
-    (come_f,) = behind((swap(out_f, "fsdp", 1),), grads_pair[1][0])
-    sum_f = added(sum_f, come_f).astype(BF16)
+    come_o = swap(out_send, "ctx", 1)
+    fc_parts, pj_parts = (grads_first[:2], grads_last[:2]), (grads_first[2:], grads_last[2:])
+    fc_come = [swap(send, "ctx", 2) for _, send in fc_parts]
+    pj_come = [swap(send, "fsdp", 1) for _, send in pj_parts]
+    grads_pair = [back(0, 0, 2, grads_all, outs)]
+    grads_left = back(PAIRS, 0, 1, [grad_last], last_out[None, None], (grads_pair[0][0],))
+    come_o, *come = behind((come_o, *fc_come, *pj_come), grads_left[0])
+    near_f = [added(keep[0], part[0]).astype(BF16) for (keep, _), part in zip(fc_parts, come[:2])]
+    far_f = [added(keep[1], part[1]).astype(BF16) for (keep, _), part in zip(fc_parts, come[:2])]
+    sum_p = [added(keep, part) for (keep, _), part in zip(pj_parts, come[2:])]
+    near_f, far_f = jnp.concatenate(near_f), jnp.concatenate(far_f)
+    sum_p = jnp.concatenate(sum_p).astype(BF16)
+    sum_o = added(out_keep, come_o).astype(BF16)
+    sum_o, out_o = sum_o[0], sum_o[1]
+    come_f, come_o = swap(far_f, "fsdp", 1), swap(out_o, "fsdp", 1)
+    grads_pair.append(back(1, 1, 2, grads_all, outs, (far_f, sum_p, out_o, grads_left[0])))
+    (come_f,) = behind((come_f,), grads_pair[1][0])
+    sum_f = added(near_f, come_f).astype(BF16)
     sum_p = over_tensor(sum_p, grads_pair[1][0]).astype(BF16)
     ordered = [entry[part] for part in range(3) for entry in (*grads_pair, grads_left)]
     vectors = jnp.concatenate([sums2, jnp.zeros((tensors, hidden_units), F32)], axis=0)
@@ -2028,8 +2048,8 @@
 
     fc_bias_sum = lax.dynamic_index_in_dim(late, 12 + tensor, 0, False)[:hidden_units]
     return (
-        prompt_out,
-        cont_out,
+        layer_out[:prompt_rows][None],
+        layer_out[prompt_rows:][None],
         prompt_grad,
         cont_grad,
         late[0, :width],

time: 661 us -> 616 us (0.932)
  Pallas kernels: 544 us -> 521 us
  waiting for transfers between devices: 28.3 us -> 7.5 us
    ppermute x18 -> x13, waiting for transfers between devices: 24.9 us -> 7.49 us  [swap(): lax.ppermute(value, axis, [(place, place ^ bit) for place in range(count)])]
    pallas_call x1, Pallas kernels: 80 us -> 67.3 us  [open_up(): pl.pallas_call(open_kernel, in_specs=[ANYWHERE] * 8 + [in_vmem] * 4, out_...]
    pallas_call x1, Pallas kernels: 129 us -> 117 us  [tail(): pl.pallas_call(body, in_specs=[in_vmem] * (len(grads) + 1) + [ANYWHERE] *...]
    pallas_call x1, Pallas kernels: 72.1 us -> 78.7 us  [attend(): pl.pallas_call(functools.partial(attend_kernel, prompt_rows), grid=(PAIRS...]
    unnamed x86 -> x76, local copies, waits for them, and re-layouts: 25.6 us -> 19.5 us
    pallas_call x14 -> x13, Pallas kernels: 263 us -> 258 us  [launch(): pl.pallas_call(body, grid_spec=pltpu.PrefetchScalarGridSpec(num_scalar_pr...]
    ppermute x18 -> x13, starting transfers between devices: 14.6 us -> 10.8 us  [swap(): lax.ppermute(value, axis, [(place, place ^ bit) for place in range(count)])]
  transfers between devices with their start and end apart: 24 -> 19, of which waited for: 7 -> 1; matrix products, arithmetic and copies ran while one was open for 3% -> 5% of each run, Pallas kernels for 57% -> 61%
where the time goes in v4:
time: 616 us; the launch traced here: 612 us
  Pallas kernels  521 us (85%)
  local copies, waits for them, and re-layouts  39 us (6%)
  other arithmetic  23.4 us (4%)
  starting transfers between devices  19.5 us (3%)
  waiting for transfers between devices  7.5 us (1%)
    pallas_call x13, Pallas kernels, launch(): pl.pallas_call(body, grid_spec=pltpu.PrefetchScalarGridSpec(num_scalar_pr...  258 us
    pallas_call x1, Pallas kernels, tail(): pl.pallas_call(body, in_specs=[in_vmem] * (len(grads) + 1) + [ANYWHERE] *...  117 us
    pallas_call x1, Pallas kernels, attend(): pl.pallas_call(functools.partial(attend_kernel, prompt_rows), grid=(PAIRS...  78.7 us
    pallas_call x1, Pallas kernels, open_up(): pl.pallas_call(open_kernel, in_specs=[ANYWHERE] * 8 + [in_vmem] * 4, out_...  67.3 us
    unnamed x76, local copies, waits for them, and re-layouts  19.5 us
  transfers between devices with their start and end apart: 19, of which 1 were waited for; matrix products, arithmetic and copies ran while one was open for 5% of the time, Pallas kernels for 61%

profile of v4, /device:TPU:0, one launch (start us, length us, event | category | flops | bytes accessed | tf_op | source)
XLA Modules:
  0.0 611.9 jit_solution(36245626359948276)
XLA Ops:
  1.7 1.7 broadcast_in_dim.58.refs_9_
  3.4 1.7 broadcast_in_dim.59.refs_10_
  5.8 1.5 broadcast_in_dim_reshape_squeeze.8.seg_col_ref.refs_6_
  8.1 67.3 %open.1 = (bf16[4,1104,896]{2,1,0:T(8,128)(2,1)}, bf16[3,4,896,128]{3,2,1,0:T(8,128)(2,1)}, bf16[3,4,896,128]{3,2,1,0:T(8,128)(2,1)}, bf16[3,4,896,128]{3,2,1,0:...) custom-call(bf16[1088,512]{1,0:T(8,128)(2,1)} %bitcast.78, ...), custom_call_target="tpu_custom_call" | custom-call | flops 8984199168 | bytes 41943040 | tf_op jit(solution)/shard_map/open/pallas_call | solution.py:606
  75.5 78.7 %attend.1 = (f32[3,4,2,896]{3,2,1,0:T(2,128)}, bf16[2,4,896,128]{3,2,1,0:T(8,128)(2,1)}, bf16[2,3,896,128]{3,2,1,0:T(8,128)(2,1)}, bf16[896,128]{1,0:T(8,128)(2,...) custom-call(bf16[3,4,896,128]{3,2,1,0:T(8,128)(2,1)} %get-tuple-elem, ...), custom_call_target="tpu_custom_call", output_to_operand_aliasing={{13}: (9, {})} | custom-call | flops 16106127360 | bytes 20971520 | tf_op jit(solution)/shard_map/attend/pallas_call | solution.py:845
  155.0 1.5 copy-done
  156.5 1.3 copy-done.1
  158.8 9.6 %merge.1 = (f32[896,1088]{1,0:T(8,128)}, bf16[896,1088]{1,0:T(8,128)(2,1)}, bf16[1088,896]{1,0:T(8,128)(2,1)S(1)}) custom-call(s32[1]{0:T(128)} %bitcast.refs_0_, bf16[896,1088]{1,0:T(8,128)(2,1)} %get-tuple-element.97.refs_1_.refs_11_, bf16[1088,1088]{1,0:T(8,128)(2,1)} %get-tuple-element.106.refs_2_.refs_4_, f32[1,1088]{1,0:T(1,128)S(1)} %broadcast_in_dim.50.refs_3_, ...), custom_call_target="tpu_custom_call" | custom-call | flops 424253856 | bytes 3355443 | tf_op jit(solution)/shard_map/merge/pallas_call | solution.py:314
  168.4 1.3 copy-done.6
  169.7 58.3 %mlp.2 = (f32[896,1088]{1,0:T(8,128)}, f32[896,1088]{1,0:T(8,128)}, bf16[2,2,136,1088]{3,2,1,0:T(8,128)(2,1)}, bf16[2,2,136,1088]{3,2,1,0:T(8,128)(2,1)}, bf16[2...) custom-call(bf16[896,1088]{1,0:T(8,128)(2,1)} %get-tuple-element.110.refs_0_, ...), custom_call_target="tpu_custom_call" | custom-call | flops 5091046400 | bytes 8388608 | tf_op jit(solution)/shard_map/mlp/pallas_call | solution.py:314
  229.1 1.8 collective-permute-start.4
  230.9 1.5 collective-permute-start.6
  233.0 1.1 copy-done.18
  234.1 60.8 %mlp.3 = (f32[896,1088]{1,0:T(8,128)}, f32[896,1088]{1,0:T(8,128)}, bf16[2,2,136,1088]{3,2,1,0:T(8,128)(2,1)}, bf16[2,2,136,1088]{3,2,1,0:T(8,128)(2,1)}, bf16[2...) custom-call(bf16[896,1088]{1,0:T(8,128)(2,1)} %get-tuple-element.110.refs_0_, ...), custom_call_target="tpu_custom_call" | custom-call | flops 5091046400 | bytes 8388608 | tf_op jit(solution)/shard_map/mlp/pallas_call | solution.py:314
  294.9 28.0 %bend.1 = (bf16[896,1088]{1,0:T(8,128)(2,1)}, f32[896,1088]{1,0:T(8,128)}, bf16[896,256]{1,0:T(8,128)(2,1)}, bf16[896,128]{1,0:T(8,128)(2,1)}, bf16[896,256]{1,0...) custom-call(f32[896,1088]{1,0:T(8,128)} %get-tuple-element.126.refs_, ...), custom_call_target="tpu_custom_call" | custom-call | flops 848507712 | bytes 6291456 | tf_op jit(solution)/shard_map/bend/pallas_call | solution.py:314
  323.8 1.2 collective-permute-start.7
  327.4 46.3 %attend_back.3 = (bf16[1,4,896,128]{3,2,1,0:T(8,128)(2,1)}, bf16[1,4,896,128]{3,2,1,0:T(8,128)(2,1)}, bf16[1,4,896,128]{3,2,1,0:T(8,128)(2,1)}) custom-call(s32[1]{0:T(128)} %bitcast.refs_0_, bf16[3,4,896,128]{3,2,1,0:T(8,128)(2,1)} %get-tuple-element.98.q_ref.refs_1_, bf16[3,4,896,128]{3,2,1,0:T(8,128)(2,1)} %get-tuple-element.99.k_ref.refs_2_, ...), custom_call_target="tpu_custom_call" | custom-call | flops 2684354560 | bytes 3355443 | tf_op jit(solution)/shard_map/attend_back/pallas_call | solution.py:314
  373.7 9.2 %attend_back.4 = (bf16[1,4,896,128]{3,2,1,0:T(8,128)(2,1)}, bf16[1,4,896,128]{3,2,1,0:T(8,128)(2,1)}, bf16[1,4,896,128]{3,2,1,0:T(8,128)(2,1)}) custom-call(s32[1]{0:T(128)} %bitcast.refs_0_, bf16[3,4,896,128]{3,2,1,0:T(8,128)(2,1)} %get-tuple-element.98.q_ref.refs_1_, bf16[3,4,896,128]{3,2,1,0:T(8,128)(2,1)} %get-tuple-element.99.k_ref.refs_2_, ...), custom_call_target="tpu_custom_call" | custom-call | flops 335544320 | bytes 3355443 | tf_op jit(solution)/shard_map/attend_back/pallas_call | solution.py:314
  382.9 1.2 copy-done.3
  384.1 1.3 copy-done.20
  385.4 1.6 add_convert_fusion.3
  387.9 1.8 collective-permute-start.10
  389.7 1.6 add_convert_fusion.2
  391.3 1.1 slice_bitcast_fusion.4
  392.8 1.8 collective-permute-start.12
  394.6 2.5 fusion.5
  397.1 1.1 fusion.6
  401.7 1.7 pad_maximum_fusion.refs_17_
  403.5 45.9 %attend_back.5 = (bf16[1,4,896,128]{3,2,1,0:T(8,128)(2,1)}, bf16[1,4,896,128]{3,2,1,0:T(8,128)(2,1)}, bf16[1,4,896,128]{3,2,1,0:T(8,128)(2,1)}) custom-call(s32[1]{0:T(128)} %bitcast.refs_0_, bf16[3,4,896,128]{3,2,1,0:T(8,128)(2,1)} %get-tuple-element.98.q_ref.refs_1_, bf16[3,4,896,128]{3,2,1,0:T(8,128)(2,1)} %get-tuple-element.99.k_ref.refs_2_, ...), custom_call_target="tpu_custom_call" | custom-call | flops 2684354560 | bytes 3355443 | tf_op jit(solution)/shard_map/attend_back/pallas_call | solution.py:314
  449.4 1.2 copy-done.4
  450.6 1.2 fusion.2.refs_18_
  451.8 2.6 collective-permute-start.17
  455.8 2.4 collective-permute-start.13
  458.9 1.5 collective-permute-start.15
  461.3 116.8 %tail.1 = (bf16[1,512,1088]{2,1,0:T(8,128)(2,1)}, bf16[1,384,1088]{2,1,0:T(8,128)(2,1)}, bf16[544,3264]{1,0:T(8,128)(2,1)}, bf16[544,1088]{1,0:T(8,128)(2,1)}, f32[16,1152]{1,0:T(8,128)}) custom-call(bf16[1,4,896,128]{3,2,1,0:T(8,128)(2,1)} %get-tuple-element.137.refs_10_.refs_0_, bf16[1,4,896,128]{3,2,1,0:T(8,128)(2,1)} %get-tuple-element.155.refs_0_.refs_1_, ...), custom_call_target="tpu_custom_call" | custom-call | flops 17968398336 | bytes 31457280 | tf_op jit(solution)/shard_map/tail/pallas_call | solution.py:1824
  579.1 1.1 fusion.10
  580.8 1.2 fusion.7
  582.0 7.5 %collective-permute-done.16 = bf16[136,1088]{1,0:T(8,128)(2,1)S(1)} collective-permute-done((bf16[136,1088]{1,0:T(8,128)(2,1)S(1)}, bf16[136,1088]{1,0:T(8,128)(2,1)S(1)}, u32[]{:S(2)}, u32[]{:S(2)}) %collective-permute-start.16) | collective-permute-done | bytes 295968 | tf_op jit(solution)/shard_map/ppermute | solution.py:276
  589.7 1.2 pad_maximum_fusion.2
  591.8 1.4 copy.58
  593.2 1.2 slice_bitcast_fusion.3
  594.4 1.3 copy.59
  596.3 5.7 convert_element_type.175
  602.0 1.6 convert_element_type.176
  603.7 1.4 copy.60
  605.0 1.3 copy.61
  607.0 1.6 broadcast_select_fusion.1
  609.0 2.6 slice_bitcast_fusion
  (137 shorter events, 21.2 us)
Async XLA Ops:
  0.6 4.5 copy-start.30
  0.7 5.1 copy-start.27
  75.4 79.5 %copy-start.31 = (f32[1088]{0:T(1024)S(1)}, f32[1088]{0:T(1024)}, u32[]{:S(2)}) copy-start(f32[1088]{0:T(1024)} %param.26) | copy-start | bytes 13060
  75.5 79.5 %copy-start.32 = (f32[1088]{0:T(1024)S(1)}, f32[1088]{0:T(1024)}, u32[]{:S(2)}) copy-start(f32[1088]{0:T(1024)} %param.25) | copy-start | bytes 13060
  75.5 79.5 %copy-start.33 = (f32[1088]{0:T(1024)S(1)}, f32[1088]{0:T(1024)}, u32[]{:S(2)}) copy-start(f32[1088]{0:T(1024)} %param.27) | copy-start | bytes 13060
  154.2 73.8 %collective-permute-start = (bf16[560,1088]{1,0:T(8,128)(2,1)}, bf16[560,1088]{1,0:T(8,128)(2,1)S(1)}, u32[]{:S(2)}, u32[]{:S(2)}) collective-permute-start(bf16[560,1088]{1,0:T(8,128)(2,1)} %get-tuple-element.114.refs_5_), channel_id=1, source_target_pairs={{0,16},{16,0},{1,17},{17,1},{2,18},{18,2},{3,19},{19,3},{4,20},{20... | collective-permute-start | bytes 3655688 | tf_op jit(solution)/shard_map/ppermute | solution.py:276
  154.8 78.2 %collective-permute-start.1 = (bf16[560,1088]{1,0:T(8,128)(2,1)}, bf16[560,1088]{1,0:T(8,128)(2,1)}, u32[]{:S(2)}, u32[]{:S(2)}) collective-permute-start(bf16[560,1088]{1,0:T(8,128)(2,1)} %get-tuple-element.114.refs_5_), channel_id=1, source_target_pairs={{0,4},{4,0},{8,12},{12,8},{1,5},{5,1},{9,13},{13,9},{2,6},{6,2},{1... | collective-permute-start | bytes 3655688 | tf_op jit(solution)/shard_map/ppermute | solution.py:276
  155.0 13.5 %copy-start.9 = (f32[1,1088]{1,0:T(1,128)}, f32[1,1088]{1,0:T(1,128)S(1)}, u32[]{:S(2)}) copy-start(f32[1,1088]{1,0:T(1,128)S(1)} %broadcast_in_dim.51.refs_4_.refs_5_) | copy-start | bytes 13060
  155.0 1.5 copy-start
  156.5 1.3 copy-start.1
  168.4 1.3 copy-start.6
  228.7 3.7 copy-start.34
  228.7 5.3 copy-start.2
  228.7 4.3 collective-permute-start.2
  229.1 153.8 %collective-permute-start.4 = (bf16[2,2,136,1088]{3,2,1,0:T(8,128)(2,1)}, bf16[2,2,136,1088]{3,2,1,0:T(8,128)(2,1)}, u32[]{:S(2)}, u32[]{:S(2)}) collective-permute-start(bf16[2,2,136,1088]{3,2,1,0:T(8,128)(2,1)} %get-tuple-element.142), channel_id=1, source_target_pairs={{0,8},{4,12},{8,0},{12,4},{1,9},{5,13},{9,1},{13,5},{2,10},{6,14},... | collective-permute-start | bytes 3551240 | tf_op jit(solution)/shard_map/ppermute | solution.py:276
  230.9 152.0 %collective-permute-start.6 = (bf16[2,272,1088]{2,1,0:T(8,128)(2,1)}, bf16[2,272,1088]{2,1,0:T(8,128)(2,1)}, u32[]{:S(2)}, u32[]{:S(2)}) collective-permute-start(bf16[2,272,1088]{2,1,0:T(8,128)(2,1)} %get-tuple-element.144), channel_id=1, source_target_pairs={{0,16},{16,0},{1,17},{17,1},{2,18},{18,2},{3,19},{19,3},{4,20},{20... | collective-permute-start | bytes 3551240 | tf_op jit(solution)/shard_map/ppermute | solution.py:276
  294.9 30.1 %copy-start.28 = (f32[1088]{0:T(1024)S(1)}, f32[1088]{0:T(1024)}, u32[]{:S(2)}) copy-start(f32[1088]{0:T(1024)} %param.20) | copy-start | bytes 13060
  294.9 30.7 %copy-start.11 = (f32[2,1,1088]{2,1,0:T(1,128)S(1)}, f32[2,1,1088]{2,1,0:T(1,128)}, u32[]{:S(2)}) copy-start(f32[2,1,1088]{2,1,0:T(1,128)} %get-tuple-element.121.refs_0_) | copy-start | bytes 26116
  294.9 31.7 %copy-start.29 = (f32[2,1,1088]{2,1,0:T(1,128)S(1)}, f32[2,1,1088]{2,1,0:T(1,128)}, u32[]{:S(2)}) copy-start(f32[2,1,1088]{2,1,0:T(1,128)} %get-tuple-element.166) | copy-start | bytes 26116
  322.9 60.0 %collective-permute-start.3 = (bf16[2,272,1088]{2,1,0:T(8,128)(2,1)}, bf16[2,272,1088]{2,1,0:T(8,128)(2,1)S(1)}, u32[]{:S(2)}, u32[]{:S(2)}) collective-permute-start(bf16[2,272,1088]{2,1,0:T(8,128)(2,1)} %get-tuple-element.141), channel_id=1, source_target_pairs={{0,4},{4,0},{8,12},{12,8},{1,5},{5,1},{9,13},{13,9},{2,6},{6,2},{1... | collective-permute-start | bytes 3551240 | tf_op jit(solution)/shard_map/ppermute | solution.py:276
  323.1 59.8 %collective-permute-start.5 = (bf16[2,2,136,1088]{3,2,1,0:T(8,128)(2,1)}, bf16[2,2,136,1088]{3,2,1,0:T(8,128)(2,1)S(1)}, u32[]{:S(2)}, u32[]{:S(2)}) collective-permute-start(bf16[2,2,136,1088]{3,2,1,0:T(8,128)(2,1)} %get-tuple-element.143), channel_id=1, source_target_pairs={{0,8},{4,12},{8,0},{12,4},{1,9},{5,13},{9,1},{13,5},{2,10},{6,14},... | collective-permute-start | bytes 3551240 | tf_op jit(solution)/shard_map/ppermute | solution.py:276
  323.8 59.1 %collective-permute-start.7 = (bf16[2,272,1088]{2,1,0:T(8,128)(2,1)}, bf16[2,272,1088]{2,1,0:T(8,128)(2,1)}, u32[]{:S(2)}, u32[]{:S(2)}) collective-permute-start(bf16[2,272,1088]{2,1,0:T(8,128)(2,1)} %get-tuple-element.145), channel_id=1, source_target_pairs={{0,16},{16,0},{1,17},{17,1},{2,18},{18,2},{3,19},{19,3},{4,20},{20... | collective-permute-start | bytes 3551240 | tf_op jit(solution)/shard_map/ppermute | solution.py:276
  384.1 1.3 copy-start.20
  387.0 2.7 copy-start.23
  387.9 61.5 %collective-permute-start.10 = (bf16[272,1088]{1,0:T(8,128)(2,1)}, bf16[272,1088]{1,0:T(8,128)(2,1)S(1)}, u32[]{:S(2)}, u32[]{:S(2)}) collective-permute-start(bf16[272,1088]{1,0:T(8,128)(2,1)} %slice_bitcast_fusion.6), channel_id=1, source_target_pairs={{0,3},{1,0},{2,1},{3,2},{4,7},{5,4},{6,5},{7,6},{8,11},{9,8},{10,9... | collective-permute-start | bytes 1775624 | tf_op jit(solution)/shard_map/ppermute | solution.py:281
  391.3 3.3 copy-start.19
  392.4 57.0 %collective-permute-start.11 = (bf16[272,1088]{1,0:T(8,128)(2,1)}, bf16[272,1088]{1,0:T(8,128)(2,1)S(1)}, u32[]{:S(2)}, u32[]{:S(2)}) collective-permute-start(bf16[272,1088]{1,0:T(8,128)(2,1)} %get-tuple-element.231), channel_id=1, source_target_pairs={{0,1},{1,2},{2,3},{3,0},{4,5},{5,6},{6,7},{7,4},{8,9},{9,10},{10,1... | collective-permute-start | bytes 1775624 | tf_op jit(solution)/shard_map/ppermute | solution.py:281
  392.8 56.6 %collective-permute-start.12 = (bf16[272,1088]{1,0:T(8,128)(2,1)}, bf16[272,1088]{1,0:T(8,128)(2,1)S(1)}, u32[]{:S(2)}, u32[]{:S(2)}) collective-permute-start(bf16[272,1088]{1,0:T(8,128)(2,1)} %get-tuple-element.230), channel_id=1, source_target_pairs={{0,2},{1,3},{2,0},{3,1},{4,6},{5,7},{6,4},{7,5},{8,10},{9,11},{10,... | collective-permute-start | bytes 1775624 | tf_op jit(solution)/shard_map/ppermute | solution.py:281
  394.6 2.5 copy-start.21
  398.2 1.8 copy-start.22
  398.4 1.9 copy-start.13
  398.4 56.0 %collective-permute-start.9 = (bf16[4,136,1088]{2,1,0:T(8,128)(2,1)S(1)}, bf16[4,136,1088]{2,1,0:T(8,128)(2,1)S(1)}, u32[]{:S(2)}, u32[]{:S(2)}) collective-permute-start(bf16[4,136,1088]{2,1,0:T(8,128)(2,1)S(1)} %pad_maximum_fusion.1.refs_16_), channel_id=1, source_target_pairs={{0,16},{16,0},{1,17},{17,1},{2,18},{18,2},{3,19},{19,3},{4,20},{20... | collective-permute-start | bytes 3551240 | tf_op jit(solution)/shard_map/ppermute | solution.py:276
  401.2 2.3 copy-start.16
  401.2 59.3 %collective-permute-start.8 = (bf16[272,1088]{1,0:T(8,128)(2,1)S(1)}, bf16[272,1088]{1,0:T(8,128)(2,1)S(1)}, u32[]{:S(2)}, u32[]{:S(2)}) collective-permute-start(bf16[272,1088]{1,0:T(8,128)(2,1)S(1)} %get-tuple-element.233.refs_18_), channel_id=1, source_target_pairs={{0,16},{16,0},{1,17},{17,1},{2,18},{18,2},{3,19},{19,3},{4,20},{20... | collective-permute-start | bytes 1775624 | tf_op jit(solution)/shard_map/ppermute | solution.py:276
  451.8 2.6 copy-start.14
  451.8 2.6 copy-start.15
  451.8 126.4 %collective-permute-start.17 = (bf16[272,1088]{1,0:T(8,128)(2,1)}, bf16[272,1088]{1,0:T(8,128)(2,1)S(1)}, u32[]{:S(2)}, u32[]{:S(2)}) collective-permute-start(bf16[272,1088]{1,0:T(8,128)(2,1)} %fusion.2.refs_18_), channel_id=1, source_target_pairs={{0,8},{4,12},{8,0},{12,4},{1,9},{5,13},{9,1},{13,5},{2,10},{6,14},... | collective-permute-start | bytes 1775624 | tf_op jit(solution)/shard_map/ppermute | solution.py:276
  454.7 4.2 copy-start.12
  455.8 123.3 %collective-permute-start.13 = (bf16[136,1088]{1,0:T(8,128)(2,1)}, bf16[136,1088]{1,0:T(8,128)(2,1)S(1)}, u32[]{:S(2)}, u32[]{:S(2)}) collective-permute-start(bf16[136,1088]{1,0:T(8,128)(2,1)} %get-tuple-element.229), channel_id=1, source_target_pairs={{0,3},{1,0},{2,1},{3,2},{4,7},{5,4},{6,5},{7,6},{8,11},{9,8},{10,9... | collective-permute-start | bytes 887816 | tf_op jit(solution)/shard_map/ppermute | solution.py:281
  458.2 120.9 %collective-permute-start.14 = (bf16[136,1088]{1,0:T(8,128)(2,1)}, bf16[136,1088]{1,0:T(8,128)(2,1)S(1)}, u32[]{:S(2)}, u32[]{:S(2)}) collective-permute-start(bf16[136,1088]{1,0:T(8,128)(2,1)} %get-tuple-element.228), channel_id=1, source_target_pairs={{0,1},{1,2},{2,3},{3,0},{4,5},{5,6},{6,7},{7,4},{8,9},{9,10},{10,1... | collective-permute-start | bytes 887816 | tf_op jit(solution)/shard_map/ppermute | solution.py:281
  458.9 120.1 %collective-permute-start.15 = (bf16[136,1088]{1,0:T(8,128)(2,1)S(1)}, bf16[136,1088]{1,0:T(8,128)(2,1)S(1)}, u32[]{:S(2)}, u32[]{:S(2)}) collective-permute-start(bf16[136,1088]{1,0:T(8,128)(2,1)S(1)} %get-tuple-element.227), channel_id=1, source_target_pairs={{0,2},{1,3},{2,0},{3,1},{4,6},{5,7},{6,4},{7,5},{8,10},{9,11},{10,... | collective-permute-start | bytes 887816 | tf_op jit(solution)/shard_map/ppermute | solution.py:281
  580.2 9.3 %collective-permute-start.16 = (bf16[136,1088]{1,0:T(8,128)(2,1)S(1)}, bf16[136,1088]{1,0:T(8,128)(2,1)S(1)}, u32[]{:S(2)}, u32[]{:S(2)}) collective-permute-start(bf16[136,1088]{1,0:T(8,128)(2,1)S(1)} %fusion.10), channel_id=1, source_target_pairs={{0,8},{4,12},{8,0},{12,4},{1,9},{5,13},{9,1},{13,5},{2,10},{6,14},... | collective-permute-start | bytes 887816 | tf_op jit(solution)/shard_map/ppermute | solution.py:276
  589.7 2.0 copy-start.17
  590.9 16.2 %collective-permute-start.18 = (bf16[2,272,1088]{2,1,0:T(8,128)(2,1)}, bf16[2,272,1088]{2,1,0:T(8,128)(2,1)}, u32[]{:S(2)}, u32[]{:S(2)}) collective-permute-start(bf16[2,272,1088]{2,1,0:T(8,128)(2,1)} %pad_maximum_fusion.2), channel_id=1, source_target_pairs={{0,4},{4,0},{8,12},{12,8},{1,5},{5,1},{9,13},{13,9},{2,6},{6,2},{1... | collective-permute-start | bytes 3551240 | tf_op jit(solution)/shard_map/ppermute | solution.py:276
  594.4 1.3 copy-start.8
  596.3 5.7 copy-start.24
  602.0 1.7 copy-start.25
  603.6 1.4 copy-start.26
  (7 other events, 6.8 us)

commit v5 on v4

--- a/solution.py
+++ b/solution.py
@@ -335,9 +335,9 @@
     return (out[: len(outs)], *out[len(outs) :]) if carry else out
 
 
-def behind(arrays, token):
+def behind(arrays, *tokens):
     out = launch(
-        lambda *refs: None, "behind", (), (1,), (), (), (), after=(token,), carry=tuple(arrays)
+        lambda *refs: None, "behind", (), (1,), (), (), (), after=tokens, carry=tuple(arrays)
     )
     return out[1:]
 
@@ -508,6 +508,8 @@
     turn_rows(rows_t.at[0], turned.at[1])
     put(turned.at[1], rows_ref)
 
+    gain_col = jnp.broadcast_to(gain_ref[...], (8, width)).T[:, :1]
+    bias_col = jnp.broadcast_to(bias_ref[...], (8, width)).T[:, :1]
     extra = norms.shape[1] - width
     at_row = lax.broadcasted_iota(jnp.int32, (extra, row_count), 0)
     ones = jnp.where(at_row == 0, 1.0, 0.0).astype(BF16)
@@ -520,7 +522,7 @@
             average = jnp.mean(values, axis=0, keepdims=True)
             centred = values - average
             variance = jnp.mean(centred * centred, axis=0, keepdims=True)
-            low = centred * lax.rsqrt(variance + 1e-05) * gain_ref[...] + bias_ref[...]
+            low = centred * lax.rsqrt(variance + 1e-05) * gain_col + bias_col
             low = low.astype(BF16)
             norms[slot, :width, rows] = low
             normed[rows, :] = low.T
@@ -646,8 +648,8 @@
         prompt_cot[0].T,
         cont_cot[0].T,
         fc_bias[None],
-        gain[:, None],
-        bias[:, None],
+        gain[None],
+        bias[None],
         col_bias[None],
     )
 
@@ -660,8 +662,8 @@
 
 def attend_kernel(prompt_rows, q_ref, k_ref, vt_ref, seg_col_ref, seg_row_ref, *refs):
     mine_ref, near_ref, one_ref, three_ref = refs[:4]
-    lse_ref, outs_ref, pieces_ref, last_ref, two_ref, one_far_ref, three_far_ref = refs[5:12]
-    beside_refs, out_ref, (acc, o_s, send_sem, recv_sem, out_sem) = refs[12:18], refs[18], refs[19:]
+    lse_ref, outs_ref, pieces_ref, last_ref, two_ref, one_far_ref = refs[5:11]
+    beside_refs, out_ref, (acc, o_s, send_sem, recv_sem, out_sem) = refs[11:17], refs[17], refs[18:]
     step = pl.program_id(0)
     place = lax.axis_index("ctx")
     fsdp = lax.axis_index("fsdp")
@@ -686,7 +688,7 @@
             device_id_type=pl.DeviceIdType.MESH,
         )
 
-    b_mine, b_near, b_one, b_one_far, b_three, b_three_far = beside_refs
+    b_mine, b_near, b_one, b_one_far, b_three, b_two = beside_refs
     returns = {}
     for pair in range(PAIRS):
         for away in range(1, count):
@@ -709,13 +711,12 @@
         copy_to(base + 3, near_ref, b_near, beside),
         copy_to(base + 4, one_ref, b_one, beside),
         copy_to(base + 5, three_ref, b_three, beside),
-        copy_to(base + 6, three_ref, three_far_ref, far),
-        copy_to(base + 9, out_rows(0), out_rows(0), far),
+        copy_to(base + 6, out_rows(0), out_rows(0), far),
     ]
     late = [
         copy_to(base + 7, one_far_ref, b_one_far, beside),
-        copy_to(base + 8, three_far_ref, b_three_far, beside),
-        copy_to(base + 10, out_rows(1), out_rows(1), beside),
+        copy_to(base + 8, out_rows(1), out_rows(1), beside),
+        copy_to(base + 9, two_ref, b_two, beside),
     ]
 
     @pl.when(step == 0)
@@ -728,7 +729,7 @@
                 barrier, inc=1, device_id=partner, device_id_type=pl.DeviceIdType.MESH
             )
         pl.semaphore_wait(barrier, len(partners))
-        for copy in early[:1] + early[7:] + early[1:7]:
+        for copy in early:
             copy.start()
 
     @pl.when(step == per_pair + 2)
@@ -738,13 +739,13 @@
 
     @pl.when(step == per_pair + 5)
     def _():
-        early[7].wait_recv()
-        late[2].start()
-
-    @pl.when(step == steps + 1)
-    def _():
         early[6].wait_recv()
         late[1].start()
+
+    @pl.when(step == per_pair + 7)
+    def _():
+        early[1].wait_recv()
+        late[2].start()
 
     def part(queries, at, start, size, mask, states):
         keys = k_ref[0, at, pl.ds(start, size), :]
@@ -820,7 +821,7 @@
         ]
         for store in stores:
             store.start()
-        for copy in early[1:6] + late + list(returns.values()):
+        for copy in early[2:6] + late + list(returns.values()):
             copy.wait_recv()
         for copy in early + late + list(returns.values()):
             copy.wait_send()
@@ -834,13 +835,13 @@
     pair = lambda i: (jnp.minimum(i // (2 * count), PAIRS), 0, 0, 0)
     pairs = groups * count * (prompt_rows + 2 * cont_rows) * prompt_rows * count // 2
     mine = weights[0].shape
-    copies = PAIRS * (count - 1) + 11
+    copies = PAIRS * (count - 1) + 10
     outs = [
         (pl.BlockSpec((1, count, 2, row_count), pair), shape_of(groups, count, 2, row_count, kind=F32)),
         (ANYWHERE, shape_of(PAIRS, count, row_count, TILE)),
         (ANYWHERE, shape_of(PAIRS, count - 1, row_count, TILE)),
         (ANYWHERE, shape_of(row_count, TILE)),
-    ] + [(ANYWHERE, shape_of(*mine))] * 9
+    ] + [(ANYWHERE, shape_of(*mine))] * 8
     outs.append((ANYWHERE, shape_of(*w_out.shape)))
     return pl.pallas_call(
         functools.partial(attend_kernel, prompt_rows),
@@ -1190,7 +1191,7 @@
                 copy.wait_send()
 
 
-def bend(mlp_out, gm, hidden, g, w_out, gain, proj_bias, pieces):
+def bend(mlp_out, gm, hidden, g, w_out, gain, proj_bias, pieces, after):
     row_count, width = hidden.shape
     size = row_count // 4
     places = pieces[0].shape[1]
@@ -1227,6 +1228,7 @@
         limit=56,
         flops=4 * row_count * width * width,
         traffic=30,
+        after=after,
         meet=6,
     )
 
@@ -1254,9 +1256,10 @@
     own, far, own_2, far_2 = (refs[i * parts : (i + 1) * parts] for i in range(4))
     before_refs = refs[4 * parts : 4 * parts + 2]
     refs = refs[4 * parts + (0 if first else 2) :]
-    out_ref, gm_ref, keep_f, send_f, keep_p, send_p, gb_ref = refs[:7]
-    wf_s, wp_s, bias_s, biases, act_s, gp_s, wide, keep_s, send_s, come_s, total = refs[7:18]
-    sems, send_sem, recv_sem = refs[18:]
+    out_ref, gm_ref, keep_f, send_f, gb_ref = refs[:5]
+    sums_p, refs = refs[5 : 5 + parts], refs[5 + parts :]
+    wf_s, wp_s, bias_s, biases, act_s, gp_s, wide, keep_s, send_s, come_s, total = refs[:11]
+    sems, send_sem, recv_sem = refs[11:]
     step = pl.program_id(0)
     place, fsdp = lax.axis_index("ctx"), lax.axis_index("fsdp")
     core, chip = place % 2, place // 2
@@ -1387,9 +1390,10 @@
                 for to, away in ((keep_f, 0), (send_f, 1)):
                     eighth = quarter // 2
                     rows = pl.ds(pl.multiple_of((chip ^ away) * eighth, 8), eighth)
-                    to[far, 0] = total[rows, :].astype(BF16)
-            for far, to in enumerate((keep_p, send_p)):
-                to[0] = (keep_s[1, far].astype(F32) + come_s[part, 1, far].astype(F32)).astype(BF16)
+                    to[0, far] = total[rows, :].astype(BF16)
+                sums_p[part][far] = (
+                    keep_s[1, far].astype(F32) + come_s[part, 1, far].astype(F32)
+                ).astype(BF16)
             if part == parts - 1:
                 exchange(part).wait_send()
 
@@ -1400,11 +1404,10 @@
     parts, quarter = len(own), width // 4
     once = pl.Buffered(buffer_count=1)
     whole = lambda *shape: pl.BlockSpec(shape, lambda k: (0,) * len(shape), pipeline_mode=once)
-    by_far = pl.BlockSpec((2, 1, quarter // 2, hidden), lambda k: (0, k, 0, 0))
-    by_part = pl.BlockSpec((1, quarter, hidden), lambda k: (k, 0, 0))
+    by_half = pl.BlockSpec((1, 2, quarter // 2, hidden), lambda k: (k, 0, 0, 0))
     total = (whole(rows, width), shape_of(rows, width, kind=F32))
-    by_far = (by_far, shape_of(2, parts, quarter // 2, hidden))
-    by_part = (by_part, shape_of(parts, quarter, hidden))
+    by_half = (by_half, shape_of(parts, 2, quarter // 2, hidden))
+    by_part = (whole(2, quarter, hidden), shape_of(2, quarter, hidden))
     return launch(
         functools.partial(mlp_kernel, parts, not before),
         "mlp",
@@ -1422,15 +1425,14 @@
         [
             total,
             total,
-            by_far,
-            by_far,
-            by_part,
-            by_part,
+            by_half,
+            by_half,
             (
                 pl.BlockSpec((1, 1, hidden), lambda k: (k, 0, 0)),
                 shape_of(parts, 1, hidden, kind=F32),
             ),
-        ],
+        ]
+        + [by_part] * parts,
         scratch=[
             pltpu.VMEM((2, width, hidden), BF16),
             pltpu.VMEM((2, width, hidden), BF16),
@@ -1754,24 +1756,35 @@
                     start = part * width + block * own
                     qkv_ref[:, start : start + own] = source[...]
 
-    partners = (beside, across, far, {"tensor": tensor ^ 1}, {"tensor": tensor ^ 2})
+    levels = (
+        (place, [(place ^ away, {"ctx": place ^ away}) for away in range(1, count)]),
+        (tensor, [(other["tensor"], other) for other in others]),
+        (fsdp, [(1 - fsdp, far)]),
+    )
 
     def exchange(level):
-        return push(vec_out.at[level], vec_in.at[level], partners[level])
-
-    def add(level, copy):
-        copy.wait_recv()
-        vec_out[level + 1] = vec_out[level] + vec_in[level]
-
-    add(0, exchange(0))
+        own_at, partners = levels[level]
+        vec_in[level, own_at] = vec_out[level]
+        return [push(vec_out.at[level], vec_in.at[level, own_at], other) for _, other in partners]
+
+    def add(level, copies):
+        for copy in copies:
+            copy.wait_recv()
+        total = vec_in[level, 0]
+        for at in range(1, len(copies) + 1):
+            total = total + vec_in[level, at]
+        vec_out[level + 1] = total
+
+    step = exchange(0)
     passed_0 = forward(0)
+    gather(2)
+    add(0, step)
     step = exchange(1)
-    gather(2)
+    passed_1 = forward(1)
+    gather(3)
+    store(0, passed_0)
     add(1, step)
     step = exchange(2)
-    gather(3)
-    store(0, passed_0)
-    add(2, step)
     wo_to_other.wait_recv()
     for at in range(2):
 
@@ -1781,17 +1794,13 @@
             wo_core[0, most_rows:] = wo_half[3 - at, 2 * most_rows - quarter :]
 
     wo_to_core = push(wo_core.at[0], wo_core.at[1], beside)
-    step = exchange(3)
-    passed_1 = forward(1)
     for part in range(3):
         cols = slice((part + 1) * width - HEAD, (part + 1) * width)
         qkv_ref[:, cols] = whole[3, :, part * HEAD : (part + 1) * HEAD]
-    add(3, step)
-    step = exchange(4)
+    add(2, step)
+    vec_ref[...] = vec_out[3]
+    passed_2 = forward(2)
     store(1, passed_1)
-    passed_2 = forward(2)
-    add(4, step)
-    vec_ref[...] = vec_out[5]
     wo_to_core.wait_recv()
     core = place % 2
     for away in range(2):
@@ -1812,7 +1821,7 @@
     padded = vectors.shape[1]
     in_vmem = pl.BlockSpec(memory_space=pltpu.VMEM)
     vmem = lambda *shape, kind=BF16: pltpu.VMEM(shape, kind)
-    copies = 4 + 4 * 2 * (tensors - 1) + 3 + 3 * 3 + 2 + 5 + 2 * (tensors - 1) + 3
+    copies = 4 + 4 * 2 * (tensors - 1) + 4 + 3 * 3 + 2 + count + tensors - 1 + 2 * (tensors - 1) + 3
     given = len(grads) + 8
     quarter = width // 4
     most_rows = -(-quarter // 2 // 16) * 16
@@ -1854,8 +1863,8 @@
             vmem(3, 3, half, own),
             vmem(2, half, own),
             vmem(2, half, own),
-            vmem(6, 16, padded, kind=F32),
-            vmem(5, 16, padded, kind=F32),
+            vmem(4, 16, padded, kind=F32),
+            vmem(3, max(count, tensors), 16, padded, kind=F32),
             vmem(quarter, width),
             vmem(tensors - 1, part_rows, width),
             vmem(4, most_rows, width),
@@ -1948,24 +1957,25 @@
 
     labels = cont_seg[0].reshape(count, cont_rows)
     seg_col, seg_row = labels[:, :, None], labels[:, None, :]
-    lse, outs, came, last_out, two_away, one_far, three_far, *others, out_full = attend(
+    lse, outs, came, last_out, two_away, one_far, *others, out_full = attend(
         q, k, vt, seg_col, seg_row, prompt_rows, (mine, near_far, one_away, three_away), out_own
     )
-    mine_2, near_2, one_2, one_far_2, three_2, three_far_2 = others
-    two_far = swap(two_away, "fsdp", 1)
+    mine_2, near_2, one_2, one_far_2, three_2, two_2 = others
+    three_far, two_far = swap(three_away, "fsdp", 1), swap(two_away, "fsdp", 1)
     pieces = (outs, came, last_out)
     hidden, mlp_low, mlp_flip = merge(
         at, rows_own, out_full, out_bias, ln2_gain, ln2_bias, pieces
     )
 
+    steps_away = (0, 1, 3, 2)
     given = (mlp_low, grad_layer, mlp_flip, grad_flip)
-    mlp_out, grad_mlp_in, *grads_first, bias_first = mlp(
+    mlp_out, grad_mlp_in, keep_1, send_1, bias_first, proj_0, proj_1 = mlp(
         4,
         *given, (mine, one_away), (near_far, one_far), (mine_2, one_2), (near_2, one_far_2)
     )
-    (two_far,) = behind((two_far,), bias_first)
-    two_2, two_far_2 = swap(two_away, "ctx", 1), swap(two_far, "ctx", 1)
-    mlp_out, grad_mlp_in, *grads_last, bias_last = mlp(
+    three_far, two_far = behind((three_far, two_far), bias_first)
+    three_far_2, two_far_2 = swap(three_far, "ctx", 1), swap(two_far, "ctx", 1)
+    mlp_out, grad_mlp_in, keep_2, send_2, bias_last, proj_2, proj_3 = mlp(
         5,
         *given,
         (three_away, two_away),
@@ -1975,47 +1985,56 @@
         before=(mlp_out, grad_mlp_in),
     )
     grad_fc_bias = jnp.concatenate([bias_first, bias_last], axis=0)
+    proj_2, proj_3 = behind((proj_2, proj_3), mlp_out)
+    come_p = [
+        turn(part, "tensor", -steps_away[k + 1]) for k, part in enumerate((proj_1, proj_2, proj_3))
+    ]
     layer_out, grad_hidden, grads_own, grad_last, *rest = bend(
-        mlp_out, grad_mlp_in, hidden, grad_layer, out_full, ln2_gain, proj_bias, pieces
+        mlp_out,
+        grad_mlp_in,
+        hidden,
+        grad_layer,
+        out_full,
+        ln2_gain,
+        proj_bias,
+        pieces,
+        (proj_2, proj_3),
     )
     grads_all, (out_keep, out_send, sums2) = [grads_own, *rest[:-3]], rest[-3:]
 
     def added(left, right):
         return left.astype(F32) + right.astype(F32)
-
-    steps_away = (0, 1, 3, 2)
-
-    def over_tensor(parts, token):
-        come = [turn(parts[k], "tensor", -steps_away[k]) for k in range(1, tensors)]
-        total = parts[0].astype(F32)
-        for part in behind(come, token):
-            total = total + part.astype(F32)
-        return total
 
     def back(pair, tile, heads, grads, outs, after=()):
         return attend_back(
             pair, tile, heads, at, q, k, v, kt, lse, seg_col, seg_row, grads, outs, prompt_rows, after
         )
 
+    (send_2,) = behind((send_2,), grads_own)
     come_o = swap(out_send, "ctx", 1)
-    fc_parts, pj_parts = (grads_first[:2], grads_last[:2]), (grads_first[2:], grads_last[2:])
-    fc_come = [swap(send, "ctx", 2) for _, send in fc_parts]
-    pj_come = [swap(send, "fsdp", 1) for _, send in pj_parts]
+    come_1, come_2 = swap(send_1, "ctx", 2), swap(send_2, "ctx", 2)
     grads_pair = [back(0, 0, 2, grads_all, outs)]
     grads_left = back(PAIRS, 0, 1, [grad_last], last_out[None, None], (grads_pair[0][0],))
-    come_o, *come = behind((come_o, *fc_come, *pj_come), grads_left[0])
-    near_f = [added(keep[0], part[0]).astype(BF16) for (keep, _), part in zip(fc_parts, come[:2])]
-    far_f = [added(keep[1], part[1]).astype(BF16) for (keep, _), part in zip(fc_parts, come[:2])]
-    sum_p = [added(keep, part) for (keep, _), part in zip(pj_parts, come[2:])]
-    near_f, far_f = jnp.concatenate(near_f), jnp.concatenate(far_f)
-    sum_p = jnp.concatenate(sum_p).astype(BF16)
-    sum_o = added(out_keep, come_o).astype(BF16)
-    sum_o, out_o = sum_o[0], sum_o[1]
-    come_f, come_o = swap(far_f, "fsdp", 1), swap(out_o, "fsdp", 1)
-    grads_pair.append(back(1, 1, 2, grads_all, outs, (far_f, sum_p, out_o, grads_left[0])))
-    (come_f,) = behind((come_f,), grads_pair[1][0])
-    sum_f = added(near_f, come_f).astype(BF16)
-    sum_p = over_tensor(sum_p, grads_pair[1][0]).astype(BF16)
+    come_o, come_1, come_2, *come_p = behind((come_o, come_1, come_2, *come_p), grads_left[0])
+    sums_f = [
+        added(keep[k], come[k]).astype(BF16)
+        for keep, come in ((keep_1, come_1), (keep_2, come_2))
+        for k in range(2)
+    ]
+    near_p, far_p = (
+        sum((come[away].astype(F32) for come in come_p), proj_0[away].astype(F32)).astype(BF16)
+        for away in range(2)
+    )
+    near_o, far_o = (added(out_keep[away], come_o[away]).astype(BF16) for away in range(2))
+    come_f = [turn(sums_f[k], "tensor", -steps_away[k]) for k in range(1, tensors)]
+    come_p, come_o = swap(far_p, "fsdp", 1), swap(far_o, "fsdp", 1)
+    grads_pair.append(back(1, 1, 2, grads_all, outs, (*sums_f[1:], far_p, far_o, grads_left[0])))
+    come_p, *come_f = behind((come_p, *come_f), grads_pair[1][0])
+    near_f, far_f = (
+        sum((come[away].astype(F32) for come in come_f), sums_f[0][away].astype(F32)).astype(BF16)
+        for away in range(2)
+    )
+    sum_p = added(near_p, come_p).astype(BF16)
     ordered = [entry[part] for part in range(3) for entry in (*grads_pair, grads_left)]
     vectors = jnp.concatenate([sums2, jnp.zeros((tensors, hidden_units), F32)], axis=0)
     for k, distance in enumerate(steps_away):
@@ -2031,20 +2050,22 @@
         grad_hidden,
         ln1_gain,
         vectors,
-        sum_o,
+        near_o,
         come_o,
         prompt_rows,
-        (sum_f, sum_p),
-    )
-    sum_f = over_tensor(sum_f, late).astype(BF16)
-    (come_p,) = behind((swap(sum_p, "ctx", 2),), late)
-    sum_p = added(sum_p, come_p).astype(BF16)
-    far_f = swap(sum_f, "ctx", 2)
-    sum_f = jnp.concatenate(in_order(sum_f, far_f, chip), axis=0)
-    both = jnp.stack([sum_f, sum_p])
-    both = jnp.concatenate(in_order(both, swap(both, "ctx", 1), core), axis=1).astype(F32)
-    own_fc, own_proj = both[0], both[1].T
-
+        (far_f, sum_p),
+    )
+    come_f, come_p = behind((swap(far_f, "fsdp", 1), swap(sum_p, "ctx", 2)), late)
+    sum_f, sum_p = added(near_f, come_f).astype(BF16), added(sum_p, come_p).astype(BF16)
+    prompt_grad, cont_grad, sum_qkv, sum_out = behind(
+        (prompt_grad, cont_grad, sum_qkv, sum_out), sum_f, sum_p
+    )
+    by_away = [sum_f] + [swap(sum_f, "ctx", away) for away in range(1, count)]
+    halves_f = [
+        jnp.concatenate(in_order(by_away[i], by_away[i ^ 2], chip), axis=0) for i in range(2)
+    ]
+    own_fc = jnp.concatenate(in_order(*halves_f, core), axis=0).astype(F32)
+    own_proj = jnp.concatenate(in_order(sum_p, swap(sum_p, "ctx", 1), core), axis=0).astype(F32).T
 
     fc_bias_sum = lax.dynamic_index_in_dim(late, 12 + tensor, 0, False)[:hidden_units]
     return (

time: 616 us -> 615 us (level)
    pallas_call x1, Pallas kernels: 78.7 us -> 70.3 us  [attend(): pl.pallas_call(functools.partial(attend_kernel, prompt_rows), grid=(PAIRS...]
    ppermute x13 -> x15, starting transfers between devices: 10.8 us -> 15.3 us  [swap(): lax.ppermute(value, axis, [(place, place ^ bit) for place in range(count)])]
    unnamed x76 -> x82, local copies, waits for them, and re-layouts: 19.5 us -> 21.3 us
    pallas_call x13 -> x14, Pallas kernels: 258 us -> 258 us  [launch(): pl.pallas_call(body, grid_spec=pltpu.PrefetchScalarGridSpec(num_scalar_pr...]
  transfers between devices with their start and end apart: 19 -> 21, of which waited for: 1 -> 3; matrix products, arithmetic and copies ran while one was open for 5% -> 6% of each run, Pallas kernels for 61% -> 63%
where the time goes in v5:
time: 615 us; the launch traced here: 605 us
  Pallas kernels  516 us (84%)
  local copies, waits for them, and re-layouts  36.9 us (6%)
  other arithmetic  25.1 us (4%)
  starting transfers between devices  23.5 us (4%)
    pallas_call x14, Pallas kernels, launch(): pl.pallas_call(body, grid_spec=pltpu.PrefetchScalarGridSpec(num_scalar_pr...  258 us
    pallas_call x1, Pallas kernels, tail(): pl.pallas_call(body, in_specs=[in_vmem] * (len(grads) + 1) + [ANYWHERE] *...  121 us
    pallas_call x1, Pallas kernels, attend(): pl.pallas_call(functools.partial(attend_kernel, prompt_rows), grid=(PAIRS...  70.3 us
    pallas_call x1, Pallas kernels, open_up(): pl.pallas_call(open_kernel, in_specs=[ANYWHERE] * 8 + [in_vmem] * 4, out_...  67.1 us
    unnamed x82, local copies, waits for them, and re-layouts  21.3 us
    ppermute x15, starting transfers between devices, swap(): lax.ppermute(value, axis, [(place, place ^ bit) for place in range(count)])  15.3 us
  transfers between devices with their start and end apart: 21, of which 3 were waited for; matrix products, arithmetic and copies ran while one was open for 6% of the time, Pallas kernels for 63%

profile of v5, /device:TPU:0, one launch (start us, length us, event | category | flops | bytes accessed | tf_op | source)
XLA Modules:
  0.0 605.4 jit_solution(15991794413578035474)
XLA Ops:
  1.7 1.3 broadcast_in_dim.43.refs_9_.refs_15_
  3.0 1.3 broadcast_in_dim.42.refs_8_
  4.3 1.3 broadcast_in_dim.44.refs_10_
  6.3 1.5 broadcast_in_dim_reshape_squeeze.8.seg_col_ref.refs_6_
  8.6 67.1 %open.1 = (bf16[4,1104,896]{2,1,0:T(8,128)(2,1)}, bf16[3,4,896,128]{3,2,1,0:T(8,128)(2,1)}, bf16[3,4,896,128]{3,2,1,0:T(8,128)(2,1)}, bf16[3,4,896,128]{3,2,1,0:...) custom-call(bf16[1088,512]{1,0:T(8,128)(2,1)} %bitcast.70, ...), custom_call_target="tpu_custom_call" | custom-call | flops 8984199168 | bytes 41943040 | tf_op jit(solution)/shard_map/open/pallas_call | solution.py:608
  75.8 70.3 %attend.1 = (f32[3,4,2,896]{3,2,1,0:T(2,128)}, bf16[2,4,896,128]{3,2,1,0:T(8,128)(2,1)}, bf16[2,3,896,128]{3,2,1,0:T(8,128)(2,1)}, bf16[896,128]{1,0:T(8,128)(2,...) custom-call(bf16[3,4,896,128]{3,2,1,0:T(8,128)(2,1)} %get-tuple-elem, ...), custom_call_target="tpu_custom_call", output_to_operand_aliasing={{12}: (9, {})} | custom-call | flops 16106127360 | bytes 20971520 | tf_op jit(solution)/shard_map/attend/pallas_call | solution.py:846
  146.1 1.6 collective-permute-start.1
  148.3 1.5 copy-done
  149.8 1.3 copy-done.1
  152.0 9.6 %merge.1 = (f32[896,1088]{1,0:T(8,128)}, bf16[896,1088]{1,0:T(8,128)(2,1)}, bf16[1088,896]{1,0:T(8,128)(2,1)S(1)}) custom-call(s32[1]{0:T(128)} %bitcast.refs_0_, bf16[896,1088]{1,0:T(8,128)(2,1)} %get-tuple-element.105.refs_1_.refs_11_, bf16[1088,1088]{1,0:T(8,128)(2,1)} %get-tuple-element.114.refs_2_.refs_4_, f32[1,1088]{1,0:T(1,128)S(1)} %broadcast_in_dim.48.refs_3_, ...), custom_call_target="tpu_custom_call" | custom-call | flops 424253856 | bytes 3355443 | tf_op jit(solution)/shard_map/merge/pallas_call | solution.py:314
  161.6 1.3 copy-done.14
  162.9 58.9 %mlp.2 = (f32[896,1088]{1,0:T(8,128)}, f32[896,1088]{1,0:T(8,128)}, bf16[2,2,136,1088]{3,2,1,0:T(8,128)(2,1)}, bf16[2,2,136,1088]{3,2,1,0:T(8,128)(2,1)}, f32[2,...) custom-call(bf16[896,1088]{1,0:T(8,128)(2,1)} %get-tuple-element.118.refs_0_, ...), custom_call_target="tpu_custom_call" | custom-call | flops 5091046400 | bytes 8388608 | tf_op jit(solution)/shard_map/mlp/pallas_call | solution.py:314
  223.1 1.8 collective-permute-start.5
  224.9 1.2 collective-permute-start.7
  228.0 61.1 %mlp.3 = (f32[896,1088]{1,0:T(8,128)}, f32[896,1088]{1,0:T(8,128)}, bf16[2,2,136,1088]{3,2,1,0:T(8,128)(2,1)}, bf16[2,2,136,1088]{3,2,1,0:T(8,128)(2,1)}, f32[2,...) custom-call(bf16[896,1088]{1,0:T(8,128)(2,1)} %get-tuple-element.118.refs_0_, ...), custom_call_target="tpu_custom_call" | custom-call | flops 5091046400 | bytes 8388608 | tf_op jit(solution)/shard_map/mlp/pallas_call | solution.py:314
  289.7 2.0 collective-permute-start.9
  291.7 27.1 %bend.1 = (bf16[896,1088]{1,0:T(8,128)(2,1)}, f32[896,1088]{1,0:T(8,128)}, bf16[896,256]{1,0:T(8,128)(2,1)}, bf16[896,128]{1,0:T(8,128)(2,1)}, bf16[896,256]{1,0...) custom-call(f32[896,1088]{1,0:T(8,128)} %get-tuple-element.135.refs_, ...), custom_call_target="tpu_custom_call" | custom-call | flops 848507712 | bytes 6291456 | tf_op jit(solution)/shard_map/bend/pallas_call | solution.py:314
  322.8 2.4 slice_bitcast_fusion
  325.2 2.7 copy.63
  327.9 1.2 slice_bitcast_fusion.1
  329.1 1.3 copy.64
  330.5 45.9 %attend_back.3 = (bf16[1,4,896,128]{3,2,1,0:T(8,128)(2,1)}, bf16[1,4,896,128]{3,2,1,0:T(8,128)(2,1)}, bf16[1,4,896,128]{3,2,1,0:T(8,128)(2,1)}) custom-call(s32[1]{0:T(128)} %bitcast.refs_0_, bf16[3,4,896,128]{3,2,1,0:T(8,128)(2,1)} %get-tuple-element.106.q_ref.refs_1_, bf16[3,4,896,128]{3,2,1,0:T(8,128)(2,1)} %get-tuple-element.107.k_ref.refs_2_, ...), custom_call_target="tpu_custom_call" | custom-call | flops 2684354560 | bytes 3355443 | tf_op jit(solution)/shard_map/attend_back/pallas_call | solution.py:314
  376.3 9.2 %attend_back.4 = (bf16[1,4,896,128]{3,2,1,0:T(8,128)(2,1)}, bf16[1,4,896,128]{3,2,1,0:T(8,128)(2,1)}, bf16[1,4,896,128]{3,2,1,0:T(8,128)(2,1)}) custom-call(s32[1]{0:T(128)} %bitcast.refs_0_, bf16[3,4,896,128]{3,2,1,0:T(8,128)(2,1)} %get-tuple-element.106.q_ref.refs_1_, bf16[3,4,896,128]{3,2,1,0:T(8,128)(2,1)} %get-tuple-element.107.k_ref.refs_2_, ...), custom_call_target="tpu_custom_call" | custom-call | flops 335544320 | bytes 3355443 | tf_op jit(solution)/shard_map/attend_back/pallas_call | solution.py:314
  386.7 1.3 copy-done.28
  388.0 1.9 fusion.4.refs_19_
  389.9 1.6 collective-permute-start.10
  391.8 1.8 collective-permute-start.12
  393.9 1.7 add_convert_fusion.8
  395.6 2.3 collective-permute-start.11
  399.0 1.4 collective-permute-start.14
  400.3 46.1 %attend_back.5 = (bf16[1,4,896,128]{3,2,1,0:T(8,128)(2,1)}, bf16[1,4,896,128]{3,2,1,0:T(8,128)(2,1)}, bf16[1,4,896,128]{3,2,1,0:T(8,128)(2,1)}) custom-call(s32[1]{0:T(128)} %bitcast.refs_0_, bf16[3,4,896,128]{3,2,1,0:T(8,128)(2,1)} %get-tuple-element.106.q_ref.refs_1_, bf16[3,4,896,128]{3,2,1,0:T(8,128)(2,1)} %get-tuple-element.107.k_ref.refs_2_, ...), custom_call_target="tpu_custom_call" | custom-call | flops 2684354560 | bytes 3355443 | tf_op jit(solution)/shard_map/attend_back/pallas_call | solution.py:314
  447.7 2.0 copy-done.29
  449.6 1.9 fusion.refs_18_
  451.5 2.6 collective-permute-start.16
  455.9 120.6 %tail.1 = (bf16[1,512,1088]{2,1,0:T(8,128)(2,1)}, bf16[1,384,1088]{2,1,0:T(8,128)(2,1)}, bf16[544,3264]{1,0:T(8,128)(2,1)}, bf16[544,1088]{1,0:T(8,128)(2,1)}, f32[16,1152]{1,0:T(8,128)}) custom-call(bf16[1,4,896,128]{3,2,1,0:T(8,128)(2,1)} %get-tuple-element.152.refs_10_.refs_0_, bf16[1,4,896,128]{3,2,1,0:T(8,128)(2,1)} %get-tuple-element.167.refs_0_.refs_1_, ...), custom_call_target="tpu_custom_call" | custom-call | flops 17968398336 | bytes 31457280 | tf_op jit(solution)/shard_map/tail/pallas_call | solution.py:1833
  576.5 1.4 slice.202
  577.9 1.7 slice_reduce_fusion
  581.3 1.5 fusion.11.refs_0_
  582.9 2.2 collective-permute-start.17
  585.2 1.2 add_convert_fusion.refs_1_
  586.9 5.6 convert_element_type.240
  592.5 1.6 convert_element_type.241
  594.1 1.4 copy.65
  595.5 1.3 copy.66
  597.8 1.7 collective-permute-done.19
  600.8 1.6 maximum_convert_fusion
  602.4 1.2 broadcast_select_fusion.1
  603.6 1.6 convert_bitcast_fusion
  (140 shorter events, 22.2 us)
Async XLA Ops:
  75.8 72.4 %copy-start.35 = (f32[1088]{0:T(1024)S(1)}, f32[1088]{0:T(1024)}, u32[]{:S(2)}) copy-start(f32[1088]{0:T(1024)} %param.26) | copy-start | bytes 13060
  75.8 72.4 %copy-start.36 = (f32[1088]{0:T(1024)S(1)}, f32[1088]{0:T(1024)}, u32[]{:S(2)}) copy-start(f32[1088]{0:T(1024)} %param.25) | copy-start | bytes 13060
  75.8 72.5 %copy-start.37 = (f32[1088]{0:T(1024)S(1)}, f32[1088]{0:T(1024)}, u32[]{:S(2)}) copy-start(f32[1088]{0:T(1024)} %param.27) | copy-start | bytes 13060
  146.1 75.7 %collective-permute-start.1 = (bf16[560,1088]{1,0:T(8,128)(2,1)}, bf16[560,1088]{1,0:T(8,128)(2,1)S(1)}, u32[]{:S(2)}, u32[]{:S(2)}) collective-permute-start(bf16[560,1088]{1,0:T(8,128)(2,1)} %get-tuple-element.122.refs_5_), channel_id=1, source_target_pairs={{0,16},{16,0},{1,17},{17,1},{2,18},{18,2},{3,19},{19,3},{4,20},{20... | collective-permute-start | bytes 3655688 | tf_op jit(solution)/shard_map/ppermute | solution.py:276
  147.7 74.2 %collective-permute-start = (bf16[560,1088]{1,0:T(8,128)(2,1)}, bf16[560,1088]{1,0:T(8,128)(2,1)}, u32[]{:S(2)}, u32[]{:S(2)}) collective-permute-start(bf16[560,1088]{1,0:T(8,128)(2,1)} %get-tuple-element.112.refs_3_.refs_4_), channel_id=1, source_target_pairs={{0,16},{16,0},{1,17},{17,1},{2,18},{18,2},{3,19},{19,3},{4,20},{20... | collective-permute-start | bytes 3655688 | tf_op jit(solution)/shard_map/ppermute | solution.py:276
  148.2 13.4 %copy-start.17 = (f32[1,1088]{1,0:T(1,128)}, f32[1,1088]{1,0:T(1,128)S(1)}, u32[]{:S(2)}) copy-start(f32[1,1088]{1,0:T(1,128)S(1)} %broadcast_in_dim.49.refs_4_.refs_5_) | copy-start | bytes 13060
  148.2 1.5 copy-start
  149.7 1.3 copy-start.1
  222.6 3.5 copy-start.38
  222.6 5.4 copy-start.2
  222.6 4.3 collective-permute-start.2
  222.6 5.0 collective-permute-start.3
  223.1 98.8 %collective-permute-start.5 = (bf16[2,2,136,1088]{3,2,1,0:T(8,128)(2,1)}, bf16[2,2,136,1088]{3,2,1,0:T(8,128)(2,1)}, u32[]{:S(2)}, u32[]{:S(2)}) collective-permute-start(bf16[2,2,136,1088]{3,2,1,0:T(8,128)(2,1)} %get-tuple-element.155), channel_id=1, source_target_pairs={{0,8},{4,12},{8,0},{12,4},{1,9},{5,13},{9,1},{13,5},{2,10},{6,14},... | collective-permute-start | bytes 3551240 | tf_op jit(solution)/shard_map/ppermute | solution.py:276
  224.9 160.6 %collective-permute-start.7 = (bf16[2,272,1088]{2,1,0:T(8,128)(2,1)}, bf16[2,272,1088]{2,1,0:T(8,128)(2,1)}, u32[]{:S(2)}, u32[]{:S(2)}) collective-permute-start(bf16[2,272,1088]{2,1,0:T(8,128)(2,1)} %get-tuple-element.157), channel_id=1, source_target_pairs={{0,3},{1,0},{2,1},{3,2},{4,7},{5,4},{6,5},{7,6},{8,11},{9,8},{10,9... | collective-permute-start | bytes 3551240 | tf_op jit(solution)/shard_map/ppermute | solution.py:281
  289.1 96.5 %collective-permute-start.8 = (bf16[2,272,1088]{2,1,0:T(8,128)(2,1)}, bf16[2,272,1088]{2,1,0:T(8,128)(2,1)}, u32[]{:S(2)}, u32[]{:S(2)}) collective-permute-start(bf16[2,272,1088]{2,1,0:T(8,128)(2,1)} %get-tuple-element.140.refs_10_), channel_id=1, source_target_pairs={{0,1},{1,2},{2,3},{3,0},{4,5},{5,6},{6,7},{7,4},{8,9},{9,10},{10,1... | collective-permute-start | bytes 3551240 | tf_op jit(solution)/shard_map/ppermute | solution.py:281
  289.7 95.8 %collective-permute-start.9 = (bf16[2,272,1088]{2,1,0:T(8,128)(2,1)}, bf16[2,272,1088]{2,1,0:T(8,128)(2,1)}, u32[]{:S(2)}, u32[]{:S(2)}) collective-permute-start(bf16[2,272,1088]{2,1,0:T(8,128)(2,1)} %get-tuple-element.141.refs_11_), channel_id=1, source_target_pairs={{0,2},{1,3},{2,0},{3,1},{4,6},{5,7},{6,4},{7,5},{8,10},{9,11},{10,... | collective-permute-start | bytes 3551240 | tf_op jit(solution)/shard_map/ppermute | solution.py:281
  319.9 65.6 %collective-permute-start.6 = (bf16[2,2,136,1088]{3,2,1,0:T(8,128)(2,1)}, bf16[2,2,136,1088]{3,2,1,0:T(8,128)(2,1)S(1)}, u32[]{:S(2)}, u32[]{:S(2)}) collective-permute-start(bf16[2,2,136,1088]{3,2,1,0:T(8,128)(2,1)} %behind.9), channel_id=1, source_target_pairs={{0,8},{4,12},{8,0},{12,4},{1,9},{5,13},{9,1},{13,5},{2,10},{6,14},... | collective-permute-start | bytes 3551240 | tf_op jit(solution)/shard_map/ppermute | solution.py:276
  321.9 63.6 %collective-permute-start.4 = (bf16[2,272,1088]{2,1,0:T(8,128)(2,1)}, bf16[2,272,1088]{2,1,0:T(8,128)(2,1)S(1)}, u32[]{:S(2)}, u32[]{:S(2)}) collective-permute-start(bf16[2,272,1088]{2,1,0:T(8,128)(2,1)} %get-tuple-element.154), channel_id=1, source_target_pairs={{0,4},{4,0},{8,12},{12,8},{1,5},{5,1},{9,13},{13,9},{2,6},{6,2},{1... | collective-permute-start | bytes 3551240 | tf_op jit(solution)/shard_map/ppermute | solution.py:276
  388.0 3.4 copy-start.31
  389.9 1.9 copy-start.23
  389.9 56.5 %collective-permute-start.10 = (bf16[272,1088]{1,0:T(8,128)(2,1)S(1)}, bf16[272,1088]{1,0:T(8,128)(2,1)S(1)}, u32[]{:S(2)}, u32[]{:S(2)}) collective-permute-start(bf16[272,1088]{1,0:T(8,128)(2,1)S(1)} %fusion.4.refs_19_), channel_id=1, source_target_pairs={{0,16},{16,0},{1,17},{17,1},{2,18},{18,2},{3,19},{19,3},{4,20},{20... | collective-permute-start | bytes 1775624 | tf_op jit(solution)/shard_map/ppermute | solution.py:276
  391.5 2.4 copy-start.30
  391.8 3.7 copy-start.20
  391.8 3.7 copy-start.21
  391.8 54.6 %collective-permute-start.12 = (bf16[2,136,1088]{2,1,0:T(8,128)(2,1)S(1)}, bf16[2,136,1088]{2,1,0:T(8,128)(2,1)S(1)}, u32[]{:S(2)}, u32[]{:S(2)}) collective-permute-start(bf16[2,136,1088]{2,1,0:T(8,128)(2,1)S(1)} %get-tuple-element.240.refs_17_), channel_id=1, source_target_pairs={{0,1},{1,2},{2,3},{3,0},{4,5},{5,6},{6,7},{7,4},{8,9},{9,10},{10,1... | collective-permute-start | bytes 1775624 | tf_op jit(solution)/shard_map/ppermute | solution.py:281
  393.6 52.8 %collective-permute-start.13 = (bf16[2,136,1088]{2,1,0:T(8,128)(2,1)S(1)}, bf16[2,136,1088]{2,1,0:T(8,128)(2,1)S(1)}, u32[]{:S(2)}, u32[]{:S(2)}) collective-permute-start(bf16[2,136,1088]{2,1,0:T(8,128)(2,1)S(1)} %get-tuple-element.239.refs_18_), channel_id=1, source_target_pairs={{0,2},{1,3},{2,0},{3,1},{4,6},{5,7},{6,4},{7,5},{8,10},{9,11},{10,... | collective-permute-start | bytes 1775624 | tf_op jit(solution)/shard_map/ppermute | solution.py:281
  393.9 4.0 copy-start.32
  395.5 3.4 copy-start.22
  395.6 58.6 %copy-start.24 = (bf16[1,2,136,1088]{3,2,1,0:T(8,128)(2,1)}, bf16[1,2,136,1088]{3,2,1,0:T(8,128)(2,1)S(1)}, u32[]{:S(2)}) copy-start(bf16[1,2,136,1088]{3,2,1,0:T(8,128)(2,1)S(1)} %get-tuple-element.235) | copy-start | bytes 1775620
  395.6 50.9 %collective-permute-start.11 = (bf16[2,136,1088]{2,1,0:T(8,128)(2,1)S(1)}, bf16[2,136,1088]{2,1,0:T(8,128)(2,1)S(1)}, u32[]{:S(2)}, u32[]{:S(2)}) collective-permute-start(bf16[2,136,1088]{2,1,0:T(8,128)(2,1)S(1)} %get-tuple-element.236.refs_16_), channel_id=1, source_target_pairs={{0,3},{1,0},{2,1},{3,2},{4,7},{5,4},{6,5},{7,6},{8,11},{9,8},{10,9... | collective-permute-start | bytes 1775624 | tf_op jit(solution)/shard_map/ppermute | solution.py:281
  399.0 1.4 copy-start.19
  399.0 56.9 %collective-permute-start.14 = (bf16[272,1088]{1,0:T(8,128)(2,1)S(1)}, bf16[272,1088]{1,0:T(8,128)(2,1)}, u32[]{:S(2)}, u32[]{:S(2)}) collective-permute-start(bf16[272,1088]{1,0:T(8,128)(2,1)S(1)} %get-tuple-element.238.refs_20_), channel_id=1, source_target_pairs={{0,16},{16,0},{1,17},{17,1},{2,18},{18,2},{3,19},{19,3},{4,20},{20... | collective-permute-start | bytes 1775624 | tf_op jit(solution)/shard_map/ppermute | solution.py:276
  447.6 2.0 copy-start.29
  447.6 6.5 %copy-start.8 = (bf16[2,136,1088]{2,1,0:T(8,128)(2,1)}, bf16[2,136,1088]{2,1,0:T(8,128)(2,1)S(1)}, u32[]{:S(2)}) copy-start(bf16[2,136,1088]{2,1,0:T(8,128)(2,1)S(1)} %get-tuple-element.169) | copy-start | bytes 1775620
  447.6 6.5 %copy-start.10 = (bf16[2,136,1088]{2,1,0:T(8,128)(2,1)}, bf16[2,136,1088]{2,1,0:T(8,128)(2,1)S(1)}, u32[]{:S(2)}) copy-start(bf16[2,136,1088]{2,1,0:T(8,128)(2,1)S(1)} %get-tuple-element.170) | copy-start | bytes 1775620
  447.7 6.5 %copy-start.11 = (bf16[2,136,1088]{2,1,0:T(8,128)(2,1)}, bf16[2,136,1088]{2,1,0:T(8,128)(2,1)S(1)}, u32[]{:S(2)}) copy-start(bf16[2,136,1088]{2,1,0:T(8,128)(2,1)S(1)} %get-tuple-element.168) | copy-start | bytes 1775620
  451.5 4.4 copy-start.25
  451.5 128.1 %collective-permute-start.16 = (bf16[272,1088]{1,0:T(8,128)(2,1)S(1)}, bf16[272,1088]{1,0:T(8,128)(2,1)S(1)}, u32[]{:S(2)}, u32[]{:S(2)}) collective-permute-start(bf16[272,1088]{1,0:T(8,128)(2,1)S(1)} %fusion.refs_18_), channel_id=1, source_target_pairs={{0,8},{4,12},{8,0},{12,4},{1,9},{5,13},{9,1},{13,5},{2,10},{6,14},... | collective-permute-start | bytes 1775624 | tf_op jit(solution)/shard_map/ppermute | solution.py:276
  455.0 124.6 %collective-permute-start.15 = (bf16[136,1088]{1,0:T(8,128)(2,1)}, bf16[136,1088]{1,0:T(8,128)(2,1)S(1)}, u32[]{:S(2)}, u32[]{:S(2)}) collective-permute-start(bf16[136,1088]{1,0:T(8,128)(2,1)} %fusion.16.refs_17_), channel_id=1, source_target_pairs={{0,16},{16,0},{1,17},{17,1},{2,18},{18,2},{3,19},{19,3},{4,20},{20... | collective-permute-start | bytes 887816 | tf_op jit(solution)/shard_map/ppermute | solution.py:276
  576.5 4.8 copy-start.9
  580.5 4.7 copy-start.26
  581.3 5.6 copy-start.4
  581.3 5.6 copy-start.7
  582.9 4.1 copy-start.3
  582.9 13.9 %collective-permute-start.17 = (bf16[136,1088]{1,0:T(8,128)(2,1)S(1)}, bf16[136,1088]{1,0:T(8,128)(2,1)}, u32[]{:S(2)}, u32[]{:S(2)}) collective-permute-start(bf16[136,1088]{1,0:T(8,128)(2,1)S(1)} %fusion.11.refs_0_), channel_id=1, source_target_pairs={{0,8},{4,12},{8,0},{12,4},{1,9},{5,13},{9,1},{13,5},{2,10},{6,14},... | collective-permute-start | bytes 887816 | tf_op jit(solution)/shard_map/ppermute | solution.py:276
  585.0 12.8 %collective-permute-start.18 = (bf16[136,1088]{1,0:T(8,128)(2,1)S(1)}, bf16[136,1088]{1,0:T(8,128)(2,1)S(1)}, u32[]{:S(2)}, u32[]{:S(2)}) collective-permute-start(bf16[136,1088]{1,0:T(8,128)(2,1)S(1)} %fusion.11.refs_0_), channel_id=1, source_target_pairs={{0,4},{4,0},{8,12},{12,8},{1,5},{5,1},{9,13},{13,9},{2,6},{6,2},{1... | collective-permute-start | bytes 887816 | tf_op jit(solution)/shard_map/ppermute | solution.py:276
  585.1 14.4 %collective-permute-start.19 = (bf16[136,1088]{1,0:T(8,128)(2,1)S(1)}, bf16[136,1088]{1,0:T(8,128)(2,1)}, u32[]{:S(2)}, u32[]{:S(2)}) collective-permute-start(bf16[136,1088]{1,0:T(8,128)(2,1)S(1)} %fusion.11.refs_0_), channel_id=1, source_target_pairs={{0,12},{4,8},{8,4},{12,0},{1,13},{5,9},{9,5},{13,1},{2,14},{6,10},... | collective-permute-start | bytes 887816 | tf_op jit(solution)/shard_map/ppermute | solution.py:276
  586.5 15.9 %collective-permute-start.20 = (bf16[272,1088]{1,0:T(8,128)(2,1)S(1)}, bf16[272,1088]{1,0:T(8,128)(2,1)}, u32[]{:S(2)}, u32[]{:S(2)}) collective-permute-start(bf16[272,1088]{1,0:T(8,128)(2,1)S(1)} %add_convert_fusion.refs_1_), channel_id=1, source_target_pairs={{0,4},{4,0},{8,12},{12,8},{1,5},{5,1},{9,13},{13,9},{2,6},{6,2},{1... | collective-permute-start | bytes 1775624 | tf_op jit(solution)/shard_map/ppermute | solution.py:276
  (12 other events, 12.4 us)

commit v6 on v5

--- a/solution.py
+++ b/solution.py
@@ -1328,15 +1328,18 @@
         if total % 256:
             body(whole * 256, total % 256)
 
-    def up(start, size):
-        cols = pl.ds(start, size)
-        pre_act = dot(x_ref[...], wf_s[slot, :, cols]) + biases[:, cols]
-        grad_act = dot(g_ref[...], wp_s[slot, :, cols])
-        activated, slope = gelu_both(pre_act)
-        grad_pre = (grad_act * slope).astype(BF16)
-        act_s[:, cols] = activated.astype(BF16)
-        gp_s[:, cols] = grad_pre
-        gb_ref[0, :, cols] = jnp.sum(grad_pre.astype(F32), axis=0, keepdims=True)
+    def up(*blocks_of):
+        made = []
+        for start, size in blocks_of:
+            cols = pl.ds(start, size)
+            pre_act = dot(x_ref[...], wf_s[slot, :, cols]) + biases[:, cols]
+            made.append((cols, pre_act, dot(g_ref[...], wp_s[slot, :, cols])))
+        for cols, pre_act, grad_act in made:
+            activated, slope = gelu_both(pre_act)
+            grad_pre = (grad_act * slope).astype(BF16)
+            act_s[:, cols] = activated.astype(BF16)
+            gp_s[:, cols] = grad_pre
+            gb_ref[0, :, cols] = jnp.sum(grad_pre.astype(F32), axis=0, keepdims=True)
 
     def weights(start, size):
         cols = pl.ds(start, size)
@@ -1346,7 +1349,16 @@
                 for across, to in enumerate((keep_s, send_s)):
                     to[weight, far, :, cols] = wide[spot(far, across), :size]
 
-    over(hidden, up)
+    pairs = hidden // 512
+
+    @pl.loop(0, pairs)
+    def _(i):
+        start = pl.multiple_of(i * 512, 512)
+        up((start, 256), (start + 256, 256))
+
+    for start in range(pairs * 512, hidden, 256):
+        up((start, min(256, hidden - start)))
+
     for part in range(1, parts):
 
         @pl.when(step == part)

time: 615 us -> 613 us (level)
  transfers between devices with their start and end apart: 21 -> 21, of which waited for: 3 -> 3; matrix products, arithmetic and copies ran while one was open for 6% -> 6% of each run, Pallas kernels for 63% -> 62%
where the time goes in v6:
time: 613 us; the launch traced here: 603 us
  Pallas kernels  514 us (84%)
  local copies, waits for them, and re-layouts  36.9 us (6%)
  other arithmetic  25.1 us (4%)
  starting transfers between devices  23.3 us (4%)
    pallas_call x14, Pallas kernels, launch(): pl.pallas_call(body, grid_spec=pltpu.PrefetchScalarGridSpec(num_scalar_pr...  255 us
    pallas_call x1, Pallas kernels, tail(): pl.pallas_call(body, in_specs=[in_vmem] * (len(grads) + 1) + [ANYWHERE] *...  121 us
    pallas_call x1, Pallas kernels, attend(): pl.pallas_call(functools.partial(attend_kernel, prompt_rows), grid=(PAIRS...  70.3 us
    pallas_call x1, Pallas kernels, open_up(): pl.pallas_call(open_kernel, in_specs=[ANYWHERE] * 8 + [in_vmem] * 4, out_...  67.1 us
    unnamed x82, local copies, waits for them, and re-layouts  21.3 us
    ppermute x15, starting transfers between devices, swap(): lax.ppermute(value, axis, [(place, place ^ bit) for place in range(count)])  15 us
  transfers between devices with their start and end apart: 21, of which 3 were waited for; matrix products, arithmetic and copies ran while one was open for 6% of the time, Pallas kernels for 62%

profile of v6, /device:TPU:0, one launch (start us, length us, event | category | flops | bytes accessed | tf_op | source)
XLA Modules:
  0.0 602.8 jit_solution(13191252475734784320)
XLA Ops:
  1.7 1.3 broadcast_in_dim.43.refs_9_.refs_15_
  3.0 1.3 broadcast_in_dim.42.refs_8_
  4.3 1.3 broadcast_in_dim.44.refs_10_
  6.3 1.5 broadcast_in_dim_reshape_squeeze.8.seg_col_ref.refs_6_
  8.6 67.1 %open.1 = (bf16[4,1104,896]{2,1,0:T(8,128)(2,1)}, bf16[3,4,896,128]{3,2,1,0:T(8,128)(2,1)}, bf16[3,4,896,128]{3,2,1,0:T(8,128)(2,1)}, bf16[3,4,896,128]{3,2,1,0:...) custom-call(bf16[1088,512]{1,0:T(8,128)(2,1)} %bitcast.70, ...), custom_call_target="tpu_custom_call" | custom-call | flops 8984199168 | bytes 41943040 | tf_op jit(solution)/shard_map/open/pallas_call | solution.py:608
  75.8 70.3 %attend.1 = (f32[3,4,2,896]{3,2,1,0:T(2,128)}, bf16[2,4,896,128]{3,2,1,0:T(8,128)(2,1)}, bf16[2,3,896,128]{3,2,1,0:T(8,128)(2,1)}, bf16[896,128]{1,0:T(8,128)(2,...) custom-call(bf16[3,4,896,128]{3,2,1,0:T(8,128)(2,1)} %get-tuple-elem, ...), custom_call_target="tpu_custom_call", output_to_operand_aliasing={{12}: (9, {})} | custom-call | flops 16106127360 | bytes 20971520 | tf_op jit(solution)/shard_map/attend/pallas_call | solution.py:846
  146.1 1.6 collective-permute-start.1
  148.3 1.5 copy-done
  149.8 1.3 copy-done.1
  152.0 9.6 %merge.1 = (f32[896,1088]{1,0:T(8,128)}, bf16[896,1088]{1,0:T(8,128)(2,1)}, bf16[1088,896]{1,0:T(8,128)(2,1)S(1)}) custom-call(s32[1]{0:T(128)} %bitcast.refs_0_, bf16[896,1088]{1,0:T(8,128)(2,1)} %get-tuple-element.105.refs_1_.refs_11_, bf16[1088,1088]{1,0:T(8,128)(2,1)} %get-tuple-element.114.refs_2_.refs_4_, f32[1,1088]{1,0:T(1,128)S(1)} %broadcast_in_dim.48.refs_3_, ...), custom_call_target="tpu_custom_call" | custom-call | flops 424253856 | bytes 3355443 | tf_op jit(solution)/shard_map/merge/pallas_call | solution.py:314
  161.6 1.3 copy-done.14
  162.9 57.7 %mlp.2 = (f32[896,1088]{1,0:T(8,128)}, f32[896,1088]{1,0:T(8,128)}, bf16[2,2,136,1088]{3,2,1,0:T(8,128)(2,1)}, bf16[2,2,136,1088]{3,2,1,0:T(8,128)(2,1)}, f32[2,...) custom-call(bf16[896,1088]{1,0:T(8,128)(2,1)} %get-tuple-element.118.refs_0_, ...), custom_call_target="tpu_custom_call" | custom-call | flops 5091046400 | bytes 8388608 | tf_op jit(solution)/shard_map/mlp/pallas_call | solution.py:314
  221.9 1.8 collective-permute-start.5
  223.6 1.2 collective-permute-start.7
  226.7 59.9 %mlp.3 = (f32[896,1088]{1,0:T(8,128)}, f32[896,1088]{1,0:T(8,128)}, bf16[2,2,136,1088]{3,2,1,0:T(8,128)(2,1)}, bf16[2,2,136,1088]{3,2,1,0:T(8,128)(2,1)}, f32[2,...) custom-call(bf16[896,1088]{1,0:T(8,128)(2,1)} %get-tuple-element.118.refs_0_, ...), custom_call_target="tpu_custom_call" | custom-call | flops 5091046400 | bytes 8388608 | tf_op jit(solution)/shard_map/mlp/pallas_call | solution.py:314
  287.3 2.0 collective-permute-start.9
  289.3 27.1 %bend.1 = (bf16[896,1088]{1,0:T(8,128)(2,1)}, f32[896,1088]{1,0:T(8,128)}, bf16[896,256]{1,0:T(8,128)(2,1)}, bf16[896,128]{1,0:T(8,128)(2,1)}, bf16[896,256]{1,0...) custom-call(f32[896,1088]{1,0:T(8,128)} %get-tuple-element.135.refs_, ...), custom_call_target="tpu_custom_call" | custom-call | flops 848507712 | bytes 6291456 | tf_op jit(solution)/shard_map/bend/pallas_call | solution.py:314
  320.4 2.4 slice_bitcast_fusion
  322.8 2.7 copy.63
  325.5 1.2 slice_bitcast_fusion.1
  326.7 1.3 copy.64
  328.0 45.9 %attend_back.3 = (bf16[1,4,896,128]{3,2,1,0:T(8,128)(2,1)}, bf16[1,4,896,128]{3,2,1,0:T(8,128)(2,1)}, bf16[1,4,896,128]{3,2,1,0:T(8,128)(2,1)}) custom-call(s32[1]{0:T(128)} %bitcast.refs_0_, bf16[3,4,896,128]{3,2,1,0:T(8,128)(2,1)} %get-tuple-element.106.q_ref.refs_1_, bf16[3,4,896,128]{3,2,1,0:T(8,128)(2,1)} %get-tuple-element.107.k_ref.refs_2_, ...), custom_call_target="tpu_custom_call" | custom-call | flops 2684354560 | bytes 3355443 | tf_op jit(solution)/shard_map/attend_back/pallas_call | solution.py:314
  373.9 9.2 %attend_back.4 = (bf16[1,4,896,128]{3,2,1,0:T(8,128)(2,1)}, bf16[1,4,896,128]{3,2,1,0:T(8,128)(2,1)}, bf16[1,4,896,128]{3,2,1,0:T(8,128)(2,1)}) custom-call(s32[1]{0:T(128)} %bitcast.refs_0_, bf16[3,4,896,128]{3,2,1,0:T(8,128)(2,1)} %get-tuple-element.106.q_ref.refs_1_, bf16[3,4,896,128]{3,2,1,0:T(8,128)(2,1)} %get-tuple-element.107.k_ref.refs_2_, ...), custom_call_target="tpu_custom_call" | custom-call | flops 335544320 | bytes 3355443 | tf_op jit(solution)/shard_map/attend_back/pallas_call | solution.py:314
  384.3 1.3 copy-done.28
  385.6 1.9 fusion.4.refs_19_
  387.5 1.6 collective-permute-start.10
  389.4 1.8 collective-permute-start.12
  391.4 1.7 add_convert_fusion.8
  393.1 2.3 collective-permute-start.11
  396.6 1.3 collective-permute-start.14
  397.9 46.1 %attend_back.5 = (bf16[1,4,896,128]{3,2,1,0:T(8,128)(2,1)}, bf16[1,4,896,128]{3,2,1,0:T(8,128)(2,1)}, bf16[1,4,896,128]{3,2,1,0:T(8,128)(2,1)}) custom-call(s32[1]{0:T(128)} %bitcast.refs_0_, bf16[3,4,896,128]{3,2,1,0:T(8,128)(2,1)} %get-tuple-element.106.q_ref.refs_1_, bf16[3,4,896,128]{3,2,1,0:T(8,128)(2,1)} %get-tuple-element.107.k_ref.refs_2_, ...), custom_call_target="tpu_custom_call" | custom-call | flops 2684354560 | bytes 3355443 | tf_op jit(solution)/shard_map/attend_back/pallas_call | solution.py:314
  445.2 2.0 copy-done.29
  447.2 1.9 fusion.refs_18_
  449.1 2.6 collective-permute-start.16
  453.4 120.9 %tail.1 = (bf16[1,512,1088]{2,1,0:T(8,128)(2,1)}, bf16[1,384,1088]{2,1,0:T(8,128)(2,1)}, bf16[544,3264]{1,0:T(8,128)(2,1)}, bf16[544,1088]{1,0:T(8,128)(2,1)}, f32[16,1152]{1,0:T(8,128)}) custom-call(bf16[1,4,896,128]{3,2,1,0:T(8,128)(2,1)} %get-tuple-element.152.refs_10_.refs_0_, bf16[1,4,896,128]{3,2,1,0:T(8,128)(2,1)} %get-tuple-element.167.refs_0_.refs_1_, ...), custom_call_target="tpu_custom_call" | custom-call | flops 17968398336 | bytes 31457280 | tf_op jit(solution)/shard_map/tail/pallas_call | solution.py:1845
  574.3 1.4 slice.202
  575.8 1.7 slice_reduce_fusion
  579.2 1.5 fusion.11.refs_0_
  580.7 1.9 collective-permute-start.17
  582.9 1.2 add_convert_fusion.refs_1_
  584.5 5.6 convert_element_type.240
  590.1 1.6 convert_element_type.241
  591.7 1.4 copy.65
  593.0 1.3 copy.66
  595.4 1.5 collective-permute-done.19
  598.1 1.6 maximum_convert_fusion
  599.8 1.2 broadcast_select_fusion.1
  601.0 1.6 convert_bitcast_fusion
  (140 shorter events, 22.2 us)
Async XLA Ops:
  75.8 72.4 %copy-start.35 = (f32[1088]{0:T(1024)S(1)}, f32[1088]{0:T(1024)}, u32[]{:S(2)}) copy-start(f32[1088]{0:T(1024)} %param.26) | copy-start | bytes 13060
  75.8 72.4 %copy-start.36 = (f32[1088]{0:T(1024)S(1)}, f32[1088]{0:T(1024)}, u32[]{:S(2)}) copy-start(f32[1088]{0:T(1024)} %param.25) | copy-start | bytes 13060
  75.8 72.5 %copy-start.37 = (f32[1088]{0:T(1024)S(1)}, f32[1088]{0:T(1024)}, u32[]{:S(2)}) copy-start(f32[1088]{0:T(1024)} %param.27) | copy-start | bytes 13060
  146.1 74.5 %collective-permute-start.1 = (bf16[560,1088]{1,0:T(8,128)(2,1)}, bf16[560,1088]{1,0:T(8,128)(2,1)S(1)}, u32[]{:S(2)}, u32[]{:S(2)}) collective-permute-start(bf16[560,1088]{1,0:T(8,128)(2,1)} %get-tuple-element.122.refs_5_), channel_id=1, source_target_pairs={{0,16},{16,0},{1,17},{17,1},{2,18},{18,2},{3,19},{19,3},{4,20},{20... | collective-permute-start | bytes 3655688 | tf_op jit(solution)/shard_map/ppermute | solution.py:276
  147.7 73.0 %collective-permute-start = (bf16[560,1088]{1,0:T(8,128)(2,1)}, bf16[560,1088]{1,0:T(8,128)(2,1)}, u32[]{:S(2)}, u32[]{:S(2)}) collective-permute-start(bf16[560,1088]{1,0:T(8,128)(2,1)} %get-tuple-element.112.refs_3_.refs_4_), channel_id=1, source_target_pairs={{0,16},{16,0},{1,17},{17,1},{2,18},{18,2},{3,19},{19,3},{4,20},{20... | collective-permute-start | bytes 3655688 | tf_op jit(solution)/shard_map/ppermute | solution.py:276
  148.2 13.4 %copy-start.17 = (f32[1,1088]{1,0:T(1,128)}, f32[1,1088]{1,0:T(1,128)S(1)}, u32[]{:S(2)}) copy-start(f32[1,1088]{1,0:T(1,128)S(1)} %broadcast_in_dim.49.refs_4_.refs_5_) | copy-start | bytes 13060
  148.2 1.5 copy-start
  149.7 1.3 copy-start.1
  221.3 3.6 copy-start.38
  221.3 5.4 copy-start.2
  221.3 4.3 collective-permute-start.2
  221.4 5.0 collective-permute-start.3
  221.9 97.7 %collective-permute-start.5 = (bf16[2,2,136,1088]{3,2,1,0:T(8,128)(2,1)}, bf16[2,2,136,1088]{3,2,1,0:T(8,128)(2,1)}, u32[]{:S(2)}, u32[]{:S(2)}) collective-permute-start(bf16[2,2,136,1088]{3,2,1,0:T(8,128)(2,1)} %get-tuple-element.155), channel_id=1, source_target_pairs={{0,8},{4,12},{8,0},{12,4},{1,9},{5,13},{9,1},{13,5},{2,10},{6,14},... | collective-permute-start | bytes 3551240 | tf_op jit(solution)/shard_map/ppermute | solution.py:276
  223.6 159.4 %collective-permute-start.7 = (bf16[2,272,1088]{2,1,0:T(8,128)(2,1)}, bf16[2,272,1088]{2,1,0:T(8,128)(2,1)}, u32[]{:S(2)}, u32[]{:S(2)}) collective-permute-start(bf16[2,272,1088]{2,1,0:T(8,128)(2,1)} %get-tuple-element.157), channel_id=1, source_target_pairs={{0,3},{1,0},{2,1},{3,2},{4,7},{5,4},{6,5},{7,6},{8,11},{9,8},{10,9... | collective-permute-start | bytes 3551240 | tf_op jit(solution)/shard_map/ppermute | solution.py:281
  286.6 96.5 %collective-permute-start.8 = (bf16[2,272,1088]{2,1,0:T(8,128)(2,1)}, bf16[2,272,1088]{2,1,0:T(8,128)(2,1)}, u32[]{:S(2)}, u32[]{:S(2)}) collective-permute-start(bf16[2,272,1088]{2,1,0:T(8,128)(2,1)} %get-tuple-element.140.refs_10_), channel_id=1, source_target_pairs={{0,1},{1,2},{2,3},{3,0},{4,5},{5,6},{6,7},{7,4},{8,9},{9,10},{10,1... | collective-permute-start | bytes 3551240 | tf_op jit(solution)/shard_map/ppermute | solution.py:281
  287.3 95.9 %collective-permute-start.9 = (bf16[2,272,1088]{2,1,0:T(8,128)(2,1)}, bf16[2,272,1088]{2,1,0:T(8,128)(2,1)}, u32[]{:S(2)}, u32[]{:S(2)}) collective-permute-start(bf16[2,272,1088]{2,1,0:T(8,128)(2,1)} %get-tuple-element.141.refs_11_), channel_id=1, source_target_pairs={{0,2},{1,3},{2,0},{3,1},{4,6},{5,7},{6,4},{7,5},{8,10},{9,11},{10,... | collective-permute-start | bytes 3551240 | tf_op jit(solution)/shard_map/ppermute | solution.py:281
  317.4 65.7 %collective-permute-start.6 = (bf16[2,2,136,1088]{3,2,1,0:T(8,128)(2,1)}, bf16[2,2,136,1088]{3,2,1,0:T(8,128)(2,1)S(1)}, u32[]{:S(2)}, u32[]{:S(2)}) collective-permute-start(bf16[2,2,136,1088]{3,2,1,0:T(8,128)(2,1)} %behind.9), channel_id=1, source_target_pairs={{0,8},{4,12},{8,0},{12,4},{1,9},{5,13},{9,1},{13,5},{2,10},{6,14},... | collective-permute-start | bytes 3551240 | tf_op jit(solution)/shard_map/ppermute | solution.py:276
  319.5 63.6 %collective-permute-start.4 = (bf16[2,272,1088]{2,1,0:T(8,128)(2,1)}, bf16[2,272,1088]{2,1,0:T(8,128)(2,1)S(1)}, u32[]{:S(2)}, u32[]{:S(2)}) collective-permute-start(bf16[2,272,1088]{2,1,0:T(8,128)(2,1)} %get-tuple-element.154), channel_id=1, source_target_pairs={{0,4},{4,0},{8,12},{12,8},{1,5},{5,1},{9,13},{13,9},{2,6},{6,2},{1... | collective-permute-start | bytes 3551240 | tf_op jit(solution)/shard_map/ppermute | solution.py:276
  385.6 3.4 copy-start.31
  387.5 1.9 copy-start.23
  387.5 56.5 %collective-permute-start.10 = (bf16[272,1088]{1,0:T(8,128)(2,1)S(1)}, bf16[272,1088]{1,0:T(8,128)(2,1)S(1)}, u32[]{:S(2)}, u32[]{:S(2)}) collective-permute-start(bf16[272,1088]{1,0:T(8,128)(2,1)S(1)} %fusion.4.refs_19_), channel_id=1, source_target_pairs={{0,16},{16,0},{1,17},{17,1},{2,18},{18,2},{3,19},{19,3},{4,20},{20... | collective-permute-start | bytes 1775624 | tf_op jit(solution)/shard_map/ppermute | solution.py:276
  389.0 2.4 copy-start.30
  389.4 3.7 copy-start.20
  389.4 3.7 copy-start.21
  389.4 54.6 %collective-permute-start.12 = (bf16[2,136,1088]{2,1,0:T(8,128)(2,1)S(1)}, bf16[2,136,1088]{2,1,0:T(8,128)(2,1)S(1)}, u32[]{:S(2)}, u32[]{:S(2)}) collective-permute-start(bf16[2,136,1088]{2,1,0:T(8,128)(2,1)S(1)} %get-tuple-element.240.refs_17_), channel_id=1, source_target_pairs={{0,1},{1,2},{2,3},{3,0},{4,5},{5,6},{6,7},{7,4},{8,9},{9,10},{10,1... | collective-permute-start | bytes 1775624 | tf_op jit(solution)/shard_map/ppermute | solution.py:281
  391.2 52.8 %collective-permute-start.13 = (bf16[2,136,1088]{2,1,0:T(8,128)(2,1)S(1)}, bf16[2,136,1088]{2,1,0:T(8,128)(2,1)S(1)}, u32[]{:S(2)}, u32[]{:S(2)}) collective-permute-start(bf16[2,136,1088]{2,1,0:T(8,128)(2,1)S(1)} %get-tuple-element.239.refs_18_), channel_id=1, source_target_pairs={{0,2},{1,3},{2,0},{3,1},{4,6},{5,7},{6,4},{7,5},{8,10},{9,11},{10,... | collective-permute-start | bytes 1775624 | tf_op jit(solution)/shard_map/ppermute | solution.py:281
  391.4 4.0 copy-start.32
  393.1 3.5 copy-start.22
  393.1 58.6 %copy-start.24 = (bf16[1,2,136,1088]{3,2,1,0:T(8,128)(2,1)}, bf16[1,2,136,1088]{3,2,1,0:T(8,128)(2,1)S(1)}, u32[]{:S(2)}) copy-start(bf16[1,2,136,1088]{3,2,1,0:T(8,128)(2,1)S(1)} %get-tuple-element.235) | copy-start | bytes 1775620
  393.1 50.9 %collective-permute-start.11 = (bf16[2,136,1088]{2,1,0:T(8,128)(2,1)S(1)}, bf16[2,136,1088]{2,1,0:T(8,128)(2,1)S(1)}, u32[]{:S(2)}, u32[]{:S(2)}) collective-permute-start(bf16[2,136,1088]{2,1,0:T(8,128)(2,1)S(1)} %get-tuple-element.236.refs_16_), channel_id=1, source_target_pairs={{0,3},{1,0},{2,1},{3,2},{4,7},{5,4},{6,5},{7,6},{8,11},{9,8},{10,9... | collective-permute-start | bytes 1775624 | tf_op jit(solution)/shard_map/ppermute | solution.py:281
  396.6 1.3 copy-start.19
  396.6 56.8 %collective-permute-start.14 = (bf16[272,1088]{1,0:T(8,128)(2,1)S(1)}, bf16[272,1088]{1,0:T(8,128)(2,1)}, u32[]{:S(2)}, u32[]{:S(2)}) collective-permute-start(bf16[272,1088]{1,0:T(8,128)(2,1)S(1)} %get-tuple-element.238.refs_20_), channel_id=1, source_target_pairs={{0,16},{16,0},{1,17},{17,1},{2,18},{18,2},{3,19},{19,3},{4,20},{20... | collective-permute-start | bytes 1775624 | tf_op jit(solution)/shard_map/ppermute | solution.py:276
  445.2 2.0 copy-start.29
  445.2 6.5 %copy-start.8 = (bf16[2,136,1088]{2,1,0:T(8,128)(2,1)}, bf16[2,136,1088]{2,1,0:T(8,128)(2,1)S(1)}, u32[]{:S(2)}) copy-start(bf16[2,136,1088]{2,1,0:T(8,128)(2,1)S(1)} %get-tuple-element.169) | copy-start | bytes 1775620
  445.2 6.5 %copy-start.10 = (bf16[2,136,1088]{2,1,0:T(8,128)(2,1)}, bf16[2,136,1088]{2,1,0:T(8,128)(2,1)S(1)}, u32[]{:S(2)}) copy-start(bf16[2,136,1088]{2,1,0:T(8,128)(2,1)S(1)} %get-tuple-element.170) | copy-start | bytes 1775620
  445.2 6.5 %copy-start.11 = (bf16[2,136,1088]{2,1,0:T(8,128)(2,1)}, bf16[2,136,1088]{2,1,0:T(8,128)(2,1)S(1)}, u32[]{:S(2)}) copy-start(bf16[2,136,1088]{2,1,0:T(8,128)(2,1)S(1)} %get-tuple-element.168) | copy-start | bytes 1775620
  449.1 4.4 copy-start.25
  449.1 128.4 %collective-permute-start.16 = (bf16[272,1088]{1,0:T(8,128)(2,1)S(1)}, bf16[272,1088]{1,0:T(8,128)(2,1)S(1)}, u32[]{:S(2)}, u32[]{:S(2)}) collective-permute-start(bf16[272,1088]{1,0:T(8,128)(2,1)S(1)} %fusion.refs_18_), channel_id=1, source_target_pairs={{0,8},{4,12},{8,0},{12,4},{1,9},{5,13},{9,1},{13,5},{2,10},{6,14},... | collective-permute-start | bytes 1775624 | tf_op jit(solution)/shard_map/ppermute | solution.py:276
  452.6 124.8 %collective-permute-start.15 = (bf16[136,1088]{1,0:T(8,128)(2,1)}, bf16[136,1088]{1,0:T(8,128)(2,1)S(1)}, u32[]{:S(2)}, u32[]{:S(2)}) collective-permute-start(bf16[136,1088]{1,0:T(8,128)(2,1)} %fusion.16.refs_17_), channel_id=1, source_target_pairs={{0,16},{16,0},{1,17},{17,1},{2,18},{18,2},{3,19},{19,3},{4,20},{20... | collective-permute-start | bytes 887816 | tf_op jit(solution)/shard_map/ppermute | solution.py:276
  574.3 4.8 copy-start.9
  578.3 4.6 copy-start.26
  579.2 5.3 copy-start.4
  579.2 5.3 copy-start.7
  580.7 3.8 copy-start.3
  580.7 13.6 %collective-permute-start.17 = (bf16[136,1088]{1,0:T(8,128)(2,1)S(1)}, bf16[136,1088]{1,0:T(8,128)(2,1)}, u32[]{:S(2)}, u32[]{:S(2)}) collective-permute-start(bf16[136,1088]{1,0:T(8,128)(2,1)S(1)} %fusion.11.refs_0_), channel_id=1, source_target_pairs={{0,8},{4,12},{8,0},{12,4},{1,9},{5,13},{9,1},{13,5},{2,10},{6,14},... | collective-permute-start | bytes 887816 | tf_op jit(solution)/shard_map/ppermute | solution.py:276
  582.6 12.8 %collective-permute-start.18 = (bf16[136,1088]{1,0:T(8,128)(2,1)S(1)}, bf16[136,1088]{1,0:T(8,128)(2,1)S(1)}, u32[]{:S(2)}, u32[]{:S(2)}) collective-permute-start(bf16[136,1088]{1,0:T(8,128)(2,1)S(1)} %fusion.11.refs_0_), channel_id=1, source_target_pairs={{0,4},{4,0},{8,12},{12,8},{1,5},{5,1},{9,13},{13,9},{2,6},{6,2},{1... | collective-permute-start | bytes 887816 | tf_op jit(solution)/shard_map/ppermute | solution.py:276
  582.7 14.2 %collective-permute-start.19 = (bf16[136,1088]{1,0:T(8,128)(2,1)S(1)}, bf16[136,1088]{1,0:T(8,128)(2,1)}, u32[]{:S(2)}, u32[]{:S(2)}) collective-permute-start(bf16[136,1088]{1,0:T(8,128)(2,1)S(1)} %fusion.11.refs_0_), channel_id=1, source_target_pairs={{0,12},{4,8},{8,4},{12,0},{1,13},{5,9},{9,5},{13,1},{2,14},{6,10},... | collective-permute-start | bytes 887816 | tf_op jit(solution)/shard_map/ppermute | solution.py:276
  584.2 15.6 %collective-permute-start.20 = (bf16[272,1088]{1,0:T(8,128)(2,1)S(1)}, bf16[272,1088]{1,0:T(8,128)(2,1)}, u32[]{:S(2)}, u32[]{:S(2)}) collective-permute-start(bf16[272,1088]{1,0:T(8,128)(2,1)S(1)} %add_convert_fusion.refs_1_), channel_id=1, source_target_pairs={{0,4},{4,0},{8,12},{12,8},{1,5},{5,1},{9,13},{13,9},{2,6},{6,2},{1... | collective-permute-start | bytes 1775624 | tf_op jit(solution)/shard_map/ppermute | solution.py:276
  (12 other events, 12.5 us)

commit v7 on v6

--- a/solution.py
+++ b/solution.py
@@ -353,9 +353,9 @@
 
 def open_kernel(*refs):
     prompt_ref, cont_ref, w_ref, fc_ref, proj_ref, wo_ref, gp_ref, gc_ref = refs[:8]
-    fc_bias_ref, gain_ref, bias_ref, col_bias_ref = refs[8:12]
-    norm_ref, q_ref, k_ref, v_ref, kt_ref, vt_ref = refs[12:18]
-    w_own_ref, rows_ref, g_ref, gt_ref, mine_ref, one_ref, three_ref, far_ref, out_ref = refs[18:27]
+    vector_ref, col_bias_ref = refs[8:10]
+    norm_ref, q_ref, k_ref, v_ref, kt_ref, vt_ref = refs[10:16]
+    w_own_ref, rows_ref, g_ref, gt_ref, mine_ref, one_ref, three_ref, far_ref, out_ref = refs[16:25]
     (
         rows_t,
         w_s,
@@ -376,7 +376,7 @@
         send_sem,
         recv_sem,
         out_sem,
-    ) = refs[27:]
+    ) = refs[25:]
     place = lax.axis_index("ctx")
     fsdp = lax.axis_index("fsdp")
     tensor = lax.axis_index("tensor")
@@ -456,7 +456,7 @@
         copy.wait()
     mine_s[:quarter] = fc_s[...].astype(BF16)
     mine_s[quarter : 2 * quarter] = proj_s[...].astype(BF16)
-    bias = fc_bias_ref[...]
+    bias = vector_ref[2:3]
     pieces = []
     for _ in range(3):
         piece = bias.astype(BF16)
@@ -508,8 +508,8 @@
     turn_rows(rows_t.at[0], turned.at[1])
     put(turned.at[1], rows_ref)
 
-    gain_col = jnp.broadcast_to(gain_ref[...], (8, width)).T[:, :1]
-    bias_col = jnp.broadcast_to(bias_ref[...], (8, width)).T[:, :1]
+    gain_col = jnp.broadcast_to(vector_ref[0:1], (8, width)).T[:, :1]
+    bias_col = jnp.broadcast_to(vector_ref[1:2], (8, width)).T[:, :1]
     extra = norms.shape[1] - width
     at_row = lax.broadcasted_iota(jnp.int32, (extra, row_count), 0)
     ones = jnp.where(at_row == 0, 1.0, 0.0).astype(BF16)
@@ -576,7 +576,7 @@
 
 
 def open_up(
-    prompt_in, cont_in, w_qkv, w_fc, w_proj, w_out, fc_bias, prompt_cot, cont_cot, gain, bias, col_bias, count
+    prompt_in, cont_in, w_qkv, w_fc, w_proj, w_out, prompt_cot, cont_cot, vectors, col_bias, count
 ):
     prompt_rows, width = prompt_in.shape[1:]
     row_count = prompt_rows + cont_in.shape[1]
@@ -607,7 +607,7 @@
     copies = 2 + 1 + 1 + 3 + 2
     return pl.pallas_call(
         open_kernel,
-        in_specs=[ANYWHERE] * 8 + [in_vmem] * 4,
+        in_specs=[ANYWHERE] * 8 + [in_vmem] * 2,
         out_specs=[ANYWHERE] * len(outs),
         out_shape=[shape_of(*out) for out in outs],
         scratch_shapes=[
@@ -647,9 +647,7 @@
         w_out,
         prompt_cot[0].T,
         cont_cot[0].T,
-        fc_bias[None],
-        gain[None],
-        bias[None],
+        vectors,
         col_bias[None],
     )
 
@@ -1730,7 +1728,7 @@
         rows = chunk_rows(i)
         unit, rate = normalize(rows_s[i % 2, :, :width].astype(F32))
         grad = hold[rows, :] + core_in[1, rows, :].astype(F32) + chip_in[rows, :].astype(F32)
-        back = normalize_back(unit, rate, grad * gain_ref[...])
+        back = normalize_back(unit, rate, grad * gain_ref[0:1])
         out = (gh_s[i % 2] + back).astype(BF16)
 
         @pl.when(i < prompt_rows // chunk)
@@ -1893,7 +1891,7 @@
             flops=4 * count * row_count * width * cols, bytes_accessed=30 << 20, transcendentals=0
         ),
         name="tail",
-    )(*grads, w_own, normed, rows, grad_hidden, out_keep, out_come, gain[None], vectors, *after)
+    )(*grads, w_own, normed, rows, grad_hidden, out_keep, out_come, gain, vectors, *after)
 
 
 def own_columns(matrix, place):
@@ -1949,6 +1947,7 @@
 
     zero_bias = jnp.zeros_like(qv_bias[0])
     col_bias = own_columns(jnp.concatenate([qv_bias[0], zero_bias, qv_bias[1]])[None], place)[0]
+    open_vectors = jnp.stack([ln1_gain, ln1_bias, fc_bias])
     normed, q, k, v, kt, vt, w_own, rows_own, grad_layer, grad_flip, *mines, out_own = open_up(
         prompt_in,
         cont_in,
@@ -1956,11 +1955,9 @@
         w_fc,
         w_proj,
         w_out,
-        fc_bias,
         prompt_cot,
         cont_cot,
-        ln1_gain,
-        ln1_bias,
+        open_vectors,
         col_bias,
         count,
     )
@@ -2060,7 +2057,7 @@
         normed,
         rows_own,
         grad_hidden,
-        ln1_gain,
+        open_vectors,
         vectors,
         near_o,
         come_o,

time: 613 us -> 612 us (level)
  no operation moved by 1% of the time
where the time goes in v7:
time: 612 us; the launch traced here: 602 us
  Pallas kernels  513 us (84%)
  local copies, waits for them, and re-layouts  35.2 us (6%)
  other arithmetic  25.8 us (4%)
  starting transfers between devices  23.5 us (4%)
    pallas_call x14, Pallas kernels, launch(): pl.pallas_call(body, grid_spec=pltpu.PrefetchScalarGridSpec(num_scalar_pr...  255 us
    pallas_call x1, Pallas kernels, tail(): pl.pallas_call(body, in_specs=[in_vmem] * (len(grads) + 1) + [ANYWHERE] *...  121 us
    pallas_call x1, Pallas kernels, attend(): pl.pallas_call(functools.partial(attend_kernel, prompt_rows), grid=(PAIRS...  70.3 us
    pallas_call x1, Pallas kernels, open_up(): pl.pallas_call(open_kernel, in_specs=[ANYWHERE] * 8 + [in_vmem] * 2, out_...  67.1 us
    unnamed x82, local copies, waits for them, and re-layouts  21.3 us
    ppermute x15, starting transfers between devices, swap(): lax.ppermute(value, axis, [(place, place ^ bit) for place in range(count)])  15.3 us
  transfers between devices with their start and end apart: 21, of which 3 were waited for; matrix products, arithmetic and copies ran while one was open for 6% of the time, Pallas kernels for 62%

profile of v7, /device:TPU:0, one launch (start us, length us, event | category | flops | bytes accessed | tf_op | source)
XLA Modules:
  0.0 601.8 jit_solution(15683709156160906037)
XLA Ops:
  4.5 1.5 broadcast_in_dim_reshape_squeeze.8.seg_col_ref.refs_6_
  7.5 67.1 %open.1 = (bf16[4,1104,896]{2,1,0:T(8,128)(2,1)}, bf16[3,4,896,128]{3,2,1,0:T(8,128)(2,1)}, bf16[3,4,896,128]{3,2,1,0:T(8,128)(2,1)}, bf16[3,4,896,128]{3,2,1,0:...) custom-call(bf16[1088,512]{1,0:T(8,128)(2,1)} %bitcast.70, ...), custom_call_target="tpu_custom_call" | custom-call | flops 8984199168 | bytes 41943040 | tf_op jit(solution)/shard_map/open/pallas_call | solution.py:608
  74.6 70.3 %attend.1 = (f32[3,4,2,896]{3,2,1,0:T(2,128)}, bf16[2,4,896,128]{3,2,1,0:T(8,128)(2,1)}, bf16[2,3,896,128]{3,2,1,0:T(8,128)(2,1)}, bf16[896,128]{1,0:T(8,128)(2,...) custom-call(bf16[3,4,896,128]{3,2,1,0:T(8,128)(2,1)} %get-tuple-elem, ...), custom_call_target="tpu_custom_call", output_to_operand_aliasing={{12}: (9, {})} | custom-call | flops 16106127360 | bytes 20971520 | tf_op jit(solution)/shard_map/attend/pallas_call | solution.py:844
  144.9 1.6 collective-permute-start.1
  147.1 1.5 copy-done
  148.6 1.3 copy-done.1
  150.9 9.6 %merge.1 = (f32[896,1088]{1,0:T(8,128)}, bf16[896,1088]{1,0:T(8,128)(2,1)}, bf16[1088,896]{1,0:T(8,128)(2,1)S(1)}) custom-call(s32[1]{0:T(128)} %bitcast.refs_0_, bf16[896,1088]{1,0:T(8,128)(2,1)} %get-tuple-element.105.refs_1_.refs_11_, bf16[1088,1088]{1,0:T(8,128)(2,1)} %get-tuple-element.114.refs_2_.refs_4_, f32[1,1088]{1,0:T(1,128)S(1)} %broadcast_in_dim.35.refs_3_, ...), custom_call_target="tpu_custom_call" | custom-call | flops 424253856 | bytes 3355443 | tf_op jit(solution)/shard_map/merge/pallas_call | solution.py:314
  160.5 1.3 copy-done.14
  161.7 57.7 %mlp.2 = (f32[896,1088]{1,0:T(8,128)}, f32[896,1088]{1,0:T(8,128)}, bf16[2,2,136,1088]{3,2,1,0:T(8,128)(2,1)}, bf16[2,2,136,1088]{3,2,1,0:T(8,128)(2,1)}, f32[2,...) custom-call(bf16[896,1088]{1,0:T(8,128)(2,1)} %get-tuple-element.118.refs_0_, ...), custom_call_target="tpu_custom_call" | custom-call | flops 5091046400 | bytes 8388608 | tf_op jit(solution)/shard_map/mlp/pallas_call | solution.py:314
  220.7 1.8 collective-permute-start.5
  222.5 1.2 collective-permute-start.7
  225.6 59.9 %mlp.3 = (f32[896,1088]{1,0:T(8,128)}, f32[896,1088]{1,0:T(8,128)}, bf16[2,2,136,1088]{3,2,1,0:T(8,128)(2,1)}, bf16[2,2,136,1088]{3,2,1,0:T(8,128)(2,1)}, f32[2,...) custom-call(bf16[896,1088]{1,0:T(8,128)(2,1)} %get-tuple-element.118.refs_0_, ...), custom_call_target="tpu_custom_call" | custom-call | flops 5091046400 | bytes 8388608 | tf_op jit(solution)/shard_map/mlp/pallas_call | solution.py:314
  286.1 2.0 collective-permute-start.9
  288.1 27.1 %bend.1 = (bf16[896,1088]{1,0:T(8,128)(2,1)}, f32[896,1088]{1,0:T(8,128)}, bf16[896,256]{1,0:T(8,128)(2,1)}, bf16[896,128]{1,0:T(8,128)(2,1)}, bf16[896,256]{1,0...) custom-call(f32[896,1088]{1,0:T(8,128)} %get-tuple-element.135.refs_, ...), custom_call_target="tpu_custom_call" | custom-call | flops 848507712 | bytes 6291456 | tf_op jit(solution)/shard_map/bend/pallas_call | solution.py:314
  319.2 2.4 slice_bitcast_fusion
  321.6 2.7 copy.63
  324.3 1.2 slice_bitcast_fusion.1
  325.6 1.3 copy.64
  326.9 45.9 %attend_back.3 = (bf16[1,4,896,128]{3,2,1,0:T(8,128)(2,1)}, bf16[1,4,896,128]{3,2,1,0:T(8,128)(2,1)}, bf16[1,4,896,128]{3,2,1,0:T(8,128)(2,1)}) custom-call(s32[1]{0:T(128)} %bitcast.refs_0_, bf16[3,4,896,128]{3,2,1,0:T(8,128)(2,1)} %get-tuple-element.106.q_ref.refs_1_, bf16[3,4,896,128]{3,2,1,0:T(8,128)(2,1)} %get-tuple-element.107.k_ref.refs_2_, ...), custom_call_target="tpu_custom_call" | custom-call | flops 2684354560 | bytes 3355443 | tf_op jit(solution)/shard_map/attend_back/pallas_call | solution.py:314
  372.8 9.2 %attend_back.4 = (bf16[1,4,896,128]{3,2,1,0:T(8,128)(2,1)}, bf16[1,4,896,128]{3,2,1,0:T(8,128)(2,1)}, bf16[1,4,896,128]{3,2,1,0:T(8,128)(2,1)}) custom-call(s32[1]{0:T(128)} %bitcast.refs_0_, bf16[3,4,896,128]{3,2,1,0:T(8,128)(2,1)} %get-tuple-element.106.q_ref.refs_1_, bf16[3,4,896,128]{3,2,1,0:T(8,128)(2,1)} %get-tuple-element.107.k_ref.refs_2_, ...), custom_call_target="tpu_custom_call" | custom-call | flops 335544320 | bytes 3355443 | tf_op jit(solution)/shard_map/attend_back/pallas_call | solution.py:314
  382.0 1.2 copy-done.6
  383.1 1.3 copy-done.28
  384.4 1.9 fusion.4.refs_19_
  386.3 1.5 collective-permute-start.10
  388.2 1.9 collective-permute-start.12
  390.3 1.7 add_convert_fusion.8
  392.0 2.3 collective-permute-start.11
  394.3 1.2 fusion.6
  395.4 1.3 collective-permute-start.14
  396.7 46.1 %attend_back.5 = (bf16[1,4,896,128]{3,2,1,0:T(8,128)(2,1)}, bf16[1,4,896,128]{3,2,1,0:T(8,128)(2,1)}, bf16[1,4,896,128]{3,2,1,0:T(8,128)(2,1)}) custom-call(s32[1]{0:T(128)} %bitcast.refs_0_, bf16[3,4,896,128]{3,2,1,0:T(8,128)(2,1)} %get-tuple-element.106.q_ref.refs_1_, bf16[3,4,896,128]{3,2,1,0:T(8,128)(2,1)} %get-tuple-element.107.k_ref.refs_2_, ...), custom_call_target="tpu_custom_call" | custom-call | flops 2684354560 | bytes 3355443 | tf_op jit(solution)/shard_map/attend_back/pallas_call | solution.py:314
  442.9 1.2 copy-done.15
  444.1 2.0 copy-done.29
  446.0 1.9 fusion.refs_18_
  447.9 2.6 collective-permute-start.16
  452.3 120.6 %tail.1 = (bf16[1,512,1088]{2,1,0:T(8,128)(2,1)}, bf16[1,384,1088]{2,1,0:T(8,128)(2,1)}, bf16[544,3264]{1,0:T(8,128)(2,1)}, bf16[544,1088]{1,0:T(8,128)(2,1)}, f32[16,1152]{1,0:T(8,128)}) custom-call(bf16[1,4,896,128]{3,2,1,0:T(8,128)(2,1)} %get-tuple-element.152.refs_10_.refs_0_, bf16[1,4,896,128]{3,2,1,0:T(8,128)(2,1)} %get-tuple-element.167.refs_0_.refs_1_, ...), custom_call_target="tpu_custom_call" | custom-call | flops 17968398336 | bytes 31457280 | tf_op jit(solution)/shard_map/tail/pallas_call | solution.py:1843
  572.9 1.4 slice.202
  574.3 1.7 slice_reduce_fusion
  577.7 1.5 fusion.11.refs_0_
  579.3 2.2 collective-permute-start.17
  581.6 1.2 add_convert_fusion.refs_1_
  583.3 5.6 convert_element_type.240
  588.9 1.6 convert_element_type.241
  590.5 1.4 copy.65
  591.9 1.3 copy.66
  594.2 1.7 collective-permute-done.19
  597.1 1.6 maximum_convert_fusion
  598.8 1.2 broadcast_select_fusion.1
  600.0 1.6 convert_bitcast_fusion
  (141 shorter events, 21.4 us)
Async XLA Ops:
  74.6 72.4 %copy-start.35 = (f32[1088]{0:T(1024)S(1)}, f32[1088]{0:T(1024)}, u32[]{:S(2)}) copy-start(f32[1088]{0:T(1024)} %param.26) | copy-start | bytes 13060
  74.6 72.4 %copy-start.36 = (f32[1088]{0:T(1024)S(1)}, f32[1088]{0:T(1024)}, u32[]{:S(2)}) copy-start(f32[1088]{0:T(1024)} %param.25) | copy-start | bytes 13060
  74.6 72.5 %copy-start.37 = (f32[1088]{0:T(1024)S(1)}, f32[1088]{0:T(1024)}, u32[]{:S(2)}) copy-start(f32[1088]{0:T(1024)} %param.27) | copy-start | bytes 13060
  144.9 74.5 %collective-permute-start.1 = (bf16[560,1088]{1,0:T(8,128)(2,1)}, bf16[560,1088]{1,0:T(8,128)(2,1)S(1)}, u32[]{:S(2)}, u32[]{:S(2)}) collective-permute-start(bf16[560,1088]{1,0:T(8,128)(2,1)} %get-tuple-element.122.refs_5_), channel_id=1, source_target_pairs={{0,16},{16,0},{1,17},{17,1},{2,18},{18,2},{3,19},{19,3},{4,20},{20... | collective-permute-start | bytes 3655688 | tf_op jit(solution)/shard_map/ppermute | solution.py:276
  146.5 73.0 %collective-permute-start = (bf16[560,1088]{1,0:T(8,128)(2,1)}, bf16[560,1088]{1,0:T(8,128)(2,1)}, u32[]{:S(2)}, u32[]{:S(2)}) collective-permute-start(bf16[560,1088]{1,0:T(8,128)(2,1)} %get-tuple-element.112.refs_3_.refs_4_), channel_id=1, source_target_pairs={{0,16},{16,0},{1,17},{17,1},{2,18},{18,2},{3,19},{19,3},{4,20},{20... | collective-permute-start | bytes 3655688 | tf_op jit(solution)/shard_map/ppermute | solution.py:276
  147.0 13.4 %copy-start.17 = (f32[1,1088]{1,0:T(1,128)}, f32[1,1088]{1,0:T(1,128)S(1)}, u32[]{:S(2)}) copy-start(f32[1,1088]{1,0:T(1,128)S(1)} %broadcast_in_dim.36.refs_4_.refs_5_) | copy-start | bytes 13060
  147.1 1.5 copy-start
  148.6 1.3 copy-start.1
  220.2 3.6 copy-start.38
  220.2 5.4 copy-start.2
  220.2 4.3 collective-permute-start.2
  220.2 5.0 collective-permute-start.3
  220.7 97.7 %collective-permute-start.5 = (bf16[2,2,136,1088]{3,2,1,0:T(8,128)(2,1)}, bf16[2,2,136,1088]{3,2,1,0:T(8,128)(2,1)}, u32[]{:S(2)}, u32[]{:S(2)}) collective-permute-start(bf16[2,2,136,1088]{3,2,1,0:T(8,128)(2,1)} %get-tuple-element.155), channel_id=1, source_target_pairs={{0,8},{4,12},{8,0},{12,4},{1,9},{5,13},{9,1},{13,5},{2,10},{6,14},... | collective-permute-start | bytes 3551240 | tf_op jit(solution)/shard_map/ppermute | solution.py:276
  222.5 159.4 %collective-permute-start.7 = (bf16[2,272,1088]{2,1,0:T(8,128)(2,1)}, bf16[2,272,1088]{2,1,0:T(8,128)(2,1)}, u32[]{:S(2)}, u32[]{:S(2)}) collective-permute-start(bf16[2,272,1088]{2,1,0:T(8,128)(2,1)} %get-tuple-element.157), channel_id=1, source_target_pairs={{0,3},{1,0},{2,1},{3,2},{4,7},{5,4},{6,5},{7,6},{8,11},{9,8},{10,9... | collective-permute-start | bytes 3551240 | tf_op jit(solution)/shard_map/ppermute | solution.py:281
  285.5 96.5 %collective-permute-start.8 = (bf16[2,272,1088]{2,1,0:T(8,128)(2,1)}, bf16[2,272,1088]{2,1,0:T(8,128)(2,1)}, u32[]{:S(2)}, u32[]{:S(2)}) collective-permute-start(bf16[2,272,1088]{2,1,0:T(8,128)(2,1)} %get-tuple-element.140.refs_10_), channel_id=1, source_target_pairs={{0,1},{1,2},{2,3},{3,0},{4,5},{5,6},{6,7},{7,4},{8,9},{9,10},{10,1... | collective-permute-start | bytes 3551240 | tf_op jit(solution)/shard_map/ppermute | solution.py:281
  286.1 95.9 %collective-permute-start.9 = (bf16[2,272,1088]{2,1,0:T(8,128)(2,1)}, bf16[2,272,1088]{2,1,0:T(8,128)(2,1)}, u32[]{:S(2)}, u32[]{:S(2)}) collective-permute-start(bf16[2,272,1088]{2,1,0:T(8,128)(2,1)} %get-tuple-element.141.refs_11_), channel_id=1, source_target_pairs={{0,2},{1,3},{2,0},{3,1},{4,6},{5,7},{6,4},{7,5},{8,10},{9,11},{10,... | collective-permute-start | bytes 3551240 | tf_op jit(solution)/shard_map/ppermute | solution.py:281
  316.3 65.7 %collective-permute-start.6 = (bf16[2,2,136,1088]{3,2,1,0:T(8,128)(2,1)}, bf16[2,2,136,1088]{3,2,1,0:T(8,128)(2,1)S(1)}, u32[]{:S(2)}, u32[]{:S(2)}) collective-permute-start(bf16[2,2,136,1088]{3,2,1,0:T(8,128)(2,1)} %behind.9), channel_id=1, source_target_pairs={{0,8},{4,12},{8,0},{12,4},{1,9},{5,13},{9,1},{13,5},{2,10},{6,14},... | collective-permute-start | bytes 3551240 | tf_op jit(solution)/shard_map/ppermute | solution.py:276
  318.4 63.6 %collective-permute-start.4 = (bf16[2,272,1088]{2,1,0:T(8,128)(2,1)}, bf16[2,272,1088]{2,1,0:T(8,128)(2,1)S(1)}, u32[]{:S(2)}, u32[]{:S(2)}) collective-permute-start(bf16[2,272,1088]{2,1,0:T(8,128)(2,1)} %get-tuple-element.154), channel_id=1, source_target_pairs={{0,4},{4,0},{8,12},{12,8},{1,5},{5,1},{9,13},{13,9},{2,6},{6,2},{1... | collective-permute-start | bytes 3551240 | tf_op jit(solution)/shard_map/ppermute | solution.py:276
  384.4 3.4 copy-start.31
  386.3 1.9 copy-start.23
  386.3 56.5 %collective-permute-start.10 = (bf16[272,1088]{1,0:T(8,128)(2,1)S(1)}, bf16[272,1088]{1,0:T(8,128)(2,1)S(1)}, u32[]{:S(2)}, u32[]{:S(2)}) collective-permute-start(bf16[272,1088]{1,0:T(8,128)(2,1)S(1)} %fusion.4.refs_19_), channel_id=1, source_target_pairs={{0,16},{16,0},{1,17},{17,1},{2,18},{18,2},{3,19},{19,3},{4,20},{20... | collective-permute-start | bytes 1775624 | tf_op jit(solution)/shard_map/ppermute | solution.py:276
  387.9 2.4 copy-start.30
  388.2 3.7 copy-start.20
  388.2 3.7 copy-start.21
  388.2 54.6 %collective-permute-start.12 = (bf16[2,136,1088]{2,1,0:T(8,128)(2,1)S(1)}, bf16[2,136,1088]{2,1,0:T(8,128)(2,1)S(1)}, u32[]{:S(2)}, u32[]{:S(2)}) collective-permute-start(bf16[2,136,1088]{2,1,0:T(8,128)(2,1)S(1)} %get-tuple-element.240.refs_17_), channel_id=1, source_target_pairs={{0,1},{1,2},{2,3},{3,0},{4,5},{5,6},{6,7},{7,4},{8,9},{9,10},{10,1... | collective-permute-start | bytes 1775624 | tf_op jit(solution)/shard_map/ppermute | solution.py:281
  390.1 52.8 %collective-permute-start.13 = (bf16[2,136,1088]{2,1,0:T(8,128)(2,1)S(1)}, bf16[2,136,1088]{2,1,0:T(8,128)(2,1)S(1)}, u32[]{:S(2)}, u32[]{:S(2)}) collective-permute-start(bf16[2,136,1088]{2,1,0:T(8,128)(2,1)S(1)} %get-tuple-element.239.refs_18_), channel_id=1, source_target_pairs={{0,2},{1,3},{2,0},{3,1},{4,6},{5,7},{6,4},{7,5},{8,10},{9,11},{10,... | collective-permute-start | bytes 1775624 | tf_op jit(solution)/shard_map/ppermute | solution.py:281
  390.2 4.0 copy-start.32
  391.9 3.5 copy-start.22
  392.0 58.6 %copy-start.24 = (bf16[1,2,136,1088]{3,2,1,0:T(8,128)(2,1)}, bf16[1,2,136,1088]{3,2,1,0:T(8,128)(2,1)S(1)}, u32[]{:S(2)}) copy-start(bf16[1,2,136,1088]{3,2,1,0:T(8,128)(2,1)S(1)} %get-tuple-element.235) | copy-start | bytes 1775620
  392.0 50.9 %collective-permute-start.11 = (bf16[2,136,1088]{2,1,0:T(8,128)(2,1)S(1)}, bf16[2,136,1088]{2,1,0:T(8,128)(2,1)S(1)}, u32[]{:S(2)}, u32[]{:S(2)}) collective-permute-start(bf16[2,136,1088]{2,1,0:T(8,128)(2,1)S(1)} %get-tuple-element.236.refs_16_), channel_id=1, source_target_pairs={{0,3},{1,0},{2,1},{3,2},{4,7},{5,4},{6,5},{7,6},{8,11},{9,8},{10,9... | collective-permute-start | bytes 1775624 | tf_op jit(solution)/shard_map/ppermute | solution.py:281
  395.4 1.3 copy-start.19
  395.4 56.8 %collective-permute-start.14 = (bf16[272,1088]{1,0:T(8,128)(2,1)S(1)}, bf16[272,1088]{1,0:T(8,128)(2,1)}, u32[]{:S(2)}, u32[]{:S(2)}) collective-permute-start(bf16[272,1088]{1,0:T(8,128)(2,1)S(1)} %get-tuple-element.238.refs_20_), channel_id=1, source_target_pairs={{0,16},{16,0},{1,17},{17,1},{2,18},{18,2},{3,19},{19,3},{4,20},{20... | collective-permute-start | bytes 1775624 | tf_op jit(solution)/shard_map/ppermute | solution.py:276
  444.0 2.0 copy-start.29
  444.1 6.5 %copy-start.8 = (bf16[2,136,1088]{2,1,0:T(8,128)(2,1)}, bf16[2,136,1088]{2,1,0:T(8,128)(2,1)S(1)}, u32[]{:S(2)}) copy-start(bf16[2,136,1088]{2,1,0:T(8,128)(2,1)S(1)} %get-tuple-element.169) | copy-start | bytes 1775620
  444.1 6.5 %copy-start.10 = (bf16[2,136,1088]{2,1,0:T(8,128)(2,1)}, bf16[2,136,1088]{2,1,0:T(8,128)(2,1)S(1)}, u32[]{:S(2)}) copy-start(bf16[2,136,1088]{2,1,0:T(8,128)(2,1)S(1)} %get-tuple-element.170) | copy-start | bytes 1775620
  444.1 6.5 %copy-start.11 = (bf16[2,136,1088]{2,1,0:T(8,128)(2,1)}, bf16[2,136,1088]{2,1,0:T(8,128)(2,1)S(1)}, u32[]{:S(2)}) copy-start(bf16[2,136,1088]{2,1,0:T(8,128)(2,1)S(1)} %get-tuple-element.168) | copy-start | bytes 1775620
  447.9 4.4 copy-start.25
  447.9 128.1 %collective-permute-start.16 = (bf16[272,1088]{1,0:T(8,128)(2,1)S(1)}, bf16[272,1088]{1,0:T(8,128)(2,1)S(1)}, u32[]{:S(2)}, u32[]{:S(2)}) collective-permute-start(bf16[272,1088]{1,0:T(8,128)(2,1)S(1)} %fusion.refs_18_), channel_id=1, source_target_pairs={{0,8},{4,12},{8,0},{12,4},{1,9},{5,13},{9,1},{13,5},{2,10},{6,14},... | collective-permute-start | bytes 1775624 | tf_op jit(solution)/shard_map/ppermute | solution.py:276
  451.4 124.6 %collective-permute-start.15 = (bf16[136,1088]{1,0:T(8,128)(2,1)}, bf16[136,1088]{1,0:T(8,128)(2,1)S(1)}, u32[]{:S(2)}, u32[]{:S(2)}) collective-permute-start(bf16[136,1088]{1,0:T(8,128)(2,1)} %fusion.16.refs_17_), channel_id=1, source_target_pairs={{0,16},{16,0},{1,17},{17,1},{2,18},{18,2},{3,19},{19,3},{4,20},{20... | collective-permute-start | bytes 887816 | tf_op jit(solution)/shard_map/ppermute | solution.py:276
  572.9 4.8 copy-start.9
  576.9 4.7 copy-start.26
  577.7 5.6 copy-start.4
  577.7 5.6 copy-start.7
  579.2 4.1 copy-start.3
  579.3 13.9 %collective-permute-start.17 = (bf16[136,1088]{1,0:T(8,128)(2,1)S(1)}, bf16[136,1088]{1,0:T(8,128)(2,1)}, u32[]{:S(2)}, u32[]{:S(2)}) collective-permute-start(bf16[136,1088]{1,0:T(8,128)(2,1)S(1)} %fusion.11.refs_0_), channel_id=1, source_target_pairs={{0,8},{4,12},{8,0},{12,4},{1,9},{5,13},{9,1},{13,5},{2,10},{6,14},... | collective-permute-start | bytes 887816 | tf_op jit(solution)/shard_map/ppermute | solution.py:276
  581.4 12.8 %collective-permute-start.18 = (bf16[136,1088]{1,0:T(8,128)(2,1)S(1)}, bf16[136,1088]{1,0:T(8,128)(2,1)S(1)}, u32[]{:S(2)}, u32[]{:S(2)}) collective-permute-start(bf16[136,1088]{1,0:T(8,128)(2,1)S(1)} %fusion.11.refs_0_), channel_id=1, source_target_pairs={{0,4},{4,0},{8,12},{12,8},{1,5},{5,1},{9,13},{13,9},{2,6},{6,2},{1... | collective-permute-start | bytes 887816 | tf_op jit(solution)/shard_map/ppermute | solution.py:276
  581.5 14.4 %collective-permute-start.19 = (bf16[136,1088]{1,0:T(8,128)(2,1)S(1)}, bf16[136,1088]{1,0:T(8,128)(2,1)}, u32[]{:S(2)}, u32[]{:S(2)}) collective-permute-start(bf16[136,1088]{1,0:T(8,128)(2,1)S(1)} %fusion.11.refs_0_), channel_id=1, source_target_pairs={{0,12},{4,8},{8,4},{12,0},{1,13},{5,9},{9,5},{13,1},{2,14},{6,10},... | collective-permute-start | bytes 887816 | tf_op jit(solution)/shard_map/ppermute | solution.py:276
  582.8 15.9 %collective-permute-start.20 = (bf16[272,1088]{1,0:T(8,128)(2,1)S(1)}, bf16[272,1088]{1,0:T(8,128)(2,1)}, u32[]{:S(2)}, u32[]{:S(2)}) collective-permute-start(bf16[272,1088]{1,0:T(8,128)(2,1)S(1)} %add_convert_fusion.refs_1_), channel_id=1, source_target_pairs={{0,4},{4,0},{8,12},{12,8},{1,5},{5,1},{9,13},{13,9},{2,6},{6,2},{1... | collective-permute-start | bytes 1775624 | tf_op jit(solution)/shard_map/ppermute | solution.py:276
  (12 other events, 12.5 us)
